TPU v7x, 32 devices: a whole 2x2x4 slice. The times are simulated.
32 devices in a mesh: grp: 2 (over y), sub: 16 (over z, x, core).
Axes of the slice: x: 2, y: 2, z: 4, core: 2. Of those that a mesh axis runs over, the one named last changes fastest.
Arguments:
- omega: bfloat16 [24576, 256], P(('grp', 'sub')), may hold values from -6 to 6
- adj_tests: bfloat16 [256, 24576], P('sub', 'grp'), may hold values from -6 to 6
- near_tiles: bfloat16 [192, 12, 128, 128], P(('grp', 'sub')), may hold values from -0.15625 to 0.15625
- tile_cols: int32 [192, 12], P(('grp', 'sub')), may hold values from 0 to 191, as said below
- leaf_perms: int32 [32, 2, 768], P(('grp', 'sub')), may hold values from 0 to 767, each once within a row
- leaf_interp: bfloat16 [32, 2, 672, 96], P(('grp', 'sub')), may hold values from -0.125 to 0.125
- node_perms: int32 [32, 5, 2, 192], P(('grp', 'sub')), may hold values from 0 to 191, as said below
- node_maps: bfloat16 [32, 5, 4, 96, 96], P(('grp', 'sub')), as said below
Outputs:
- path_panels: bfloat16 [32, 5, 2, 96, 256], P(('grp', 'sub'))
Inputs may be any that keep to these rules, and one draw needn't show every extreme that they name: `tile_cols`: the 12 column tiles of tile row q are distinct and lie in the tile rows of its own leaf or of the leaves just before and after it within the same block of 16 leaves; each block of 16 leaves is one index of grp. `leaf_perms`: each of the two orders of a leaf is a permutation of 0 to 767. `node_perms`: each order is a permutation of 0 to 191; entries [d, j] are equal for all d with the same d // 2^(j+1). `node_maps`: entries [d, j] are equal for all d with the same d // 2^(j+1).
All inputs are finite; a program needn't handle non-finite values.
Results may differ from a plain program's by a relative error of at most 0.0065.
Values may be sent and summed in bfloat16 or wider, within the bound.
No kernel may reach another device: no remote copies, remote signals or barrier semaphores. Data moves between devices by JAX's collectives and lax.ppermute only.
A program may use at most 64 MiB of HBM per device.

v0:
```python
import jax
import jax.numpy as jnp
from jax import lax
from jax.sharding import PartitionSpec as P

HIGHEST = lax.Precision.HIGHEST


def extended(block, sides, width):
    for axis, dim in sides:
        count = lax.axis_size(axis)
        forward = [(i, i + 1) for i in range(count - 1)]
        backward = [(target, source) for source, target in forward]
        low = lax.ppermute(
            lax.slice_in_dim(block, block.shape[dim] - width, None, axis=dim), axis, forward
        )
        high = lax.ppermute(lax.slice_in_dim(block, 0, width, axis=dim), axis, backward)
        block = jnp.concatenate([low, block, high], axis=dim)
    return block


def passed_along(block, axis, distance):
    devices = range(lax.axis_size(axis))
    route = [(i - distance, i) for i in devices if i - distance in devices]
    return lax.ppermute(block, axis, route)


def partner_2(block, axis, distance):
    count = lax.axis_size(axis)
    route = []
    for low in range(count):
        high = low | 1 << distance
        if high != low and high < count:
            route += [(low, high), (high, low)]
    return lax.ppermute(block, axis, route)


def for_sending(x):
    return jax.tree.map(lambda a: a.astype(jnp.bfloat16) if a.dtype == jnp.float32 else a, x)


def apply_rows(matrix, panel):
    return jnp.einsum("...ij,...js->...is", matrix, panel, precision=HIGHEST)


def apply_cols(matrix, panel):
    return jnp.einsum("...ji,...js->...is", matrix, panel, precision=HIGHEST)


def pick_rows(panel, order):
    return jnp.take_along_axis(panel, order[..., None], axis=-2)


def squeeze_node(
    fwd_rows, fwd_tests, adj_rows, adj_panel, row_order, col_order, row_interp, col_interp
):
    rank = row_interp.shape[-1]
    fwd_skel = pick_rows(fwd_rows, row_order[..., :rank])
    test_skel = pick_rows(fwd_tests, col_order[..., :rank]) + apply_cols(
        col_interp, pick_rows(fwd_tests, col_order[..., rank:])
    )
    adj_skel = pick_rows(adj_rows, col_order[..., :rank])
    adj_test_skel = pick_rows(adj_panel, row_order[..., :rank]) + apply_cols(
        row_interp, pick_rows(adj_panel, row_order[..., rank:])
    )
    return (fwd_skel, test_skel, adj_skel, adj_test_skel)


def merge_pair(lower, upper, maps, orders):
    maps = maps.astype(jnp.float32)
    row_interp = maps[..., 0, :, :]
    col_interp = maps[..., 1, :, :]
    low_high = maps[..., 2, :, :]
    high_low = maps[..., 3, :, :]
    fwd_rows = jnp.concatenate(
        [lower[0] - apply_rows(low_high, upper[1]), upper[0] - apply_rows(high_low, lower[1])],
        axis=-2,
    )
    fwd_tests = jnp.concatenate([lower[1], upper[1]], axis=-2)
    adj_rows = jnp.concatenate(
        [lower[2] - apply_cols(high_low, upper[3]), upper[2] - apply_cols(low_high, lower[3])],
        axis=-2,
    )
    adj_panel = jnp.concatenate([lower[3], upper[3]], axis=-2)
    return squeeze_node(
        fwd_rows,
        fwd_tests,
        adj_rows,
        adj_panel,
        orders[..., 0, :],
        orders[..., 1, :],
        row_interp,
        col_interp,
    )


def pair_up(panels, partner, upper_side):
    lower = tuple((jnp.where(upper_side, b, a) for a, b in zip(panels, partner)))
    upper = tuple((jnp.where(upper_side, a, b) for a, b in zip(panels, partner)))
    return (lower, upper)


def local(omega, adj_tests, near_tiles, tile_cols, leaf_perms, leaf_interp, node_perms, node_maps):
    rows_dev, samples = omega.shape
    tile_size = near_tiles.shape[-1]
    per_dev = rows_dev // tile_size
    sub_count = lax.axis_size("sub")
    sub_place = lax.axis_index("sub")
    grp_place = lax.axis_index("grp")
    device = grp_place * sub_count + sub_place
    local_cols = tile_cols - (device - 1) * per_dev
    widened = extended(omega, (("sub", 0),), rows_dev)
    blocks = widened.reshape(3 * per_dev, tile_size, samples)
    picked = jnp.take(blocks, local_cols, axis=0)
    forward = jnp.einsum(
        "rtij,rtjs->ris", near_tiles, picked, preferred_element_type=jnp.float32
    ).reshape(rows_dev, samples)
    adj_cols = lax.all_to_all(adj_tests, "sub", split_axis=1, concat_axis=0, tiled=True)
    adj_blocks = adj_cols.reshape(samples, per_dev, tile_size)
    onehot = (
        local_cols[:, :, None] == jnp.arange(3 * per_dev, dtype=jnp.int32)[None, None, :]
    ).astype(jnp.bfloat16)
    placed = jnp.einsum(
        "rtk,rtij->rkij", onehot, near_tiles, preferred_element_type=jnp.float32
    ).astype(jnp.bfloat16)
    spread = jnp.einsum("rkij,sri->kjs", placed, adj_blocks, preferred_element_type=jnp.float32)
    lower_rim = spread[:per_dev].reshape(rows_dev, samples)
    own_part = spread[per_dev : 2 * per_dev].reshape(rows_dev, samples)
    upper_rim = spread[2 * per_dev :].reshape(rows_dev, samples)
    from_after = passed_along(lower_rim.astype(jnp.bfloat16), "sub", -1).astype(lower_rim.dtype)
    from_before = passed_along(upper_rim.astype(jnp.bfloat16), "sub", 1).astype(upper_rim.dtype)
    adjoint = own_part + from_after + from_before
    rank = leaf_interp.shape[-1]
    row_order = leaf_perms[0, 0]
    col_order = leaf_perms[0, 1]
    fwd_skel = forward[row_order[:rank]]
    test_skel = omega[col_order[:rank]].astype(jnp.float32) + lax.dot_general(
        leaf_interp[0, 1],
        omega[col_order[rank:]],
        (((0,), (0,)), ((), ())),
        preferred_element_type=jnp.float32,
    )
    adj_skel = adjoint[col_order[:rank]]
    ordered = jnp.take(adj_cols, row_order, axis=1)
    adj_test_skel = ordered[:, :rank].T.astype(jnp.float32) + lax.dot_general(
        leaf_interp[0, 0],
        ordered[:, rank:],
        (((0,), (1,)), ((), ())),
        preferred_element_type=jnp.float32,
    )
    panels = (fwd_skel, test_skel, adj_skel, adj_test_skel)
    sub_bits = lax.axis_size("sub").bit_length() - 1
    grp_bits = lax.axis_size("grp").bit_length() - 1
    results = []
    for bit in range(sub_bits):
        partner = partner_2((panels[0], panels[1], panels[2], panels[3]), "sub", bit)
        upper_side = jnp.right_shift(sub_place, bit) & 1 == 1
        lower, upper = pair_up(panels, partner, upper_side)
        panels = merge_pair(lower, upper, node_maps[0, bit], node_perms[0, bit])
        results.append(jnp.stack([panels[0], panels[2]]).astype(jnp.bfloat16))
    for bit in range(grp_bits):
        partner = partner_2(
            (
                for_sending(panels[0]),
                for_sending(panels[1]),
                for_sending(panels[2]),
                for_sending(panels[3]),
            ),
            "grp",
            bit,
        )
        upper_side = jnp.right_shift(grp_place, bit) & 1 == 1
        lower, upper = pair_up(panels, partner, upper_side)
        level = sub_bits + bit
        panels = merge_pair(lower, upper, node_maps[0, level], node_perms[0, level])
        results.append(jnp.stack([panels[0], panels[2]]).astype(jnp.bfloat16))
    return jnp.stack(results)[None]


def solution(mesh):
    placed = (
        P(("grp", "sub"), None),
        P("sub", "grp"),
        P(("grp", "sub"), None, None, None),
        P(("grp", "sub"), None),
        P(("grp", "sub"), None, None),
        P(("grp", "sub"), None, None, None),
        P(("grp", "sub"), None, None, None),
        P(("grp", "sub"), None, None, None, None),
    )
    return jax.shard_map(
        local,
        mesh=mesh,
        in_specs=placed,
        out_specs=P(("grp", "sub"), None, None, None, None),
        check_vma=False,
    )
```

profile of v0, /device:TPU:0, one launch (start us, length us, event | category | flops | bytes accessed | tf_op | source)
XLA Modules:
  0.0 201.7 jit_solution(8161583130632190482)
XLA Ops:
  1.6 3.8 %collective-permute-start = (bf16[768,256]{1,0:T(8,128)(2,1)}, bf16[768,256]{1,0:T(8,128)(2,1)}, u32[]{:S(2)}, u32[]{:S(2)}) collective-permute-start(bf16[768,256]{1,0:T(8,128)(2,1)} %param.10), channel_id=1, source_target_pairs={{0,1},{1,2},{2,3},{3,4},{4,5},{5,6},{6,7},{7,8},{8,9},{9,10},{10,1... | collective-permute-start | bytes 1179656 | tf_op jit(solution)/shard_map/ppermute | solution.py:14
  7.1 7.5 %all-to-all-start = ((bf16[16,16,768]{2,0,1:T(8,128)(2,1)}), bf16[16,16,768]{2,0,1:T(8,128)(2,1)S(1)}, u32[]{:S(2)}, u32[]{:S(2)}) async-start(bf16[16,16,768]{2,0,1:T(8,128)(2,1)} %bitcast.516), calls=%async_computation | async-start | bytes 786432 | tf_op jit(solution)/shard_map/all_to_all | solution.py:118
  16.8 2.8 %gather_fusion.3 = bf16[672,256]{1,0:T(8,128)(2,1)S(1)} fusion(bf16[768,256]{1,0:T(8,128)(2,1)S(1)} %copy-done.1, s32[1024]{0:T(1024)S(1)} %pad_clamp_fusion.19), kind=kCustom, calls=%fused_computation.29 | custom fusion | bytes 690816 | tf_op jit(solution)/shard_map/gather | solution.py:139
  26.5 3.8 %fusion.7 = bf16[6,18,128,128]{3,1,2,0:T(8,128)(2,1)} fusion(bf16[6,12,128,128]{3,2,1,0:T(8,128)(2,1)S(1)} %copy-done, s32[6,12]{1,0:T(8,128)S(1)} %get-tuple-element.17), kind=kOutput, calls=%fused_computation.39 | convolution fusion | flops 44238096 | bytes 5898528 | tf_op jit(solution)/shard_map/rtk,rtij->rkij/dot_general | solution.py:123
  44.7 2.1 %collective-permute-done.9 = f32[96,256]{1,0:T(8,128)S(1)} collective-permute-done((f32[96,256]{1,0:T(8,128)S(1)}, f32[96,256]{1,0:T(8,128)S(1)}, u32[]{:S(2)}, u32[]{:S(2)}) %collective-permute-start.9) | collective-permute-done | bytes 98336 | tf_op jit(solution)/shard_map/ppermute | solution.py:35
  59.1 2.7 %collective-permute-start.17 = (f32[96,256]{1,0:T(8,128)S(1)}, f32[96,256]{1,0:T(8,128)}, u32[]{:S(2)}, u32[]{:S(2)}) collective-permute-start(f32[96,256]{1,0:T(8,128)S(1)} %select_add_fusion.3), channel_id=1, source_target_pairs={{0,8},{8,0},{1,9},{9,1},{2,10},{10,2},{3,11},{11,3},{4,12},{12,4},... | collective-permute-start | bytes 294920 | tf_op jit(solution)/shard_map/ppermute | solution.py:35
  61.8 2.2 %pad_maximum_fusion = bf16[2304,256]{1,0:T(8,128)(2,1)} fusion(bf16[768,256]{1,0:T(8,128)(2,1)} %collective-permute-done.1, bf16[768,256]{1,0:T(8,128)(2,1)S(1)} %copy-done.1, bf16[768,256]{1,0:T(8,128)(2,1)} %collective-permute-done), kind=kLoop, calls=%fused_computation.42 | loop fusion | flops 3538944 | bytes 2359296 | tf_op jit(solution)/shard_map/concatenate | solution.py:18
  64.0 6.8 %gather_fusion = bf16[72,128,256]{2,1,0:T(8,128)(2,1)} fusion(bf16[18,128,256]{2,1,0:T(8,128)(2,1)} %bitcast.517, s32[1024]{0:T(1024)S(1)} %pad_clamp_fusion.22), kind=kCustom, calls=%fused_computation.26 | custom fusion | bytes 9437472 | tf_op jit(solution)/shard_map/jit(_take)/gather | solution.py:114
  70.8 4.4 %fusion = f32[6,256,128,1]{1,2,3,0:T(8,128)} fusion(bf16[6,12,128,128]{3,2,1,0:T(8,128)(2,1)S(1)} %copy-done, bf16[6,12,128,256]{3,2,1,0:T(8,128)(2,1)} %bitcast.518, pred[6,12]{1,0:T(8,128)(4,1)S(1)} %copy-done.40), kind=kOutput, calls=%fused_computation.32 | convolution fusion | flops 606339072 | bytes 7864392 | tf_op jit(solution)/shard_map/rtij,rtjs->ris/dot_general | solution.py:115
  75.2 2.0 gather_fusion.1
  94.6 1.9 fusion.199
  103.3 3.7 %fusion.197 = (bf16[18,128,256]{2,1,0:T(8,128)(2,1)S(1)}, f32[18,128,256]{2,1,0:T(8,128)S(1)}) fusion(bf16[256,6,128]{2,1,0:T(8,128)(2,1)} %reshape.407, bf16[6,18,128,128]{3,1,2,0:T(8,128)(2,1)} %fusion.7), kind=kOutput, calls=%fused_computation.367 | convolution fusion | flops 906559488 | bytes 7471104 | tf_op jit(solution)/shard_map/rkij,sri->kjs/dot_general | solution.py:126
  108.9 2.0 %collective-permute-start.5 = (bf16[768,256]{1,0:T(8,128)(2,1)}, bf16[768,256]{1,0:T(8,128)(2,1)}, u32[]{:S(2)}, u32[]{:S(2)}) collective-permute-start(bf16[768,256]{1,0:T(8,128)(2,1)} %bitcast.31), channel_id=1, source_target_pairs={{0,1},{1,2},{2,3},{3,4},{4,5},{5,6},{6,7},{7,8},{8,9},{9,10},{10,1... | collective-permute-start | bytes 1179656 | tf_op jit(solution)/shard_map/ppermute | solution.py:25
  112.5 2.7 %gather_fusion.5 = bf16[768,256]{1,0:T(8,128)(2,1)S(1)} fusion(bf16[256,768]{0,1:T(8,128)(2,1)S(1)} %copy.22, s32[1024]{0:T(1024)S(1)} %pad_clamp_fusion.17), kind=kCustom, calls=%fused_computation.31 | custom fusion | bytes 789504 | tf_op jit(solution)/shard_map/jit(_take)/gather | solution.py:144
  117.2 2.2 %collective-permute-start.7 = (f32[96,256]{1,0:T(8,128)S(1)}, f32[96,256]{1,0:T(8,128)S(1)}, u32[]{:S(2)}, u32[]{:S(2)}) collective-permute-start(f32[96,256]{1,0:T(8,128)S(1)} %fusion.14), channel_id=1, source_target_pairs={{0,1},{1,0},{2,3},{3,2},{4,5},{5,4},{6,7},{7,6},{8,9},{9,8},{10,11... | collective-permute-start | bytes 294920 | tf_op jit(solution)/shard_map/ppermute | solution.py:35
  124.2 2.2 %collective-permute-done.20 = bf16[96,256]{1,0:T(8,128)(2,1)S(1)} collective-permute-done((bf16[96,256]{1,0:T(8,128)(2,1)S(1)}, bf16[96,256]{1,0:T(8,128)(2,1)S(1)}, u32[]{:S(2)}, u32[]{:S(2)}) %collective-permute-start.20) | collective-permute-done | bytes 49184 | tf_op jit(solution)/shard_map/ppermute | solution.py:35
  140.8 2.4 %collective-permute-start.15 = (f32[96,256]{1,0:T(8,128)S(1)}, f32[96,256]{1,0:T(8,128)S(1)}, u32[]{:S(2)}, u32[]{:S(2)}) collective-permute-start(f32[96,256]{1,0:T(8,128)S(1)} %select_add_fusion.4), channel_id=1, source_target_pairs={{0,4},{4,0},{1,5},{5,1},{2,6},{6,2},{3,7},{7,3},{8,12},{12,8},{9,1... | collective-permute-start | bytes 294920 | tf_op jit(solution)/shard_map/ppermute | solution.py:35
  150.6 3.3 %collective-permute-start.19 = (f32[96,256]{1,0:T(8,128)S(1)}, f32[96,256]{1,0:T(8,128)}, u32[]{:S(2)}, u32[]{:S(2)}) collective-permute-start(f32[96,256]{1,0:T(8,128)S(1)} %select_add_fusion.2), channel_id=1, source_target_pairs={{0,8},{8,0},{1,9},{9,1},{2,10},{10,2},{3,11},{11,3},{4,12},{12,4},... | collective-permute-start | bytes 294920 | tf_op jit(solution)/shard_map/ppermute | solution.py:35
  153.9 2.2 %fusion.16 = f32[768,256]{1,0:T(8,128)} fusion(f32[6,128,256]{2,1,0:T(8,128)S(1)} %copy-done.2, bf16[768,256]{1,0:T(8,128)(2,1)} %collective-permute-done.5, bf16[768,256]{1,0:T(8,128)(2,1)} %collective-permute-done.4), kind=kLoop, calls=%fused_computation.76 | loop fusion | flops 786432 | bytes 2359296 | tf_op jit(solution)/shard_map/add | solution.py:132
  156.1 2.0 %gather_fusion.4 = f32[96,256]{1,0:T(8,128)S(1)} fusion(f32[768,256]{1,0:T(8,128)} %fusion.16, s32[1024]{0:T(1024)} %copy-done.29), kind=kCustom, calls=%fused_computation.30 | custom fusion | bytes 196992 | tf_op jit(solution)/shard_map/gather | solution.py:143
  162.7 1.8 fusion.198
  170.9 2.9 %collective-permute-done.10 = f32[96,256]{1,0:T(8,128)S(1)} collective-permute-done((f32[96,256]{1,0:T(8,128)S(1)}, f32[96,256]{1,0:T(8,128)S(1)}, u32[]{:S(2)}, u32[]{:S(2)}) %collective-permute-start.10) | collective-permute-done | bytes 98336 | tf_op jit(solution)/shard_map/ppermute | solution.py:35
  187.9 3.6 %collective-permute-done.18 = f32[96,256]{1,0:T(8,128)S(1)} collective-permute-done((f32[96,256]{1,0:T(8,128)S(1)}, f32[96,256]{1,0:T(8,128)S(1)}, u32[]{:S(2)}, u32[]{:S(2)}) %collective-permute-start.18) | collective-permute-done | bytes 98336 | tf_op jit(solution)/shard_map/ppermute | solution.py:35
  195.3 1.9 collective-permute-done.22
  (253 shorter events, 128.1 us)
Async XLA Ops:
  0.0 61.8 %collective-permute-start.1 = (bf16[768,256]{1,0:T(8,128)(2,1)}, bf16[768,256]{1,0:T(8,128)(2,1)}, u32[]{:S(2)}, u32[]{:S(2)}) collective-permute-start(bf16[768,256]{1,0:T(8,128)(2,1)} %param.10), channel_id=1, source_target_pairs={{1,0},{2,1},{3,2},{4,3},{5,4},{6,5},{7,6},{8,7},{9,8},{10,9},{11,1... | collective-permute-start | bytes 1179656 | tf_op jit(solution)/shard_map/ppermute | solution.py:17
  1.6 60.2 %collective-permute-start = (bf16[768,256]{1,0:T(8,128)(2,1)}, bf16[768,256]{1,0:T(8,128)(2,1)}, u32[]{:S(2)}, u32[]{:S(2)}) collective-permute-start(bf16[768,256]{1,0:T(8,128)(2,1)} %param.10), channel_id=1, source_target_pairs={{0,1},{1,2},{2,3},{3,4},{4,5},{5,6},{6,7},{7,8},{8,9},{9,10},{10,1... | collective-permute-start | bytes 1179656 | tf_op jit(solution)/shard_map/ppermute | solution.py:14
  7.1 94.9 %all-to-all-start = ((bf16[16,16,768]{2,0,1:T(8,128)(2,1)}), bf16[16,16,768]{2,0,1:T(8,128)(2,1)S(1)}, u32[]{:S(2)}, u32[]{:S(2)}) async-start(bf16[16,16,768]{2,0,1:T(8,128)(2,1)} %bitcast.516), calls=%async_computation | async-start | bytes 786432 | tf_op jit(solution)/shard_map/all_to_all | solution.py:118
  22.1 15.5 %collective-permute-start.3 = (f32[96,256]{1,0:T(8,128)}, f32[96,256]{1,0:T(8,128)S(1)}, u32[]{:S(2)}, u32[]{:S(2)}) collective-permute-start(f32[96,256]{1,0:T(8,128)} %fusion.15), channel_id=1, source_target_pairs={{0,1},{1,0},{2,3},{3,2},{4,5},{5,4},{6,7},{7,6},{8,9},{9,8},{10,11... | collective-permute-start | bytes 294920 | tf_op jit(solution)/shard_map/ppermute | solution.py:35
  41.7 5.1 %collective-permute-start.9 = (f32[96,256]{1,0:T(8,128)S(1)}, f32[96,256]{1,0:T(8,128)S(1)}, u32[]{:S(2)}, u32[]{:S(2)}) collective-permute-start(f32[96,256]{1,0:T(8,128)S(1)} %select_add_fusion.7), channel_id=1, source_target_pairs={{0,2},{2,0},{1,3},{3,1},{4,6},{6,4},{5,7},{7,5},{8,10},{10,8},{9,1... | collective-permute-start | bytes 294920 | tf_op jit(solution)/shard_map/ppermute | solution.py:35
  50.2 4.7 %collective-permute-start.13 = (f32[96,256]{1,0:T(8,128)S(1)}, f32[96,256]{1,0:T(8,128)S(1)}, u32[]{:S(2)}, u32[]{:S(2)}) collective-permute-start(f32[96,256]{1,0:T(8,128)S(1)} %select_add_fusion.5), channel_id=1, source_target_pairs={{0,4},{4,0},{1,5},{5,1},{2,6},{6,2},{3,7},{7,3},{8,12},{12,8},{9,1... | collective-permute-start | bytes 294920 | tf_op jit(solution)/shard_map/ppermute | solution.py:35
  59.1 18.1 %collective-permute-start.17 = (f32[96,256]{1,0:T(8,128)S(1)}, f32[96,256]{1,0:T(8,128)}, u32[]{:S(2)}, u32[]{:S(2)}) collective-permute-start(f32[96,256]{1,0:T(8,128)S(1)} %select_add_fusion.3), channel_id=1, source_target_pairs={{0,8},{8,0},{1,9},{9,1},{2,10},{10,2},{3,11},{11,3},{4,12},{12,4},... | collective-permute-start | bytes 294920 | tf_op jit(solution)/shard_map/ppermute | solution.py:35
  83.5 5.2 %collective-permute-start.8 = (f32[96,256]{1,0:T(8,128)}, f32[96,256]{1,0:T(8,128)}, u32[]{:S(2)}, u32[]{:S(2)}) collective-permute-start(f32[96,256]{1,0:T(8,128)} %get-tuple-element.15), channel_id=1, source_target_pairs={{0,2},{2,0},{1,3},{3,1},{4,6},{6,4},{5,7},{7,5},{8,10},{10,8},{9,1... | collective-permute-start | bytes 294920 | tf_op jit(solution)/shard_map/ppermute | solution.py:35
  93.1 4.9 %collective-permute-start.12 = (f32[96,256]{1,0:T(8,128)S(1)}, f32[96,256]{1,0:T(8,128)S(1)}, u32[]{:S(2)}, u32[]{:S(2)}) collective-permute-start(f32[96,256]{1,0:T(8,128)S(1)} %get-tuple-element.11), channel_id=1, source_target_pairs={{0,4},{4,0},{1,5},{5,1},{2,6},{6,2},{3,7},{7,3},{8,12},{12,8},{9,1... | collective-permute-start | bytes 294920 | tf_op jit(solution)/shard_map/ppermute | solution.py:35
  96.5 27.7 %collective-permute-start.21 = (bf16[96,256]{1,0:T(8,128)(2,1)}, bf16[96,256]{1,0:T(8,128)(2,1)}, u32[]{:S(2)}, u32[]{:S(2)}) collective-permute-start(bf16[96,256]{1,0:T(8,128)(2,1)} %get-tuple-element.80), channel_id=1, source_target_pairs={{0,16},{16,0},{1,17},{17,1},{2,18},{18,2},{3,19},{19,3},{4,20},{20... | collective-permute-start | bytes 147464 | tf_op jit(solution)/shard_map/ppermute | solution.py:35
  101.4 17.9 %collective-permute-start.16 = (f32[96,256]{1,0:T(8,128)S(1)}, f32[96,256]{1,0:T(8,128)S(1)}, u32[]{:S(2)}, u32[]{:S(2)}) collective-permute-start(f32[96,256]{1,0:T(8,128)S(1)} %get-tuple-element.7), channel_id=1, source_target_pairs={{0,8},{8,0},{1,9},{9,1},{2,10},{10,2},{3,11},{11,3},{4,12},{12,4},... | collective-permute-start | bytes 294920 | tf_op jit(solution)/shard_map/ppermute | solution.py:35
  108.9 45.0 %collective-permute-start.5 = (bf16[768,256]{1,0:T(8,128)(2,1)}, bf16[768,256]{1,0:T(8,128)(2,1)}, u32[]{:S(2)}, u32[]{:S(2)}) collective-permute-start(bf16[768,256]{1,0:T(8,128)(2,1)} %bitcast.31), channel_id=1, source_target_pairs={{0,1},{1,2},{2,3},{3,4},{4,5},{5,6},{6,7},{7,8},{8,9},{9,10},{10,1... | collective-permute-start | bytes 1179656 | tf_op jit(solution)/shard_map/ppermute | solution.py:25
  110.9 43.0 %collective-permute-start.4 = (bf16[768,256]{1,0:T(8,128)(2,1)}, bf16[768,256]{1,0:T(8,128)(2,1)}, u32[]{:S(2)}, u32[]{:S(2)}) collective-permute-start(bf16[768,256]{1,0:T(8,128)(2,1)} %bitcast.30), channel_id=1, source_target_pairs={{1,0},{2,1},{3,2},{4,3},{5,4},{6,5},{7,6},{8,7},{9,8},{10,9},{11,1... | collective-permute-start | bytes 1179656 | tf_op jit(solution)/shard_map/ppermute | solution.py:25
  117.2 11.2 %collective-permute-start.7 = (f32[96,256]{1,0:T(8,128)S(1)}, f32[96,256]{1,0:T(8,128)S(1)}, u32[]{:S(2)}, u32[]{:S(2)}) collective-permute-start(f32[96,256]{1,0:T(8,128)S(1)} %fusion.14), channel_id=1, source_target_pairs={{0,1},{1,0},{2,3},{3,2},{4,5},{5,4},{6,7},{7,6},{8,9},{9,8},{10,11... | collective-permute-start | bytes 294920 | tf_op jit(solution)/shard_map/ppermute | solution.py:35
  122.2 4.2 %collective-permute-start.20 = (bf16[96,256]{1,0:T(8,128)(2,1)S(1)}, bf16[96,256]{1,0:T(8,128)(2,1)S(1)}, u32[]{:S(2)}, u32[]{:S(2)}) collective-permute-start(bf16[96,256]{1,0:T(8,128)(2,1)S(1)} %select_convert_fusion.3), channel_id=1, source_target_pairs={{0,16},{16,0},{1,17},{17,1},{2,18},{18,2},{3,19},{19,3},{4,20},{20... | collective-permute-start | bytes 147464 | tf_op jit(solution)/shard_map/ppermute | solution.py:35
  131.1 4.7 %collective-permute-start.11 = (f32[96,256]{1,0:T(8,128)S(1)}, f32[96,256]{1,0:T(8,128)S(1)}, u32[]{:S(2)}, u32[]{:S(2)}) collective-permute-start(f32[96,256]{1,0:T(8,128)S(1)} %select_add_fusion.6), channel_id=1, source_target_pairs={{0,2},{2,0},{1,3},{3,1},{4,6},{6,4},{5,7},{7,5},{8,10},{10,8},{9,1... | collective-permute-start | bytes 294920 | tf_op jit(solution)/shard_map/ppermute | solution.py:35
  140.8 5.0 %collective-permute-start.15 = (f32[96,256]{1,0:T(8,128)S(1)}, f32[96,256]{1,0:T(8,128)S(1)}, u32[]{:S(2)}, u32[]{:S(2)}) collective-permute-start(f32[96,256]{1,0:T(8,128)S(1)} %select_add_fusion.4), channel_id=1, source_target_pairs={{0,4},{4,0},{1,5},{5,1},{2,6},{6,2},{3,7},{7,3},{8,12},{12,8},{9,1... | collective-permute-start | bytes 294920 | tf_op jit(solution)/shard_map/ppermute | solution.py:35
  150.6 7.6 %collective-permute-start.19 = (f32[96,256]{1,0:T(8,128)S(1)}, f32[96,256]{1,0:T(8,128)}, u32[]{:S(2)}, u32[]{:S(2)}) collective-permute-start(f32[96,256]{1,0:T(8,128)S(1)} %select_add_fusion.2), channel_id=1, source_target_pairs={{0,8},{8,0},{1,9},{9,1},{2,10},{10,2},{3,11},{11,3},{4,12},{12,4},... | collective-permute-start | bytes 294920 | tf_op jit(solution)/shard_map/ppermute | solution.py:35
  158.1 7.7 %collective-permute-start.6 = (f32[96,256]{1,0:T(8,128)S(1)}, f32[96,256]{1,0:T(8,128)}, u32[]{:S(2)}, u32[]{:S(2)}) collective-permute-start(f32[96,256]{1,0:T(8,128)S(1)} %gather_fusion.4), channel_id=1, source_target_pairs={{0,1},{1,0},{2,3},{3,2},{4,5},{5,4},{6,7},{7,6},{8,9},{9,8},{10,11... | collective-permute-start | bytes 294920 | tf_op jit(solution)/shard_map/ppermute | solution.py:35
  164.6 30.7 %collective-permute-start.23 = (bf16[96,256]{1,0:T(8,128)(2,1)}, bf16[96,256]{1,0:T(8,128)(2,1)}, u32[]{:S(2)}, u32[]{:S(2)}) collective-permute-start(bf16[96,256]{1,0:T(8,128)(2,1)} %get-tuple-element.78), channel_id=1, source_target_pairs={{0,16},{16,0},{1,17},{17,1},{2,18},{18,2},{3,19},{19,3},{4,20},{20... | collective-permute-start | bytes 147464 | tf_op jit(solution)/shard_map/ppermute | solution.py:35
  168.8 5.0 %collective-permute-start.10 = (f32[96,256]{1,0:T(8,128)S(1)}, f32[96,256]{1,0:T(8,128)S(1)}, u32[]{:S(2)}, u32[]{:S(2)}) collective-permute-start(f32[96,256]{1,0:T(8,128)S(1)} %get-tuple-element.19), channel_id=1, source_target_pairs={{0,2},{2,0},{1,3},{3,1},{4,6},{6,4},{5,7},{7,5},{8,10},{10,8},{9,1... | collective-permute-start | bytes 294920 | tf_op jit(solution)/shard_map/ppermute | solution.py:35
  178.7 4.7 %collective-permute-start.14 = (f32[96,256]{1,0:T(8,128)S(1)}, f32[96,256]{1,0:T(8,128)S(1)}, u32[]{:S(2)}, u32[]{:S(2)}) collective-permute-start(f32[96,256]{1,0:T(8,128)S(1)} %get-tuple-element.13), channel_id=1, source_target_pairs={{0,4},{4,0},{1,5},{5,1},{2,6},{6,2},{3,7},{7,3},{8,12},{12,8},{9,1... | collective-permute-start | bytes 294920 | tf_op jit(solution)/shard_map/ppermute | solution.py:35
  184.9 6.6 %collective-permute-start.18 = (f32[96,256]{1,0:T(8,128)S(1)}, f32[96,256]{1,0:T(8,128)S(1)}, u32[]{:S(2)}, u32[]{:S(2)}) collective-permute-start(f32[96,256]{1,0:T(8,128)S(1)} %get-tuple-element.9), channel_id=1, source_target_pairs={{0,8},{8,0},{1,9},{9,1},{2,10},{10,2},{3,11},{11,3},{4,12},{12,4},... | collective-permute-start | bytes 294920 | tf_op jit(solution)/shard_map/ppermute | solution.py:35
  193.0 4.2 %collective-permute-start.22 = (bf16[96,256]{1,0:T(8,128)(2,1)S(1)}, bf16[96,256]{1,0:T(8,128)(2,1)S(1)}, u32[]{:S(2)}, u32[]{:S(2)}) collective-permute-start(bf16[96,256]{1,0:T(8,128)(2,1)S(1)} %select_convert_fusion.2), channel_id=1, source_target_pairs={{0,16},{16,0},{1,17},{17,1},{2,18},{18,2},{3,19},{19,3},{4,20},{20... | collective-permute-start | bytes 147464 | tf_op jit(solution)/shard_map/ppermute | solution.py:35
  (42 other events, 384.8 us)
where the time goes:
time: 204 us; the launch traced here: 202 us
  local copies, waits for them, and re-layouts  55.9 us (27%)
  starting transfers between devices  44.8 us (22%)
  matrix products  41.9 us (21%)
  other arithmetic  38.3 us (19%)
  waiting for transfers between devices  19.9 us (10%)
    gather x26, local copies, waits for them, and re-layouts, pick_rows(): return jnp.take_along_axis(panel, order[..., None], axis=-2)  29.7 us
    ppermute x20, starting transfers between devices, partner_2(): return lax.ppermute(block, axis, route)  28.5 us
    ppermute x20, waiting for transfers between devices, partner_2(): return lax.ppermute(block, axis, route)  19.9 us
    dot_general x18, matrix products, apply_cols(): return jnp.einsum('...ji,...js->...is', matrix, panel, precision=HIGHEST)  17.3 us
    dot_general x10, matrix products, apply_rows(): return jnp.einsum('...ij,...js->...is', matrix, panel, precision=HIGHEST)  9.84 us
    gather x14, other arithmetic  8.33 us
    another operation x10, other arithmetic, local(): results.append(jnp.stack([panels[0], panels[2]]).astype(jnp.bfloat16))  7.72 us
    all_to_all x1, starting transfers between devices, local(): lax.all_to_all(adj_tests, 'sub', split_axis=1, concat_axis=0, tiled=True)  7.46 us
  transfers between devices with their start and end apart: 25, of which 11 were waited for; matrix products, arithmetic and copies ran while one was open for 64% of the time, Pallas kernels for 0%

commit v1 on v0

v1 whole, which is shorter than its diff:
```python
import functools

import jax
import jax.numpy as jnp
from jax import lax
from jax.experimental import pallas as pl
from jax.experimental.pallas import tpu as pltpu
from jax.sharding import PartitionSpec as P

BF = jnp.bfloat16
F32 = jnp.float32
VMEM = pl.BlockSpec(memory_space=pltpu.VMEM)
SMEM = pl.BlockSpec(memory_space=pltpu.SMEM)


def mm(a, b):
    return jnp.dot(a, b, preferred_element_type=F32)


def mm_t(a, b):
    return lax.dot_general(a, b, (((1,), (1,)), ((), ())), preferred_element_type=F32)


def eye(n):
    same = lax.broadcasted_iota(jnp.int32, (n, n), 0) == lax.broadcasted_iota(jnp.int32, (n, n), 1)
    return jnp.where(same, 1.0, 0.0).astype(BF)


def one_hot(order, n):
    hit = lax.broadcasted_iota(jnp.int32, (n, order.shape[1]), 0) == order
    return jnp.where(hit, 1.0, 0.0).astype(BF)


def call(body, out_shape, args, scratch=(), smem=0, limit=40 << 20, flops=0):
    nbytes = sum(a.size * a.dtype.itemsize for a in args)
    outs = out_shape if isinstance(out_shape, (list, tuple)) else [out_shape]
    return pl.pallas_call(
        body,
        out_shape=out_shape,
        in_specs=[SMEM] * smem + [VMEM] * (len(args) - smem),
        out_specs=jax.tree.map(lambda _: VMEM, out_shape),
        scratch_shapes=list(scratch),
        compiler_params=pltpu.CompilerParams(vmem_limit_bytes=limit),
        cost_estimate=pl.CostEstimate(
            flops=flops,
            bytes_accessed=nbytes + sum(o.size * o.dtype.itemsize for o in outs),
            transcendentals=0,
        ),
    )(*args)


def shape(dims, dtype=BF):
    return jax.ShapeDtypeStruct(dims, dtype)


def split_body(width, tests_ref, out_ref):
    for chip in range(out_ref.shape[0]):
        out_ref[chip] = tests_ref[:, chip * width : (chip + 1) * width]


def select_body(
    cols_ref, tiles_ref, own_ref, inner_ref, outer_ref, interp_ref, near_ref, tests_ref, adj_ref, dense_ref
):
    per_dev, slots, tile = tiles_ref.shape[:3]
    rows = per_dev * tile
    rank = interp_ref.shape[-1]
    core = lax.axis_index("sub") & 1
    first = (lax.axis_index("grp") * lax.axis_size("sub") + lax.axis_index("sub")) * per_dev
    dense_ref[...] = jnp.zeros_like(dense_ref)
    for q in range(per_dev):
        for t in range(slots):
            col = cols_ref[q, t] - first
            below, above = col < 0, col >= per_dev
            place = jnp.where(below, col + per_dev, jnp.where(above, col - per_dev, col))
            inner = jnp.where(core == 0, above, below)
            block = jnp.where(below | above, jnp.where(inner, 1, 2), 0)
            at = pl.multiple_of((block * per_dev + place) * tile, tile)
            dense_ref[q * tile : (q + 1) * tile, pl.ds(at, tile)] = tiles_ref[q, t]
    unit = eye(rank)
    row_hot = one_hot(own_ref[0, 0:1, :], rows)
    col_hot = one_hot(own_ref[0, 1:2, :], rows)
    row_all = mm(row_hot, jnp.concatenate([unit, interp_ref[0, 0]], axis=0)).astype(BF)
    col_all = mm(col_hot, jnp.concatenate([unit, interp_ref[0, 1]], axis=0)).astype(BF)
    tests_ref[...] = mm_t(unit, col_all).astype(BF)
    adj_ref[3 * rank :] = mm_t(unit, row_all).astype(BF)
    row_keep = mm_t(unit, row_hot[:, :rank]).astype(BF)
    near_ref[...] = mm(row_keep, dense_ref[...]).astype(BF)
    hots = (
        col_hot[:, :rank],
        one_hot(inner_ref[0, 1:2, :rank], rows),
        one_hot(outer_ref[0, 1:2, :rank], rows),
    )
    for b, hot in enumerate(hots):
        keep = mm_t(unit, hot).astype(BF)
        adj_ref[b * rank : (b + 1) * rank] = mm_t(keep, dense_ref[:, b * rows : (b + 1) * rows]).astype(BF)


def maps_body(maps_ref, perms_ref, *out_refs):
    rank = maps_ref.shape[-1]
    unit = eye(rank)
    for level, out_ref in enumerate(out_refs):
        row_interp, col_interp, low_high, high_low = (maps_ref[0, level, i] for i in range(4))
        row_hot = one_hot(perms_ref[0, level, 0:1, :], 2 * rank)
        col_hot = one_hot(perms_ref[0, level, 1:2, :], 2 * rank)
        row_all = mm(row_hot, jnp.concatenate([unit, row_interp], axis=0)).astype(BF)
        col_all = mm(col_hot, jnp.concatenate([unit, col_interp], axis=0)).astype(BF)
        for kind, (hot, every) in enumerate(((row_hot, col_all), (col_hot, row_all))):
            keep = [mm_t(unit, hot[side * rank : (side + 1) * rank, :rank]).astype(BF) for side in range(2)]
            if kind == 0:
                cross = [mm(keep[1], high_low), mm(keep[0], low_high)]
            else:
                cross = [mm_t(keep[1], low_high), mm_t(keep[0], high_low)]
            for side in range(2):
                out_ref[kind, side, :rank] = keep[side]
                out_ref[kind, side, rank : 2 * rank] = (-cross[side]).astype(BF)
                out_ref[kind, side, 2 * rank :] = mm_t(
                    unit, every[side * rank : (side + 1) * rank]
                ).astype(BF)


def forward_body(near_ref, tests_ref, own_ref, inner_ref, outer_ref, mine_ref, other_ref):
    rows = own_ref.shape[0]
    rank = near_ref.shape[0]
    half = own_ref.shape[1] // 2
    core = lax.axis_index("sub") & 1
    for out_ref, place in ((mine_ref, core), (other_ref, 1 - core)):
        cols = pl.ds(pl.multiple_of(place * half, half), half)
        own = own_ref[:, cols]
        fwd = (
            mm(near_ref[:, :rows], own)
            + mm(near_ref[:, rows : 2 * rows], inner_ref[:, cols])
            + mm(near_ref[:, 2 * rows :], outer_ref[:, cols])
        )
        out_ref[:rank] = fwd.astype(BF)
        out_ref[rank:] = mm(tests_ref[...], own).astype(BF)


def rim_place():
    sub = lax.axis_index("sub")
    return (sub & 1) != ((sub >> 1) & 1)


def adjoint_body(adj_ref, other_ref, panel_ref, mine_out, other_out, even_out, odd_out):
    rows = adj_ref.shape[1]
    rank = adj_ref.shape[0] // 4
    core = lax.axis_index("sub") & 1
    mine = mm_t(adj_ref[...], panel_ref[:, pl.ds(pl.multiple_of(core * rows, 128), rows)])
    other = mm_t(other_ref[...], panel_ref[:, pl.ds(pl.multiple_of((1 - core) * rows, 128), rows)])
    mine_out[:rank] = mine[:rank] + other[rank : 2 * rank]
    mine_out[rank:] = mine[3 * rank :]
    other_out[:rank] = other[:rank] + mine[rank : 2 * rank]
    other_out[rank:] = other[3 * rank :]
    mine_rim = mine[2 * rank : 3 * rank]
    other_rim = other[2 * rank : 3 * rank]
    even = rim_place()
    even_out[...] = jnp.where(even, mine_rim, other_rim).astype(BF)
    odd_out[...] = jnp.where(even, other_rim, mine_rim).astype(BF)


def merged(maps_ref, kind, side, mine_first, mine_second, other_first, other_second, rank):
    wide = mm(maps_ref[kind, side, rank:], mine_second) + mm(maps_ref[kind, 1 - side, rank:], other_second)
    kept = mm(maps_ref[kind, side, :rank], mine_first) + mm(maps_ref[kind, 1 - side, :rank], other_first)
    return kept + wide[:rank], wide[rank:]


def first_body(maps_ref, fwd_ref, fwd_other, adj_ref, adj_other, even_ref, odd_ref, out_ref):
    rank = even_ref.shape[0]
    core = lax.axis_index("sub") & 1
    kept, tests = merged(
        maps_ref, 0, core, fwd_ref[:rank], fwd_ref[rank:], fwd_other[:rank], fwd_other[rank:], rank
    )
    out_ref[0, :rank] = kept.astype(BF)
    out_ref[0, rank:] = tests.astype(BF)
    even = rim_place()
    from_even = even_ref[...].astype(F32)
    from_odd = odd_ref[...].astype(F32)
    mine = adj_ref[:rank] + jnp.where(even, from_even, from_odd)
    other = adj_other[:rank] + jnp.where(even, from_odd, from_even)
    kept, tests = merged(
        maps_ref,
        1,
        core,
        mine.astype(BF),
        adj_ref[rank:].astype(BF),
        other.astype(BF),
        adj_other[rank:].astype(BF),
        rank,
    )
    out_ref[1, :rank] = kept.astype(BF)
    out_ref[1, rank:] = tests.astype(BF)


def level_body(axis, bit, last, maps_ref, mine_ref, other_ref, out_ref):
    rank = mine_ref.shape[1] // 2
    side = (lax.axis_index(axis) >> bit) & 1
    for kind in range(2):
        kept, tests = merged(
            maps_ref,
            kind,
            side,
            mine_ref[kind, :rank],
            mine_ref[kind, rank:],
            other_ref[kind, :rank],
            other_ref[kind, rank:],
            rank,
        )
        out_ref[kind, :rank] = kept.astype(BF)
        if not last:
            out_ref[kind, rank:] = tests.astype(BF)


def collect_body(*refs):
    out_ref = refs[-1]
    rank = out_ref.shape[2]
    for level, ref in enumerate(refs[:-1]):
        out_ref[level] = ref[:, :rank]


def output_body(vectors, early_ref, early_other, late_ref, late_other, out_ref):
    levels = early_ref.shape[0]
    half = early_ref.shape[-1]
    core = lax.axis_index("sub") & 1
    k = lax.broadcasted_iota(jnp.int32, (half, 2 * half), 0)
    s = lax.broadcasted_iota(jnp.int32, (half, 2 * half), 1)
    base = k + k // vectors * vectors
    to_mine = jnp.where(s == base + core * vectors, 1.0, 0.0).astype(BF)
    to_other = jnp.where(s == base + (1 - core) * vectors, 1.0, 0.0).astype(BF)
    mine_cols = pl.ds(pl.multiple_of(core * half, half), half)
    other_cols = pl.ds(pl.multiple_of((1 - core) * half, half), half)
    for level in range(levels + 1):
        mine = early_ref[level] if level < levels else late_ref[...]
        other = early_other[level] if level < levels else late_other[...]
        out_ref[0, level, 0, :, mine_cols] = mine[0]
        out_ref[0, level, 0, :, other_cols] = other[0]
        out_ref[0, level, 1] = (mm(mine[1], to_mine) + mm(other[1], to_other)).astype(BF)


def swapped(x, axis, bit):
    return lax.ppermute(x, axis, [(i, i ^ (1 << bit)) for i in range(lax.axis_size(axis))])


def local(omega, adj_tests, near_tiles, tile_cols, leaf_perms, leaf_interp, node_perms, node_maps):
    rows, samples = omega.shape
    half = samples // 2
    vectors = adj_tests.shape[0]
    rank = leaf_interp.shape[-1]
    levels = node_maps.shape[1]
    count = lax.axis_size("sub")
    chips = count // 2
    sub_bits = count.bit_length() - 1
    outward = [(i, j) for i in range(1, count - 1, 2) for j in (i + 1,)]
    outward += [(j, i) for i, j in outward]

    blocks = call(
        functools.partial(split_body, 2 * rows), shape((chips, vectors, 2 * rows)), (adj_tests,)
    )
    groups = [[2 * m + c for m in range(chips)] for c in range(2)]
    panel = lax.all_to_all(
        blocks, "sub", split_axis=0, concat_axis=0, tiled=True, axis_index_groups=groups
    ).reshape(half, 2 * rows)

    perms_inner = swapped(leaf_perms, "sub", 0)
    perms_outer = lax.ppermute(leaf_perms, "sub", outward)
    omega_inner = swapped(omega, "sub", 0)
    omega_outer = lax.ppermute(omega, "sub", outward)
    near, tests, adj = call(
        select_body,
        [shape((rank, 3 * rows)), shape((rank, rows)), shape((4 * rank, rows))],
        (tile_cols, near_tiles, leaf_perms, perms_inner, perms_outer, leaf_interp),
        scratch=[pltpu.VMEM((rows, 3 * rows), BF)],
        smem=1,
        flops=8 * rank * rows * rows * 2,
    )
    adj_other = swapped(adj, "sub", 0)
    maps = call(maps_body, [shape((2, 2, 3 * rank, rank))] * levels, (node_maps, node_perms))
    fwd_mine, fwd_send = call(
        forward_body,
        [shape((2 * rank, half))] * 2,
        (near, tests, omega, omega_inner, omega_outer),
        flops=4 * rank * rows * samples * 2,
    )
    fwd_other = swapped(fwd_send, "sub", 0)

    adj_leaf, adj_leaf_other, even_rim, odd_rim = call(
        adjoint_body,
        [shape((2 * rank, half), F32)] * 2 + [shape((rank, half))] * 2,
        (adj, adj_other, panel),
    )
    even_rim = swapped(even_rim, "sub", 1)
    beside = [(2 * i + c, 2 * i + 2 + c) for i in range(1, chips - 1, 2) for c in range(2)]
    odd_rim = lax.ppermute(odd_rim, "sub", beside + [(j, i) for i, j in beside])
    x = call(
        first_body,
        shape((2, 2 * rank, half)),
        (maps[0], fwd_mine, fwd_other, adj_leaf, adj_leaf_other, even_rim, odd_rim),
    )
    nodes = [x]
    steps = [("sub", bit) for bit in range(1, sub_bits)]
    steps += [("grp", bit) for bit in range(levels - sub_bits)]
    for level, (axis, bit) in enumerate(steps, 1):
        last = level == levels - 1
        x = call(
            functools.partial(level_body, axis, bit, last),
            shape((2, rank if last else 2 * rank, half)),
            (maps[level], x, swapped(x, axis, bit)),
        )
        nodes.append(x)
    early = call(collect_body, shape((levels - 1, 2, rank, half)), nodes[:-1])
    early_other = swapped(early, "sub", 0)
    late_other = swapped(x, "sub", 0)
    return call(
        functools.partial(output_body, vectors),
        shape((1, levels, 2, rank, samples)),
        (early, early_other, x, late_other),
    )


def solution(mesh):
    both = ("grp", "sub")
    return jax.shard_map(
        local,
        mesh=mesh,
        in_specs=(
            P(both, None),
            P("sub", "grp"),
            P(both, None, None, None),
            P(both, None),
            P(both, None, None),
            P(both, None, None, None),
            P(both, None, None, None),
            P(both, None, None, None, None),
        ),
        out_specs=P(both, None, None, None, None),
        check_vma=False,
    )
```

time: 204 us -> 73.7 us (0.36)
  local copies, waits for them, and re-layouts: 55.9 us -> 5.23 us
  matrix products: 41.9 us -> 0 us
  other arithmetic: 38.3 us -> 0 us
  Pallas kernels: 0 us -> 10.6 us
  waiting for transfers between devices: 19.9 us -> 15.8 us
  starting transfers between devices: 44.8 us -> 41.4 us
    gather x32 -> x0, local copies, waits for them, and re-layouts: 46.7 us -> none  [the longest x26 29.7 us: pick_rows(): return jnp.take_along_axis(panel, order[..., None], axis=-2)]
    dot_general x33 -> x0, matrix products: 41.9 us -> none  [the longest x18 17.3 us: apply_cols(): return jnp.einsum('...ji,...js->...is', matrix, panel, precision=HIGHEST)]
    pallas_call x0 -> x12, Pallas kernels: none -> 10.6 us  [call(): pl.pallas_call(body, out_shape=out_shape, in_specs=[SMEM] * smem + [VMEM]...]
    another operation x13 -> x0, other arithmetic: 9.33 us -> none  [the longest x10 7.72 us: local(): results.append(jnp.stack([panels[0], panels[2]]).astype(jnp.bfloat16))]
    gather x19 -> x0, other arithmetic: 8.94 us -> none
    select_n x14 -> x0, other arithmetic: 7.07 us -> none  [the longest x8 2.86 us: pair_up(): jnp.where(upper_side, a, b)]
    unnamed x4 -> x0, other arithmetic: 5.78 us -> none
    ppermute x24 -> x14, waiting for transfers between devices: 19.9 us -> 15.8 us  [the longest x11 15.8 us: swapped(): lax.ppermute(x, axis, [(i, i ^ 1 << bit) for i in range(lax.axis_size(axi...]
  transfers between devices with their start and end apart: 25 -> 15, of which waited for: 11 -> 6; matrix products, arithmetic and copies ran while one was open for 64% -> 2% of each run, Pallas kernels for 0% -> 11%
where the time goes in v1:
time: 73.7 us; the launch traced here: 73.3 us
  starting transfers between devices  41.4 us (56%)
  waiting for transfers between devices  15.8 us (21%)
  Pallas kernels  10.6 us (14%)
  local copies, waits for them, and re-layouts  5.23 us (7%)
    ppermute x11, starting transfers between devices, swapped(): lax.ppermute(x, axis, [(i, i ^ 1 << bit) for i in range(lax.axis_size(axi...  32 us
    ppermute x11, waiting for transfers between devices, swapped(): lax.ppermute(x, axis, [(i, i ^ 1 << bit) for i in range(lax.axis_size(axi...  15.8 us
    pallas_call x12, Pallas kernels, call(): pl.pallas_call(body, out_shape=out_shape, in_specs=[SMEM] * smem + [VMEM]...  10.6 us
    all_to_all x1, starting transfers between devices, local(): lax.all_to_all(blocks, 'sub', split_axis=0, concat_axis=0, tiled=True, ax...  7.38 us
    unnamed x15, local copies, waits for them, and re-layouts  5.23 us
  transfers between devices with their start and end apart: 15, of which 6 were waited for; matrix products, arithmetic and copies ran while one was open for 2% of the time, Pallas kernels for 11%

profile of v1, /device:TPU:0, one launch (start us, length us, event | category | flops | bytes accessed | tf_op | source)
XLA Modules:
  0.0 73.3 jit_solution(14505510587351147464)
XLA Ops:
  0.0 1.0 %copy-done.2 = bf16[16,12288]{1,0:T(8,128)(2,1)S(1)} copy-done((bf16[16,12288]{1,0:T(8,128)(2,1)S(1)}, bf16[16,12288]{1,0:T(8,128)(2,1)}, u32[]{:S(2)}) %copy-start.2) | copy-done | bytes 393240
  1.0 0.8 %shard_map.85 = bf16[8,16,1536]{2,1,0:T(8,128)(2,1)} custom-call(bf16[16,12288]{1,0:T(8,128)(2,1)S(1)} %copy-done.2), custom_call_target="tpu_custom_call" | custom-call | bytes 786432 | tf_op jit(solution)/shard_map/pallas_call | solution.py:37
  1.8 7.4 %all-to-all-start = ((bf16[8,16,1536]{2,1,0:T(8,128)(2,1)}), bf16[8,16,1536]{2,1,0:T(8,128)(2,1)S(1)}, u32[]{:S(2)}, u32[]{:S(2)}) async-start(bf16[8,16,1536]{2,1,0:T(8,128)(2,1)} %shard_map.85), calls=%async_computation | async-start | bytes 786432 | tf_op jit(solution)/shard_map/all_to_all | solution.py:258
  9.8 1.2 %copy.9.interp_ref = bf16[1,2,672,96]{3,2,1,0:T(8,128)(2,1)S(1)} copy(bf16[1,2,672,96]{2,3,1,0:T(8,128)(2,1)} %param.13) | data formatting | bytes 516096 | tf_op args[5]
  11.1 1.7 %copy-done.4 = bf16[6,12,128,128]{3,2,1,0:T(8,128)(2,1)S(1)} copy-done((bf16[6,12,128,128]{3,2,1,0:T(8,128)(2,1)S(1)}, bf16[6,12,128,128]{3,2,1,0:T(8,128)(2,1)}, u32[]{:S(2)}) %copy-start.4) | copy-done | bytes 2359320
  12.7 0.7 copy-done.5
  13.4 0.7 copy-done.6
  14.1 4.3 %shard_map.83 = (bf16[96,2304]{1,0:T(8,128)(2,1)S(1)}, bf16[96,768]{1,0:T(8,128)(2,1)S(1)}, bf16[384,768]{1,0:T(8,128)(2,1)S(1)}) custom-call(s32[6,12]{1,0:T(8,128)S(1)} %copy-done.6, bf16[6,12,128,128]{3,2,1,0:T(8,128)(2,1)S(1)} %copy-done.4, s32[1,2,768]{2,1,0:T(2,128)S(1)} %copy-done.5, s32[1,2,768]{2,1,0:T(2,128)S(1)} %collective-permute-done.inner_ref, ...), custom_call_target="tpu_custom_call" | custom-call | flops 905969664 | bytes 3815712 | tf_op jit(solution)/shard_map/pallas_call | solution.py:37
  18.4 4.5 %collective-permute-start.5 = (bf16[384,768]{1,0:T(8,128)(2,1)S(1)}, bf16[384,768]{1,0:T(8,128)(2,1)S(1)}, u32[]{:S(2)}, u32[]{:S(2)}) collective-permute-start(bf16[384,768]{1,0:T(8,128)(2,1)S(1)} %get-tuple-element.24.adj_ref), channel_id=1, source_target_pairs={{0,1},{1,0},{2,3},{3,2},{4,5},{5,4},{6,7},{7,6},{8,9},{9,8},{10,11... | collective-permute-start | bytes 1769480 | tf_op jit(solution)/shard_map/ppermute | solution.py:239
  23.0 0.7 collective-permute-start.3
  23.7 1.4 %collective-permute-done.2.inner_ref = bf16[768,256]{1,0:T(8,128)(2,1)S(1)} collective-permute-done((bf16[768,256]{1,0:T(8,128)(2,1)S(1)}, bf16[768,256]{1,0:T(8,128)(2,1)S(1)}, u32[]{:S(2)}, u32[]{:S(2)}) %collective-permute-start.2) | collective-permute-done | bytes 393248 | tf_op jit(solution)/shard_map/ppermute | solution.py:239
  25.6 11.5 %collective-permute-start.4 = (bf16[192,128]{1,0:T(8,128)(2,1)S(1)}, bf16[192,128]{1,0:T(8,128)(2,1)S(1)}, u32[]{:S(2)}, u32[]{:S(2)}) collective-permute-start(bf16[192,128]{1,0:T(8,128)(2,1)S(1)} %get-tuple-element.23), channel_id=1, source_target_pairs={{0,1},{1,0},{2,3},{3,2},{4,5},{5,4},{6,7},{7,6},{8,9},{9,8},{10,11... | collective-permute-start | bytes 147464 | tf_op jit(solution)/shard_map/ppermute | solution.py:239
  37.6 2.5 %collective-permute-start.6 = (bf16[96,128]{1,0:T(8,128)(2,1)S(1)}, bf16[96,128]{1,0:T(8,128)(2,1)S(1)}, u32[]{:S(2)}, u32[]{:S(2)}) collective-permute-start(bf16[96,128]{1,0:T(8,128)(2,1)S(1)} %get-tuple-element.27), channel_id=1, source_target_pairs={{0,2},{1,3},{2,0},{3,1},{4,6},{5,7},{6,4},{7,5},{8,10},{9,11},{10,... | collective-permute-start | bytes 73736 | tf_op jit(solution)/shard_map/ppermute | solution.py:239
  40.8 2.4 %shard_map.82 = (bf16[2,2,288,96]{3,2,1,0:T(8,128)(2,1)S(1)}, bf16[2,2,288,96]{3,2,1,0:T(8,128)(2,1)S(1)}, bf16[2,2,288,96]{3,2,1,0:T(8,128)(2,1)S(1)}, bf16[2,2...) custom-call(bf16[1,5,4,96,96]{4,3,2,1,0:T(8,128)(2,1)S(1)} %copy-done, s32[1,5,2,192]{3,2,1,0:T(2,128)S(1)} %copy-done.3), custom_call_target="tpu_custom_call" | custom-call | bytes 1482240 | tf_op jit(solution)/shard_map/pallas_call | solution.py:37
  43.4 7.4 %collective-permute-start.8 = (bf16[2,192,128]{2,1,0:T(8,128)(2,1)S(1)}, bf16[2,192,128]{2,1,0:T(8,128)(2,1)S(1)}, u32[]{:S(2)}, u32[]{:S(2)}) collective-permute-start(bf16[2,192,128]{2,1,0:T(8,128)(2,1)S(1)} %shard_map.87.mine_ref.refs_0_), channel_id=1, source_target_pairs={{0,2},{1,3},{2,0},{3,1},{4,6},{5,7},{6,4},{7,5},{8,10},{9,11},{10,... | collective-permute-start | bytes 294920 | tf_op jit(solution)/shard_map/ppermute | solution.py:239
  50.9 2.9 %collective-permute-done.8.other_ref = bf16[2,192,128]{2,1,0:T(8,128)(2,1)S(1)} collective-permute-done((bf16[2,192,128]{2,1,0:T(8,128)(2,1)S(1)}, bf16[2,192,128]{2,1,0:T(8,128)(2,1)S(1)}, u32[]{:S(2)}, u32[]{:S(2)}) %collective-permute-start.8) | collective-permute-done | bytes 98336 | tf_op jit(solution)/shard_map/ppermute | solution.py:239
  54.0 2.6 %collective-permute-start.9 = (bf16[2,192,128]{2,1,0:T(8,128)(2,1)S(1)}, bf16[2,192,128]{2,1,0:T(8,128)(2,1)S(1)}, u32[]{:S(2)}, u32[]{:S(2)}) collective-permute-start(bf16[2,192,128]{2,1,0:T(8,128)(2,1)S(1)} %shard_map.88.mine_ref.refs_1_), channel_id=1, source_target_pairs={{0,4},{1,5},{2,6},{3,7},{4,0},{5,1},{6,2},{7,3},{8,12},{9,13},{10,... | collective-permute-start | bytes 294920 | tf_op jit(solution)/shard_map/ppermute | solution.py:239
  56.6 2.8 %collective-permute-done.9.other_ref = bf16[2,192,128]{2,1,0:T(8,128)(2,1)S(1)} collective-permute-done((bf16[2,192,128]{2,1,0:T(8,128)(2,1)S(1)}, bf16[2,192,128]{2,1,0:T(8,128)(2,1)S(1)}, u32[]{:S(2)}, u32[]{:S(2)}) %collective-permute-start.9) | collective-permute-done | bytes 98336 | tf_op jit(solution)/shard_map/ppermute | solution.py:239
  59.6 1.7 %collective-permute-start.10 = (bf16[2,192,128]{2,1,0:T(8,128)(2,1)S(1)}, bf16[2,192,128]{2,1,0:T(8,128)(2,1)S(1)}, u32[]{:S(2)}, u32[]{:S(2)}) collective-permute-start(bf16[2,192,128]{2,1,0:T(8,128)(2,1)S(1)} %shard_map.89.mine_ref.refs_2_), channel_id=1, source_target_pairs={{0,8},{1,9},{2,10},{3,11},{4,12},{5,13},{6,14},{7,15},{8,0},{9,1},... | collective-permute-start | bytes 294920 | tf_op jit(solution)/shard_map/ppermute | solution.py:239
  61.2 3.9 %collective-permute-done.10.other_ref = bf16[2,192,128]{2,1,0:T(8,128)(2,1)S(1)} collective-permute-done((bf16[2,192,128]{2,1,0:T(8,128)(2,1)S(1)}, bf16[2,192,128]{2,1,0:T(8,128)(2,1)S(1)}, u32[]{:S(2)}, u32[]{:S(2)}) %collective-permute-start.10) | collective-permute-done | bytes 98336 | tf_op jit(solution)/shard_map/ppermute | solution.py:239
  65.5 1.6 %collective-permute-start.12 = (bf16[2,192,128]{2,1,0:T(8,128)(2,1)S(1)}, bf16[2,192,128]{2,1,0:T(8,128)(2,1)S(1)}, u32[]{:S(2)}, u32[]{:S(2)}) collective-permute-start(bf16[2,192,128]{2,1,0:T(8,128)(2,1)S(1)} %shard_map.90.refs_3_.mine_ref), channel_id=1, source_target_pairs={{0,16},{16,0},{1,17},{17,1},{2,18},{18,2},{3,19},{19,3},{4,20},{20... | collective-permute-start | bytes 294920 | tf_op jit(solution)/shard_map/ppermute | solution.py:239
  67.1 3.6 %collective-permute-done.12.other_ref = bf16[2,192,128]{2,1,0:T(8,128)(2,1)S(1)} collective-permute-done((bf16[2,192,128]{2,1,0:T(8,128)(2,1)S(1)}, bf16[2,192,128]{2,1,0:T(8,128)(2,1)S(1)}, u32[]{:S(2)}, u32[]{:S(2)}) %collective-permute-start.12) | collective-permute-done | bytes 98336 | tf_op jit(solution)/shard_map/ppermute | solution.py:239
  71.0 1.2 %collective-permute-done.13.late_other = bf16[2,96,128]{2,1,0:T(8,128)(2,1)S(1)} collective-permute-done((bf16[2,96,128]{2,1,0:T(8,128)(2,1)S(1)}, bf16[2,96,128]{2,1,0:T(8,128)(2,1)S(1)}, u32[]{:S(2)}, u32[]{:S(2)}) %collective-permute-start.13) | collective-permute-done | bytes 49184 | tf_op jit(solution)/shard_map/ppermute | solution.py:239
  72.2 1.1 %shard_map.93 = bf16[1,5,2,96,256]{4,3,2,1,0:T(8,128)(2,1)} custom-call(bf16[4,2,96,128]{3,2,1,0:T(8,128)(2,1)S(1)} %shard_map.91.early_ref, bf16[4,2,96,128]{3,2,1,0:T(8,128)(2,1)S(1)} %collective-permute-done.11.early_other, bf16[2,96,128]{2,1,0:T(8,128)(2,1)S(1)} %shard_map.92.late_ref, bf16[2,96,128]{2,1,0:T(8,128)(2,1)S(1)} %collective-permute-done.13.late_other), custom_call_target="tpu_custom_call" | custom-call | bytes 983040 | tf_op jit(solution)/shard_map/pallas_call | solution.py:37
  (33 shorter events, 3.7 us)
Async XLA Ops:
  0.0 1.0 %copy-start.2 = (bf16[16,12288]{1,0:T(8,128)(2,1)S(1)}, bf16[16,12288]{1,0:T(8,128)(2,1)}, u32[]{:S(2)}) copy-start(bf16[16,12288]{1,0:T(8,128)(2,1)} %tests_ref.1) | copy-start | bytes 1179652
  1.8 21.1 %copy-start.1 = (bf16[768,256]{1,0:T(8,128)(2,1)S(1)}, bf16[768,256]{1,0:T(8,128)(2,1)}, u32[]{:S(2)}) copy-start(bf16[768,256]{1,0:T(8,128)(2,1)} %own_ref.3) | copy-start | bytes 1179652
  1.8 35.4 %all-to-all-start = ((bf16[8,16,1536]{2,1,0:T(8,128)(2,1)}), bf16[8,16,1536]{2,1,0:T(8,128)(2,1)S(1)}, u32[]{:S(2)}, u32[]{:S(2)}) async-start(bf16[8,16,1536]{2,1,0:T(8,128)(2,1)} %shard_map.85), calls=%async_computation | async-start | bytes 786432 | tf_op jit(solution)/shard_map/all_to_all | solution.py:258
  9.2 1.9 %collective-permute-start = (s32[1,2,768]{2,1,0:T(2,128)}, s32[1,2,768]{2,1,0:T(2,128)S(1)}, u32[]{:S(2)}, u32[]{:S(2)}) collective-permute-start(s32[1,2,768]{2,1,0:T(2,128)} %own_ref.2), channel_id=1, source_target_pairs={{0,1},{1,0},{2,3},{3,2},{4,5},{5,4},{6,7},{7,6},{8,9},{9,8},{10,11... | collective-permute-start | bytes 18440 | tf_op jit(solution)/shard_map/ppermute | solution.py:239
  9.2 1.9 %collective-permute-start.1 = (s32[1,2,768]{2,1,0:T(2,128)}, s32[1,2,768]{2,1,0:T(2,128)S(1)}, u32[]{:S(2)}, u32[]{:S(2)}) collective-permute-start(s32[1,2,768]{2,1,0:T(2,128)} %own_ref.2), channel_id=1, source_target_pairs={{1,2},{3,4},{5,6},{7,8},{9,10},{11,12},{13,14},{2,1},{4,3},{6,5},{... | collective-permute-start | bytes 18440 | tf_op jit(solution)/shard_map/ppermute | solution.py:263
  11.0 1.7 %copy-start.4 = (bf16[6,12,128,128]{3,2,1,0:T(8,128)(2,1)S(1)}, bf16[6,12,128,128]{3,2,1,0:T(8,128)(2,1)}, u32[]{:S(2)}) copy-start(bf16[6,12,128,128]{3,2,1,0:T(8,128)(2,1)} %tiles_ref.1) | copy-start | bytes 7077892
  12.7 0.7 copy-start.5
  13.4 0.7 copy-start.6
  18.4 22.3 %copy-start = (bf16[1,5,4,96,96]{4,3,2,1,0:T(8,128)(2,1)S(1)}, bf16[1,5,4,96,96]{4,3,2,1,0:T(8,128)(2,1)}, u32[]{:S(2)}) copy-start(bf16[1,5,4,96,96]{4,3,2,1,0:T(8,128)(2,1)} %maps_ref.1) | copy-start | bytes 1105924
  18.4 22.3 %copy-start.3 = (s32[1,5,2,192]{3,2,1,0:T(2,128)S(1)}, s32[1,5,2,192]{3,2,1,0:T(2,128)}, u32[]{:S(2)}) copy-start(s32[1,5,2,192]{3,2,1,0:T(2,128)} %perms_ref.1) | copy-start | bytes 23044
  18.4 18.7 %collective-permute-start.5 = (bf16[384,768]{1,0:T(8,128)(2,1)S(1)}, bf16[384,768]{1,0:T(8,128)(2,1)S(1)}, u32[]{:S(2)}, u32[]{:S(2)}) collective-permute-start(bf16[384,768]{1,0:T(8,128)(2,1)S(1)} %get-tuple-element.24.adj_ref), channel_id=1, source_target_pairs={{0,1},{1,0},{2,3},{3,2},{4,5},{5,4},{6,7},{7,6},{8,9},{9,8},{10,11... | collective-permute-start | bytes 1769480 | tf_op jit(solution)/shard_map/ppermute | solution.py:239
  22.9 2.2 %collective-permute-start.2 = (bf16[768,256]{1,0:T(8,128)(2,1)S(1)}, bf16[768,256]{1,0:T(8,128)(2,1)S(1)}, u32[]{:S(2)}, u32[]{:S(2)}) collective-permute-start(bf16[768,256]{1,0:T(8,128)(2,1)S(1)} %copy-done.1), channel_id=1, source_target_pairs={{0,1},{1,0},{2,3},{3,2},{4,5},{5,4},{6,7},{7,6},{8,9},{9,8},{10,11... | collective-permute-start | bytes 1179656 | tf_op jit(solution)/shard_map/ppermute | solution.py:239
  23.0 2.1 %collective-permute-start.3 = (bf16[768,256]{1,0:T(8,128)(2,1)S(1)}, bf16[768,256]{1,0:T(8,128)(2,1)S(1)}, u32[]{:S(2)}, u32[]{:S(2)}) collective-permute-start(bf16[768,256]{1,0:T(8,128)(2,1)S(1)} %copy-done.1), channel_id=1, source_target_pairs={{1,2},{3,4},{5,6},{7,8},{9,10},{11,12},{13,14},{2,1},{4,3},{6,5},{... | collective-permute-start | bytes 1179656 | tf_op jit(solution)/shard_map/ppermute | solution.py:265
  25.6 17.5 %collective-permute-start.4 = (bf16[192,128]{1,0:T(8,128)(2,1)S(1)}, bf16[192,128]{1,0:T(8,128)(2,1)S(1)}, u32[]{:S(2)}, u32[]{:S(2)}) collective-permute-start(bf16[192,128]{1,0:T(8,128)(2,1)S(1)} %get-tuple-element.23), channel_id=1, source_target_pairs={{0,1},{1,0},{2,3},{3,2},{4,5},{5,4},{6,7},{7,6},{8,9},{9,8},{10,11... | collective-permute-start | bytes 147464 | tf_op jit(solution)/shard_map/ppermute | solution.py:239
  37.6 5.5 %collective-permute-start.6 = (bf16[96,128]{1,0:T(8,128)(2,1)S(1)}, bf16[96,128]{1,0:T(8,128)(2,1)S(1)}, u32[]{:S(2)}, u32[]{:S(2)}) collective-permute-start(bf16[96,128]{1,0:T(8,128)(2,1)S(1)} %get-tuple-element.27), channel_id=1, source_target_pairs={{0,2},{1,3},{2,0},{3,1},{4,6},{5,7},{6,4},{7,5},{8,10},{9,11},{10,... | collective-permute-start | bytes 73736 | tf_op jit(solution)/shard_map/ppermute | solution.py:239
  40.1 3.1 %collective-permute-start.7 = (bf16[96,128]{1,0:T(8,128)(2,1)S(1)}, bf16[96,128]{1,0:T(8,128)(2,1)S(1)}, u32[]{:S(2)}, u32[]{:S(2)}) collective-permute-start(bf16[96,128]{1,0:T(8,128)(2,1)S(1)} %get-tuple-element.28), channel_id=1, source_target_pairs={{2,4},{3,5},{6,8},{7,9},{10,12},{11,13},{4,2},{5,3},{8,6},{9,7},{1... | collective-permute-start | bytes 73736 | tf_op jit(solution)/shard_map/ppermute | solution.py:291
  43.4 10.3 %collective-permute-start.8 = (bf16[2,192,128]{2,1,0:T(8,128)(2,1)S(1)}, bf16[2,192,128]{2,1,0:T(8,128)(2,1)S(1)}, u32[]{:S(2)}, u32[]{:S(2)}) collective-permute-start(bf16[2,192,128]{2,1,0:T(8,128)(2,1)S(1)} %shard_map.87.mine_ref.refs_0_), channel_id=1, source_target_pairs={{0,2},{1,3},{2,0},{3,1},{4,6},{5,7},{6,4},{7,5},{8,10},{9,11},{10,... | collective-permute-start | bytes 294920 | tf_op jit(solution)/shard_map/ppermute | solution.py:239
  54.0 5.4 %collective-permute-start.9 = (bf16[2,192,128]{2,1,0:T(8,128)(2,1)S(1)}, bf16[2,192,128]{2,1,0:T(8,128)(2,1)S(1)}, u32[]{:S(2)}, u32[]{:S(2)}) collective-permute-start(bf16[2,192,128]{2,1,0:T(8,128)(2,1)S(1)} %shard_map.88.mine_ref.refs_1_), channel_id=1, source_target_pairs={{0,4},{1,5},{2,6},{3,7},{4,0},{5,1},{6,2},{7,3},{8,12},{9,13},{10,... | collective-permute-start | bytes 294920 | tf_op jit(solution)/shard_map/ppermute | solution.py:239
  59.6 5.6 %collective-permute-start.10 = (bf16[2,192,128]{2,1,0:T(8,128)(2,1)S(1)}, bf16[2,192,128]{2,1,0:T(8,128)(2,1)S(1)}, u32[]{:S(2)}, u32[]{:S(2)}) collective-permute-start(bf16[2,192,128]{2,1,0:T(8,128)(2,1)S(1)} %shard_map.89.mine_ref.refs_2_), channel_id=1, source_target_pairs={{0,8},{1,9},{2,10},{3,11},{4,12},{5,13},{6,14},{7,15},{8,0},{9,1},... | collective-permute-start | bytes 294920 | tf_op jit(solution)/shard_map/ppermute | solution.py:239
  65.4 6.8 %collective-permute-start.11 = (bf16[4,2,96,128]{3,2,1,0:T(8,128)(2,1)S(1)}, bf16[4,2,96,128]{3,2,1,0:T(8,128)(2,1)S(1)}, u32[]{:S(2)}, u32[]{:S(2)}) collective-permute-start(bf16[4,2,96,128]{3,2,1,0:T(8,128)(2,1)S(1)} %shard_map.91.early_ref), channel_id=1, source_target_pairs={{0,1},{1,0},{2,3},{3,2},{4,5},{5,4},{6,7},{7,6},{8,9},{9,8},{10,11... | collective-permute-start | bytes 589832 | tf_op jit(solution)/shard_map/ppermute | solution.py:239
  65.5 5.2 %collective-permute-start.12 = (bf16[2,192,128]{2,1,0:T(8,128)(2,1)S(1)}, bf16[2,192,128]{2,1,0:T(8,128)(2,1)S(1)}, u32[]{:S(2)}, u32[]{:S(2)}) collective-permute-start(bf16[2,192,128]{2,1,0:T(8,128)(2,1)S(1)} %shard_map.90.refs_3_.mine_ref), channel_id=1, source_target_pairs={{0,16},{16,0},{1,17},{17,1},{2,18},{18,2},{3,19},{19,3},{4,20},{20... | collective-permute-start | bytes 294920 | tf_op jit(solution)/shard_map/ppermute | solution.py:239
  70.9 1.3 %collective-permute-start.13 = (bf16[2,96,128]{2,1,0:T(8,128)(2,1)S(1)}, bf16[2,96,128]{2,1,0:T(8,128)(2,1)S(1)}, u32[]{:S(2)}, u32[]{:S(2)}) collective-permute-start(bf16[2,96,128]{2,1,0:T(8,128)(2,1)S(1)} %shard_map.92.late_ref), channel_id=1, source_target_pairs={{0,1},{1,0},{2,3},{3,2},{4,5},{5,4},{6,7},{7,6},{8,9},{9,8},{10,11... | collective-permute-start | bytes 147464 | tf_op jit(solution)/shard_map/ppermute | solution.py:239

commit v2 on v1

--- a/solution.py
+++ b/solution.py
@@ -31,21 +31,16 @@
     return jnp.where(hit, 1.0, 0.0).astype(BF)
 
 
-def call(body, out_shape, args, scratch=(), smem=0, limit=40 << 20, flops=0):
-    nbytes = sum(a.size * a.dtype.itemsize for a in args)
-    outs = out_shape if isinstance(out_shape, (list, tuple)) else [out_shape]
+def call(body, out_shape, args, scratch=(), smem=0, anywhere=False, limit=40 << 20):
+    space = pl.BlockSpec(memory_space=pl.ANY) if anywhere else VMEM
     return pl.pallas_call(
         body,
         out_shape=out_shape,
-        in_specs=[SMEM] * smem + [VMEM] * (len(args) - smem),
-        out_specs=jax.tree.map(lambda _: VMEM, out_shape),
+        in_specs=[SMEM] * smem + [space] * (len(args) - smem),
+        out_specs=jax.tree.map(lambda _: space, out_shape),
         scratch_shapes=list(scratch),
         compiler_params=pltpu.CompilerParams(vmem_limit_bytes=limit),
-        cost_estimate=pl.CostEstimate(
-            flops=flops,
-            bytes_accessed=nbytes + sum(o.size * o.dtype.itemsize for o in outs),
-            transcendentals=0,
-        ),
+        cost_estimate=pl.CostEstimate(flops=1000, bytes_accessed=1000, transcendentals=0),
     )(*args)
 
 
@@ -53,17 +48,37 @@
     return jax.ShapeDtypeStruct(dims, dtype)
 
 
-def split_body(width, tests_ref, out_ref):
-    for chip in range(out_ref.shape[0]):
-        out_ref[chip] = tests_ref[:, chip * width : (chip + 1) * width]
+def split_body(width, tests_ref, out_ref, sems):
+    copies = [
+        pltpu.make_async_copy(
+            tests_ref.at[:, chip * width : (chip + 1) * width], out_ref.at[chip], sems.at[chip]
+        )
+        for chip in range(out_ref.shape[0])
+    ]
+    for copy in copies:
+        copy.start()
+    for copy in copies:
+        copy.wait()
 
 
 def select_body(
-    cols_ref, tiles_ref, own_ref, inner_ref, outer_ref, interp_ref, near_ref, tests_ref, adj_ref, dense_ref
+    cols_ref,
+    tiles_ref,
+    own_ref,
+    inner_ref,
+    outer_ref,
+    interp_ref,
+    omega_ref,
+    omega_inner,
+    omega_outer,
+    adj_ref,
+    mine_ref,
+    other_ref,
+    dense_ref,
 ):
     per_dev, slots, tile = tiles_ref.shape[:3]
     rows = per_dev * tile
-    rank = interp_ref.shape[-1]
+    rank = interp_ref.shape[-2]
     core = lax.axis_index("sub") & 1
     first = (lax.axis_index("grp") * lax.axis_size("sub") + lax.axis_index("sub")) * per_dev
     dense_ref[...] = jnp.zeros_like(dense_ref)
@@ -77,22 +92,33 @@
             at = pl.multiple_of((block * per_dev + place) * tile, tile)
             dense_ref[q * tile : (q + 1) * tile, pl.ds(at, tile)] = tiles_ref[q, t]
     unit = eye(rank)
-    row_hot = one_hot(own_ref[0, 0:1, :], rows)
-    col_hot = one_hot(own_ref[0, 1:2, :], rows)
-    row_all = mm(row_hot, jnp.concatenate([unit, interp_ref[0, 0]], axis=0)).astype(BF)
-    col_all = mm(col_hot, jnp.concatenate([unit, interp_ref[0, 1]], axis=0)).astype(BF)
-    tests_ref[...] = mm_t(unit, col_all).astype(BF)
-    adj_ref[3 * rank :] = mm_t(unit, row_all).astype(BF)
-    row_keep = mm_t(unit, row_hot[:, :rank]).astype(BF)
-    near_ref[...] = mm(row_keep, dense_ref[...]).astype(BF)
-    hots = (
-        col_hot[:, :rank],
-        one_hot(inner_ref[0, 1:2, :rank], rows),
-        one_hot(outer_ref[0, 1:2, :rank], rows),
-    )
-    for b, hot in enumerate(hots):
-        keep = mm_t(unit, hot).astype(BF)
+    keeps = []
+    for i in range(2):
+        keep = mm_t(unit, one_hot(own_ref[0, i : i + 1, :rank], rows))
+        rest = one_hot(own_ref[0, i : i + 1, rank:], rows)
+        every = (keep + mm_t(interp_ref[0, i], rest)).astype(BF)
+        keeps.append(keep.astype(BF))
+        if i == 0:
+            adj_ref[3 * rank :] = every
+        else:
+            tests = every
+    keeps += [
+        mm_t(unit, one_hot(ref[0, 1:2, :rank], rows)).astype(BF) for ref in (inner_ref, outer_ref)
+    ]
+    for b, keep in enumerate(keeps[1:]):
         adj_ref[b * rank : (b + 1) * rank] = mm_t(keep, dense_ref[:, b * rows : (b + 1) * rows]).astype(BF)
+    near = mm(keeps[0], dense_ref[...]).astype(BF)
+    half = omega_ref.shape[1] // 2
+    for out_ref, place in ((mine_ref, core), (other_ref, 1 - core)):
+        cols = pl.ds(pl.multiple_of(place * half, half), half)
+        own = omega_ref[:, cols]
+        fwd = (
+            mm(near[:, :rows], own)
+            + mm(near[:, rows : 2 * rows], omega_inner[:, cols])
+            + mm(near[:, 2 * rows :], omega_outer[:, cols])
+        )
+        out_ref[:rank] = fwd.astype(BF)
+        out_ref[rank:] = mm(tests, own).astype(BF)
 
 
 def maps_body(maps_ref, perms_ref, *out_refs):
@@ -118,23 +144,6 @@
                 ).astype(BF)
 
 
-def forward_body(near_ref, tests_ref, own_ref, inner_ref, outer_ref, mine_ref, other_ref):
-    rows = own_ref.shape[0]
-    rank = near_ref.shape[0]
-    half = own_ref.shape[1] // 2
-    core = lax.axis_index("sub") & 1
-    for out_ref, place in ((mine_ref, core), (other_ref, 1 - core)):
-        cols = pl.ds(pl.multiple_of(place * half, half), half)
-        own = own_ref[:, cols]
-        fwd = (
-            mm(near_ref[:, :rows], own)
-            + mm(near_ref[:, rows : 2 * rows], inner_ref[:, cols])
-            + mm(near_ref[:, 2 * rows :], outer_ref[:, cols])
-        )
-        out_ref[:rank] = fwd.astype(BF)
-        out_ref[rank:] = mm(tests_ref[...], own).astype(BF)
-
-
 def rim_place():
     sub = lax.axis_index("sub")
     return (sub & 1) != ((sub >> 1) & 1)
@@ -190,9 +199,13 @@
     out_ref[1, rank:] = tests.astype(BF)
 
 
-def level_body(axis, bit, last, maps_ref, mine_ref, other_ref, out_ref):
+def level_body(axis, bit, last, maps_ref, mine_ref, other_ref, *refs):
     rank = mine_ref.shape[1] // 2
     side = (lax.axis_index(axis) >> bit) & 1
+    out_ref = refs[-1]
+    if last:
+        for level, ref in enumerate((*refs[:-1], mine_ref)):
+            out_ref[level] = ref[:, :rank]
     for kind in range(2):
         kept, tests = merged(
             maps_ref,
@@ -204,21 +217,15 @@
             other_ref[kind, rank:],
             rank,
         )
-        out_ref[kind, :rank] = kept.astype(BF)
-        if not last:
+        if last:
+            out_ref[len(refs), kind] = kept.astype(BF)
+        else:
+            out_ref[kind, :rank] = kept.astype(BF)
             out_ref[kind, rank:] = tests.astype(BF)
 
 
-def collect_body(*refs):
-    out_ref = refs[-1]
-    rank = out_ref.shape[2]
-    for level, ref in enumerate(refs[:-1]):
-        out_ref[level] = ref[:, :rank]
-
-
-def output_body(vectors, early_ref, early_other, late_ref, late_other, out_ref):
-    levels = early_ref.shape[0]
-    half = early_ref.shape[-1]
+def output_body(vectors, mine_ref, other_ref, out_ref):
+    half = mine_ref.shape[-1]
     core = lax.axis_index("sub") & 1
     k = lax.broadcasted_iota(jnp.int32, (half, 2 * half), 0)
     s = lax.broadcasted_iota(jnp.int32, (half, 2 * half), 1)
@@ -227,9 +234,8 @@
     to_other = jnp.where(s == base + (1 - core) * vectors, 1.0, 0.0).astype(BF)
     mine_cols = pl.ds(pl.multiple_of(core * half, half), half)
     other_cols = pl.ds(pl.multiple_of((1 - core) * half, half), half)
-    for level in range(levels + 1):
-        mine = early_ref[level] if level < levels else late_ref[...]
-        other = early_other[level] if level < levels else late_other[...]
+    for level in range(mine_ref.shape[0]):
+        mine, other = mine_ref[level], other_ref[level]
         out_ref[0, level, 0, :, mine_cols] = mine[0]
         out_ref[0, level, 0, :, other_cols] = other[0]
         out_ref[0, level, 1] = (mm(mine[1], to_mine) + mm(other[1], to_other)).astype(BF)
@@ -252,33 +258,37 @@
     outward += [(j, i) for i, j in outward]
 
     blocks = call(
-        functools.partial(split_body, 2 * rows), shape((chips, vectors, 2 * rows)), (adj_tests,)
+        functools.partial(split_body, 2 * rows), shape((chips, vectors, 2 * rows)), (adj_tests,),
+        scratch=[pltpu.SemaphoreType.DMA((chips,))], anywhere=True,
     )
     groups = [[2 * m + c for m in range(chips)] for c in range(2)]
     panel = lax.all_to_all(
         blocks, "sub", split_axis=0, concat_axis=0, tiled=True, axis_index_groups=groups
     ).reshape(half, 2 * rows)
 
+    omega_outer = lax.ppermute(omega, "sub", outward)
+    omega_inner = swapped(omega, "sub", 0)
+    perms_outer = lax.ppermute(leaf_perms, "sub", outward)
     perms_inner = swapped(leaf_perms, "sub", 0)
-    perms_outer = lax.ppermute(leaf_perms, "sub", outward)
-    omega_inner = swapped(omega, "sub", 0)
-    omega_outer = lax.ppermute(omega, "sub", outward)
-    near, tests, adj = call(
+    adj, fwd_mine, fwd_send = call(
         select_body,
-        [shape((rank, 3 * rows)), shape((rank, rows)), shape((4 * rank, rows))],
-        (tile_cols, near_tiles, leaf_perms, perms_inner, perms_outer, leaf_interp),
+        [shape((4 * rank, rows))] + [shape((2 * rank, half))] * 2,
+        (
+            tile_cols,
+            near_tiles,
+            leaf_perms,
+            perms_inner,
+            perms_outer,
+            jnp.swapaxes(leaf_interp, 2, 3),
+            omega,
+            omega_inner,
+            omega_outer,
+        ),
         scratch=[pltpu.VMEM((rows, 3 * rows), BF)],
         smem=1,
-        flops=8 * rank * rows * rows * 2,
     )
     adj_other = swapped(adj, "sub", 0)
     maps = call(maps_body, [shape((2, 2, 3 * rank, rank))] * levels, (node_maps, node_perms))
-    fwd_mine, fwd_send = call(
-        forward_body,
-        [shape((2 * rank, half))] * 2,
-        (near, tests, omega, omega_inner, omega_outer),
-        flops=4 * rank * rows * samples * 2,
-    )
     fwd_other = swapped(fwd_send, "sub", 0)
 
     adj_leaf, adj_leaf_other, even_rim, odd_rim = call(
@@ -294,24 +304,22 @@
         shape((2, 2 * rank, half)),
         (maps[0], fwd_mine, fwd_other, adj_leaf, adj_leaf_other, even_rim, odd_rim),
     )
-    nodes = [x]
+    nodes = []
     steps = [("sub", bit) for bit in range(1, sub_bits)]
     steps += [("grp", bit) for bit in range(levels - sub_bits)]
     for level, (axis, bit) in enumerate(steps, 1):
         last = level == levels - 1
-        x = call(
+        new = call(
             functools.partial(level_body, axis, bit, last),
-            shape((2, rank if last else 2 * rank, half)),
-            (maps[level], x, swapped(x, axis, bit)),
+            shape((levels, 2, rank, half) if last else (2, 2 * rank, half)),
+            (maps[level], x, swapped(x, axis, bit), *(nodes if last else ())),
         )
         nodes.append(x)
-    early = call(collect_body, shape((levels - 1, 2, rank, half)), nodes[:-1])
-    early_other = swapped(early, "sub", 0)
-    late_other = swapped(x, "sub", 0)
+        x = new
     return call(
         functools.partial(output_body, vectors),
         shape((1, levels, 2, rank, samples)),
-        (early, early_other, x, late_other),
+        (x, swapped(x, "sub", 0)),
     )
 
 

time: 73.7 us -> 65.7 us (0.89)
  starting transfers between devices: 41.4 us -> 32.8 us
  local copies, waits for them, and re-layouts: 5.23 us -> 5.99 us
    ppermute x11 -> x10, starting transfers between devices: 32 us -> 22.1 us  [swapped(): lax.ppermute(x, axis, [(i, i ^ 1 << bit) for i in range(lax.axis_size(axi...]
    all_to_all x1, starting transfers between devices: 7.38 us -> 8.69 us  [local(): lax.all_to_all(blocks, 'sub', split_axis=0, concat_axis=0, tiled=True, ax...]
    unnamed x15 -> x16, local copies, waits for them, and re-layouts: 5.23 us -> 5.99 us
    pallas_call x12 -> x10, Pallas kernels: 10.6 us -> 10.3 us  [call(): pl.pallas_call(body, out_shape=out_shape, in_specs=[SMEM] * smem + [space...]
    ppermute x11 -> x10, waiting for transfers between devices: 15.8 us -> 16 us  [swapped(): lax.ppermute(x, axis, [(i, i ^ 1 << bit) for i in range(lax.axis_size(axi...]
  transfers between devices with their start and end apart: 15 -> 14, of which waited for: 6 -> 7; matrix products, arithmetic and copies ran while one was open for 2% -> 0% of each run, Pallas kernels for 11% -> 12%
where the time goes in v2:
time: 65.7 us; the launch traced here: 65.2 us
  starting transfers between devices  32.8 us (50%)
  waiting for transfers between devices  16 us (24%)
  Pallas kernels  10.3 us (16%)
  local copies, waits for them, and re-layouts  5.99 us (9%)
    ppermute x10, starting transfers between devices, swapped(): lax.ppermute(x, axis, [(i, i ^ 1 << bit) for i in range(lax.axis_size(axi...  22.1 us
    ppermute x10, waiting for transfers between devices, swapped(): lax.ppermute(x, axis, [(i, i ^ 1 << bit) for i in range(lax.axis_size(axi...  16 us
    pallas_call x10, Pallas kernels, call(): pl.pallas_call(body, out_shape=out_shape, in_specs=[SMEM] * smem + [space...  10.3 us
    all_to_all x1, starting transfers between devices, local(): lax.all_to_all(blocks, 'sub', split_axis=0, concat_axis=0, tiled=True, ax...  8.69 us
    unnamed x16, local copies, waits for them, and re-layouts  5.99 us
  transfers between devices with their start and end apart: 14, of which 7 were waited for; matrix products, arithmetic and copies ran while one was open for 0% of the time, Pallas kernels for 12%

profile of v2, /device:TPU:0, one launch (start us, length us, event | category | flops | bytes accessed | tf_op | source)
XLA Modules:
  0.0 65.2 jit_solution(17542602163588478161)
XLA Ops:
  1.1 1.0 %copy-done.3 = bf16[16,12288]{1,0:T(8,128)(2,1)S(1)} copy-done((bf16[16,12288]{1,0:T(8,128)(2,1)S(1)}, bf16[16,12288]{1,0:T(8,128)(2,1)}, u32[]{:S(2)}) %copy-start.3) | copy-done | bytes 393240
  2.1 0.8 %shard_map.84 = bf16[8,16,1536]{2,1,0:T(8,128)(2,1)} custom-call(bf16[16,12288]{1,0:T(8,128)(2,1)S(1)} %copy-done.3), custom_call_target="tpu_custom_call" | custom-call | flops 1000 | bytes 1000 | tf_op jit(solution)/shard_map/pallas_call | solution.py:36
  2.9 8.7 %all-to-all-start = ((bf16[8,16,1536]{2,1,0:T(8,128)(2,1)}), bf16[8,16,1536]{2,1,0:T(8,128)(2,1)S(1)}, u32[]{:S(2)}, u32[]{:S(2)}) async-start(bf16[8,16,1536]{2,1,0:T(8,128)(2,1)} %shard_map.84), calls=%async_computation | async-start | bytes 786432 | tf_op jit(solution)/shard_map/all_to_all | solution.py:265
  12.3 0.7 %collective-permute-done.inner_ref = s32[1,2,768]{2,1,0:T(2,128)S(1)} collective-permute-done((s32[1,2,768]{2,1,0:T(2,128)}, s32[1,2,768]{2,1,0:T(2,128)S(1)}, u32[]{:S(2)}, u32[]{:S(2)}) %collective-permute-start) | collective-permute-done | bytes 6176 | tf_op jit(solution)/shard_map/ppermute | solution.py:245
  13.0 1.7 %copy-done = bf16[6,12,128,128]{3,2,1,0:T(8,128)(2,1)S(1)} copy-done((bf16[6,12,128,128]{3,2,1,0:T(8,128)(2,1)S(1)}, bf16[6,12,128,128]{3,2,1,0:T(8,128)(2,1)}, u32[]{:S(2)}) %copy-start) | copy-done | bytes 2359320
  14.7 1.0 %copy-done.2 = bf16[768,256]{1,0:T(8,128)(2,1)S(1)} copy-done((bf16[768,256]{1,0:T(8,128)(2,1)S(1)}, bf16[768,256]{1,0:T(8,128)(2,1)}, u32[]{:S(2)}) %copy-start.2) | copy-done | bytes 393240
  15.7 1.0 %copy-done.4 = bf16[1,2,672,96]{2,3,1,0:T(8,128)(2,1)S(1)} copy-done((bf16[1,2,672,96]{2,3,1,0:T(8,128)(2,1)S(1)}, bf16[1,2,672,96]{2,3,1,0:T(8,128)(2,1)}, u32[]{:S(2)}) %copy-start.4) | copy-done | bytes 258072
  16.6 0.7 %copy-done.6 = s32[1,2,768]{2,1,0:T(2,128)S(1)} copy-done((s32[1,2,768]{2,1,0:T(2,128)S(1)}, s32[1,2,768]{2,1,0:T(2,128)}, u32[]{:S(2)}) %copy-start.6) | copy-done | bytes 6168
  17.3 0.7 %copy-done.7 = s32[6,12]{1,0:T(8,128)S(1)} copy-done((s32[6,12]{1,0:T(8,128)S(1)}, s32[6,12]{1,0:T(8,128)}, u32[]{:S(2)}) %copy-start.7) | copy-done | bytes 312
  18.0 4.4 %shard_map.83 = (bf16[384,768]{1,0:T(8,128)(2,1)S(1)}, bf16[192,128]{1,0:T(8,128)(2,1)S(1)}, bf16[192,128]{1,0:T(8,128)(2,1)S(1)}) custom-call(s32[6,12]{1,0:T(8,128)S(1)} %copy-done.7, bf16[6,12,128,128]{3,2,1,0:T(8,128)(2,1)S(1)} %copy-done, s32[1,2,768]{2,1,0:T(2,128)S(1)} %copy-done.6, s32[1,2,768]{2,1,0:T(2,128)S(1)} %collective-permute-done.inner_ref, ...), custom_call_target="tpu_custom_call" | custom-call | flops 1000 | bytes 1000 | tf_op jit(solution)/shard_map/pallas_call | solution.py:36
  22.5 5.2 %collective-permute-start.5 = (bf16[384,768]{1,0:T(8,128)(2,1)S(1)}, bf16[384,768]{1,0:T(8,128)(2,1)S(1)}, u32[]{:S(2)}, u32[]{:S(2)}) collective-permute-start(bf16[384,768]{1,0:T(8,128)(2,1)S(1)} %get-tuple-element.24.adj_ref), channel_id=1, source_target_pairs={{0,1},{1,0},{2,3},{3,2},{4,5},{5,4},{6,7},{7,6},{8,9},{9,8},{10,11... | collective-permute-start | bytes 1769480 | tf_op jit(solution)/shard_map/ppermute | solution.py:245
  27.7 1.5 %collective-permute-done.5.other_ref = bf16[384,768]{1,0:T(8,128)(2,1)S(1)} collective-permute-done((bf16[384,768]{1,0:T(8,128)(2,1)S(1)}, bf16[384,768]{1,0:T(8,128)(2,1)S(1)}, u32[]{:S(2)}, u32[]{:S(2)}) %collective-permute-start.5) | collective-permute-done | bytes 589856 | tf_op jit(solution)/shard_map/ppermute | solution.py:245
  29.8 2.7 %collective-permute-start.6 = (bf16[96,128]{1,0:T(8,128)(2,1)S(1)}, bf16[96,128]{1,0:T(8,128)(2,1)S(1)}, u32[]{:S(2)}, u32[]{:S(2)}) collective-permute-start(bf16[96,128]{1,0:T(8,128)(2,1)S(1)} %get-tuple-element.27), channel_id=1, source_target_pairs={{0,2},{1,3},{2,0},{3,1},{4,6},{5,7},{6,4},{7,5},{8,10},{9,11},{10,... | collective-permute-start | bytes 73736 | tf_op jit(solution)/shard_map/ppermute | solution.py:245
  33.1 2.4 %shard_map.82 = (bf16[2,2,288,96]{3,2,1,0:T(8,128)(2,1)S(1)}, bf16[2,2,288,96]{3,2,1,0:T(8,128)(2,1)S(1)}, bf16[2,2,288,96]{3,2,1,0:T(8,128)(2,1)S(1)}, bf16[2,2...) custom-call(bf16[1,5,4,96,96]{4,3,2,1,0:T(8,128)(2,1)S(1)} %copy-done.1, s32[1,5,2,192]{3,2,1,0:T(2,128)S(1)} %copy-done.5), custom_call_target="tpu_custom_call" | custom-call | flops 1000 | bytes 1000 | tf_op jit(solution)/shard_map/pallas_call | solution.py:36
  35.8 7.4 %collective-permute-start.8 = (bf16[2,192,128]{2,1,0:T(8,128)(2,1)S(1)}, bf16[2,192,128]{2,1,0:T(8,128)(2,1)S(1)}, u32[]{:S(2)}, u32[]{:S(2)}) collective-permute-start(bf16[2,192,128]{2,1,0:T(8,128)(2,1)S(1)} %shard_map.86.mine_ref.refs_0_), channel_id=1, source_target_pairs={{0,2},{1,3},{2,0},{3,1},{4,6},{5,7},{6,4},{7,5},{8,10},{9,11},{10,... | collective-permute-start | bytes 294920 | tf_op jit(solution)/shard_map/ppermute | solution.py:245
  43.2 2.8 %collective-permute-done.8.other_ref = bf16[2,192,128]{2,1,0:T(8,128)(2,1)S(1)} collective-permute-done((bf16[2,192,128]{2,1,0:T(8,128)(2,1)S(1)}, bf16[2,192,128]{2,1,0:T(8,128)(2,1)S(1)}, u32[]{:S(2)}, u32[]{:S(2)}) %collective-permute-start.8) | collective-permute-done | bytes 98336 | tf_op jit(solution)/shard_map/ppermute | solution.py:245
  46.2 2.7 %collective-permute-start.9 = (bf16[2,192,128]{2,1,0:T(8,128)(2,1)S(1)}, bf16[2,192,128]{2,1,0:T(8,128)(2,1)S(1)}, u32[]{:S(2)}, u32[]{:S(2)}) collective-permute-start(bf16[2,192,128]{2,1,0:T(8,128)(2,1)S(1)} %shard_map.87.mine_ref.refs_1_), channel_id=1, source_target_pairs={{0,4},{1,5},{2,6},{3,7},{4,0},{5,1},{6,2},{7,3},{8,12},{9,13},{10,... | collective-permute-start | bytes 294920 | tf_op jit(solution)/shard_map/ppermute | solution.py:245
  48.9 2.7 %collective-permute-done.9.other_ref = bf16[2,192,128]{2,1,0:T(8,128)(2,1)S(1)} collective-permute-done((bf16[2,192,128]{2,1,0:T(8,128)(2,1)S(1)}, bf16[2,192,128]{2,1,0:T(8,128)(2,1)S(1)}, u32[]{:S(2)}, u32[]{:S(2)}) %collective-permute-start.9) | collective-permute-done | bytes 98336 | tf_op jit(solution)/shard_map/ppermute | solution.py:245
  51.8 1.9 %collective-permute-start.10 = (bf16[2,192,128]{2,1,0:T(8,128)(2,1)S(1)}, bf16[2,192,128]{2,1,0:T(8,128)(2,1)S(1)}, u32[]{:S(2)}, u32[]{:S(2)}) collective-permute-start(bf16[2,192,128]{2,1,0:T(8,128)(2,1)S(1)} %shard_map.88.mine_ref.refs_2_), channel_id=1, source_target_pairs={{0,8},{1,9},{2,10},{3,11},{4,12},{5,13},{6,14},{7,15},{8,0},{9,1},... | collective-permute-start | bytes 294920 | tf_op jit(solution)/shard_map/ppermute | solution.py:245
  53.7 3.7 %collective-permute-done.10.other_ref = bf16[2,192,128]{2,1,0:T(8,128)(2,1)S(1)} collective-permute-done((bf16[2,192,128]{2,1,0:T(8,128)(2,1)S(1)}, bf16[2,192,128]{2,1,0:T(8,128)(2,1)S(1)}, u32[]{:S(2)}, u32[]{:S(2)}) %collective-permute-start.10) | collective-permute-done | bytes 98336 | tf_op jit(solution)/shard_map/ppermute | solution.py:245
  57.7 1.6 %collective-permute-start.11 = (bf16[2,192,128]{2,1,0:T(8,128)(2,1)S(1)}, bf16[2,192,128]{2,1,0:T(8,128)(2,1)S(1)}, u32[]{:S(2)}, u32[]{:S(2)}) collective-permute-start(bf16[2,192,128]{2,1,0:T(8,128)(2,1)S(1)} %shard_map.89.mine_ref), channel_id=1, source_target_pairs={{0,16},{16,0},{1,17},{17,1},{2,18},{18,2},{3,19},{19,3},{4,20},{20... | collective-permute-start | bytes 294920 | tf_op jit(solution)/shard_map/ppermute | solution.py:245
  59.2 3.1 %collective-permute-done.11.other_ref = bf16[2,192,128]{2,1,0:T(8,128)(2,1)S(1)} collective-permute-done((bf16[2,192,128]{2,1,0:T(8,128)(2,1)S(1)}, bf16[2,192,128]{2,1,0:T(8,128)(2,1)S(1)}, u32[]{:S(2)}, u32[]{:S(2)}) %collective-permute-start.11) | collective-permute-done | bytes 98336 | tf_op jit(solution)/shard_map/ppermute | solution.py:245
  62.7 1.5 %collective-permute-done.12.other_ref = bf16[5,2,96,128]{3,2,1,0:T(8,128)(2,1)S(1)} collective-permute-done((bf16[5,2,96,128]{3,2,1,0:T(8,128)(2,1)S(1)}, bf16[5,2,96,128]{3,2,1,0:T(8,128)(2,1)S(1)}, u32[]{:S(2)}, u32[]{:S(2)}) %collective-permute-start.12) | collective-permute-done | bytes 245792 | tf_op jit(solution)/shard_map/ppermute | solution.py:245
  64.2 1.1 %shard_map.91 = bf16[1,5,2,96,256]{4,3,2,1,0:T(8,128)(2,1)} custom-call(bf16[5,2,96,128]{3,2,1,0:T(8,128)(2,1)S(1)} %shard_map.90.mine_ref, bf16[5,2,96,128]{3,2,1,0:T(8,128)(2,1)S(1)} %collective-permute-done.12.other_ref), custom_call_target="tpu_custom_call" | custom-call | flops 1000 | bytes 1000 | tf_op jit(solution)/shard_map/pallas_call | solution.py:36
  (30 shorter events, 4.2 us)
Async XLA Ops:
  0.0 13.0 %collective-permute-start.2 = (bf16[768,256]{1,0:T(8,128)(2,1)}, bf16[768,256]{1,0:T(8,128)(2,1)S(1)}, u32[]{:S(2)}, u32[]{:S(2)}) collective-permute-start(bf16[768,256]{1,0:T(8,128)(2,1)} %omega_ref.1), channel_id=1, source_target_pairs={{0,1},{1,0},{2,3},{3,2},{4,5},{5,4},{6,7},{7,6},{8,9},{9,8},{10,11... | collective-permute-start | bytes 1179656 | tf_op jit(solution)/shard_map/ppermute | solution.py:245
  0.5 12.6 %collective-permute-start.3 = (bf16[768,256]{1,0:T(8,128)(2,1)}, bf16[768,256]{1,0:T(8,128)(2,1)S(1)}, u32[]{:S(2)}, u32[]{:S(2)}) collective-permute-start(bf16[768,256]{1,0:T(8,128)(2,1)} %omega_ref.1), channel_id=1, source_target_pairs={{1,2},{3,4},{5,6},{7,8},{9,10},{11,12},{13,14},{2,1},{4,3},{6,5},{... | collective-permute-start | bytes 1179656 | tf_op jit(solution)/shard_map/ppermute | solution.py:269
  1.1 1.0 %copy-start.3 = (bf16[16,12288]{1,0:T(8,128)(2,1)S(1)}, bf16[16,12288]{1,0:T(8,128)(2,1)}, u32[]{:S(2)}) copy-start(bf16[16,12288]{1,0:T(8,128)(2,1)} %tests_ref.1) | copy-start | bytes 1179652
  2.9 24.8 %all-to-all-start = ((bf16[8,16,1536]{2,1,0:T(8,128)(2,1)}), bf16[8,16,1536]{2,1,0:T(8,128)(2,1)S(1)}, u32[]{:S(2)}, u32[]{:S(2)}) async-start(bf16[8,16,1536]{2,1,0:T(8,128)(2,1)} %shard_map.84), calls=%async_computation | async-start | bytes 786432 | tf_op jit(solution)/shard_map/all_to_all | solution.py:265
  11.6 1.4 %collective-permute-start = (s32[1,2,768]{2,1,0:T(2,128)}, s32[1,2,768]{2,1,0:T(2,128)S(1)}, u32[]{:S(2)}, u32[]{:S(2)}) collective-permute-start(s32[1,2,768]{2,1,0:T(2,128)} %own_ref.1), channel_id=1, source_target_pairs={{0,1},{1,0},{2,3},{3,2},{4,5},{5,4},{6,7},{7,6},{8,9},{9,8},{10,11... | collective-permute-start | bytes 18440 | tf_op jit(solution)/shard_map/ppermute | solution.py:245
  11.6 1.4 %collective-permute-start.1 = (s32[1,2,768]{2,1,0:T(2,128)}, s32[1,2,768]{2,1,0:T(2,128)S(1)}, u32[]{:S(2)}, u32[]{:S(2)}) collective-permute-start(s32[1,2,768]{2,1,0:T(2,128)} %own_ref.1), channel_id=1, source_target_pairs={{1,2},{3,4},{5,6},{7,8},{9,10},{11,12},{13,14},{2,1},{4,3},{6,5},{... | collective-permute-start | bytes 18440 | tf_op jit(solution)/shard_map/ppermute | solution.py:271
  13.0 1.7 %copy-start = (bf16[6,12,128,128]{3,2,1,0:T(8,128)(2,1)S(1)}, bf16[6,12,128,128]{3,2,1,0:T(8,128)(2,1)}, u32[]{:S(2)}) copy-start(bf16[6,12,128,128]{3,2,1,0:T(8,128)(2,1)} %tiles_ref.1) | copy-start | bytes 7077892
  14.7 1.0 %copy-start.2 = (bf16[768,256]{1,0:T(8,128)(2,1)S(1)}, bf16[768,256]{1,0:T(8,128)(2,1)}, u32[]{:S(2)}) copy-start(bf16[768,256]{1,0:T(8,128)(2,1)} %omega_ref.1) | copy-start | bytes 1179652
  15.7 1.0 %copy-start.4 = (bf16[1,2,672,96]{2,3,1,0:T(8,128)(2,1)S(1)}, bf16[1,2,672,96]{2,3,1,0:T(8,128)(2,1)}, u32[]{:S(2)}) copy-start(bf16[1,2,672,96]{2,3,1,0:T(8,128)(2,1)} %param.13) | copy-start | bytes 774148
  16.6 0.7 %copy-start.6 = (s32[1,2,768]{2,1,0:T(2,128)S(1)}, s32[1,2,768]{2,1,0:T(2,128)}, u32[]{:S(2)}) copy-start(s32[1,2,768]{2,1,0:T(2,128)} %own_ref.1) | copy-start | bytes 18436
  17.3 0.7 %copy-start.7 = (s32[6,12]{1,0:T(8,128)S(1)}, s32[6,12]{1,0:T(8,128)}, u32[]{:S(2)}) copy-start(s32[6,12]{1,0:T(8,128)} %cols_ref.1) | copy-start | bytes 868
  18.0 15.1 %copy-start.1 = (bf16[1,5,4,96,96]{4,3,2,1,0:T(8,128)(2,1)S(1)}, bf16[1,5,4,96,96]{4,3,2,1,0:T(8,128)(2,1)}, u32[]{:S(2)}) copy-start(bf16[1,5,4,96,96]{4,3,2,1,0:T(8,128)(2,1)} %maps_ref.1) | copy-start | bytes 1105924
  18.0 15.1 %copy-start.5 = (s32[1,5,2,192]{3,2,1,0:T(2,128)S(1)}, s32[1,5,2,192]{3,2,1,0:T(2,128)}, u32[]{:S(2)}) copy-start(s32[1,5,2,192]{3,2,1,0:T(2,128)} %perms_ref.1) | copy-start | bytes 23044
  22.5 6.8 %collective-permute-start.5 = (bf16[384,768]{1,0:T(8,128)(2,1)S(1)}, bf16[384,768]{1,0:T(8,128)(2,1)S(1)}, u32[]{:S(2)}, u32[]{:S(2)}) collective-permute-start(bf16[384,768]{1,0:T(8,128)(2,1)S(1)} %get-tuple-element.24.adj_ref), channel_id=1, source_target_pairs={{0,1},{1,0},{2,3},{3,2},{4,5},{5,4},{6,7},{7,6},{8,9},{9,8},{10,11... | collective-permute-start | bytes 1769480 | tf_op jit(solution)/shard_map/ppermute | solution.py:245
  27.6 7.9 %collective-permute-start.4 = (bf16[192,128]{1,0:T(8,128)(2,1)S(1)}, bf16[192,128]{1,0:T(8,128)(2,1)S(1)}, u32[]{:S(2)}, u32[]{:S(2)}) collective-permute-start(bf16[192,128]{1,0:T(8,128)(2,1)S(1)} %get-tuple-element.23), channel_id=1, source_target_pairs={{0,1},{1,0},{2,3},{3,2},{4,5},{5,4},{6,7},{7,6},{8,9},{9,8},{10,11... | collective-permute-start | bytes 147464 | tf_op jit(solution)/shard_map/ppermute | solution.py:245
  29.8 5.8 %collective-permute-start.6 = (bf16[96,128]{1,0:T(8,128)(2,1)S(1)}, bf16[96,128]{1,0:T(8,128)(2,1)S(1)}, u32[]{:S(2)}, u32[]{:S(2)}) collective-permute-start(bf16[96,128]{1,0:T(8,128)(2,1)S(1)} %get-tuple-element.27), channel_id=1, source_target_pairs={{0,2},{1,3},{2,0},{3,1},{4,6},{5,7},{6,4},{7,5},{8,10},{9,11},{10,... | collective-permute-start | bytes 73736 | tf_op jit(solution)/shard_map/ppermute | solution.py:245
  32.5 3.1 %collective-permute-start.7 = (bf16[96,128]{1,0:T(8,128)(2,1)S(1)}, bf16[96,128]{1,0:T(8,128)(2,1)S(1)}, u32[]{:S(2)}, u32[]{:S(2)}) collective-permute-start(bf16[96,128]{1,0:T(8,128)(2,1)S(1)} %get-tuple-element.28), channel_id=1, source_target_pairs={{2,4},{3,5},{6,8},{7,9},{10,12},{11,13},{4,2},{5,3},{8,6},{9,7},{1... | collective-permute-start | bytes 73736 | tf_op jit(solution)/shard_map/ppermute | solution.py:301
  35.8 10.2 %collective-permute-start.8 = (bf16[2,192,128]{2,1,0:T(8,128)(2,1)S(1)}, bf16[2,192,128]{2,1,0:T(8,128)(2,1)S(1)}, u32[]{:S(2)}, u32[]{:S(2)}) collective-permute-start(bf16[2,192,128]{2,1,0:T(8,128)(2,1)S(1)} %shard_map.86.mine_ref.refs_0_), channel_id=1, source_target_pairs={{0,2},{1,3},{2,0},{3,1},{4,6},{5,7},{6,4},{7,5},{8,10},{9,11},{10,... | collective-permute-start | bytes 294920 | tf_op jit(solution)/shard_map/ppermute | solution.py:245
  46.2 5.4 %collective-permute-start.9 = (bf16[2,192,128]{2,1,0:T(8,128)(2,1)S(1)}, bf16[2,192,128]{2,1,0:T(8,128)(2,1)S(1)}, u32[]{:S(2)}, u32[]{:S(2)}) collective-permute-start(bf16[2,192,128]{2,1,0:T(8,128)(2,1)S(1)} %shard_map.87.mine_ref.refs_1_), channel_id=1, source_target_pairs={{0,4},{1,5},{2,6},{3,7},{4,0},{5,1},{6,2},{7,3},{8,12},{9,13},{10,... | collective-permute-start | bytes 294920 | tf_op jit(solution)/shard_map/ppermute | solution.py:245
  51.8 5.6 %collective-permute-start.10 = (bf16[2,192,128]{2,1,0:T(8,128)(2,1)S(1)}, bf16[2,192,128]{2,1,0:T(8,128)(2,1)S(1)}, u32[]{:S(2)}, u32[]{:S(2)}) collective-permute-start(bf16[2,192,128]{2,1,0:T(8,128)(2,1)S(1)} %shard_map.88.mine_ref.refs_2_), channel_id=1, source_target_pairs={{0,8},{1,9},{2,10},{3,11},{4,12},{5,13},{6,14},{7,15},{8,0},{9,1},... | collective-permute-start | bytes 294920 | tf_op jit(solution)/shard_map/ppermute | solution.py:245
  57.7 4.7 %collective-permute-start.11 = (bf16[2,192,128]{2,1,0:T(8,128)(2,1)S(1)}, bf16[2,192,128]{2,1,0:T(8,128)(2,1)S(1)}, u32[]{:S(2)}, u32[]{:S(2)}) collective-permute-start(bf16[2,192,128]{2,1,0:T(8,128)(2,1)S(1)} %shard_map.89.mine_ref), channel_id=1, source_target_pairs={{0,16},{16,0},{1,17},{17,1},{2,18},{18,2},{3,19},{19,3},{4,20},{20... | collective-permute-start | bytes 294920 | tf_op jit(solution)/shard_map/ppermute | solution.py:245
  62.6 1.6 %collective-permute-start.12 = (bf16[5,2,96,128]{3,2,1,0:T(8,128)(2,1)S(1)}, bf16[5,2,96,128]{3,2,1,0:T(8,128)(2,1)S(1)}, u32[]{:S(2)}, u32[]{:S(2)}) collective-permute-start(bf16[5,2,96,128]{3,2,1,0:T(8,128)(2,1)S(1)} %shard_map.90.mine_ref), channel_id=1, source_target_pairs={{0,1},{1,0},{2,3},{3,2},{4,5},{5,4},{6,7},{7,6},{8,9},{9,8},{10,11... | collective-permute-start | bytes 737288 | tf_op jit(solution)/shard_map/ppermute | solution.py:245

commit v3 on v2

--- a/solution.py
+++ b/solution.py
@@ -9,8 +9,11 @@
 
 BF = jnp.bfloat16
 F32 = jnp.float32
-VMEM = pl.BlockSpec(memory_space=pltpu.VMEM)
-SMEM = pl.BlockSpec(memory_space=pltpu.SMEM)
+SPACES = {
+    "h": pl.BlockSpec(memory_space=pltpu.HBM),
+    "a": pl.BlockSpec(memory_space=pl.ANY),
+    "v": pl.BlockSpec(memory_space=pltpu.VMEM),
+}
 
 
 def mm(a, b):
@@ -31,16 +34,15 @@
     return jnp.where(hit, 1.0, 0.0).astype(BF)
 
 
-def call(body, out_shape, args, scratch=(), smem=0, anywhere=False, limit=40 << 20):
-    space = pl.BlockSpec(memory_space=pl.ANY) if anywhere else VMEM
+def call(body, out_shape, args, scratch=(), specs=None, out="v", limit=40 << 20, flops=1000):
     return pl.pallas_call(
         body,
         out_shape=out_shape,
-        in_specs=[SMEM] * smem + [space] * (len(args) - smem),
-        out_specs=jax.tree.map(lambda _: space, out_shape),
+        in_specs=[SPACES[c] for c in specs or "v" * len(args)],
+        out_specs=jax.tree.map(lambda _: SPACES[out], out_shape),
         scratch_shapes=list(scratch),
         compiler_params=pltpu.CompilerParams(vmem_limit_bytes=limit),
-        cost_estimate=pl.CostEstimate(flops=1000, bytes_accessed=1000, transcendentals=0),
+        cost_estimate=pl.CostEstimate(flops=flops, bytes_accessed=1000, transcendentals=0),
     )(*args)
 
 
@@ -48,40 +50,73 @@
     return jax.ShapeDtypeStruct(dims, dtype)
 
 
-def split_body(width, tests_ref, out_ref, sems):
-    copies = [
-        pltpu.make_async_copy(
-            tests_ref.at[:, chip * width : (chip + 1) * width], out_ref.at[chip], sems.at[chip]
+DIGIT = 32
+
+
+def pack_body(width, tests_ref, omega_ref, perms_ref, out_ref, packed_ref, order_ref, sems):
+    rows, cols = omega_ref.shape
+    chips = out_ref.shape[0]
+    copies = [pltpu.make_async_copy(omega_ref, packed_ref.at[:rows], sems.at[chips])]
+    for chip in range(chips):
+        copies.append(
+            pltpu.make_async_copy(
+                tests_ref.at[:, chip * width : (chip + 1) * width], out_ref.at[chip], sems.at[chip]
+            )
         )
-        for chip in range(out_ref.shape[0])
-    ]
     for copy in copies:
         copy.start()
+    order = perms_ref[0, 1:2, :cols]
+    row = lax.broadcasted_iota(jnp.int32, order_ref.shape, 0)
+    digits = jnp.where(row == 0, order // DIGIT, jnp.where(row == 1, order % DIGIT, 0))
+    order_ref[...] = digits.astype(F32).astype(BF)
+    copies.append(pltpu.make_async_copy(order_ref, packed_ref.at[rows:], sems.at[chips + 1]))
+    copies[-1].start()
     for copy in copies:
         copy.wait()
 
 
 def select_body(
-    cols_ref,
-    tiles_ref,
-    own_ref,
-    inner_ref,
-    outer_ref,
-    interp_ref,
-    omega_ref,
-    omega_inner,
-    omega_outer,
+    cols_hbm,
+    tiles_hbm,
+    perms_hbm,
+    interp_hbm,
+    omega_hbm,
+    inner_hbm,
+    outer_hbm,
+    after_hbm,
     adj_ref,
     mine_ref,
     other_ref,
     dense_ref,
+    cols_ref,
+    perms_ref,
+    interp_ref,
+    omega_ref,
+    inner_ref,
+    outer_ref,
+    sems,
 ):
-    per_dev, slots, tile = tiles_ref.shape[:3]
+    del after_hbm
+    per_dev, slots, tile = tiles_hbm.shape[:3]
     rows = per_dev * tile
     rank = interp_ref.shape[-2]
+    half = omega_ref.shape[1] // 2
     core = lax.axis_index("sub") & 1
     first = (lax.axis_index("grp") * lax.axis_size("sub") + lax.axis_index("sub")) * per_dev
+    pairs = (
+        (cols_hbm, cols_ref),
+        (perms_hbm, perms_ref),
+        (interp_hbm, interp_ref),
+        (inner_hbm, inner_ref),
+        (outer_hbm, outer_ref),
+        (omega_hbm, omega_ref),
+    )
+    copies = [pltpu.make_async_copy(a, b, sems.at[i]) for i, (a, b) in enumerate(pairs)]
+    for copy in copies:
+        copy.start()
     dense_ref[...] = jnp.zeros_like(dense_ref)
+    moves = []
+    copies[0].wait()
     for q in range(per_dev):
         for t in range(slots):
             col = cols_ref[q, t] - first
@@ -90,32 +125,44 @@
             inner = jnp.where(core == 0, above, below)
             block = jnp.where(below | above, jnp.where(inner, 1, 2), 0)
             at = pl.multiple_of((block * per_dev + place) * tile, tile)
-            dense_ref[q * tile : (q + 1) * tile, pl.ds(at, tile)] = tiles_ref[q, t]
+            move = pltpu.make_async_copy(
+                tiles_hbm.at[q, t],
+                dense_ref.at[q * tile : (q + 1) * tile, pl.ds(at, tile)],
+                sems.at[len(pairs) + q * slots + t],
+            )
+            move.start()
+            moves.append(move)
     unit = eye(rank)
     keeps = []
+    for copy in copies[1:3]:
+        copy.wait()
     for i in range(2):
-        keep = mm_t(unit, one_hot(own_ref[0, i : i + 1, :rank], rows))
-        rest = one_hot(own_ref[0, i : i + 1, rank:], rows)
+        keep = mm_t(unit, one_hot(perms_ref[0, i : i + 1, :rank], rows))
+        rest = one_hot(perms_ref[0, i : i + 1, rank:], rows)
         every = (keep + mm_t(interp_ref[0, i], rest)).astype(BF)
         keeps.append(keep.astype(BF))
         if i == 0:
             adj_ref[3 * rank :] = every
         else:
             tests = every
-    keeps += [
-        mm_t(unit, one_hot(ref[0, 1:2, :rank], rows)).astype(BF) for ref in (inner_ref, outer_ref)
-    ]
+    for copy in copies[3:]:
+        copy.wait()
+    for ref in (inner_ref, outer_ref):
+        digits = ref[rows:].astype(F32)
+        order = (digits[0:1, :rank] * DIGIT + digits[1:2, :rank]).astype(jnp.int32)
+        keeps.append(mm_t(unit, one_hot(order, rows)).astype(BF))
+    for move in moves:
+        move.wait()
     for b, keep in enumerate(keeps[1:]):
         adj_ref[b * rank : (b + 1) * rank] = mm_t(keep, dense_ref[:, b * rows : (b + 1) * rows]).astype(BF)
     near = mm(keeps[0], dense_ref[...]).astype(BF)
-    half = omega_ref.shape[1] // 2
     for out_ref, place in ((mine_ref, core), (other_ref, 1 - core)):
         cols = pl.ds(pl.multiple_of(place * half, half), half)
         own = omega_ref[:, cols]
         fwd = (
             mm(near[:, :rows], own)
-            + mm(near[:, rows : 2 * rows], omega_inner[:, cols])
-            + mm(near[:, 2 * rows :], omega_outer[:, cols])
+            + mm(near[:, rows : 2 * rows], inner_ref[:rows, cols])
+            + mm(near[:, 2 * rows :], outer_ref[:rows, cols])
         )
         out_ref[:rank] = fwd.astype(BF)
         out_ref[rank:] = mm(tests, own).astype(BF)
@@ -257,38 +304,46 @@
     outward = [(i, j) for i in range(1, count - 1, 2) for j in (i + 1,)]
     outward += [(j, i) for i, j in outward]
 
-    blocks = call(
-        functools.partial(split_body, 2 * rows), shape((chips, vectors, 2 * rows)), (adj_tests,),
-        scratch=[pltpu.SemaphoreType.DMA((chips,))], anywhere=True,
-    )
+    blocks, packed = call(
+        functools.partial(pack_body, 2 * rows),
+        [shape((chips, vectors, 2 * rows)), shape((rows + 16, samples))],
+        (adj_tests, omega, leaf_perms),
+        scratch=[pltpu.VMEM((16, samples), BF), pltpu.SemaphoreType.DMA((chips + 2,))],
+        specs="hhv",
+        out="a",
+        limit=56 << 20,
+    )
+    packed_outer = lax.ppermute(packed, "sub", outward)
+    packed_inner = swapped(packed, "sub", 0)
     groups = [[2 * m + c for m in range(chips)] for c in range(2)]
     panel = lax.all_to_all(
         blocks, "sub", split_axis=0, concat_axis=0, tiled=True, axis_index_groups=groups
     ).reshape(half, 2 * rows)
 
-    omega_outer = lax.ppermute(omega, "sub", outward)
-    omega_inner = swapped(omega, "sub", 0)
-    perms_outer = lax.ppermute(leaf_perms, "sub", outward)
-    perms_inner = swapped(leaf_perms, "sub", 0)
+    maps = call(
+        maps_body,
+        [shape((2, 2, 3 * rank, rank))] * levels,
+        (node_maps, node_perms),
+        flops=4 << 30,
+    )
+    interp = jnp.swapaxes(leaf_interp, 2, 3)
     adj, fwd_mine, fwd_send = call(
         select_body,
         [shape((4 * rank, rows))] + [shape((2 * rank, half))] * 2,
-        (
-            tile_cols,
-            near_tiles,
-            leaf_perms,
-            perms_inner,
-            perms_outer,
-            jnp.swapaxes(leaf_interp, 2, 3),
-            omega,
-            omega_inner,
-            omega_outer,
-        ),
-        scratch=[pltpu.VMEM((rows, 3 * rows), BF)],
-        smem=1,
+        (tile_cols, near_tiles, leaf_perms, interp, omega, packed_inner, packed_outer, maps[0]),
+        scratch=[
+            pltpu.VMEM((rows, 3 * rows), BF),
+            pltpu.SMEM(tile_cols.shape, jnp.int32),
+            pltpu.VMEM(leaf_perms.shape, jnp.int32),
+            pltpu.VMEM(interp.shape, BF),
+            pltpu.VMEM(omega.shape, BF),
+            pltpu.VMEM(packed.shape, BF),
+            pltpu.VMEM(packed.shape, BF),
+            pltpu.SemaphoreType.DMA((6 + near_tiles.shape[0] * near_tiles.shape[1],)),
+        ],
+        specs="hhhhhaaa",
     )
     adj_other = swapped(adj, "sub", 0)
-    maps = call(maps_body, [shape((2, 2, 3 * rank, rank))] * levels, (node_maps, node_perms))
     fwd_other = swapped(fwd_send, "sub", 0)
 
     adj_leaf, adj_leaf_other, even_rim, odd_rim = call(

time: 65.7 us -> 87.1 us (1.33)
  Pallas kernels: 10.3 us -> 37.2 us
  local copies, waits for them, and re-layouts: 5.99 us -> 1.75 us
  starting transfers between devices: 32.8 us -> 31.4 us
    pallas_call x10, Pallas kernels: 10.3 us -> 37.2 us  [call(): pl.pallas_call(body, out_shape=out_shape, in_specs=[SPACES[c] for c in sp...]
    unnamed x16 -> x14, local copies, waits for them, and re-layouts: 5.99 us -> 1.75 us
    all_to_all x1, starting transfers between devices: 8.69 us -> 4.88 us  [local(): lax.all_to_all(blocks, 'sub', split_axis=0, concat_axis=0, tiled=True, ax...]
    ppermute x10 -> x9, starting transfers between devices: 22.1 us -> 25.2 us  [swapped(): lax.ppermute(x, axis, [(i, i ^ 1 << bit) for i in range(lax.axis_size(axi...]
    ppermute x10 -> x9, waiting for transfers between devices: 16 us -> 16.1 us  [swapped(): lax.ppermute(x, axis, [(i, i ^ 1 << bit) for i in range(lax.axis_size(axi...]
  transfers between devices with their start and end apart: 14 -> 12, of which waited for: 7 -> 7; matrix products, arithmetic and copies ran while one was open for 0% -> 0% of each run, Pallas kernels for 12% -> 11%
where the time goes in v3:
time: 87.1 us; the launch traced here: 86.7 us
  Pallas kernels  37.2 us (43%)
  starting transfers between devices  31.4 us (36%)
  waiting for transfers between devices  16.1 us (18%)
  local copies, waits for them, and re-layouts  1.75 us (2%)
    pallas_call x10, Pallas kernels, call(): pl.pallas_call(body, out_shape=out_shape, in_specs=[SPACES[c] for c in sp...  37.2 us
    ppermute x9, starting transfers between devices, swapped(): lax.ppermute(x, axis, [(i, i ^ 1 << bit) for i in range(lax.axis_size(axi...  25.2 us
    ppermute x9, waiting for transfers between devices, swapped(): lax.ppermute(x, axis, [(i, i ^ 1 << bit) for i in range(lax.axis_size(axi...  16.1 us
    all_to_all x1, starting transfers between devices, local(): lax.all_to_all(blocks, 'sub', split_axis=0, concat_axis=0, tiled=True, ax...  4.88 us
    unnamed x14, local copies, waits for them, and re-layouts  1.75 us
  transfers between devices with their start and end apart: 12, of which 7 were waited for; matrix products, arithmetic and copies ran while one was open for 0% of the time, Pallas kernels for 11%

profile of v3, /device:TPU:0, one launch (start us, length us, event | category | flops | bytes accessed | tf_op | source)
XLA Modules:
  0.0 86.7 jit_solution(1146670804295122992)
XLA Ops:
  0.0 25.7 %shard_map.83 = (bf16[8,16,1536]{2,1,0:T(8,128)(2,1)}, bf16[784,256]{1,0:T(8,128)(2,1)}) custom-call(bf16[16,12288]{1,0:T(8,128)(2,1)} %tests_ref.1, bf16[768,256]{1,0:T(8,128)(2,1)} %omega_hbm.1, s32[1,2,768]{2,1,0:T(2,128)} %perms_hbm.1), custom_call_target="tpu_custom_call" | custom-call | flops 1000 | bytes 1000 | tf_op jit(solution)/shard_map/pallas_call | solution.py:38
  25.7 0.7 collective-permute-start.1
  26.4 4.3 %collective-permute-start = (bf16[784,256]{1,0:T(8,128)(2,1)}, bf16[784,256]{1,0:T(8,128)(2,1)S(1)}, u32[]{:S(2)}, u32[]{:S(2)}) collective-permute-start(bf16[784,256]{1,0:T(8,128)(2,1)} %get-tuple-element.24), channel_id=1, source_target_pairs={{0,1},{1,0},{2,3},{3,2},{4,5},{5,4},{6,7},{7,6},{8,9},{9,8},{10,11... | collective-permute-start | bytes 1204232 | tf_op jit(solution)/shard_map/ppermute | solution.py:292
  30.7 4.9 %all-to-all-start = ((bf16[8,16,1536]{2,1,0:T(8,128)(2,1)}), bf16[8,16,1536]{2,1,0:T(8,128)(2,1)S(1)}, u32[]{:S(2)}, u32[]{:S(2)}) async-start(bf16[8,16,1536]{2,1,0:T(8,128)(2,1)} %get-tuple-element.28), calls=%async_computation | async-start | bytes 786432 | tf_op jit(solution)/shard_map/all_to_all | solution.py:319
  35.6 1.0 %copy-done.5 = bf16[1,5,4,96,96]{4,3,2,1,0:T(8,128)(2,1)S(1)} copy-done((bf16[1,5,4,96,96]{4,3,2,1,0:T(8,128)(2,1)S(1)}, bf16[1,5,4,96,96]{4,3,2,1,0:T(8,128)(2,1)}, u32[]{:S(2)}) %copy-start.5) | copy-done | bytes 368664
  36.7 0.7 copy-done.6
  37.4 2.4 %shard_map.82 = (bf16[2,2,288,96]{3,2,1,0:T(8,128)(2,1)S(1)}, bf16[2,2,288,96]{3,2,1,0:T(8,128)(2,1)S(1)}, bf16[2,2,288,96]{3,2,1,0:T(8,128)(2,1)S(1)}, bf16[2,2...) custom-call(bf16[1,5,4,96,96]{4,3,2,1,0:T(8,128)(2,1)S(1)} %copy-done.5, s32[1,5,2,192]{3,2,1,0:T(2,128)S(1)} %copy-done.6), custom_call_target="tpu_custom_call" | custom-call | flops 4294967296 | bytes 1000 | tf_op jit(solution)/shard_map/pallas_call | solution.py:38
  39.8 6.5 %shard_map.84 = (bf16[384,768]{1,0:T(8,128)(2,1)S(1)}, bf16[192,128]{1,0:T(8,128)(2,1)S(1)}, bf16[192,128]{1,0:T(8,128)(2,1)S(1)}) custom-call(s32[6,12]{1,0:T(8,128)S(1)} %copy-done.4, bf16[6,12,128,128]{3,2,1,0:T(8,128)(2,1)S(1)} %copy-done, s32[1,2,768]{2,1,0:T(2,128)S(1)} %copy-done.3, bf16[1,2,96,672]{3,2,1,0:T(8,128)(2,1)S(1)} %bitcast.3, ...), custom_call_target="tpu_custom_call" | custom-call | flops 1000 | bytes 1000 | tf_op jit(solution)/shard_map/pallas_call | solution.py:38
  46.3 3.5 %collective-permute-start.3 = (bf16[384,768]{1,0:T(8,128)(2,1)S(1)}, bf16[384,768]{1,0:T(8,128)(2,1)S(1)}, u32[]{:S(2)}, u32[]{:S(2)}) collective-permute-start(bf16[384,768]{1,0:T(8,128)(2,1)S(1)} %get-tuple-element.27.adj_ref), channel_id=1, source_target_pairs={{0,1},{1,0},{2,3},{3,2},{4,5},{5,4},{6,7},{7,6},{8,9},{9,8},{10,11... | collective-permute-start | bytes 1769480 | tf_op jit(solution)/shard_map/ppermute | solution.py:292
  49.9 1.5 %collective-permute-done.3.other_ref = bf16[384,768]{1,0:T(8,128)(2,1)S(1)} collective-permute-done((bf16[384,768]{1,0:T(8,128)(2,1)S(1)}, bf16[384,768]{1,0:T(8,128)(2,1)S(1)}, u32[]{:S(2)}, u32[]{:S(2)}) %collective-permute-start.3) | collective-permute-done | bytes 589856 | tf_op jit(solution)/shard_map/ppermute | solution.py:292
  51.5 0.5 shard_map.85
  52.0 2.7 %collective-permute-start.4 = (bf16[96,128]{1,0:T(8,128)(2,1)S(1)}, bf16[96,128]{1,0:T(8,128)(2,1)S(1)}, u32[]{:S(2)}, u32[]{:S(2)}) collective-permute-start(bf16[96,128]{1,0:T(8,128)(2,1)S(1)} %get-tuple-element.31), channel_id=1, source_target_pairs={{0,2},{1,3},{2,0},{3,1},{4,6},{5,7},{6,4},{7,5},{8,10},{9,11},{10,... | collective-permute-start | bytes 73736 | tf_op jit(solution)/shard_map/ppermute | solution.py:292
  54.7 0.7 collective-permute-start.5
  55.3 1.1 %collective-permute-done.4.even_ref = bf16[96,128]{1,0:T(8,128)(2,1)S(1)} collective-permute-done((bf16[96,128]{1,0:T(8,128)(2,1)S(1)}, bf16[96,128]{1,0:T(8,128)(2,1)S(1)}, u32[]{:S(2)}, u32[]{:S(2)}) %collective-permute-start.4) | collective-permute-done | bytes 24608 | tf_op jit(solution)/shard_map/ppermute | solution.py:292
  56.7 5.0 %collective-permute-start.6 = (bf16[2,192,128]{2,1,0:T(8,128)(2,1)S(1)}, bf16[2,192,128]{2,1,0:T(8,128)(2,1)S(1)}, u32[]{:S(2)}, u32[]{:S(2)}) collective-permute-start(bf16[2,192,128]{2,1,0:T(8,128)(2,1)S(1)} %shard_map.86.mine_ref.refs_0_), channel_id=1, source_target_pairs={{0,2},{1,3},{2,0},{3,1},{4,6},{5,7},{6,4},{7,5},{8,10},{9,11},{10,... | collective-permute-start | bytes 294920 | tf_op jit(solution)/shard_map/ppermute | solution.py:292
  61.7 2.6 %collective-permute-done.6.other_ref = bf16[2,192,128]{2,1,0:T(8,128)(2,1)S(1)} collective-permute-done((bf16[2,192,128]{2,1,0:T(8,128)(2,1)S(1)}, bf16[2,192,128]{2,1,0:T(8,128)(2,1)S(1)}, u32[]{:S(2)}, u32[]{:S(2)}) %collective-permute-start.6) | collective-permute-done | bytes 98336 | tf_op jit(solution)/shard_map/ppermute | solution.py:292
  64.5 3.5 %collective-permute-start.7 = (bf16[2,192,128]{2,1,0:T(8,128)(2,1)S(1)}, bf16[2,192,128]{2,1,0:T(8,128)(2,1)S(1)}, u32[]{:S(2)}, u32[]{:S(2)}) collective-permute-start(bf16[2,192,128]{2,1,0:T(8,128)(2,1)S(1)} %shard_map.87.mine_ref.refs_1_), channel_id=1, source_target_pairs={{0,4},{1,5},{2,6},{3,7},{4,0},{5,1},{6,2},{7,3},{8,12},{9,13},{10,... | collective-permute-start | bytes 294920 | tf_op jit(solution)/shard_map/ppermute | solution.py:292
  68.0 2.6 %collective-permute-done.7.other_ref = bf16[2,192,128]{2,1,0:T(8,128)(2,1)S(1)} collective-permute-done((bf16[2,192,128]{2,1,0:T(8,128)(2,1)S(1)}, bf16[2,192,128]{2,1,0:T(8,128)(2,1)S(1)}, u32[]{:S(2)}, u32[]{:S(2)}) %collective-permute-start.7) | collective-permute-done | bytes 98336 | tf_op jit(solution)/shard_map/ppermute | solution.py:292
  70.9 4.4 %collective-permute-start.8 = (bf16[2,192,128]{2,1,0:T(8,128)(2,1)S(1)}, bf16[2,192,128]{2,1,0:T(8,128)(2,1)S(1)}, u32[]{:S(2)}, u32[]{:S(2)}) collective-permute-start(bf16[2,192,128]{2,1,0:T(8,128)(2,1)S(1)} %shard_map.88.mine_ref.refs_2_), channel_id=1, source_target_pairs={{0,8},{1,9},{2,10},{3,11},{4,12},{5,13},{6,14},{7,15},{8,0},{9,1},... | collective-permute-start | bytes 294920 | tf_op jit(solution)/shard_map/ppermute | solution.py:292
  75.3 3.6 %collective-permute-done.8.other_ref = bf16[2,192,128]{2,1,0:T(8,128)(2,1)S(1)} collective-permute-done((bf16[2,192,128]{2,1,0:T(8,128)(2,1)S(1)}, bf16[2,192,128]{2,1,0:T(8,128)(2,1)S(1)}, u32[]{:S(2)}, u32[]{:S(2)}) %collective-permute-start.8) | collective-permute-done | bytes 98336 | tf_op jit(solution)/shard_map/ppermute | solution.py:292
  79.1 1.6 %collective-permute-start.9 = (bf16[2,192,128]{2,1,0:T(8,128)(2,1)S(1)}, bf16[2,192,128]{2,1,0:T(8,128)(2,1)S(1)}, u32[]{:S(2)}, u32[]{:S(2)}) collective-permute-start(bf16[2,192,128]{2,1,0:T(8,128)(2,1)S(1)} %shard_map.89.mine_ref), channel_id=1, source_target_pairs={{0,16},{16,0},{1,17},{17,1},{2,18},{18,2},{3,19},{19,3},{4,20},{20... | collective-permute-start | bytes 294920 | tf_op jit(solution)/shard_map/ppermute | solution.py:292
  80.7 3.1 %collective-permute-done.9.other_ref = bf16[2,192,128]{2,1,0:T(8,128)(2,1)S(1)} collective-permute-done((bf16[2,192,128]{2,1,0:T(8,128)(2,1)S(1)}, bf16[2,192,128]{2,1,0:T(8,128)(2,1)S(1)}, u32[]{:S(2)}, u32[]{:S(2)}) %collective-permute-start.9) | collective-permute-done | bytes 98336 | tf_op jit(solution)/shard_map/ppermute | solution.py:292
  84.1 1.5 %collective-permute-done.10.other_ref = bf16[5,2,96,128]{3,2,1,0:T(8,128)(2,1)S(1)} collective-permute-done((bf16[5,2,96,128]{3,2,1,0:T(8,128)(2,1)S(1)}, bf16[5,2,96,128]{3,2,1,0:T(8,128)(2,1)S(1)}, u32[]{:S(2)}, u32[]{:S(2)}) %collective-permute-start.10) | collective-permute-done | bytes 245792 | tf_op jit(solution)/shard_map/ppermute | solution.py:292
  85.6 1.1 %shard_map.91 = bf16[1,5,2,96,256]{4,3,2,1,0:T(8,128)(2,1)} custom-call(bf16[5,2,96,128]{3,2,1,0:T(8,128)(2,1)S(1)} %shard_map.90.mine_ref, bf16[5,2,96,128]{3,2,1,0:T(8,128)(2,1)S(1)} %collective-permute-done.10.other_ref), custom_call_target="tpu_custom_call" | custom-call | flops 1000 | bytes 1000 | tf_op jit(solution)/shard_map/pallas_call | solution.py:38
  (24 shorter events, 1.3 us)
Async XLA Ops:
  25.7 14.1 %collective-permute-start.1 = (bf16[784,256]{1,0:T(8,128)(2,1)}, bf16[784,256]{1,0:T(8,128)(2,1)S(1)}, u32[]{:S(2)}, u32[]{:S(2)}) collective-permute-start(bf16[784,256]{1,0:T(8,128)(2,1)} %get-tuple-element.24), channel_id=1, source_target_pairs={{1,2},{3,4},{5,6},{7,8},{9,10},{11,12},{13,14},{2,1},{4,3},{6,5},{... | collective-permute-start | bytes 1204232 | tf_op jit(solution)/shard_map/ppermute | solution.py:316
  26.4 13.4 %collective-permute-start = (bf16[784,256]{1,0:T(8,128)(2,1)}, bf16[784,256]{1,0:T(8,128)(2,1)S(1)}, u32[]{:S(2)}, u32[]{:S(2)}) collective-permute-start(bf16[784,256]{1,0:T(8,128)(2,1)} %get-tuple-element.24), channel_id=1, source_target_pairs={{0,1},{1,0},{2,3},{3,2},{4,5},{5,4},{6,7},{7,6},{8,9},{9,8},{10,11... | collective-permute-start | bytes 1204232 | tf_op jit(solution)/shard_map/ppermute | solution.py:292
  30.7 19.2 %all-to-all-start = ((bf16[8,16,1536]{2,1,0:T(8,128)(2,1)}), bf16[8,16,1536]{2,1,0:T(8,128)(2,1)S(1)}, u32[]{:S(2)}, u32[]{:S(2)}) async-start(bf16[8,16,1536]{2,1,0:T(8,128)(2,1)} %get-tuple-element.28), calls=%async_computation | async-start | bytes 786432 | tf_op jit(solution)/shard_map/all_to_all | solution.py:319
  35.6 1.0 %copy-start.5 = (bf16[1,5,4,96,96]{4,3,2,1,0:T(8,128)(2,1)S(1)}, bf16[1,5,4,96,96]{4,3,2,1,0:T(8,128)(2,1)}, u32[]{:S(2)}) copy-start(bf16[1,5,4,96,96]{4,3,2,1,0:T(8,128)(2,1)} %maps_ref.1) | copy-start | bytes 1105924
  36.7 0.7 copy-start.6
  37.4 2.4 %copy-start = (bf16[6,12,128,128]{3,2,1,0:T(8,128)(2,1)S(1)}, bf16[6,12,128,128]{3,2,1,0:T(8,128)(2,1)}, u32[]{:S(2)}) copy-start(bf16[6,12,128,128]{3,2,1,0:T(8,128)(2,1)} %tiles_hbm.1) | copy-start | bytes 7077892
  37.4 2.4 %copy-start.1 = (bf16[768,256]{1,0:T(8,128)(2,1)S(1)}, bf16[768,256]{1,0:T(8,128)(2,1)}, u32[]{:S(2)}) copy-start(bf16[768,256]{1,0:T(8,128)(2,1)} %omega_hbm.1) | copy-start | bytes 1179652
  37.4 2.4 %copy-start.2 = (bf16[1,2,672,96]{2,3,1,0:T(8,128)(2,1)S(1)}, bf16[1,2,672,96]{2,3,1,0:T(8,128)(2,1)}, u32[]{:S(2)}) copy-start(bf16[1,2,672,96]{2,3,1,0:T(8,128)(2,1)} %param.13) | copy-start | bytes 774148
  37.4 2.5 %copy-start.3 = (s32[1,2,768]{2,1,0:T(2,128)S(1)}, s32[1,2,768]{2,1,0:T(2,128)}, u32[]{:S(2)}) copy-start(s32[1,2,768]{2,1,0:T(2,128)} %perms_hbm.1) | copy-start | bytes 18436
  37.4 2.5 %copy-start.4 = (s32[6,12]{1,0:T(8,128)S(1)}, s32[6,12]{1,0:T(8,128)}, u32[]{:S(2)}) copy-start(s32[6,12]{1,0:T(8,128)} %cols_hbm.1) | copy-start | bytes 868
  46.3 5.2 %collective-permute-start.3 = (bf16[384,768]{1,0:T(8,128)(2,1)S(1)}, bf16[384,768]{1,0:T(8,128)(2,1)S(1)}, u32[]{:S(2)}, u32[]{:S(2)}) collective-permute-start(bf16[384,768]{1,0:T(8,128)(2,1)S(1)} %get-tuple-element.27.adj_ref), channel_id=1, source_target_pairs={{0,1},{1,0},{2,3},{3,2},{4,5},{5,4},{6,7},{7,6},{8,9},{9,8},{10,11... | collective-permute-start | bytes 1769480 | tf_op jit(solution)/shard_map/ppermute | solution.py:292
  49.9 5.5 %collective-permute-start.2 = (bf16[192,128]{1,0:T(8,128)(2,1)S(1)}, bf16[192,128]{1,0:T(8,128)(2,1)S(1)}, u32[]{:S(2)}, u32[]{:S(2)}) collective-permute-start(bf16[192,128]{1,0:T(8,128)(2,1)S(1)} %get-tuple-element.26), channel_id=1, source_target_pairs={{0,1},{1,0},{2,3},{3,2},{4,5},{5,4},{6,7},{7,6},{8,9},{9,8},{10,11... | collective-permute-start | bytes 147464 | tf_op jit(solution)/shard_map/ppermute | solution.py:292
  52.0 4.5 %collective-permute-start.4 = (bf16[96,128]{1,0:T(8,128)(2,1)S(1)}, bf16[96,128]{1,0:T(8,128)(2,1)S(1)}, u32[]{:S(2)}, u32[]{:S(2)}) collective-permute-start(bf16[96,128]{1,0:T(8,128)(2,1)S(1)} %get-tuple-element.31), channel_id=1, source_target_pairs={{0,2},{1,3},{2,0},{3,1},{4,6},{5,7},{6,4},{7,5},{8,10},{9,11},{10,... | collective-permute-start | bytes 73736 | tf_op jit(solution)/shard_map/ppermute | solution.py:292
  54.7 1.8 %collective-permute-start.5 = (bf16[96,128]{1,0:T(8,128)(2,1)S(1)}, bf16[96,128]{1,0:T(8,128)(2,1)S(1)}, u32[]{:S(2)}, u32[]{:S(2)}) collective-permute-start(bf16[96,128]{1,0:T(8,128)(2,1)S(1)} %get-tuple-element.32), channel_id=1, source_target_pairs={{2,4},{3,5},{6,8},{7,9},{10,12},{11,13},{4,2},{5,3},{8,6},{9,7},{1... | collective-permute-start | bytes 73736 | tf_op jit(solution)/shard_map/ppermute | solution.py:356
  56.7 7.6 %collective-permute-start.6 = (bf16[2,192,128]{2,1,0:T(8,128)(2,1)S(1)}, bf16[2,192,128]{2,1,0:T(8,128)(2,1)S(1)}, u32[]{:S(2)}, u32[]{:S(2)}) collective-permute-start(bf16[2,192,128]{2,1,0:T(8,128)(2,1)S(1)} %shard_map.86.mine_ref.refs_0_), channel_id=1, source_target_pairs={{0,2},{1,3},{2,0},{3,1},{4,6},{5,7},{6,4},{7,5},{8,10},{9,11},{10,... | collective-permute-start | bytes 294920 | tf_op jit(solution)/shard_map/ppermute | solution.py:292
  64.5 6.1 %collective-permute-start.7 = (bf16[2,192,128]{2,1,0:T(8,128)(2,1)S(1)}, bf16[2,192,128]{2,1,0:T(8,128)(2,1)S(1)}, u32[]{:S(2)}, u32[]{:S(2)}) collective-permute-start(bf16[2,192,128]{2,1,0:T(8,128)(2,1)S(1)} %shard_map.87.mine_ref.refs_1_), channel_id=1, source_target_pairs={{0,4},{1,5},{2,6},{3,7},{4,0},{5,1},{6,2},{7,3},{8,12},{9,13},{10,... | collective-permute-start | bytes 294920 | tf_op jit(solution)/shard_map/ppermute | solution.py:292
  70.9 8.0 %collective-permute-start.8 = (bf16[2,192,128]{2,1,0:T(8,128)(2,1)S(1)}, bf16[2,192,128]{2,1,0:T(8,128)(2,1)S(1)}, u32[]{:S(2)}, u32[]{:S(2)}) collective-permute-start(bf16[2,192,128]{2,1,0:T(8,128)(2,1)S(1)} %shard_map.88.mine_ref.refs_2_), channel_id=1, source_target_pairs={{0,8},{1,9},{2,10},{3,11},{4,12},{5,13},{6,14},{7,15},{8,0},{9,1},... | collective-permute-start | bytes 294920 | tf_op jit(solution)/shard_map/ppermute | solution.py:292
  79.1 4.7 %collective-permute-start.9 = (bf16[2,192,128]{2,1,0:T(8,128)(2,1)S(1)}, bf16[2,192,128]{2,1,0:T(8,128)(2,1)S(1)}, u32[]{:S(2)}, u32[]{:S(2)}) collective-permute-start(bf16[2,192,128]{2,1,0:T(8,128)(2,1)S(1)} %shard_map.89.mine_ref), channel_id=1, source_target_pairs={{0,16},{16,0},{1,17},{17,1},{2,18},{18,2},{3,19},{19,3},{4,20},{20... | collective-permute-start | bytes 294920 | tf_op jit(solution)/shard_map/ppermute | solution.py:292
  84.1 1.6 %collective-permute-start.10 = (bf16[5,2,96,128]{3,2,1,0:T(8,128)(2,1)S(1)}, bf16[5,2,96,128]{3,2,1,0:T(8,128)(2,1)S(1)}, u32[]{:S(2)}, u32[]{:S(2)}) collective-permute-start(bf16[5,2,96,128]{3,2,1,0:T(8,128)(2,1)S(1)} %shard_map.90.mine_ref), channel_id=1, source_target_pairs={{0,1},{1,0},{2,3},{3,2},{4,5},{5,4},{6,7},{7,6},{8,9},{9,8},{10,11... | collective-permute-start | bytes 737288 | tf_op jit(solution)/shard_map/ppermute | solution.py:292

commit v4 on v3

--- a/solution.py
+++ b/solution.py
@@ -12,6 +12,7 @@
 SPACES = {
     "h": pl.BlockSpec(memory_space=pltpu.HBM),
     "a": pl.BlockSpec(memory_space=pl.ANY),
+    "s": pl.BlockSpec(memory_space=pltpu.SMEM),
     "v": pl.BlockSpec(memory_space=pltpu.VMEM),
 }
 
@@ -75,48 +76,14 @@
         copy.wait()
 
 
-def select_body(
-    cols_hbm,
-    tiles_hbm,
-    perms_hbm,
-    interp_hbm,
-    omega_hbm,
-    inner_hbm,
-    outer_hbm,
-    after_hbm,
-    adj_ref,
-    mine_ref,
-    other_ref,
-    dense_ref,
-    cols_ref,
-    perms_ref,
-    interp_ref,
-    omega_ref,
-    inner_ref,
-    outer_ref,
-    sems,
-):
-    del after_hbm
-    per_dev, slots, tile = tiles_hbm.shape[:3]
+def dense_body(cols_ref, tiles_ref, perms_ref, interp_ref, after_ref, keep_ref, near_ref, tests_ref, dense_ref):
+    del after_ref
+    per_dev, slots, tile = tiles_ref.shape[:3]
     rows = per_dev * tile
     rank = interp_ref.shape[-2]
-    half = omega_ref.shape[1] // 2
     core = lax.axis_index("sub") & 1
     first = (lax.axis_index("grp") * lax.axis_size("sub") + lax.axis_index("sub")) * per_dev
-    pairs = (
-        (cols_hbm, cols_ref),
-        (perms_hbm, perms_ref),
-        (interp_hbm, interp_ref),
-        (inner_hbm, inner_ref),
-        (outer_hbm, outer_ref),
-        (omega_hbm, omega_ref),
-    )
-    copies = [pltpu.make_async_copy(a, b, sems.at[i]) for i, (a, b) in enumerate(pairs)]
-    for copy in copies:
-        copy.start()
     dense_ref[...] = jnp.zeros_like(dense_ref)
-    moves = []
-    copies[0].wait()
     for q in range(per_dev):
         for t in range(slots):
             col = cols_ref[q, t] - first
@@ -125,47 +92,46 @@
             inner = jnp.where(core == 0, above, below)
             block = jnp.where(below | above, jnp.where(inner, 1, 2), 0)
             at = pl.multiple_of((block * per_dev + place) * tile, tile)
-            move = pltpu.make_async_copy(
-                tiles_hbm.at[q, t],
-                dense_ref.at[q * tile : (q + 1) * tile, pl.ds(at, tile)],
-                sems.at[len(pairs) + q * slots + t],
-            )
-            move.start()
-            moves.append(move)
+            dense_ref[q * tile : (q + 1) * tile, pl.ds(at, tile)] = tiles_ref[q, t]
     unit = eye(rank)
     keeps = []
-    for copy in copies[1:3]:
-        copy.wait()
     for i in range(2):
         keep = mm_t(unit, one_hot(perms_ref[0, i : i + 1, :rank], rows))
         rest = one_hot(perms_ref[0, i : i + 1, rank:], rows)
         every = (keep + mm_t(interp_ref[0, i], rest)).astype(BF)
         keeps.append(keep.astype(BF))
         if i == 0:
-            adj_ref[3 * rank :] = every
+            keep_ref[rank:] = every
         else:
-            tests = every
-    for copy in copies[3:]:
-        copy.wait()
-    for ref in (inner_ref, outer_ref):
+            tests_ref[...] = every
+    keep_ref[:rank] = mm_t(keeps[1], dense_ref[:, :rows]).astype(BF)
+    near_ref[...] = mm(keeps[0], dense_ref[...]).astype(BF)
+
+
+def halo_body(
+    dense_ref, near_ref, tests_ref, omega_ref, inner_ref, outer_ref, beside_ref, mine_ref, other_ref
+):
+    rows = dense_ref.shape[0]
+    rank = near_ref.shape[0]
+    half = omega_ref.shape[1] // 2
+    core = lax.axis_index("sub") & 1
+    unit = eye(rank)
+    for b, ref in enumerate((inner_ref, outer_ref)):
         digits = ref[rows:].astype(F32)
         order = (digits[0:1, :rank] * DIGIT + digits[1:2, :rank]).astype(jnp.int32)
-        keeps.append(mm_t(unit, one_hot(order, rows)).astype(BF))
-    for move in moves:
-        move.wait()
-    for b, keep in enumerate(keeps[1:]):
-        adj_ref[b * rank : (b + 1) * rank] = mm_t(keep, dense_ref[:, b * rows : (b + 1) * rows]).astype(BF)
-    near = mm(keeps[0], dense_ref[...]).astype(BF)
+        keep = mm_t(unit, one_hot(order, rows)).astype(BF)
+        block = dense_ref[:, (b + 1) * rows : (b + 2) * rows]
+        beside_ref[b * rank : (b + 1) * rank] = mm_t(keep, block).astype(BF)
     for out_ref, place in ((mine_ref, core), (other_ref, 1 - core)):
         cols = pl.ds(pl.multiple_of(place * half, half), half)
         own = omega_ref[:, cols]
         fwd = (
-            mm(near[:, :rows], own)
-            + mm(near[:, rows : 2 * rows], inner_ref[:rows, cols])
-            + mm(near[:, 2 * rows :], outer_ref[:rows, cols])
+            mm(near_ref[:, :rows], own)
+            + mm(near_ref[:, rows : 2 * rows], inner_ref[:rows, cols])
+            + mm(near_ref[:, 2 * rows :], outer_ref[:rows, cols])
         )
         out_ref[:rank] = fwd.astype(BF)
-        out_ref[rank:] = mm(tests, own).astype(BF)
+        out_ref[rank:] = mm(tests_ref[...], own).astype(BF)
 
 
 def maps_body(maps_ref, perms_ref, *out_refs):
@@ -196,18 +162,24 @@
     return (sub & 1) != ((sub >> 1) & 1)
 
 
-def adjoint_body(adj_ref, other_ref, panel_ref, mine_out, other_out, even_out, odd_out):
-    rows = adj_ref.shape[1]
-    rank = adj_ref.shape[0] // 4
-    core = lax.axis_index("sub") & 1
-    mine = mm_t(adj_ref[...], panel_ref[:, pl.ds(pl.multiple_of(core * rows, 128), rows)])
-    other = mm_t(other_ref[...], panel_ref[:, pl.ds(pl.multiple_of((1 - core) * rows, 128), rows)])
-    mine_out[:rank] = mine[:rank] + other[rank : 2 * rank]
-    mine_out[rank:] = mine[3 * rank :]
-    other_out[:rank] = other[:rank] + mine[rank : 2 * rank]
-    other_out[rank:] = other[3 * rank :]
-    mine_rim = mine[2 * rank : 3 * rank]
-    other_rim = other[2 * rank : 3 * rank]
+def adjoint_body(
+    keep_ref, keep_other, beside_ref, beside_other, panel_ref, mine_out, other_out, even_out, odd_out
+):
+    rows = keep_ref.shape[1]
+    rank = keep_ref.shape[0] // 2
+    core = lax.axis_index("sub") & 1
+    panel = panel_ref[:, pl.ds(pl.multiple_of(core * rows, 128), rows)]
+    panel_other = panel_ref[:, pl.ds(pl.multiple_of((1 - core) * rows, 128), rows)]
+    mine = mm_t(keep_ref[...], panel)
+    other = mm_t(keep_other[...], panel_other)
+    from_mine = mm_t(beside_ref[...], panel)
+    from_other = mm_t(beside_other[...], panel_other)
+    mine_out[:rank] = mine[:rank] + from_other[:rank]
+    mine_out[rank:] = mine[rank:]
+    other_out[:rank] = other[:rank] + from_mine[:rank]
+    other_out[rank:] = other[rank:]
+    mine_rim = from_mine[rank:]
+    other_rim = from_other[rank:]
     even = rim_place()
     even_out[...] = jnp.where(even, mine_rim, other_rim).astype(BF)
     odd_out[...] = jnp.where(even, other_rim, mine_rim).astype(BF)
@@ -310,7 +282,6 @@
         (adj_tests, omega, leaf_perms),
         scratch=[pltpu.VMEM((16, samples), BF), pltpu.SemaphoreType.DMA((chips + 2,))],
         specs="hhv",
-        out="a",
         limit=56 << 20,
     )
     packed_outer = lax.ppermute(packed, "sub", outward)
@@ -326,34 +297,35 @@
         (node_maps, node_perms),
         flops=4 << 30,
     )
-    interp = jnp.swapaxes(leaf_interp, 2, 3)
-    adj, fwd_mine, fwd_send = call(
-        select_body,
-        [shape((4 * rank, rows))] + [shape((2 * rank, half))] * 2,
-        (tile_cols, near_tiles, leaf_perms, interp, omega, packed_inner, packed_outer, maps[0]),
-        scratch=[
-            pltpu.VMEM((rows, 3 * rows), BF),
-            pltpu.SMEM(tile_cols.shape, jnp.int32),
-            pltpu.VMEM(leaf_perms.shape, jnp.int32),
-            pltpu.VMEM(interp.shape, BF),
-            pltpu.VMEM(omega.shape, BF),
-            pltpu.VMEM(packed.shape, BF),
-            pltpu.VMEM(packed.shape, BF),
-            pltpu.SemaphoreType.DMA((6 + near_tiles.shape[0] * near_tiles.shape[1],)),
+    keep, near, tests, dense = call(
+        dense_body,
+        [
+            shape((2 * rank, rows)),
+            shape((rank, 3 * rows)),
+            shape((rank, rows)),
+            shape((rows, 3 * rows)),
         ],
-        specs="hhhhhaaa",
-    )
-    adj_other = swapped(adj, "sub", 0)
+        (tile_cols, near_tiles, leaf_perms, jnp.swapaxes(leaf_interp, 2, 3), maps[0]),
+        specs="svvva",
+        flops=4 << 30,
+    )
+    keep_other = swapped(keep, "sub", 0)
+    beside, fwd_mine, fwd_send = call(
+        halo_body,
+        [shape((2 * rank, rows))] + [shape((2 * rank, half))] * 2,
+        (dense, near, tests, omega, packed_inner, packed_outer),
+    )
+    beside_other = swapped(beside, "sub", 0)
     fwd_other = swapped(fwd_send, "sub", 0)
 
     adj_leaf, adj_leaf_other, even_rim, odd_rim = call(
         adjoint_body,
         [shape((2 * rank, half), F32)] * 2 + [shape((rank, half))] * 2,
-        (adj, adj_other, panel),
+        (keep, keep_other, beside, beside_other, panel),
     )
     even_rim = swapped(even_rim, "sub", 1)
-    beside = [(2 * i + c, 2 * i + 2 + c) for i in range(1, chips - 1, 2) for c in range(2)]
-    odd_rim = lax.ppermute(odd_rim, "sub", beside + [(j, i) for i, j in beside])
+    route = [(2 * i + c, 2 * i + 2 + c) for i in range(1, chips - 1, 2) for c in range(2)]
+    odd_rim = lax.ppermute(odd_rim, "sub", route + [(j, i) for i, j in route])
     x = call(
         first_body,
         shape((2, 2 * rank, half)),

time: 87.1 us -> 60.5 us (0.69)
  Pallas kernels: 37.2 us -> 12.9 us
  starting transfers between devices: 31.4 us -> 28 us
  local copies, waits for them, and re-layouts: 1.75 us -> 3.17 us
    pallas_call x10 -> x11, Pallas kernels: 37.2 us -> 12.9 us  [call(): pl.pallas_call(body, out_shape=out_shape, in_specs=[SPACES[c] for c in sp...]
    ppermute x9 -> x10, starting transfers between devices: 25.2 us -> 21.8 us  [swapped(): lax.ppermute(x, axis, [(i, i ^ 1 << bit) for i in range(lax.axis_size(axi...]
    ppermute x9 -> x10, waiting for transfers between devices: 16.1 us -> 14.6 us  [swapped(): lax.ppermute(x, axis, [(i, i ^ 1 << bit) for i in range(lax.axis_size(axi...]
    unnamed x14 -> x18, local copies, waits for them, and re-layouts: 1.75 us -> 3.17 us
    all_to_all x1, waiting for transfers between devices: 0.01 us -> 1.3 us  [local(): lax.all_to_all(blocks, 'sub', split_axis=0, concat_axis=0, tiled=True, ax...]
  transfers between devices with their start and end apart: 12 -> 13, of which waited for: 7 -> 7; matrix products, arithmetic and copies ran while one was open for 0% -> 0% of each run, Pallas kernels for 11% -> 13%
where the time goes in v4:
time: 60.5 us; the launch traced here: 60.1 us
  starting transfers between devices  28 us (46%)
  waiting for transfers between devices  15.9 us (26%)
  Pallas kernels  12.9 us (21%)
  local copies, waits for them, and re-layouts  3.17 us (5%)
    ppermute x10, starting transfers between devices, swapped(): lax.ppermute(x, axis, [(i, i ^ 1 << bit) for i in range(lax.axis_size(axi...  21.8 us
    ppermute x10, waiting for transfers between devices, swapped(): lax.ppermute(x, axis, [(i, i ^ 1 << bit) for i in range(lax.axis_size(axi...  14.6 us
    pallas_call x11, Pallas kernels, call(): pl.pallas_call(body, out_shape=out_shape, in_specs=[SPACES[c] for c in sp...  12.9 us
    all_to_all x1, starting transfers between devices, local(): lax.all_to_all(blocks, 'sub', split_axis=0, concat_axis=0, tiled=True, ax...  4.88 us
    unnamed x18, local copies, waits for them, and re-layouts  3.17 us
    all_to_all x1, waiting for transfers between devices, local(): lax.all_to_all(blocks, 'sub', split_axis=0, concat_axis=0, tiled=True, ax...  1.3 us
  transfers between devices with their start and end apart: 13, of which 7 were waited for; matrix products, arithmetic and copies ran while one was open for 0% of the time, Pallas kernels for 13%

profile of v4, /device:TPU:0, one launch (start us, length us, event | category | flops | bytes accessed | tf_op | source)
XLA Modules:
  0.0 60.1 jit_solution(14846385455148295159)
XLA Ops:
  0.0 2.7 %shard_map.84 = (bf16[8,16,1536]{2,1,0:T(8,128)(2,1)}, bf16[784,256]{1,0:T(8,128)(2,1)}) custom-call(bf16[16,12288]{1,0:T(8,128)(2,1)} %tests_ref.1, bf16[768,256]{1,0:T(8,128)(2,1)} %omega_ref.3, s32[1,2,768]{2,1,0:T(2,128)} %perms_ref.5), custom_call_target="tpu_custom_call" | custom-call | flops 1000 | bytes 1000 | tf_op jit(solution)/shard_map/pallas_call | solution.py:39
  2.7 0.7 %collective-permute-start.1 = (bf16[784,256]{1,0:T(8,128)(2,1)}, bf16[784,256]{1,0:T(8,128)(2,1)S(1)}, u32[]{:S(2)}, u32[]{:S(2)}) collective-permute-start(bf16[784,256]{1,0:T(8,128)(2,1)} %get-tuple-element.31), channel_id=1, source_target_pairs={{1,2},{3,4},{5,6},{7,8},{9,10},{11,12},{13,14},{2,1},{4,3},{6,5},{... | collective-permute-start | bytes 1204232 | tf_op jit(solution)/shard_map/ppermute | solution.py:287
  3.4 4.3 %collective-permute-start = (bf16[784,256]{1,0:T(8,128)(2,1)}, bf16[784,256]{1,0:T(8,128)(2,1)S(1)}, u32[]{:S(2)}, u32[]{:S(2)}) collective-permute-start(bf16[784,256]{1,0:T(8,128)(2,1)} %get-tuple-element.31), channel_id=1, source_target_pairs={{0,1},{1,0},{2,3},{3,2},{4,5},{5,4},{6,7},{7,6},{8,9},{9,8},{10,11... | collective-permute-start | bytes 1204232 | tf_op jit(solution)/shard_map/ppermute | solution.py:264
  7.8 4.9 %all-to-all-start = ((bf16[8,16,1536]{2,1,0:T(8,128)(2,1)}), bf16[8,16,1536]{2,1,0:T(8,128)(2,1)S(1)}, u32[]{:S(2)}, u32[]{:S(2)}) async-start(bf16[8,16,1536]{2,1,0:T(8,128)(2,1)} %get-tuple-element.36), calls=%async_computation | async-start | bytes 786432 | tf_op jit(solution)/shard_map/all_to_all | solution.py:290
  12.6 1.0 %copy-done.5 = bf16[1,5,4,96,96]{4,3,2,1,0:T(8,128)(2,1)S(1)} copy-done((bf16[1,5,4,96,96]{4,3,2,1,0:T(8,128)(2,1)S(1)}, bf16[1,5,4,96,96]{4,3,2,1,0:T(8,128)(2,1)}, u32[]{:S(2)}) %copy-start.5) | copy-done | bytes 368664
  13.7 0.7 %copy-done.7 = s32[1,5,2,192]{3,2,1,0:T(2,128)S(1)} copy-done((s32[1,5,2,192]{3,2,1,0:T(2,128)S(1)}, s32[1,5,2,192]{3,2,1,0:T(2,128)}, u32[]{:S(2)}) %copy-start.7) | copy-done | bytes 7704
  14.4 2.4 %shard_map.82 = (bf16[2,2,288,96]{3,2,1,0:T(8,128)(2,1)S(1)}, bf16[2,2,288,96]{3,2,1,0:T(8,128)(2,1)S(1)}, bf16[2,2,288,96]{3,2,1,0:T(8,128)(2,1)S(1)}, bf16[2,2...) custom-call(bf16[1,5,4,96,96]{4,3,2,1,0:T(8,128)(2,1)S(1)} %copy-done.5, s32[1,5,2,192]{3,2,1,0:T(2,128)S(1)} %copy-done.7), custom_call_target="tpu_custom_call" | custom-call | flops 4294967296 | bytes 1000 | tf_op jit(solution)/shard_map/pallas_call | solution.py:39
  16.8 3.2 %shard_map.83 = (bf16[192,768]{1,0:T(8,128)(2,1)S(1)}, bf16[96,2304]{1,0:T(8,128)(2,1)S(1)}, bf16[96,768]{1,0:T(8,128)(2,1)S(1)}, bf16[768,2304]{1,0:T(8,128)(2,1)S(1)}) custom-call(s32[6,12]{1,0:T(8,128)S(1)} %copy-done.8, bf16[6,12,128,128]{3,2,1,0:T(8,128)(2,1)S(1)} %copy-done.4, s32[1,2,768]{2,1,0:T(2,128)S(1)} %copy-done.3, ...), custom_call_target="tpu_custom_call" | custom-call | flops 4294967296 | bytes 1000 | tf_op jit(solution)/shard_map/pallas_call | solution.py:39
  20.2 1.9 %shard_map.85 = (bf16[192,768]{1,0:T(8,128)(2,1)S(1)}, bf16[192,128]{1,0:T(8,128)(2,1)S(1)}, bf16[192,128]{1,0:T(8,128)(2,1)}) custom-call(bf16[768,2304]{1,0:T(8,128)(2,1)S(1)} %get-tuple-element.28.dense_ref, bf16[96,2304]{1,0:T(8,128)(2,1)S(1)} %get-tuple-element.29.near_ref, bf16[96,768]{1,0:T(8,128)(2,1)S(1)} %get-tuple-element.30.tests_ref, ...), custom_call_target="tpu_custom_call" | custom-call | flops 1000 | bytes 1000 | tf_op jit(solution)/shard_map/pallas_call | solution.py:39
  23.2 1.3 %all-to-all-done = bf16[8,16,1536]{2,1,0:T(8,128)(2,1)S(1)} async-done(((bf16[8,16,1536]{2,1,0:T(8,128)(2,1)}), bf16[8,16,1536]{2,1,0:T(8,128)(2,1)S(1)}, u32[]{:S(2)}, u32[]{:S(2)}) %all-to-all-start) | async-done | bytes 393248 | tf_op jit(solution)/shard_map/all_to_all | solution.py:290
  25.0 2.2 %collective-permute-start.5 = (bf16[96,128]{1,0:T(8,128)(2,1)S(1)}, bf16[96,128]{1,0:T(8,128)(2,1)S(1)}, u32[]{:S(2)}, u32[]{:S(2)}) collective-permute-start(bf16[96,128]{1,0:T(8,128)(2,1)S(1)} %get-tuple-element.39), channel_id=1, source_target_pairs={{0,2},{1,3},{2,0},{3,1},{4,6},{5,7},{6,4},{7,5},{8,10},{9,11},{10,... | collective-permute-start | bytes 73736 | tf_op jit(solution)/shard_map/ppermute | solution.py:264
  27.2 0.7 %collective-permute-start.6 = (bf16[96,128]{1,0:T(8,128)(2,1)S(1)}, bf16[96,128]{1,0:T(8,128)(2,1)S(1)}, u32[]{:S(2)}, u32[]{:S(2)}) collective-permute-start(bf16[96,128]{1,0:T(8,128)(2,1)S(1)} %get-tuple-element.40), channel_id=1, source_target_pairs={{2,4},{3,5},{6,8},{7,9},{10,12},{11,13},{4,2},{5,3},{8,6},{9,7},{1... | collective-permute-start | bytes 73736 | tf_op jit(solution)/shard_map/ppermute | solution.py:328
  27.8 1.1 %collective-permute-done.5.even_ref = bf16[96,128]{1,0:T(8,128)(2,1)S(1)} collective-permute-done((bf16[96,128]{1,0:T(8,128)(2,1)S(1)}, bf16[96,128]{1,0:T(8,128)(2,1)S(1)}, u32[]{:S(2)}, u32[]{:S(2)}) %collective-permute-start.5) | collective-permute-done | bytes 24608 | tf_op jit(solution)/shard_map/ppermute | solution.py:264
  29.0 0.8 %copy-done.2 = bf16[192,128]{1,0:T(8,128)(2,1)S(1)} copy-done((bf16[192,128]{1,0:T(8,128)(2,1)S(1)}, bf16[192,128]{1,0:T(8,128)(2,1)}, u32[]{:S(2)}) %copy-start.2) | copy-done | bytes 49176
  30.0 5.1 %collective-permute-start.7 = (bf16[2,192,128]{2,1,0:T(8,128)(2,1)S(1)}, bf16[2,192,128]{2,1,0:T(8,128)(2,1)S(1)}, u32[]{:S(2)}, u32[]{:S(2)}) collective-permute-start(bf16[2,192,128]{2,1,0:T(8,128)(2,1)S(1)} %shard_map.87.mine_ref.refs_0_), channel_id=1, source_target_pairs={{0,2},{1,3},{2,0},{3,1},{4,6},{5,7},{6,4},{7,5},{8,10},{9,11},{10,... | collective-permute-start | bytes 294920 | tf_op jit(solution)/shard_map/ppermute | solution.py:264
  35.1 2.6 %collective-permute-done.7.other_ref = bf16[2,192,128]{2,1,0:T(8,128)(2,1)S(1)} collective-permute-done((bf16[2,192,128]{2,1,0:T(8,128)(2,1)S(1)}, bf16[2,192,128]{2,1,0:T(8,128)(2,1)S(1)}, u32[]{:S(2)}, u32[]{:S(2)}) %collective-permute-start.7) | collective-permute-done | bytes 98336 | tf_op jit(solution)/shard_map/ppermute | solution.py:264
  37.9 3.5 %collective-permute-start.8 = (bf16[2,192,128]{2,1,0:T(8,128)(2,1)S(1)}, bf16[2,192,128]{2,1,0:T(8,128)(2,1)S(1)}, u32[]{:S(2)}, u32[]{:S(2)}) collective-permute-start(bf16[2,192,128]{2,1,0:T(8,128)(2,1)S(1)} %shard_map.88.mine_ref.refs_1_), channel_id=1, source_target_pairs={{0,4},{1,5},{2,6},{3,7},{4,0},{5,1},{6,2},{7,3},{8,12},{9,13},{10,... | collective-permute-start | bytes 294920 | tf_op jit(solution)/shard_map/ppermute | solution.py:264
  41.4 2.6 %collective-permute-done.8.other_ref = bf16[2,192,128]{2,1,0:T(8,128)(2,1)S(1)} collective-permute-done((bf16[2,192,128]{2,1,0:T(8,128)(2,1)S(1)}, bf16[2,192,128]{2,1,0:T(8,128)(2,1)S(1)}, u32[]{:S(2)}, u32[]{:S(2)}) %collective-permute-start.8) | collective-permute-done | bytes 98336 | tf_op jit(solution)/shard_map/ppermute | solution.py:264
  44.3 4.4 %collective-permute-start.9 = (bf16[2,192,128]{2,1,0:T(8,128)(2,1)S(1)}, bf16[2,192,128]{2,1,0:T(8,128)(2,1)S(1)}, u32[]{:S(2)}, u32[]{:S(2)}) collective-permute-start(bf16[2,192,128]{2,1,0:T(8,128)(2,1)S(1)} %shard_map.89.mine_ref.refs_2_), channel_id=1, source_target_pairs={{0,8},{1,9},{2,10},{3,11},{4,12},{5,13},{6,14},{7,15},{8,0},{9,1},... | collective-permute-start | bytes 294920 | tf_op jit(solution)/shard_map/ppermute | solution.py:264
  48.7 3.6 %collective-permute-done.9.other_ref = bf16[2,192,128]{2,1,0:T(8,128)(2,1)S(1)} collective-permute-done((bf16[2,192,128]{2,1,0:T(8,128)(2,1)S(1)}, bf16[2,192,128]{2,1,0:T(8,128)(2,1)S(1)}, u32[]{:S(2)}, u32[]{:S(2)}) %collective-permute-start.9) | collective-permute-done | bytes 98336 | tf_op jit(solution)/shard_map/ppermute | solution.py:264
  52.5 1.6 %collective-permute-start.10 = (bf16[2,192,128]{2,1,0:T(8,128)(2,1)S(1)}, bf16[2,192,128]{2,1,0:T(8,128)(2,1)S(1)}, u32[]{:S(2)}, u32[]{:S(2)}) collective-permute-start(bf16[2,192,128]{2,1,0:T(8,128)(2,1)S(1)} %shard_map.90.mine_ref), channel_id=1, source_target_pairs={{0,16},{16,0},{1,17},{17,1},{2,18},{18,2},{3,19},{19,3},{4,20},{20... | collective-permute-start | bytes 294920 | tf_op jit(solution)/shard_map/ppermute | solution.py:264
  54.1 3.1 %collective-permute-done.10.other_ref = bf16[2,192,128]{2,1,0:T(8,128)(2,1)S(1)} collective-permute-done((bf16[2,192,128]{2,1,0:T(8,128)(2,1)S(1)}, bf16[2,192,128]{2,1,0:T(8,128)(2,1)S(1)}, u32[]{:S(2)}, u32[]{:S(2)}) %collective-permute-start.10) | collective-permute-done | bytes 98336 | tf_op jit(solution)/shard_map/ppermute | solution.py:264
  57.5 1.5 %collective-permute-done.11.other_ref = bf16[5,2,96,128]{3,2,1,0:T(8,128)(2,1)S(1)} collective-permute-done((bf16[5,2,96,128]{3,2,1,0:T(8,128)(2,1)S(1)}, bf16[5,2,96,128]{3,2,1,0:T(8,128)(2,1)S(1)}, u32[]{:S(2)}, u32[]{:S(2)}) %collective-permute-start.11) | collective-permute-done | bytes 245792 | tf_op jit(solution)/shard_map/ppermute | solution.py:264
  59.0 1.1 %shard_map.92 = bf16[1,5,2,96,256]{4,3,2,1,0:T(8,128)(2,1)} custom-call(bf16[5,2,96,128]{3,2,1,0:T(8,128)(2,1)S(1)} %shard_map.91.mine_ref, bf16[5,2,96,128]{3,2,1,0:T(8,128)(2,1)S(1)} %collective-permute-done.11.other_ref), custom_call_target="tpu_custom_call" | custom-call | flops 1000 | bytes 1000 | tf_op jit(solution)/shard_map/pallas_call | solution.py:39
  (31 shorter events, 2.9 us)
Async XLA Ops:
  2.7 17.4 %collective-permute-start.1 = (bf16[784,256]{1,0:T(8,128)(2,1)}, bf16[784,256]{1,0:T(8,128)(2,1)S(1)}, u32[]{:S(2)}, u32[]{:S(2)}) collective-permute-start(bf16[784,256]{1,0:T(8,128)(2,1)} %get-tuple-element.31), channel_id=1, source_target_pairs={{1,2},{3,4},{5,6},{7,8},{9,10},{11,12},{13,14},{2,1},{4,3},{6,5},{... | collective-permute-start | bytes 1204232 | tf_op jit(solution)/shard_map/ppermute | solution.py:287
  3.4 16.7 %collective-permute-start = (bf16[784,256]{1,0:T(8,128)(2,1)}, bf16[784,256]{1,0:T(8,128)(2,1)S(1)}, u32[]{:S(2)}, u32[]{:S(2)}) collective-permute-start(bf16[784,256]{1,0:T(8,128)(2,1)} %get-tuple-element.31), channel_id=1, source_target_pairs={{0,1},{1,0},{2,3},{3,2},{4,5},{5,4},{6,7},{7,6},{8,9},{9,8},{10,11... | collective-permute-start | bytes 1204232 | tf_op jit(solution)/shard_map/ppermute | solution.py:264
  7.8 16.7 %all-to-all-start = ((bf16[8,16,1536]{2,1,0:T(8,128)(2,1)}), bf16[8,16,1536]{2,1,0:T(8,128)(2,1)S(1)}, u32[]{:S(2)}, u32[]{:S(2)}) async-start(bf16[8,16,1536]{2,1,0:T(8,128)(2,1)} %get-tuple-element.36), calls=%async_computation | async-start | bytes 786432 | tf_op jit(solution)/shard_map/all_to_all | solution.py:290
  12.6 1.0 %copy-start.5 = (bf16[1,5,4,96,96]{4,3,2,1,0:T(8,128)(2,1)S(1)}, bf16[1,5,4,96,96]{4,3,2,1,0:T(8,128)(2,1)}, u32[]{:S(2)}) copy-start(bf16[1,5,4,96,96]{4,3,2,1,0:T(8,128)(2,1)} %maps_ref.1) | copy-start | bytes 1105924
  13.7 0.7 %copy-start.7 = (s32[1,5,2,192]{3,2,1,0:T(2,128)S(1)}, s32[1,5,2,192]{3,2,1,0:T(2,128)}, u32[]{:S(2)}) copy-start(s32[1,5,2,192]{3,2,1,0:T(2,128)} %perms_ref.3) | copy-start | bytes 23044
  14.4 2.4 %copy-start.3 = (s32[1,2,768]{2,1,0:T(2,128)S(1)}, s32[1,2,768]{2,1,0:T(2,128)}, u32[]{:S(2)}) copy-start(s32[1,2,768]{2,1,0:T(2,128)} %perms_ref.5) | copy-start | bytes 18436
  14.4 2.4 %copy-start.4 = (bf16[6,12,128,128]{3,2,1,0:T(8,128)(2,1)S(1)}, bf16[6,12,128,128]{3,2,1,0:T(8,128)(2,1)}, u32[]{:S(2)}) copy-start(bf16[6,12,128,128]{3,2,1,0:T(8,128)(2,1)} %tiles_ref.1) | copy-start | bytes 7077892
  14.4 2.4 %copy-start.6 = (bf16[1,2,672,96]{2,3,1,0:T(8,128)(2,1)S(1)}, bf16[1,2,672,96]{2,3,1,0:T(8,128)(2,1)}, u32[]{:S(2)}) copy-start(bf16[1,2,672,96]{2,3,1,0:T(8,128)(2,1)} %param.13) | copy-start | bytes 774148
  14.4 2.4 %copy-start.8 = (s32[6,12]{1,0:T(8,128)S(1)}, s32[6,12]{1,0:T(8,128)}, u32[]{:S(2)}) copy-start(s32[6,12]{1,0:T(8,128)} %cols_ref.1) | copy-start | bytes 868
  16.8 3.3 %copy-start = (bf16[768,256]{1,0:T(8,128)(2,1)S(1)}, bf16[768,256]{1,0:T(8,128)(2,1)}, u32[]{:S(2)}) copy-start(bf16[768,256]{1,0:T(8,128)(2,1)} %omega_ref.3) | copy-start | bytes 1179652
  20.0 3.2 %collective-permute-start.3 = (bf16[192,768]{1,0:T(8,128)(2,1)S(1)}, bf16[192,768]{1,0:T(8,128)(2,1)S(1)}, u32[]{:S(2)}, u32[]{:S(2)}) collective-permute-start(bf16[192,768]{1,0:T(8,128)(2,1)S(1)} %get-tuple-element.34.keep_ref), channel_id=1, source_target_pairs={{0,1},{1,0},{2,3},{3,2},{4,5},{5,4},{6,7},{7,6},{8,9},{9,8},{10,11... | collective-permute-start | bytes 884744 | tf_op jit(solution)/shard_map/ppermute | solution.py:264
  22.1 0.6 %copy-start.1 = (bf16[192,128]{1,0:T(8,128)(2,1)}, bf16[192,128]{1,0:T(8,128)(2,1)S(1)}, u32[]{:S(2)}) copy-start(bf16[192,128]{1,0:T(8,128)(2,1)S(1)} %get-tuple-element.32.fwd_ref) | copy-start | bytes 147460
  22.7 1.8 %collective-permute-start.4 = (bf16[192,768]{1,0:T(8,128)(2,1)S(1)}, bf16[192,768]{1,0:T(8,128)(2,1)S(1)}, u32[]{:S(2)}, u32[]{:S(2)}) collective-permute-start(bf16[192,768]{1,0:T(8,128)(2,1)S(1)} %get-tuple-element.35.beside_ref), channel_id=1, source_target_pairs={{0,1},{1,0},{2,3},{3,2},{4,5},{5,4},{6,7},{7,6},{8,9},{9,8},{10,11... | collective-permute-start | bytes 884744 | tf_op jit(solution)/shard_map/ppermute | solution.py:264
  23.2 4.7 %collective-permute-start.2 = (bf16[192,128]{1,0:T(8,128)(2,1)}, bf16[192,128]{1,0:T(8,128)(2,1)S(1)}, u32[]{:S(2)}, u32[]{:S(2)}) collective-permute-start(bf16[192,128]{1,0:T(8,128)(2,1)} %get-tuple-element.33), channel_id=1, source_target_pairs={{0,1},{1,0},{2,3},{3,2},{4,5},{5,4},{6,7},{7,6},{8,9},{9,8},{10,11... | collective-permute-start | bytes 147464 | tf_op jit(solution)/shard_map/ppermute | solution.py:264
  25.0 4.0 %collective-permute-start.5 = (bf16[96,128]{1,0:T(8,128)(2,1)S(1)}, bf16[96,128]{1,0:T(8,128)(2,1)S(1)}, u32[]{:S(2)}, u32[]{:S(2)}) collective-permute-start(bf16[96,128]{1,0:T(8,128)(2,1)S(1)} %get-tuple-element.39), channel_id=1, source_target_pairs={{0,2},{1,3},{2,0},{3,1},{4,6},{5,7},{6,4},{7,5},{8,10},{9,11},{10,... | collective-permute-start | bytes 73736 | tf_op jit(solution)/shard_map/ppermute | solution.py:264
  27.2 1.8 %collective-permute-start.6 = (bf16[96,128]{1,0:T(8,128)(2,1)S(1)}, bf16[96,128]{1,0:T(8,128)(2,1)S(1)}, u32[]{:S(2)}, u32[]{:S(2)}) collective-permute-start(bf16[96,128]{1,0:T(8,128)(2,1)S(1)} %get-tuple-element.40), channel_id=1, source_target_pairs={{2,4},{3,5},{6,8},{7,9},{10,12},{11,13},{4,2},{5,3},{8,6},{9,7},{1... | collective-permute-start | bytes 73736 | tf_op jit(solution)/shard_map/ppermute | solution.py:328
  29.0 0.8 %copy-start.2 = (bf16[192,128]{1,0:T(8,128)(2,1)S(1)}, bf16[192,128]{1,0:T(8,128)(2,1)}, u32[]{:S(2)}) copy-start(bf16[192,128]{1,0:T(8,128)(2,1)} %copy-done.1) | copy-start | bytes 147460
  30.0 7.7 %collective-permute-start.7 = (bf16[2,192,128]{2,1,0:T(8,128)(2,1)S(1)}, bf16[2,192,128]{2,1,0:T(8,128)(2,1)S(1)}, u32[]{:S(2)}, u32[]{:S(2)}) collective-permute-start(bf16[2,192,128]{2,1,0:T(8,128)(2,1)S(1)} %shard_map.87.mine_ref.refs_0_), channel_id=1, source_target_pairs={{0,2},{1,3},{2,0},{3,1},{4,6},{5,7},{6,4},{7,5},{8,10},{9,11},{10,... | collective-permute-start | bytes 294920 | tf_op jit(solution)/shard_map/ppermute | solution.py:264
  37.9 6.1 %collective-permute-start.8 = (bf16[2,192,128]{2,1,0:T(8,128)(2,1)S(1)}, bf16[2,192,128]{2,1,0:T(8,128)(2,1)S(1)}, u32[]{:S(2)}, u32[]{:S(2)}) collective-permute-start(bf16[2,192,128]{2,1,0:T(8,128)(2,1)S(1)} %shard_map.88.mine_ref.refs_1_), channel_id=1, source_target_pairs={{0,4},{1,5},{2,6},{3,7},{4,0},{5,1},{6,2},{7,3},{8,12},{9,13},{10,... | collective-permute-start | bytes 294920 | tf_op jit(solution)/shard_map/ppermute | solution.py:264
  44.3 8.0 %collective-permute-start.9 = (bf16[2,192,128]{2,1,0:T(8,128)(2,1)S(1)}, bf16[2,192,128]{2,1,0:T(8,128)(2,1)S(1)}, u32[]{:S(2)}, u32[]{:S(2)}) collective-permute-start(bf16[2,192,128]{2,1,0:T(8,128)(2,1)S(1)} %shard_map.89.mine_ref.refs_2_), channel_id=1, source_target_pairs={{0,8},{1,9},{2,10},{3,11},{4,12},{5,13},{6,14},{7,15},{8,0},{9,1},... | collective-permute-start | bytes 294920 | tf_op jit(solution)/shard_map/ppermute | solution.py:264
  52.5 4.7 %collective-permute-start.10 = (bf16[2,192,128]{2,1,0:T(8,128)(2,1)S(1)}, bf16[2,192,128]{2,1,0:T(8,128)(2,1)S(1)}, u32[]{:S(2)}, u32[]{:S(2)}) collective-permute-start(bf16[2,192,128]{2,1,0:T(8,128)(2,1)S(1)} %shard_map.90.mine_ref), channel_id=1, source_target_pairs={{0,16},{16,0},{1,17},{17,1},{2,18},{18,2},{3,19},{19,3},{4,20},{20... | collective-permute-start | bytes 294920 | tf_op jit(solution)/shard_map/ppermute | solution.py:264
  57.5 1.6 %collective-permute-start.11 = (bf16[5,2,96,128]{3,2,1,0:T(8,128)(2,1)S(1)}, bf16[5,2,96,128]{3,2,1,0:T(8,128)(2,1)S(1)}, u32[]{:S(2)}, u32[]{:S(2)}) collective-permute-start(bf16[5,2,96,128]{3,2,1,0:T(8,128)(2,1)S(1)} %shard_map.91.mine_ref), channel_id=1, source_target_pairs={{0,1},{1,0},{2,3},{3,2},{4,5},{5,4},{6,7},{7,6},{8,9},{9,8},{10,11... | collective-permute-start | bytes 737288 | tf_op jit(solution)/shard_map/ppermute | solution.py:264

commit v5 on v4

--- a/solution.py
+++ b/solution.py
@@ -134,7 +134,7 @@
         out_ref[rank:] = mm(tests_ref[...], own).astype(BF)
 
 
-def maps_body(maps_ref, perms_ref, *out_refs):
+def maps_body(maps_ref, perms_ref, keep_ref, *out_refs):
     rank = maps_ref.shape[-1]
     unit = eye(rank)
     for level, out_ref in enumerate(out_refs):
@@ -145,6 +145,9 @@
         col_all = mm(col_hot, jnp.concatenate([unit, col_interp], axis=0)).astype(BF)
         for kind, (hot, every) in enumerate(((row_hot, col_all), (col_hot, row_all))):
             keep = [mm_t(unit, hot[side * rank : (side + 1) * rank, :rank]).astype(BF) for side in range(2)]
+            if level == 0 and kind == 1:
+                for side in range(2):
+                    keep_ref[side] = keep[side]
             if kind == 0:
                 cross = [mm(keep[1], high_low), mm(keep[0], low_high)]
             else:
@@ -157,65 +160,82 @@
                 ).astype(BF)
 
 
-def rim_place():
+def near_rim():
     sub = lax.axis_index("sub")
     return (sub & 1) != ((sub >> 1) & 1)
 
 
+def merged(maps_ref, kind, side, mine_first, mine_second, other_first, other_second, rank):
+    wide = mm(maps_ref[kind, side, rank:], mine_second) + mm(maps_ref[kind, 1 - side, rank:], other_second)
+    kept = mm(maps_ref[kind, side, :rank], mine_first) + mm(maps_ref[kind, 1 - side, :rank], other_first)
+    return kept + wide[:rank], wide[rank:]
+
+
 def adjoint_body(
-    keep_ref, keep_other, beside_ref, beside_other, panel_ref, mine_out, other_out, even_out, odd_out
+    maps_ref,
+    fwd_ref,
+    fwd_other,
+    keep_ref,
+    keep_other,
+    beside_ref,
+    beside_other,
+    panel_ref,
+    after_ref,
+    out_ref,
+    near_out,
+    far_out,
 ):
+    del after_ref
     rows = keep_ref.shape[1]
     rank = keep_ref.shape[0] // 2
     core = lax.axis_index("sub") & 1
+    kept, tests = merged(
+        maps_ref, 0, core, fwd_ref[:rank], fwd_ref[rank:], fwd_other[:rank], fwd_other[rank:], rank
+    )
+    out_ref[0, :rank] = kept.astype(BF)
+    out_ref[0, rank:] = tests.astype(BF)
     panel = panel_ref[:, pl.ds(pl.multiple_of(core * rows, 128), rows)]
     panel_other = panel_ref[:, pl.ds(pl.multiple_of((1 - core) * rows, 128), rows)]
     mine = mm_t(keep_ref[...], panel)
     other = mm_t(keep_other[...], panel_other)
     from_mine = mm_t(beside_ref[...], panel)
     from_other = mm_t(beside_other[...], panel_other)
-    mine_out[:rank] = mine[:rank] + from_other[:rank]
-    mine_out[rank:] = mine[rank:]
-    other_out[:rank] = other[:rank] + from_mine[:rank]
-    other_out[rank:] = other[rank:]
-    mine_rim = from_mine[rank:]
-    other_rim = from_other[rank:]
-    even = rim_place()
-    even_out[...] = jnp.where(even, mine_rim, other_rim).astype(BF)
-    odd_out[...] = jnp.where(even, other_rim, mine_rim).astype(BF)
-
-
-def merged(maps_ref, kind, side, mine_first, mine_second, other_first, other_second, rank):
-    wide = mm(maps_ref[kind, side, rank:], mine_second) + mm(maps_ref[kind, 1 - side, rank:], other_second)
-    kept = mm(maps_ref[kind, side, :rank], mine_first) + mm(maps_ref[kind, 1 - side, :rank], other_first)
-    return kept + wide[:rank], wide[rank:]
-
-
-def first_body(maps_ref, fwd_ref, fwd_other, adj_ref, adj_other, even_ref, odd_ref, out_ref):
-    rank = even_ref.shape[0]
-    core = lax.axis_index("sub") & 1
-    kept, tests = merged(
-        maps_ref, 0, core, fwd_ref[:rank], fwd_ref[rank:], fwd_other[:rank], fwd_other[rank:], rank
-    )
-    out_ref[0, :rank] = kept.astype(BF)
-    out_ref[0, rank:] = tests.astype(BF)
-    even = rim_place()
-    from_even = even_ref[...].astype(F32)
-    from_odd = odd_ref[...].astype(F32)
-    mine = adj_ref[:rank] + jnp.where(even, from_even, from_odd)
-    other = adj_other[:rank] + jnp.where(even, from_odd, from_even)
     kept, tests = merged(
         maps_ref,
         1,
         core,
-        mine.astype(BF),
-        adj_ref[rank:].astype(BF),
-        other.astype(BF),
-        adj_other[rank:].astype(BF),
+        (mine[:rank] + from_other[:rank]).astype(BF),
+        mine[rank:].astype(BF),
+        (other[:rank] + from_mine[:rank]).astype(BF),
+        other[rank:].astype(BF),
         rank,
     )
     out_ref[1, :rank] = kept.astype(BF)
     out_ref[1, rank:] = tests.astype(BF)
+    near = near_rim()
+    near_out[...] = jnp.where(near, from_mine[rank:], from_other[rank:]).astype(BF)
+    far_out[...] = jnp.where(near, from_other[rank:], from_mine[rank:]).astype(BF)
+
+
+def rim_body(keep_ref, near_ref, far_ref, out_ref):
+    chip = (lax.axis_index("sub") >> 1) & 1
+    added = mm(keep_ref[chip], near_ref[...]) + mm(keep_ref[1 - chip], far_ref[...])
+    out_ref[...] = added.astype(BF)
+
+
+def joined_body(bit, maps_ref, mine_ref, other_ref, added_ref, given_ref, out_ref, node_ref):
+    rank = added_ref.shape[0]
+    side = (lax.axis_index("sub") >> bit) & 1
+    mine = (mine_ref[1, :rank].astype(F32) + added_ref[...].astype(F32)).astype(BF)
+    other = (other_ref[1, :rank].astype(F32) + given_ref[...].astype(F32)).astype(BF)
+    node_ref[0] = mine_ref[0, :rank]
+    node_ref[1] = mine
+    for kind, (first, second) in enumerate(((mine_ref[0, :rank], other_ref[0, :rank]), (mine, other))):
+        kept, tests = merged(
+            maps_ref, kind, side, first, mine_ref[kind, rank:], second, other_ref[kind, rank:], rank
+        )
+        out_ref[kind, :rank] = kept.astype(BF)
+        out_ref[kind, rank:] = tests.astype(BF)
 
 
 def level_body(axis, bit, last, maps_ref, mine_ref, other_ref, *refs):
@@ -291,9 +311,9 @@
         blocks, "sub", split_axis=0, concat_axis=0, tiled=True, axis_index_groups=groups
     ).reshape(half, 2 * rows)
 
-    maps = call(
+    picks, *maps = call(
         maps_body,
-        [shape((2, 2, 3 * rank, rank))] * levels,
+        [shape((2, rank, rank))] + [shape((2, 2, 3 * rank, rank))] * levels,
         (node_maps, node_perms),
         flops=4 << 30,
     )
@@ -318,23 +338,26 @@
     beside_other = swapped(beside, "sub", 0)
     fwd_other = swapped(fwd_send, "sub", 0)
 
-    adj_leaf, adj_leaf_other, even_rim, odd_rim = call(
+    picks_other = swapped(picks, "sub", 1)
+    x, near_rims, far_rims = call(
         adjoint_body,
-        [shape((2 * rank, half), F32)] * 2 + [shape((rank, half))] * 2,
-        (keep, keep_other, beside, beside_other, panel),
-    )
-    even_rim = swapped(even_rim, "sub", 1)
-    route = [(2 * i + c, 2 * i + 2 + c) for i in range(1, chips - 1, 2) for c in range(2)]
-    odd_rim = lax.ppermute(odd_rim, "sub", route + [(j, i) for i, j in route])
-    x = call(
-        first_body,
-        shape((2, 2 * rank, half)),
-        (maps[0], fwd_mine, fwd_other, adj_leaf, adj_leaf_other, even_rim, odd_rim),
-    )
-    nodes = []
-    steps = [("sub", bit) for bit in range(1, sub_bits)]
+        [shape((2, 2 * rank, half))] + [shape((rank, half))] * 2,
+        (maps[0], fwd_mine, fwd_other, keep, keep_other, beside, beside_other, panel, picks_other),
+        specs="vvvvvvvva",
+    )
+    route = [(i, i + 4 if i & 2 else i - 4) for i in range(count)]
+    far_rims = lax.ppermute(far_rims, "sub", [(i, j) for i, j in route if 0 <= j < count])
+    x_other = swapped(x, "sub", 1)
+    given = call(rim_body, shape((rank, half)), (picks_other, near_rims, far_rims))
+    new, node = call(
+        functools.partial(joined_body, 1),
+        [shape((2, 2 * rank, half)), shape((2, rank, half))],
+        (maps[1], x, x_other, swapped(given, "sub", 1), given),
+    )
+    nodes, x = [node], new
+    steps = [("sub", bit) for bit in range(2, sub_bits)]
     steps += [("grp", bit) for bit in range(levels - sub_bits)]
-    for level, (axis, bit) in enumerate(steps, 1):
+    for level, (axis, bit) in enumerate(steps, 2):
         last = level == levels - 1
         new = call(
             functools.partial(level_body, axis, bit, last),

time: 60.5 us -> 61.3 us (1.013)
  waiting for transfers between devices: 15.9 us -> 23.2 us
  starting transfers between devices: 28 us -> 21.9 us
    ppermute x10 -> x11, starting transfers between devices: 21.8 us -> 15.1 us  [swapped(): lax.ppermute(x, axis, [(i, i ^ 1 << bit) for i in range(lax.axis_size(axi...]
    ppermute x1, waiting for transfers between devices: 0.01 us -> 4.42 us  [local(): lax.ppermute(far_rims, 'sub', [(i, j) for i, j in route if 0 <= j < count])]
    ppermute x10 -> x11, waiting for transfers between devices: 14.6 us -> 18.8 us  [swapped(): lax.ppermute(x, axis, [(i, i ^ 1 << bit) for i in range(lax.axis_size(axi...]
    all_to_all x1, waiting for transfers between devices: 1.3 us -> 0.01 us  [local(): lax.all_to_all(blocks, 'sub', split_axis=0, concat_axis=0, tiled=True, ax...]
    ppermute x1, starting transfers between devices: 0.65 us -> 1.28 us  [local(): lax.ppermute(far_rims, 'sub', [(i, j) for i, j in route if 0 <= j < count])]
  transfers between devices with their start and end apart: 13 -> 14, of which waited for: 7 -> 7; matrix products, arithmetic and copies ran while one was open for 0% -> 0% of each run, Pallas kernels for 13% -> 12%
where the time goes in v5:
time: 61.3 us; the launch traced here: 60.9 us
  waiting for transfers between devices  23.2 us (38%)
  starting transfers between devices  21.9 us (36%)
  Pallas kernels  12.4 us (20%)
  local copies, waits for them, and re-layouts  3.16 us (5%)
    ppermute x11, waiting for transfers between devices, swapped(): lax.ppermute(x, axis, [(i, i ^ 1 << bit) for i in range(lax.axis_size(axi...  18.8 us
    ppermute x11, starting transfers between devices, swapped(): lax.ppermute(x, axis, [(i, i ^ 1 << bit) for i in range(lax.axis_size(axi...  15.1 us
    pallas_call x11, Pallas kernels, call(): pl.pallas_call(body, out_shape=out_shape, in_specs=[SPACES[c] for c in sp...  12.4 us
    all_to_all x1, starting transfers between devices, local(): lax.all_to_all(blocks, 'sub', split_axis=0, concat_axis=0, tiled=True, ax...  4.88 us
    ppermute x1, waiting for transfers between devices, local(): lax.ppermute(far_rims, 'sub', [(i, j) for i, j in route if 0 <= j < count])  4.42 us
    unnamed x18, local copies, waits for them, and re-layouts  3.16 us
    ppermute x1, starting transfers between devices, local(): lax.ppermute(far_rims, 'sub', [(i, j) for i, j in route if 0 <= j < count])  1.28 us
  transfers between devices with their start and end apart: 14, of which 7 were waited for; matrix products, arithmetic and copies ran while one was open for 0% of the time, Pallas kernels for 12%

profile of v5, /device:TPU:0, one launch (start us, length us, event | category | flops | bytes accessed | tf_op | source)
XLA Modules:
  0.0 60.9 jit_solution(9288326887429415000)
XLA Ops:
  0.0 2.7 %shard_map.84 = (bf16[8,16,1536]{2,1,0:T(8,128)(2,1)}, bf16[784,256]{1,0:T(8,128)(2,1)}) custom-call(bf16[16,12288]{1,0:T(8,128)(2,1)} %tests_ref.1, bf16[768,256]{1,0:T(8,128)(2,1)} %omega_ref.3, s32[1,2,768]{2,1,0:T(2,128)} %perms_ref.5), custom_call_target="tpu_custom_call" | custom-call | flops 1000 | bytes 1000 | tf_op jit(solution)/shard_map/pallas_call | solution.py:39
  2.7 0.7 %collective-permute-start.1 = (bf16[784,256]{1,0:T(8,128)(2,1)}, bf16[784,256]{1,0:T(8,128)(2,1)S(1)}, u32[]{:S(2)}, u32[]{:S(2)}) collective-permute-start(bf16[784,256]{1,0:T(8,128)(2,1)} %get-tuple-element.33), channel_id=1, source_target_pairs={{1,2},{3,4},{5,6},{7,8},{9,10},{11,12},{13,14},{2,1},{4,3},{6,5},{... | collective-permute-start | bytes 1204232 | tf_op jit(solution)/shard_map/ppermute | solution.py:307
  3.4 4.3 %collective-permute-start = (bf16[784,256]{1,0:T(8,128)(2,1)}, bf16[784,256]{1,0:T(8,128)(2,1)S(1)}, u32[]{:S(2)}, u32[]{:S(2)}) collective-permute-start(bf16[784,256]{1,0:T(8,128)(2,1)} %get-tuple-element.33), channel_id=1, source_target_pairs={{0,1},{1,0},{2,3},{3,2},{4,5},{5,4},{6,7},{7,6},{8,9},{9,8},{10,11... | collective-permute-start | bytes 1204232 | tf_op jit(solution)/shard_map/ppermute | solution.py:284
  7.8 4.9 %all-to-all-start = ((bf16[8,16,1536]{2,1,0:T(8,128)(2,1)}), bf16[8,16,1536]{2,1,0:T(8,128)(2,1)S(1)}, u32[]{:S(2)}, u32[]{:S(2)}) async-start(bf16[8,16,1536]{2,1,0:T(8,128)(2,1)} %get-tuple-element.38), calls=%async_computation | async-start | bytes 786432 | tf_op jit(solution)/shard_map/all_to_all | solution.py:310
  12.6 1.0 %copy-done.5 = bf16[1,5,4,96,96]{4,3,2,1,0:T(8,128)(2,1)S(1)} copy-done((bf16[1,5,4,96,96]{4,3,2,1,0:T(8,128)(2,1)S(1)}, bf16[1,5,4,96,96]{4,3,2,1,0:T(8,128)(2,1)}, u32[]{:S(2)}) %copy-start.5) | copy-done | bytes 368664
  13.7 0.7 %copy-done.7 = s32[1,5,2,192]{3,2,1,0:T(2,128)S(1)} copy-done((s32[1,5,2,192]{3,2,1,0:T(2,128)S(1)}, s32[1,5,2,192]{3,2,1,0:T(2,128)}, u32[]{:S(2)}) %copy-start.7) | copy-done | bytes 7704
  14.4 2.4 %shard_map.82 = (bf16[2,96,96]{2,1,0:T(8,128)(2,1)S(1)}, bf16[2,2,288,96]{3,2,1,0:T(8,128)(2,1)S(1)}, bf16[2,2,288,96]{3,2,1,0:T(8,128)(2,1)S(1)}, bf16[2,2,288,...) custom-call(bf16[1,5,4,96,96]{4,3,2,1,0:T(8,128)(2,1)S(1)} %copy-done.5, ...), custom_call_target="tpu_custom_call" | custom-call | flops 4294967296 | bytes 1000 | tf_op jit(solution)/shard_map/pallas_call | solution.py:39
  16.8 3.2 %shard_map.83 = (bf16[192,768]{1,0:T(8,128)(2,1)S(1)}, bf16[96,2304]{1,0:T(8,128)(2,1)S(1)}, bf16[96,768]{1,0:T(8,128)(2,1)S(1)}, bf16[768,2304]{1,0:T(8,128)(2,1)S(1)}) custom-call(s32[6,12]{1,0:T(8,128)S(1)} %copy-done.8, bf16[6,12,128,128]{3,2,1,0:T(8,128)(2,1)S(1)} %copy-done.4, s32[1,2,768]{2,1,0:T(2,128)S(1)} %copy-done.3, ...), custom_call_target="tpu_custom_call" | custom-call | flops 4294967296 | bytes 1000 | tf_op jit(solution)/shard_map/pallas_call | solution.py:39
  20.2 1.3 %shard_map.85 = (bf16[192,768]{1,0:T(8,128)(2,1)S(1)}, bf16[192,128]{1,0:T(8,128)(2,1)S(1)}, bf16[192,128]{1,0:T(8,128)(2,1)S(1)}) custom-call(bf16[768,2304]{1,0:T(8,128)(2,1)S(1)} %get-tuple-element.30.dense_ref, bf16[96,2304]{1,0:T(8,128)(2,1)S(1)} %get-tuple-element.31.near_ref, bf16[96,768]{1,0:T(8,128)(2,1)S(1)} %get-tuple-element.32.tests_ref, ...), custom_call_target="tpu_custom_call" | custom-call | flops 1000 | bytes 1000 | tf_op jit(solution)/shard_map/pallas_call | solution.py:39
  22.6 2.4 %collective-permute-start.5 = (bf16[2,96,96]{2,1,0:T(8,128)(2,1)S(1)}, bf16[2,96,96]{2,1,0:T(8,128)(2,1)S(1)}, u32[]{:S(2)}, u32[]{:S(2)}) collective-permute-start(bf16[2,96,96]{2,1,0:T(8,128)(2,1)S(1)} %get-tuple-element.39), channel_id=1, source_target_pairs={{0,2},{1,3},{2,0},{3,1},{4,6},{5,7},{6,4},{7,5},{8,10},{9,11},{10,... | collective-permute-start | bytes 110600 | tf_op jit(solution)/shard_map/ppermute | solution.py:284
  24.9 2.1 %collective-permute-done.5.after_ref.keep_ref = bf16[2,96,96]{2,1,0:T(8,128)(2,1)S(1)} collective-permute-done((bf16[2,96,96]{2,1,0:T(8,128)(2,1)S(1)}, bf16[2,96,96]{2,1,0:T(8,128)(2,1)S(1)}, u32[]{:S(2)}, u32[]{:S(2)}) %collective-permute-start.5) | collective-permute-done | bytes 36896 | tf_op jit(solution)/shard_map/ppermute | solution.py:284
  27.0 0.8 %copy-done.2 = bf16[192,128]{1,0:T(8,128)(2,1)S(1)} copy-done((bf16[192,128]{1,0:T(8,128)(2,1)S(1)}, bf16[192,128]{1,0:T(8,128)(2,1)}, u32[]{:S(2)}) %copy-start.2) | copy-done | bytes 49176
  28.5 2.1 %collective-permute-start.6 = (bf16[2,192,128]{2,1,0:T(8,128)(2,1)S(1)}, bf16[2,192,128]{2,1,0:T(8,128)(2,1)S(1)}, u32[]{:S(2)}, u32[]{:S(2)}) collective-permute-start(bf16[2,192,128]{2,1,0:T(8,128)(2,1)S(1)} %get-tuple-element.40.mine_ref), channel_id=1, source_target_pairs={{0,2},{1,3},{2,0},{3,1},{4,6},{5,7},{6,4},{7,5},{8,10},{9,11},{10,... | collective-permute-start | bytes 294920 | tf_op jit(solution)/shard_map/ppermute | solution.py:284
  30.6 1.3 %collective-permute-start.7 = (bf16[96,128]{1,0:T(8,128)(2,1)S(1)}, bf16[96,128]{1,0:T(8,128)(2,1)S(1)}, u32[]{:S(2)}, u32[]{:S(2)}) collective-permute-start(bf16[96,128]{1,0:T(8,128)(2,1)S(1)} %get-tuple-element.42), channel_id=1, source_target_pairs={{2,6},{3,7},{4,0},{5,1},{6,10},{7,11},{8,4},{9,5},{10,14},{11,15},... | collective-permute-start | bytes 73736 | tf_op jit(solution)/shard_map/ppermute | solution.py:349
  31.9 4.4 %collective-permute-done.7.far_ref = bf16[96,128]{1,0:T(8,128)(2,1)S(1)} collective-permute-done((bf16[96,128]{1,0:T(8,128)(2,1)S(1)}, bf16[96,128]{1,0:T(8,128)(2,1)S(1)}, u32[]{:S(2)}, u32[]{:S(2)}) %collective-permute-start.7) | collective-permute-done | bytes 24608 | tf_op jit(solution)/shard_map/ppermute | solution.py:349
  36.5 3.8 %collective-permute-done.8.added_ref = bf16[96,128]{1,0:T(8,128)(2,1)S(1)} collective-permute-done((bf16[96,128]{1,0:T(8,128)(2,1)S(1)}, bf16[96,128]{1,0:T(8,128)(2,1)S(1)}, u32[]{:S(2)}, u32[]{:S(2)}) %collective-permute-start.8) | collective-permute-done | bytes 24608 | tf_op jit(solution)/shard_map/ppermute | solution.py:284
  40.6 1.7 %collective-permute-start.9 = (bf16[2,192,128]{2,1,0:T(8,128)(2,1)S(1)}, bf16[2,192,128]{2,1,0:T(8,128)(2,1)S(1)}, u32[]{:S(2)}, u32[]{:S(2)}) collective-permute-start(bf16[2,192,128]{2,1,0:T(8,128)(2,1)S(1)} %get-tuple-element.43.mine_ref.refs_1_), channel_id=1, source_target_pairs={{0,4},{1,5},{2,6},{3,7},{4,0},{5,1},{6,2},{7,3},{8,12},{9,13},{10,... | collective-permute-start | bytes 294920 | tf_op jit(solution)/shard_map/ppermute | solution.py:284
  42.3 3.9 %collective-permute-done.9.other_ref = bf16[2,192,128]{2,1,0:T(8,128)(2,1)S(1)} collective-permute-done((bf16[2,192,128]{2,1,0:T(8,128)(2,1)S(1)}, bf16[2,192,128]{2,1,0:T(8,128)(2,1)S(1)}, u32[]{:S(2)}, u32[]{:S(2)}) %collective-permute-start.9) | collective-permute-done | bytes 98336 | tf_op jit(solution)/shard_map/ppermute | solution.py:284
  46.4 2.2 %collective-permute-start.10 = (bf16[2,192,128]{2,1,0:T(8,128)(2,1)S(1)}, bf16[2,192,128]{2,1,0:T(8,128)(2,1)S(1)}, u32[]{:S(2)}, u32[]{:S(2)}) collective-permute-start(bf16[2,192,128]{2,1,0:T(8,128)(2,1)S(1)} %shard_map.89.mine_ref.refs_2_), channel_id=1, source_target_pairs={{0,8},{1,9},{2,10},{3,11},{4,12},{5,13},{6,14},{7,15},{8,0},{9,1},... | collective-permute-start | bytes 294920 | tf_op jit(solution)/shard_map/ppermute | solution.py:284
  48.7 4.4 %collective-permute-done.10.other_ref = bf16[2,192,128]{2,1,0:T(8,128)(2,1)S(1)} collective-permute-done((bf16[2,192,128]{2,1,0:T(8,128)(2,1)S(1)}, bf16[2,192,128]{2,1,0:T(8,128)(2,1)S(1)}, u32[]{:S(2)}, u32[]{:S(2)}) %collective-permute-start.10) | collective-permute-done | bytes 98336 | tf_op jit(solution)/shard_map/ppermute | solution.py:284
  53.3 1.6 %collective-permute-start.11 = (bf16[2,192,128]{2,1,0:T(8,128)(2,1)S(1)}, bf16[2,192,128]{2,1,0:T(8,128)(2,1)S(1)}, u32[]{:S(2)}, u32[]{:S(2)}) collective-permute-start(bf16[2,192,128]{2,1,0:T(8,128)(2,1)S(1)} %shard_map.90.mine_ref), channel_id=1, source_target_pairs={{0,16},{16,0},{1,17},{17,1},{2,18},{18,2},{3,19},{19,3},{4,20},{20... | collective-permute-start | bytes 294920 | tf_op jit(solution)/shard_map/ppermute | solution.py:284
  54.9 3.1 %collective-permute-done.11.other_ref = bf16[2,192,128]{2,1,0:T(8,128)(2,1)S(1)} collective-permute-done((bf16[2,192,128]{2,1,0:T(8,128)(2,1)S(1)}, bf16[2,192,128]{2,1,0:T(8,128)(2,1)S(1)}, u32[]{:S(2)}, u32[]{:S(2)}) %collective-permute-start.11) | collective-permute-done | bytes 98336 | tf_op jit(solution)/shard_map/ppermute | solution.py:284
  58.3 1.5 %collective-permute-done.12.other_ref = bf16[5,2,96,128]{3,2,1,0:T(8,128)(2,1)S(1)} collective-permute-done((bf16[5,2,96,128]{3,2,1,0:T(8,128)(2,1)S(1)}, bf16[5,2,96,128]{3,2,1,0:T(8,128)(2,1)S(1)}, u32[]{:S(2)}, u32[]{:S(2)}) %collective-permute-start.12) | collective-permute-done | bytes 245792 | tf_op jit(solution)/shard_map/ppermute | solution.py:284
  59.8 1.1 %shard_map.92 = bf16[1,5,2,96,256]{4,3,2,1,0:T(8,128)(2,1)} custom-call(bf16[5,2,96,128]{3,2,1,0:T(8,128)(2,1)S(1)} %shard_map.91.mine_ref, bf16[5,2,96,128]{3,2,1,0:T(8,128)(2,1)S(1)} %collective-permute-done.12.other_ref), custom_call_target="tpu_custom_call" | custom-call | flops 1000 | bytes 1000 | tf_op jit(solution)/shard_map/pallas_call | solution.py:39
  (33 shorter events, 3.1 us)
Async XLA Ops:
  2.7 17.4 %collective-permute-start.1 = (bf16[784,256]{1,0:T(8,128)(2,1)}, bf16[784,256]{1,0:T(8,128)(2,1)S(1)}, u32[]{:S(2)}, u32[]{:S(2)}) collective-permute-start(bf16[784,256]{1,0:T(8,128)(2,1)} %get-tuple-element.33), channel_id=1, source_target_pairs={{1,2},{3,4},{5,6},{7,8},{9,10},{11,12},{13,14},{2,1},{4,3},{6,5},{... | collective-permute-start | bytes 1204232 | tf_op jit(solution)/shard_map/ppermute | solution.py:307
  3.4 16.7 %collective-permute-start = (bf16[784,256]{1,0:T(8,128)(2,1)}, bf16[784,256]{1,0:T(8,128)(2,1)S(1)}, u32[]{:S(2)}, u32[]{:S(2)}) collective-permute-start(bf16[784,256]{1,0:T(8,128)(2,1)} %get-tuple-element.33), channel_id=1, source_target_pairs={{0,1},{1,0},{2,3},{3,2},{4,5},{5,4},{6,7},{7,6},{8,9},{9,8},{10,11... | collective-permute-start | bytes 1204232 | tf_op jit(solution)/shard_map/ppermute | solution.py:284
  7.8 19.3 %all-to-all-start = ((bf16[8,16,1536]{2,1,0:T(8,128)(2,1)}), bf16[8,16,1536]{2,1,0:T(8,128)(2,1)S(1)}, u32[]{:S(2)}, u32[]{:S(2)}) async-start(bf16[8,16,1536]{2,1,0:T(8,128)(2,1)} %get-tuple-element.38), calls=%async_computation | async-start | bytes 786432 | tf_op jit(solution)/shard_map/all_to_all | solution.py:310
  12.6 1.0 %copy-start.5 = (bf16[1,5,4,96,96]{4,3,2,1,0:T(8,128)(2,1)S(1)}, bf16[1,5,4,96,96]{4,3,2,1,0:T(8,128)(2,1)}, u32[]{:S(2)}) copy-start(bf16[1,5,4,96,96]{4,3,2,1,0:T(8,128)(2,1)} %maps_ref.1) | copy-start | bytes 1105924
  13.7 0.7 %copy-start.7 = (s32[1,5,2,192]{3,2,1,0:T(2,128)S(1)}, s32[1,5,2,192]{3,2,1,0:T(2,128)}, u32[]{:S(2)}) copy-start(s32[1,5,2,192]{3,2,1,0:T(2,128)} %perms_ref.3) | copy-start | bytes 23044
  14.4 2.4 %copy-start.3 = (s32[1,2,768]{2,1,0:T(2,128)S(1)}, s32[1,2,768]{2,1,0:T(2,128)}, u32[]{:S(2)}) copy-start(s32[1,2,768]{2,1,0:T(2,128)} %perms_ref.5) | copy-start | bytes 18436
  14.4 2.4 %copy-start.4 = (bf16[6,12,128,128]{3,2,1,0:T(8,128)(2,1)S(1)}, bf16[6,12,128,128]{3,2,1,0:T(8,128)(2,1)}, u32[]{:S(2)}) copy-start(bf16[6,12,128,128]{3,2,1,0:T(8,128)(2,1)} %tiles_ref.1) | copy-start | bytes 7077892
  14.4 2.4 %copy-start.6 = (bf16[1,2,672,96]{2,3,1,0:T(8,128)(2,1)S(1)}, bf16[1,2,672,96]{2,3,1,0:T(8,128)(2,1)}, u32[]{:S(2)}) copy-start(bf16[1,2,672,96]{2,3,1,0:T(8,128)(2,1)} %param.13) | copy-start | bytes 774148
  14.4 2.4 %copy-start.8 = (s32[6,12]{1,0:T(8,128)S(1)}, s32[6,12]{1,0:T(8,128)}, u32[]{:S(2)}) copy-start(s32[6,12]{1,0:T(8,128)} %cols_ref.1) | copy-start | bytes 868
  16.8 3.4 %copy-start = (bf16[768,256]{1,0:T(8,128)(2,1)S(1)}, bf16[768,256]{1,0:T(8,128)(2,1)}, u32[]{:S(2)}) copy-start(bf16[768,256]{1,0:T(8,128)(2,1)} %omega_ref.3) | copy-start | bytes 1179652
  20.1 7.0 %collective-permute-start.3 = (bf16[192,768]{1,0:T(8,128)(2,1)S(1)}, bf16[192,768]{1,0:T(8,128)(2,1)S(1)}, u32[]{:S(2)}, u32[]{:S(2)}) collective-permute-start(bf16[192,768]{1,0:T(8,128)(2,1)S(1)} %get-tuple-element.36.keep_ref), channel_id=1, source_target_pairs={{0,1},{1,0},{2,3},{3,2},{4,5},{5,4},{6,7},{7,6},{8,9},{9,8},{10,11... | collective-permute-start | bytes 884744 | tf_op jit(solution)/shard_map/ppermute | solution.py:284
  21.5 0.6 %copy-start.1 = (bf16[192,128]{1,0:T(8,128)(2,1)}, bf16[192,128]{1,0:T(8,128)(2,1)S(1)}, u32[]{:S(2)}) copy-start(bf16[192,128]{1,0:T(8,128)(2,1)S(1)} %get-tuple-element.34.fwd_ref) | copy-start | bytes 147460
  22.1 4.9 %collective-permute-start.4 = (bf16[192,768]{1,0:T(8,128)(2,1)S(1)}, bf16[192,768]{1,0:T(8,128)(2,1)S(1)}, u32[]{:S(2)}, u32[]{:S(2)}) collective-permute-start(bf16[192,768]{1,0:T(8,128)(2,1)S(1)} %get-tuple-element.37.beside_ref), channel_id=1, source_target_pairs={{0,1},{1,0},{2,3},{3,2},{4,5},{5,4},{6,7},{7,6},{8,9},{9,8},{10,11... | collective-permute-start | bytes 884744 | tf_op jit(solution)/shard_map/ppermute | solution.py:284
  22.5 4.5 %collective-permute-start.2 = (bf16[192,128]{1,0:T(8,128)(2,1)S(1)}, bf16[192,128]{1,0:T(8,128)(2,1)S(1)}, u32[]{:S(2)}, u32[]{:S(2)}) collective-permute-start(bf16[192,128]{1,0:T(8,128)(2,1)S(1)} %get-tuple-element.35), channel_id=1, source_target_pairs={{0,1},{1,0},{2,3},{3,2},{4,5},{5,4},{6,7},{7,6},{8,9},{9,8},{10,11... | collective-permute-start | bytes 147464 | tf_op jit(solution)/shard_map/ppermute | solution.py:284
  22.6 4.4 %collective-permute-start.5 = (bf16[2,96,96]{2,1,0:T(8,128)(2,1)S(1)}, bf16[2,96,96]{2,1,0:T(8,128)(2,1)S(1)}, u32[]{:S(2)}, u32[]{:S(2)}) collective-permute-start(bf16[2,96,96]{2,1,0:T(8,128)(2,1)S(1)} %get-tuple-element.39), channel_id=1, source_target_pairs={{0,2},{1,3},{2,0},{3,1},{4,6},{5,7},{6,4},{7,5},{8,10},{9,11},{10,... | collective-permute-start | bytes 110600 | tf_op jit(solution)/shard_map/ppermute | solution.py:284
  27.0 0.8 %copy-start.2 = (bf16[192,128]{1,0:T(8,128)(2,1)S(1)}, bf16[192,128]{1,0:T(8,128)(2,1)}, u32[]{:S(2)}) copy-start(bf16[192,128]{1,0:T(8,128)(2,1)} %copy-done.1) | copy-start | bytes 147460
  28.5 11.8 %collective-permute-start.6 = (bf16[2,192,128]{2,1,0:T(8,128)(2,1)S(1)}, bf16[2,192,128]{2,1,0:T(8,128)(2,1)S(1)}, u32[]{:S(2)}, u32[]{:S(2)}) collective-permute-start(bf16[2,192,128]{2,1,0:T(8,128)(2,1)S(1)} %get-tuple-element.40.mine_ref), channel_id=1, source_target_pairs={{0,2},{1,3},{2,0},{3,1},{4,6},{5,7},{6,4},{7,5},{8,10},{9,11},{10,... | collective-permute-start | bytes 294920 | tf_op jit(solution)/shard_map/ppermute | solution.py:284
  30.6 5.7 %collective-permute-start.7 = (bf16[96,128]{1,0:T(8,128)(2,1)S(1)}, bf16[96,128]{1,0:T(8,128)(2,1)S(1)}, u32[]{:S(2)}, u32[]{:S(2)}) collective-permute-start(bf16[96,128]{1,0:T(8,128)(2,1)S(1)} %get-tuple-element.42), channel_id=1, source_target_pairs={{2,6},{3,7},{4,0},{5,1},{6,10},{7,11},{8,4},{9,5},{10,14},{11,15},... | collective-permute-start | bytes 73736 | tf_op jit(solution)/shard_map/ppermute | solution.py:349
  36.4 3.9 %collective-permute-start.8 = (bf16[96,128]{1,0:T(8,128)(2,1)S(1)}, bf16[96,128]{1,0:T(8,128)(2,1)S(1)}, u32[]{:S(2)}, u32[]{:S(2)}) collective-permute-start(bf16[96,128]{1,0:T(8,128)(2,1)S(1)} %shard_map.87.given_ref), channel_id=1, source_target_pairs={{0,2},{1,3},{2,0},{3,1},{4,6},{5,7},{6,4},{7,5},{8,10},{9,11},{10,... | collective-permute-start | bytes 73736 | tf_op jit(solution)/shard_map/ppermute | solution.py:284
  40.6 5.6 %collective-permute-start.9 = (bf16[2,192,128]{2,1,0:T(8,128)(2,1)S(1)}, bf16[2,192,128]{2,1,0:T(8,128)(2,1)S(1)}, u32[]{:S(2)}, u32[]{:S(2)}) collective-permute-start(bf16[2,192,128]{2,1,0:T(8,128)(2,1)S(1)} %get-tuple-element.43.mine_ref.refs_1_), channel_id=1, source_target_pairs={{0,4},{1,5},{2,6},{3,7},{4,0},{5,1},{6,2},{7,3},{8,12},{9,13},{10,... | collective-permute-start | bytes 294920 | tf_op jit(solution)/shard_map/ppermute | solution.py:284
  46.4 6.6 %collective-permute-start.10 = (bf16[2,192,128]{2,1,0:T(8,128)(2,1)S(1)}, bf16[2,192,128]{2,1,0:T(8,128)(2,1)S(1)}, u32[]{:S(2)}, u32[]{:S(2)}) collective-permute-start(bf16[2,192,128]{2,1,0:T(8,128)(2,1)S(1)} %shard_map.89.mine_ref.refs_2_), channel_id=1, source_target_pairs={{0,8},{1,9},{2,10},{3,11},{4,12},{5,13},{6,14},{7,15},{8,0},{9,1},... | collective-permute-start | bytes 294920 | tf_op jit(solution)/shard_map/ppermute | solution.py:284
  53.3 4.7 %collective-permute-start.11 = (bf16[2,192,128]{2,1,0:T(8,128)(2,1)S(1)}, bf16[2,192,128]{2,1,0:T(8,128)(2,1)S(1)}, u32[]{:S(2)}, u32[]{:S(2)}) collective-permute-start(bf16[2,192,128]{2,1,0:T(8,128)(2,1)S(1)} %shard_map.90.mine_ref), channel_id=1, source_target_pairs={{0,16},{16,0},{1,17},{17,1},{2,18},{18,2},{3,19},{19,3},{4,20},{20... | collective-permute-start | bytes 294920 | tf_op jit(solution)/shard_map/ppermute | solution.py:284
  58.2 1.6 %collective-permute-start.12 = (bf16[5,2,96,128]{3,2,1,0:T(8,128)(2,1)S(1)}, bf16[5,2,96,128]{3,2,1,0:T(8,128)(2,1)S(1)}, u32[]{:S(2)}, u32[]{:S(2)}) collective-permute-start(bf16[5,2,96,128]{3,2,1,0:T(8,128)(2,1)S(1)} %shard_map.91.mine_ref), channel_id=1, source_target_pairs={{0,1},{1,0},{2,3},{3,2},{4,5},{5,4},{6,7},{7,6},{8,9},{9,8},{10,11... | collective-permute-start | bytes 737288 | tf_op jit(solution)/shard_map/ppermute | solution.py:284

commit v6 on v5

--- a/solution.py
+++ b/solution.py
@@ -109,12 +109,11 @@
 
 
 def halo_body(
-    dense_ref, near_ref, tests_ref, omega_ref, inner_ref, outer_ref, beside_ref, mine_ref, other_ref
+    dense_ref, near_ref, tests_ref, omega_ref, inner_ref, outer_ref, after_ref, beside_ref, fwd_ref
 ):
+    del after_ref
     rows = dense_ref.shape[0]
     rank = near_ref.shape[0]
-    half = omega_ref.shape[1] // 2
-    core = lax.axis_index("sub") & 1
     unit = eye(rank)
     for b, ref in enumerate((inner_ref, outer_ref)):
         digits = ref[rows:].astype(F32)
@@ -122,16 +121,13 @@
         keep = mm_t(unit, one_hot(order, rows)).astype(BF)
         block = dense_ref[:, (b + 1) * rows : (b + 2) * rows]
         beside_ref[b * rank : (b + 1) * rank] = mm_t(keep, block).astype(BF)
-    for out_ref, place in ((mine_ref, core), (other_ref, 1 - core)):
-        cols = pl.ds(pl.multiple_of(place * half, half), half)
-        own = omega_ref[:, cols]
-        fwd = (
-            mm(near_ref[:, :rows], own)
-            + mm(near_ref[:, rows : 2 * rows], inner_ref[:rows, cols])
-            + mm(near_ref[:, 2 * rows :], outer_ref[:rows, cols])
-        )
-        out_ref[:rank] = fwd.astype(BF)
-        out_ref[rank:] = mm(tests_ref[...], own).astype(BF)
+    fwd = (
+        mm(near_ref[:, :rows], omega_ref[...])
+        + mm(near_ref[:, rows : 2 * rows], inner_ref[:rows])
+        + mm(near_ref[:, 2 * rows :], outer_ref[:rows])
+    )
+    fwd_ref[:rank] = fwd.astype(BF)
+    fwd_ref[rank:] = mm(tests_ref[...], omega_ref[...]).astype(BF)
 
 
 def maps_body(maps_ref, perms_ref, keep_ref, *out_refs):
@@ -171,29 +167,10 @@
     return kept + wide[:rank], wide[rank:]
 
 
-def adjoint_body(
-    maps_ref,
-    fwd_ref,
-    fwd_other,
-    keep_ref,
-    keep_other,
-    beside_ref,
-    beside_other,
-    panel_ref,
-    after_ref,
-    out_ref,
-    near_out,
-    far_out,
-):
-    del after_ref
+def adjoint_body(maps_ref, keep_ref, keep_other, beside_ref, beside_other, panel_ref, out_ref):
     rows = keep_ref.shape[1]
     rank = keep_ref.shape[0] // 2
     core = lax.axis_index("sub") & 1
-    kept, tests = merged(
-        maps_ref, 0, core, fwd_ref[:rank], fwd_ref[rank:], fwd_other[:rank], fwd_other[rank:], rank
-    )
-    out_ref[0, :rank] = kept.astype(BF)
-    out_ref[0, rank:] = tests.astype(BF)
     panel = panel_ref[:, pl.ds(pl.multiple_of(core * rows, 128), rows)]
     panel_other = panel_ref[:, pl.ds(pl.multiple_of((1 - core) * rows, 128), rows)]
     mine = mm_t(keep_ref[...], panel)
@@ -210,11 +187,27 @@
         other[rank:].astype(BF),
         rank,
     )
-    out_ref[1, :rank] = kept.astype(BF)
-    out_ref[1, rank:] = tests.astype(BF)
+    out_ref[:rank] = kept.astype(BF)
+    out_ref[rank : 2 * rank] = tests.astype(BF)
     near = near_rim()
-    near_out[...] = jnp.where(near, from_mine[rank:], from_other[rank:]).astype(BF)
-    far_out[...] = jnp.where(near, from_other[rank:], from_mine[rank:]).astype(BF)
+    out_ref[2 * rank : 3 * rank] = jnp.where(near, from_mine[rank:], from_other[rank:]).astype(BF)
+    out_ref[3 * rank :] = jnp.where(near, from_other[rank:], from_mine[rank:]).astype(BF)
+
+
+def side_by_side(first, other_ref, mine_ref, out_ref):
+    half = mine_ref.shape[1]
+    out_ref[:, :half] = other_ref[first : first + out_ref.shape[0]]
+    out_ref[:, half:] = mine_ref[first : first + out_ref.shape[0]]
+
+
+def far_body(other_ref, mine_ref, out_ref):
+    side_by_side(3 * out_ref.shape[0], other_ref, mine_ref, out_ref)
+
+
+def both_body(other_ref, mine_ref, after_ref, out_ref, near_ref):
+    del after_ref
+    side_by_side(0, other_ref, mine_ref, out_ref)
+    side_by_side(2 * near_ref.shape[0], other_ref, mine_ref, near_ref)
 
 
 def rim_body(keep_ref, near_ref, far_ref, out_ref):
@@ -223,65 +216,84 @@
     out_ref[...] = added.astype(BF)
 
 
+def level_body(kind, axis, bit, maps_ref, mine_ref, other_ref, out_ref):
+    rank = mine_ref.shape[0] // 2
+    side = 0 if axis is None else (lax.axis_index(axis) >> bit) & 1
+    kept, tests = merged(
+        maps_ref, kind, side, mine_ref[:rank], mine_ref[rank:], other_ref[:rank], other_ref[rank:], rank
+    )
+    out_ref[:rank] = kept.astype(BF)
+    out_ref[rank:] = tests.astype(BF)
+
+
 def joined_body(bit, maps_ref, mine_ref, other_ref, added_ref, given_ref, out_ref, node_ref):
     rank = added_ref.shape[0]
     side = (lax.axis_index("sub") >> bit) & 1
-    mine = (mine_ref[1, :rank].astype(F32) + added_ref[...].astype(F32)).astype(BF)
-    other = (other_ref[1, :rank].astype(F32) + given_ref[...].astype(F32)).astype(BF)
-    node_ref[0] = mine_ref[0, :rank]
-    node_ref[1] = mine
-    for kind, (first, second) in enumerate(((mine_ref[0, :rank], other_ref[0, :rank]), (mine, other))):
-        kept, tests = merged(
-            maps_ref, kind, side, first, mine_ref[kind, rank:], second, other_ref[kind, rank:], rank
-        )
-        out_ref[kind, :rank] = kept.astype(BF)
-        out_ref[kind, rank:] = tests.astype(BF)
-
-
-def level_body(axis, bit, last, maps_ref, mine_ref, other_ref, *refs):
-    rank = mine_ref.shape[1] // 2
+    mine = (mine_ref[:rank].astype(F32) + added_ref[...].astype(F32)).astype(BF)
+    other = (other_ref[:rank].astype(F32) + given_ref[...].astype(F32)).astype(BF)
+    node_ref[...] = mine
+    kept, tests = merged(maps_ref, 1, side, mine, mine_ref[rank:], other, other_ref[rank:], rank)
+    out_ref[:rank] = kept.astype(BF)
+    out_ref[rank:] = tests.astype(BF)
+
+
+def last_body(axis, bit, levels, maps_ref, *refs):
+    out_ref = refs[-1]
+    rank = out_ref.shape[1]
     side = (lax.axis_index(axis) >> bit) & 1
-    out_ref = refs[-1]
-    if last:
-        for level, ref in enumerate((*refs[:-1], mine_ref)):
-            out_ref[level] = ref[:, :rank]
+    core = lax.axis_index("sub") & 1
     for kind in range(2):
-        kept, tests = merged(
-            maps_ref,
-            kind,
-            side,
-            mine_ref[kind, :rank],
-            mine_ref[kind, rank:],
-            other_ref[kind, :rank],
-            other_ref[kind, rank:],
-            rank,
-        )
-        if last:
-            out_ref[len(refs), kind] = kept.astype(BF)
-        else:
-            out_ref[kind, :rank] = kept.astype(BF)
-            out_ref[kind, rank:] = tests.astype(BF)
+
+        @pl.when(core == kind)
+        def _(kind=kind):
+            nodes = refs[kind * levels : kind * levels + levels - 1]
+            mine_ref, other_ref = nodes[-1], refs[kind * levels + levels - 1]
+            for level, ref in enumerate(nodes):
+                out_ref[level] = ref[:rank]
+            kept, _ = merged(
+                maps_ref,
+                kind,
+                side,
+                mine_ref[:rank],
+                mine_ref[rank:],
+                other_ref[:rank],
+                other_ref[rank:],
+                rank,
+            )
+            out_ref[levels - 1] = kept.astype(BF)
 
 
 def output_body(vectors, mine_ref, other_ref, out_ref):
-    half = mine_ref.shape[-1]
+    samples = mine_ref.shape[-1]
+    half = samples // 2
+    k = lax.broadcasted_iota(jnp.int32, (samples, samples), 0)
+    s = lax.broadcasted_iota(jnp.int32, (samples, samples), 1)
     core = lax.axis_index("sub") & 1
-    k = lax.broadcasted_iota(jnp.int32, (half, 2 * half), 0)
-    s = lax.broadcasted_iota(jnp.int32, (half, 2 * half), 1)
-    base = k + k // vectors * vectors
-    to_mine = jnp.where(s == base + core * vectors, 1.0, 0.0).astype(BF)
-    to_other = jnp.where(s == base + (1 - core) * vectors, 1.0, 0.0).astype(BF)
-    mine_cols = pl.ds(pl.multiple_of(core * half, half), half)
-    other_cols = pl.ds(pl.multiple_of((1 - core) * half, half), half)
-    for level in range(mine_ref.shape[0]):
-        mine, other = mine_ref[level], other_ref[level]
-        out_ref[0, level, 0, :, mine_cols] = mine[0]
-        out_ref[0, level, 0, :, other_cols] = other[0]
-        out_ref[0, level, 1] = (mm(mine[1], to_mine) + mm(other[1], to_other)).astype(BF)
+    part = jnp.where(k >= half, 1, 0)
+    m = k - part * half
+    place = jnp.where(s == m + m // vectors * vectors + part * vectors, 1.0, 0.0).astype(BF)
+    for kind, refs in enumerate(((mine_ref, other_ref), (other_ref, mine_ref))):
+
+        @pl.when(core == kind)
+        def _(refs=refs):
+            for level in range(mine_ref.shape[0]):
+                out_ref[0, level, 0] = refs[0][level]
+                out_ref[0, level, 1] = mm(refs[1][level], place).astype(BF)
 
 
 def swapped(x, axis, bit):
     return lax.ppermute(x, axis, [(i, i ^ (1 << bit)) for i in range(lax.axis_size(axis))])
+
+
+def traded(x, core, axis, bit):
+    groups, count = lax.axis_size("grp"), lax.axis_size("sub")
+    flip = 1 << bit
+    pairs = []
+    for g in range(groups):
+        for s in range(core, count, 2):
+            to = (g, s ^ flip) if axis == "sub" else (g ^ flip, s)
+            pairs.append((g * count + s, to[0] * count + to[1]))
+    return lax.ppermute(x, ("grp", "sub"), pairs)
 
 
 def local(omega, adj_tests, near_tiles, tile_cols, leaf_perms, leaf_interp, node_perms, node_maps):
@@ -293,7 +305,7 @@
     count = lax.axis_size("sub")
     chips = count // 2
     sub_bits = count.bit_length() - 1
-    outward = [(i, j) for i in range(1, count - 1, 2) for j in (i + 1,)]
+    outward = [(i, i + 1) for i in range(1, count - 1, 2)]
     outward += [(j, i) for i, j in outward]
 
     blocks, packed = call(
@@ -330,46 +342,66 @@
         flops=4 << 30,
     )
     keep_other = swapped(keep, "sub", 0)
-    beside, fwd_mine, fwd_send = call(
+    picks_other = traded(picks, 1, "sub", 1)
+    beside, fwd = call(
         halo_body,
-        [shape((2 * rank, rows))] + [shape((2 * rank, half))] * 2,
-        (dense, near, tests, omega, packed_inner, packed_outer),
+        [shape((2 * rank, rows)), shape((2 * rank, samples))],
+        (dense, near, tests, omega, packed_inner, packed_outer, picks_other),
+        specs="vvvvvva",
     )
     beside_other = swapped(beside, "sub", 0)
-    fwd_other = swapped(fwd_send, "sub", 0)
-
-    picks_other = swapped(picks, "sub", 1)
-    x, near_rims, far_rims = call(
+    fwd_other = lax.ppermute(fwd, "sub", [(i + 1, i) for i in range(0, count, 2)])
+    fwd = call(
+        functools.partial(level_body, 0, None, 0), shape((2 * rank, samples)), (maps[0], fwd, fwd_other)
+    )
+
+    part = call(
         adjoint_body,
-        [shape((2, 2 * rank, half))] + [shape((rank, half))] * 2,
-        (maps[0], fwd_mine, fwd_other, keep, keep_other, beside, beside_other, panel, picks_other),
-        specs="vvvvvvvva",
-    )
-    route = [(i, i + 4 if i & 2 else i - 4) for i in range(count)]
-    far_rims = lax.ppermute(far_rims, "sub", [(i, j) for i, j in route if 0 <= j < count])
-    x_other = swapped(x, "sub", 1)
-    given = call(rim_body, shape((rank, half)), (picks_other, near_rims, far_rims))
-    new, node = call(
+        shape((4 * rank, half)),
+        (maps[0], keep, keep_other, beside, beside_other, panel),
+    )
+    part_other = lax.ppermute(part, "sub", [(i, i + 1) for i in range(0, count, 2)])
+    far = call(far_body, shape((rank, samples)), (part_other, part))
+    route = [(i, i + 4 if i & 2 else i - 4) for i in range(1, count, 2)]
+    far_other = lax.ppermute(far, "sub", [(i, j) for i, j in route if 0 <= j < count])
+    adj, near_rims = call(
+        both_body,
+        [shape((2 * rank, samples)), shape((rank, samples))],
+        (part_other, part, far),
+        specs="vva",
+        flops=4 << 30,
+    )
+    given = call(rim_body, shape((rank, samples)), (picks_other, near_rims, far_other))
+    adj, node = call(
         functools.partial(joined_body, 1),
-        [shape((2, 2 * rank, half)), shape((2, rank, half))],
-        (maps[1], x, x_other, swapped(given, "sub", 1), given),
-    )
-    nodes, x = [node], new
-    steps = [("sub", bit) for bit in range(2, sub_bits)]
+        [shape((2 * rank, samples)), shape((rank, samples))],
+        (maps[1], adj, traded(adj, 1, "sub", 1), traded(given, 1, "sub", 1), given),
+    )
+    chains = [[fwd], [node, adj]]
+    steps = [("sub", bit) for bit in range(1, sub_bits)]
     steps += [("grp", bit) for bit in range(levels - sub_bits)]
-    for level, (axis, bit) in enumerate(steps, 2):
-        last = level == levels - 1
-        new = call(
-            functools.partial(level_body, axis, bit, last),
-            shape((levels, 2, rank, half) if last else (2, 2 * rank, half)),
-            (maps[level], x, swapped(x, axis, bit), *(nodes if last else ())),
-        )
-        nodes.append(x)
-        x = new
+    for level, (axis, bit) in enumerate(steps[:-1], 1):
+        for kind, chain in enumerate(chains):
+            if len(chain) > level:
+                continue
+            chain.append(
+                call(
+                    functools.partial(level_body, kind, axis, bit),
+                    shape((2 * rank, samples)),
+                    (maps[level], chain[-1], traded(chain[-1], kind, axis, bit)),
+                )
+            )
+    axis, bit = steps[-1]
+    ends = [traded(chain[-1], kind, axis, bit) for kind, chain in enumerate(chains)]
+    mine = call(
+        functools.partial(last_body, axis, bit, levels),
+        shape((levels, rank, samples)),
+        (maps[-1], *chains[0], ends[0], *chains[1], ends[1]),
+    )
     return call(
         functools.partial(output_body, vectors),
         shape((1, levels, 2, rank, samples)),
-        (x, swapped(x, "sub", 0)),
+        (mine, swapped(mine, "sub", 0)),
     )
 
 

time: 61.3 us -> 64.3 us (1.049)
  starting transfers between devices: 21.9 us -> 35.6 us
  waiting for transfers between devices: 23.2 us -> 10.9 us
  Pallas kernels: 12.4 us -> 14.7 us
  local copies, waits for them, and re-layouts: 3.16 us -> 1.76 us
    ppermute x1 -> x13, starting transfers between devices: 1.28 us -> 22.2 us  [the longest x10 17.3 us: traded(): return lax.ppermute(x, ('grp', 'sub'), pairs)]
    ppermute x11 -> x4, waiting for transfers between devices: 18.8 us -> 1.37 us  [swapped(): lax.ppermute(x, axis, [(i, i ^ 1 << bit) for i in range(lax.axis_size(axi...]
    ppermute x11 -> x4, starting transfers between devices: 15.1 us -> 7.9 us  [swapped(): lax.ppermute(x, axis, [(i, i ^ 1 << bit) for i in range(lax.axis_size(axi...]
    ppermute x1 -> x13, waiting for transfers between devices: 4.42 us -> 9.53 us  [the longest x10 9.52 us: traded(): return lax.ppermute(x, ('grp', 'sub'), pairs)]
    pallas_call x11 -> x17, Pallas kernels: 12.4 us -> 14.7 us  [call(): pl.pallas_call(body, out_shape=out_shape, in_specs=[SPACES[c] for c in sp...]
    unnamed x18, local copies, waits for them, and re-layouts: 3.16 us -> 1.76 us
  transfers between devices with their start and end apart: 14 -> 19, of which waited for: 7 -> 6; matrix products, arithmetic and copies ran while one was open for 0% -> 0% of each run, Pallas kernels for 12% -> 17%
where the time goes in v6:
time: 64.3 us; the launch traced here: 63.4 us
  starting transfers between devices  35.6 us (55%)
  Pallas kernels  14.7 us (23%)
  waiting for transfers between devices  10.9 us (17%)
  local copies, waits for them, and re-layouts  1.76 us (3%)
    ppermute x10, starting transfers between devices, traded(): return lax.ppermute(x, ('grp', 'sub'), pairs)  17.3 us
    pallas_call x17, Pallas kernels, call(): pl.pallas_call(body, out_shape=out_shape, in_specs=[SPACES[c] for c in sp...  14.7 us
    ppermute x10, waiting for transfers between devices, traded(): return lax.ppermute(x, ('grp', 'sub'), pairs)  9.52 us
    ppermute x4, starting transfers between devices, swapped(): lax.ppermute(x, axis, [(i, i ^ 1 << bit) for i in range(lax.axis_size(axi...  7.9 us
    all_to_all x1, starting transfers between devices, local(): lax.all_to_all(blocks, 'sub', split_axis=0, concat_axis=0, tiled=True, ax...  4.88 us
    ppermute x1, starting transfers between devices, local(): lax.ppermute(part, 'sub', [(i, i + 1) for i in range(0, count, 2)])  2.82 us
    unnamed x18, local copies, waits for them, and re-layouts  1.76 us
    ppermute x4, waiting for transfers between devices, swapped(): lax.ppermute(x, axis, [(i, i ^ 1 << bit) for i in range(lax.axis_size(axi...  1.37 us
  transfers between devices with their start and end apart: 19, of which 6 were waited for; matrix products, arithmetic and copies ran while one was open for 0% of the time, Pallas kernels for 17%

profile of v6, /device:TPU:0, one launch (start us, length us, event | category | flops | bytes accessed | tf_op | source)
XLA Modules:
  0.0 63.4 jit_solution(10913585230007301002)
XLA Ops:
  0.0 2.7 %shard_map.84 = (bf16[8,16,1536]{2,1,0:T(8,128)(2,1)}, bf16[784,256]{1,0:T(8,128)(2,1)}) custom-call(bf16[16,12288]{1,0:T(8,128)(2,1)} %tests_ref.1, bf16[768,256]{1,0:T(8,128)(2,1)} %omega_ref.3, s32[1,2,768]{2,1,0:T(2,128)} %perms_ref.5), custom_call_target="tpu_custom_call" | custom-call | flops 1000 | bytes 1000 | tf_op jit(solution)/shard_map/pallas_call | solution.py:39
  3.4 4.3 %collective-permute-start = (bf16[784,256]{1,0:T(8,128)(2,1)}, bf16[784,256]{1,0:T(8,128)(2,1)S(1)}, u32[]{:S(2)}, u32[]{:S(2)}) collective-permute-start(bf16[784,256]{1,0:T(8,128)(2,1)} %get-tuple-element.28), channel_id=1, source_target_pairs={{0,1},{1,0},{2,3},{3,2},{4,5},{5,4},{6,7},{7,6},{8,9},{9,8},{10,11... | collective-permute-start | bytes 1204232 | tf_op jit(solution)/shard_map/ppermute | solution.py:285
  7.8 4.9 %all-to-all-start = ((bf16[8,16,1536]{2,1,0:T(8,128)(2,1)}), bf16[8,16,1536]{2,1,0:T(8,128)(2,1)S(1)}, u32[]{:S(2)}, u32[]{:S(2)}) async-start(bf16[8,16,1536]{2,1,0:T(8,128)(2,1)} %get-tuple-element.36), calls=%async_computation | async-start | bytes 786432 | tf_op jit(solution)/shard_map/all_to_all | solution.py:322
  12.6 1.0 %copy-done.5 = bf16[1,5,4,96,96]{4,3,2,1,0:T(8,128)(2,1)S(1)} copy-done((bf16[1,5,4,96,96]{4,3,2,1,0:T(8,128)(2,1)S(1)}, bf16[1,5,4,96,96]{4,3,2,1,0:T(8,128)(2,1)}, u32[]{:S(2)}) %copy-start.5) | copy-done | bytes 368664
  13.7 0.7 %copy-done.7 = s32[1,5,2,192]{3,2,1,0:T(2,128)S(1)} copy-done((s32[1,5,2,192]{3,2,1,0:T(2,128)S(1)}, s32[1,5,2,192]{3,2,1,0:T(2,128)}, u32[]{:S(2)}) %copy-start.7) | copy-done | bytes 7704
  14.4 2.4 %shard_map.82 = (bf16[2,96,96]{2,1,0:T(8,128)(2,1)S(1)}, bf16[2,2,288,96]{3,2,1,0:T(8,128)(2,1)S(1)}, bf16[2,2,288,96]{3,2,1,0:T(8,128)(2,1)S(1)}, bf16[2,2,288,...) custom-call(bf16[1,5,4,96,96]{4,3,2,1,0:T(8,128)(2,1)S(1)} %copy-done.5, ...), custom_call_target="tpu_custom_call" | custom-call | flops 4294967296 | bytes 1000 | tf_op jit(solution)/shard_map/pallas_call | solution.py:39
  17.5 3.2 %shard_map.83 = (bf16[192,768]{1,0:T(8,128)(2,1)S(1)}, bf16[96,2304]{1,0:T(8,128)(2,1)S(1)}, bf16[96,768]{1,0:T(8,128)(2,1)S(1)}, bf16[768,2304]{1,0:T(8,128)(2,1)S(1)}) custom-call(s32[6,12]{1,0:T(8,128)S(1)} %copy-done.8, bf16[6,12,128,128]{3,2,1,0:T(8,128)(2,1)S(1)} %copy-done.4, s32[1,2,768]{2,1,0:T(2,128)S(1)} %copy-done.3, ...), custom_call_target="tpu_custom_call" | custom-call | flops 4294967296 | bytes 1000 | tf_op jit(solution)/shard_map/pallas_call | solution.py:39
  20.7 2.5 %collective-permute-start.8 = (bf16[192,768]{1,0:T(8,128)(2,1)S(1)}, bf16[192,768]{1,0:T(8,128)(2,1)S(1)}, u32[]{:S(2)}, u32[]{:S(2)}) collective-permute-start(bf16[192,768]{1,0:T(8,128)(2,1)S(1)} %get-tuple-element.34.keep_ref), channel_id=1, source_target_pairs={{0,1},{1,0},{2,3},{3,2},{4,5},{5,4},{6,7},{7,6},{8,9},{9,8},{10,11... | collective-permute-start | bytes 884744 | tf_op jit(solution)/shard_map/ppermute | solution.py:285
  23.3 1.8 %shard_map.85 = (bf16[192,768]{1,0:T(8,128)(2,1)S(1)}, bf16[192,256]{1,0:T(8,128)(2,1)}) custom-call(bf16[768,2304]{1,0:T(8,128)(2,1)S(1)} %get-tuple-element.25.dense_ref, bf16[96,2304]{1,0:T(8,128)(2,1)S(1)} %get-tuple-element.26.near_ref, bf16[96,768]{1,0:T(8,128)(2,1)S(1)} %get-tuple-element.27.tests_ref, bf16[768,256]{1,0:T(8,128)(2,1)S(1)} %copy-done, ...), custom_call_target="tpu_custom_call" | custom-call | flops 1000 | bytes 1000 | tf_op jit(solution)/shard_map/pallas_call | solution.py:39
  25.1 1.3 %collective-permute-start.3 = (bf16[192,256]{1,0:T(8,128)(2,1)}, bf16[192,256]{1,0:T(8,128)(2,1)S(1)}, u32[]{:S(2)}, u32[]{:S(2)}) collective-permute-start(bf16[192,256]{1,0:T(8,128)(2,1)} %get-tuple-element.30.mine_ref), channel_id=1, source_target_pairs={{1,0},{3,2},{5,4},{7,6},{9,8},{11,10},{13,12},{15,14},{17,16},{19,... | collective-permute-start | bytes 294920 | tf_op jit(solution)/shard_map/ppermute | solution.py:353
  27.3 2.8 %collective-permute-start.10 = (bf16[384,128]{1,0:T(8,128)(2,1)S(1)}, bf16[384,128]{1,0:T(8,128)(2,1)S(1)}, u32[]{:S(2)}, u32[]{:S(2)}) collective-permute-start(bf16[384,128]{1,0:T(8,128)(2,1)S(1)} %shard_map.90.mine_ref), channel_id=1, source_target_pairs={{0,1},{2,3},{4,5},{6,7},{8,9},{10,11},{12,13},{14,15},{16,17},{18,... | collective-permute-start | bytes 294920 | tf_op jit(solution)/shard_map/ppermute | solution.py:363
  30.1 1.1 %shard_map.86.mine_ref.refs_0_ = bf16[192,256]{1,0:T(8,128)(2,1)S(1)} custom-call(bf16[2,2,288,96]{3,2,1,0:T(8,128)(2,1)S(1)} %get-tuple-element.24.after_ref.maps_ref, bf16[192,256]{1,0:T(8,128)(2,1)} %get-tuple-element.30.mine_ref, bf16[192,256]{1,0:T(8,128)(2,1)S(1)} %collective-permute-done.3.other_ref), custom_call_target="tpu_custom_call" | custom-call | flops 1000 | bytes 1000 | tf_op jit(solution)/shard_map/pallas_call | solution.py:39
  31.3 2.2 %collective-permute-start.4 = (bf16[192,256]{1,0:T(8,128)(2,1)S(1)}, bf16[192,256]{1,0:T(8,128)(2,1)S(1)}, u32[]{:S(2)}, u32[]{:S(2)}) collective-permute-start(bf16[192,256]{1,0:T(8,128)(2,1)S(1)} %shard_map.86.mine_ref.refs_0_), channel_id=1, source_target_pairs={{0,2},{2,0},{4,6},{6,4},{8,10},{10,8},{12,14},{14,12},{16,18},{18,... | collective-permute-start | bytes 294920 | tf_op jit(solution)/shard_map/ppermute | solution.py:296
  33.5 0.8 %collective-permute-start.12 = (bf16[96,256]{1,0:T(8,128)(2,1)S(1)}, bf16[96,256]{1,0:T(8,128)(2,1)S(1)}, u32[]{:S(2)}, u32[]{:S(2)}) collective-permute-start(bf16[96,256]{1,0:T(8,128)(2,1)S(1)} %shard_map.91.after_ref), channel_id=1, source_target_pairs={{3,7},{5,1},{7,11},{9,5},{11,15},{13,9},{19,23},{21,17},{23,27},{2... | collective-permute-start | bytes 147464 | tf_op jit(solution)/shard_map/ppermute | solution.py:366
  35.9 1.9 %collective-permute-done.4.other_ref = bf16[192,256]{1,0:T(8,128)(2,1)S(1)} collective-permute-done((bf16[192,256]{1,0:T(8,128)(2,1)S(1)}, bf16[192,256]{1,0:T(8,128)(2,1)S(1)}, u32[]{:S(2)}, u32[]{:S(2)}) %collective-permute-start.4) | collective-permute-done | bytes 98336 | tf_op jit(solution)/shard_map/ppermute | solution.py:296
  38.0 3.4 %collective-permute-start.5 = (bf16[192,256]{1,0:T(8,128)(2,1)S(1)}, bf16[192,256]{1,0:T(8,128)(2,1)S(1)}, u32[]{:S(2)}, u32[]{:S(2)}) collective-permute-start(bf16[192,256]{1,0:T(8,128)(2,1)S(1)} %shard_map.87.mine_ref.refs_1_), channel_id=1, source_target_pairs={{0,4},{2,6},{4,0},{6,2},{8,12},{10,14},{12,8},{14,10},{16,20},{18,... | collective-permute-start | bytes 294920 | tf_op jit(solution)/shard_map/ppermute | solution.py:296
  42.3 2.2 %collective-permute-done.5.other_ref = bf16[192,256]{1,0:T(8,128)(2,1)S(1)} collective-permute-done((bf16[192,256]{1,0:T(8,128)(2,1)S(1)}, bf16[192,256]{1,0:T(8,128)(2,1)S(1)}, u32[]{:S(2)}, u32[]{:S(2)}) %collective-permute-start.5) | collective-permute-done | bytes 98336 | tf_op jit(solution)/shard_map/ppermute | solution.py:296
  44.8 4.3 %collective-permute-start.6 = (bf16[192,256]{1,0:T(8,128)(2,1)S(1)}, bf16[192,256]{1,0:T(8,128)(2,1)S(1)}, u32[]{:S(2)}, u32[]{:S(2)}) collective-permute-start(bf16[192,256]{1,0:T(8,128)(2,1)S(1)} %shard_map.88.mine_ref.refs_2_), channel_id=1, source_target_pairs={{0,8},{2,10},{4,12},{6,14},{8,0},{10,2},{12,4},{14,6},{16,24},{18,... | collective-permute-start | bytes 294920 | tf_op jit(solution)/shard_map/ppermute | solution.py:296
  50.0 3.3 %collective-permute-done.6.other_ref = bf16[192,256]{1,0:T(8,128)(2,1)S(1)} collective-permute-done((bf16[192,256]{1,0:T(8,128)(2,1)S(1)}, bf16[192,256]{1,0:T(8,128)(2,1)S(1)}, u32[]{:S(2)}, u32[]{:S(2)}) %collective-permute-start.6) | collective-permute-done | bytes 98336 | tf_op jit(solution)/shard_map/ppermute | solution.py:296
  53.4 3.4 %collective-permute-start.7 = (bf16[192,256]{1,0:T(8,128)(2,1)S(1)}, bf16[192,256]{1,0:T(8,128)(2,1)S(1)}, u32[]{:S(2)}, u32[]{:S(2)}) collective-permute-start(bf16[192,256]{1,0:T(8,128)(2,1)S(1)} %shard_map.89.refs_3_), channel_id=1, source_target_pairs={{0,16},{2,18},{4,20},{6,22},{8,24},{10,26},{12,28},{14,30},{16,0},... | collective-permute-start | bytes 294920 | tf_op jit(solution)/shard_map/ppermute | solution.py:296
  57.8 2.2 %collective-permute-done.7.refs_4_ = bf16[192,256]{1,0:T(8,128)(2,1)S(1)} collective-permute-done((bf16[192,256]{1,0:T(8,128)(2,1)S(1)}, bf16[192,256]{1,0:T(8,128)(2,1)S(1)}, u32[]{:S(2)}, u32[]{:S(2)}) %collective-permute-start.7) | collective-permute-done | bytes 98336 | tf_op jit(solution)/shard_map/ppermute | solution.py:296
  60.2 1.0 %collective-permute-start.17 = (bf16[5,96,256]{2,1,0:T(8,128)(2,1)S(1)}, bf16[5,96,256]{2,1,0:T(8,128)(2,1)S(1)}, u32[]{:S(2)}, u32[]{:S(2)}) collective-permute-start(bf16[5,96,256]{2,1,0:T(8,128)(2,1)S(1)} %shard_map.97.mine_ref), channel_id=1, source_target_pairs={{0,1},{1,0},{2,3},{3,2},{4,5},{5,4},{6,7},{7,6},{8,9},{9,8},{10,11... | collective-permute-start | bytes 737288 | tf_op jit(solution)/shard_map/ppermute | solution.py:285
  61.2 1.1 %collective-permute-done.17.other_ref = bf16[5,96,256]{2,1,0:T(8,128)(2,1)S(1)} collective-permute-done((bf16[5,96,256]{2,1,0:T(8,128)(2,1)S(1)}, bf16[5,96,256]{2,1,0:T(8,128)(2,1)S(1)}, u32[]{:S(2)}, u32[]{:S(2)}) %collective-permute-start.17) | collective-permute-done | bytes 245792 | tf_op jit(solution)/shard_map/ppermute | solution.py:285
  62.4 1.1 %shard_map.98 = bf16[1,5,2,96,256]{4,3,2,1,0:T(8,128)(2,1)} custom-call(bf16[5,96,256]{2,1,0:T(8,128)(2,1)S(1)} %shard_map.97.mine_ref, bf16[5,96,256]{2,1,0:T(8,128)(2,1)S(1)} %collective-permute-done.17.other_ref), custom_call_target="tpu_custom_call" | custom-call | flops 1000 | bytes 1000 | tf_op jit(solution)/shard_map/pallas_call | solution.py:39
  (49 shorter events, 7.4 us)
Async XLA Ops:
  2.7 20.5 %collective-permute-start.1 = (bf16[784,256]{1,0:T(8,128)(2,1)}, bf16[784,256]{1,0:T(8,128)(2,1)S(1)}, u32[]{:S(2)}, u32[]{:S(2)}) collective-permute-start(bf16[784,256]{1,0:T(8,128)(2,1)} %get-tuple-element.28), channel_id=1, source_target_pairs={{1,2},{3,4},{5,6},{7,8},{9,10},{11,12},{13,14},{2,1},{4,3},{6,5},{... | collective-permute-start | bytes 1204232 | tf_op jit(solution)/shard_map/ppermute | solution.py:319
  3.4 19.8 %collective-permute-start = (bf16[784,256]{1,0:T(8,128)(2,1)}, bf16[784,256]{1,0:T(8,128)(2,1)S(1)}, u32[]{:S(2)}, u32[]{:S(2)}) collective-permute-start(bf16[784,256]{1,0:T(8,128)(2,1)} %get-tuple-element.28), channel_id=1, source_target_pairs={{0,1},{1,0},{2,3},{3,2},{4,5},{5,4},{6,7},{7,6},{8,9},{9,8},{10,11... | collective-permute-start | bytes 1204232 | tf_op jit(solution)/shard_map/ppermute | solution.py:285
  7.8 18.7 %all-to-all-start = ((bf16[8,16,1536]{2,1,0:T(8,128)(2,1)}), bf16[8,16,1536]{2,1,0:T(8,128)(2,1)S(1)}, u32[]{:S(2)}, u32[]{:S(2)}) async-start(bf16[8,16,1536]{2,1,0:T(8,128)(2,1)} %get-tuple-element.36), calls=%async_computation | async-start | bytes 786432 | tf_op jit(solution)/shard_map/all_to_all | solution.py:322
  14.4 3.1 %copy-start.4 = (bf16[6,12,128,128]{3,2,1,0:T(8,128)(2,1)S(1)}, bf16[6,12,128,128]{3,2,1,0:T(8,128)(2,1)}, u32[]{:S(2)}) copy-start(bf16[6,12,128,128]{3,2,1,0:T(8,128)(2,1)} %tiles_ref.1) | copy-start | bytes 7077892
  14.4 3.1 %copy-start.6 = (bf16[1,2,672,96]{2,3,1,0:T(8,128)(2,1)S(1)}, bf16[1,2,672,96]{2,3,1,0:T(8,128)(2,1)}, u32[]{:S(2)}) copy-start(bf16[1,2,672,96]{2,3,1,0:T(8,128)(2,1)} %param.13) | copy-start | bytes 774148
  14.4 3.1 %copy-start.8 = (s32[6,12]{1,0:T(8,128)S(1)}, s32[6,12]{1,0:T(8,128)}, u32[]{:S(2)}) copy-start(s32[6,12]{1,0:T(8,128)} %cols_ref.1) | copy-start | bytes 868
  16.8 6.5 %collective-permute-start.2 = (bf16[2,96,96]{2,1,0:T(8,128)(2,1)S(1)}, bf16[2,96,96]{2,1,0:T(8,128)(2,1)S(1)}, u32[]{:S(2)}, u32[]{:S(2)}) collective-permute-start(bf16[2,96,96]{2,1,0:T(8,128)(2,1)S(1)} %get-tuple-element.29), channel_id=1, source_target_pairs={{1,3},{3,1},{5,7},{7,5},{9,11},{11,9},{13,15},{15,13},{17,19},{19,... | collective-permute-start | bytes 110600 | tf_op jit(solution)/shard_map/ppermute | solution.py:296
  17.5 5.8 %copy-start = (bf16[768,256]{1,0:T(8,128)(2,1)S(1)}, bf16[768,256]{1,0:T(8,128)(2,1)}, u32[]{:S(2)}) copy-start(bf16[768,256]{1,0:T(8,128)(2,1)} %omega_ref.3) | copy-start | bytes 1179652
  20.7 5.7 %collective-permute-start.8 = (bf16[192,768]{1,0:T(8,128)(2,1)S(1)}, bf16[192,768]{1,0:T(8,128)(2,1)S(1)}, u32[]{:S(2)}, u32[]{:S(2)}) collective-permute-start(bf16[192,768]{1,0:T(8,128)(2,1)S(1)} %get-tuple-element.34.keep_ref), channel_id=1, source_target_pairs={{0,1},{1,0},{2,3},{3,2},{4,5},{5,4},{6,7},{7,6},{8,9},{9,8},{10,11... | collective-permute-start | bytes 884744 | tf_op jit(solution)/shard_map/ppermute | solution.py:285
  23.2 3.2 %copy-start.1 = (bf16[2,96,96]{2,1,0:T(8,128)(2,1)}, bf16[2,96,96]{2,1,0:T(8,128)(2,1)S(1)}, u32[]{:S(2)}) copy-start(bf16[2,96,96]{2,1,0:T(8,128)(2,1)S(1)} %collective-permute-done.2.after_ref.keep_ref) | copy-start | bytes 110596
  25.1 1.6 %collective-permute-start.9 = (bf16[192,768]{1,0:T(8,128)(2,1)S(1)}, bf16[192,768]{1,0:T(8,128)(2,1)S(1)}, u32[]{:S(2)}, u32[]{:S(2)}) collective-permute-start(bf16[192,768]{1,0:T(8,128)(2,1)S(1)} %get-tuple-element.35.beside_ref), channel_id=1, source_target_pairs={{0,1},{1,0},{2,3},{3,2},{4,5},{5,4},{6,7},{7,6},{8,9},{9,8},{10,11... | collective-permute-start | bytes 884744 | tf_op jit(solution)/shard_map/ppermute | solution.py:285
  25.1 5.0 %collective-permute-start.3 = (bf16[192,256]{1,0:T(8,128)(2,1)}, bf16[192,256]{1,0:T(8,128)(2,1)S(1)}, u32[]{:S(2)}, u32[]{:S(2)}) collective-permute-start(bf16[192,256]{1,0:T(8,128)(2,1)} %get-tuple-element.30.mine_ref), channel_id=1, source_target_pairs={{1,0},{3,2},{5,4},{7,6},{9,8},{11,10},{13,12},{15,14},{17,16},{19,... | collective-permute-start | bytes 294920 | tf_op jit(solution)/shard_map/ppermute | solution.py:353
  27.3 6.2 %collective-permute-start.10 = (bf16[384,128]{1,0:T(8,128)(2,1)S(1)}, bf16[384,128]{1,0:T(8,128)(2,1)S(1)}, u32[]{:S(2)}, u32[]{:S(2)}) collective-permute-start(bf16[384,128]{1,0:T(8,128)(2,1)S(1)} %shard_map.90.mine_ref), channel_id=1, source_target_pairs={{0,1},{2,3},{4,5},{6,7},{8,9},{10,11},{12,13},{14,15},{16,17},{18,... | collective-permute-start | bytes 294920 | tf_op jit(solution)/shard_map/ppermute | solution.py:363
  31.3 6.5 %collective-permute-start.4 = (bf16[192,256]{1,0:T(8,128)(2,1)S(1)}, bf16[192,256]{1,0:T(8,128)(2,1)S(1)}, u32[]{:S(2)}, u32[]{:S(2)}) collective-permute-start(bf16[192,256]{1,0:T(8,128)(2,1)S(1)} %shard_map.86.mine_ref.refs_0_), channel_id=1, source_target_pairs={{0,2},{2,0},{4,6},{6,4},{8,10},{10,8},{12,14},{14,12},{16,18},{18,... | collective-permute-start | bytes 294920 | tf_op jit(solution)/shard_map/ppermute | solution.py:296
  33.5 1.5 %collective-permute-start.12 = (bf16[96,256]{1,0:T(8,128)(2,1)S(1)}, bf16[96,256]{1,0:T(8,128)(2,1)S(1)}, u32[]{:S(2)}, u32[]{:S(2)}) collective-permute-start(bf16[96,256]{1,0:T(8,128)(2,1)S(1)} %shard_map.91.after_ref), channel_id=1, source_target_pairs={{3,7},{5,1},{7,11},{9,5},{11,15},{13,9},{19,23},{21,17},{23,27},{2... | collective-permute-start | bytes 147464 | tf_op jit(solution)/shard_map/ppermute | solution.py:366
  34.4 7.1 %collective-permute-start.11 = (bf16[192,256]{1,0:T(8,128)(2,1)S(1)}, bf16[192,256]{1,0:T(8,128)(2,1)S(1)}, u32[]{:S(2)}, u32[]{:S(2)}) collective-permute-start(bf16[192,256]{1,0:T(8,128)(2,1)S(1)} %get-tuple-element.37.mine_ref), channel_id=1, source_target_pairs={{1,3},{3,1},{5,7},{7,5},{9,11},{11,9},{13,15},{15,13},{17,19},{19,... | collective-permute-start | bytes 294920 | tf_op jit(solution)/shard_map/ppermute | solution.py:296
  35.2 6.2 %collective-permute-start.13 = (bf16[96,256]{1,0:T(8,128)(2,1)S(1)}, bf16[96,256]{1,0:T(8,128)(2,1)S(1)}, u32[]{:S(2)}, u32[]{:S(2)}) collective-permute-start(bf16[96,256]{1,0:T(8,128)(2,1)S(1)} %shard_map.93.given_ref), channel_id=1, source_target_pairs={{1,3},{3,1},{5,7},{7,5},{9,11},{11,9},{13,15},{15,13},{17,19},{19,... | collective-permute-start | bytes 147464 | tf_op jit(solution)/shard_map/ppermute | solution.py:296
  38.0 6.5 %collective-permute-start.5 = (bf16[192,256]{1,0:T(8,128)(2,1)S(1)}, bf16[192,256]{1,0:T(8,128)(2,1)S(1)}, u32[]{:S(2)}, u32[]{:S(2)}) collective-permute-start(bf16[192,256]{1,0:T(8,128)(2,1)S(1)} %shard_map.87.mine_ref.refs_1_), channel_id=1, source_target_pairs={{0,4},{2,6},{4,0},{6,2},{8,12},{10,14},{12,8},{14,10},{16,20},{18,... | collective-permute-start | bytes 294920 | tf_op jit(solution)/shard_map/ppermute | solution.py:296
  41.7 7.4 %collective-permute-start.14 = (bf16[192,256]{1,0:T(8,128)(2,1)S(1)}, bf16[192,256]{1,0:T(8,128)(2,1)S(1)}, u32[]{:S(2)}, u32[]{:S(2)}) collective-permute-start(bf16[192,256]{1,0:T(8,128)(2,1)S(1)} %get-tuple-element.40.mine_ref.refs_6_), channel_id=1, source_target_pairs={{1,5},{3,7},{5,1},{7,3},{9,13},{11,15},{13,9},{15,11},{17,21},{19,... | collective-permute-start | bytes 294920 | tf_op jit(solution)/shard_map/ppermute | solution.py:296
  44.8 8.5 %collective-permute-start.6 = (bf16[192,256]{1,0:T(8,128)(2,1)S(1)}, bf16[192,256]{1,0:T(8,128)(2,1)S(1)}, u32[]{:S(2)}, u32[]{:S(2)}) collective-permute-start(bf16[192,256]{1,0:T(8,128)(2,1)S(1)} %shard_map.88.mine_ref.refs_2_), channel_id=1, source_target_pairs={{0,8},{2,10},{4,12},{6,14},{8,0},{10,2},{12,4},{14,6},{16,24},{18,... | collective-permute-start | bytes 294920 | tf_op jit(solution)/shard_map/ppermute | solution.py:296
  49.3 7.6 %collective-permute-start.15 = (bf16[192,256]{1,0:T(8,128)(2,1)S(1)}, bf16[192,256]{1,0:T(8,128)(2,1)S(1)}, u32[]{:S(2)}, u32[]{:S(2)}) collective-permute-start(bf16[192,256]{1,0:T(8,128)(2,1)S(1)} %shard_map.95.mine_ref.refs_7_), channel_id=1, source_target_pairs={{1,9},{3,11},{5,13},{7,15},{9,1},{11,3},{13,5},{15,7},{17,25},{19,... | collective-permute-start | bytes 294920 | tf_op jit(solution)/shard_map/ppermute | solution.py:296
  53.4 6.5 %collective-permute-start.7 = (bf16[192,256]{1,0:T(8,128)(2,1)S(1)}, bf16[192,256]{1,0:T(8,128)(2,1)S(1)}, u32[]{:S(2)}, u32[]{:S(2)}) collective-permute-start(bf16[192,256]{1,0:T(8,128)(2,1)S(1)} %shard_map.89.refs_3_), channel_id=1, source_target_pairs={{0,16},{2,18},{4,20},{6,22},{8,24},{10,26},{12,28},{14,30},{16,0},... | collective-permute-start | bytes 294920 | tf_op jit(solution)/shard_map/ppermute | solution.py:296
  57.1 2.8 %collective-permute-start.16 = (bf16[192,256]{1,0:T(8,128)(2,1)S(1)}, bf16[192,256]{1,0:T(8,128)(2,1)S(1)}, u32[]{:S(2)}, u32[]{:S(2)}) collective-permute-start(bf16[192,256]{1,0:T(8,128)(2,1)S(1)} %shard_map.96.refs_8_), channel_id=1, source_target_pairs={{1,17},{3,19},{5,21},{7,23},{9,25},{11,27},{13,29},{15,31},{17,1},... | collective-permute-start | bytes 294920 | tf_op jit(solution)/shard_map/ppermute | solution.py:296
  60.2 2.2 %collective-permute-start.17 = (bf16[5,96,256]{2,1,0:T(8,128)(2,1)S(1)}, bf16[5,96,256]{2,1,0:T(8,128)(2,1)S(1)}, u32[]{:S(2)}, u32[]{:S(2)}) collective-permute-start(bf16[5,96,256]{2,1,0:T(8,128)(2,1)S(1)} %shard_map.97.mine_ref), channel_id=1, source_target_pairs={{0,1},{1,0},{2,3},{3,2},{4,5},{5,4},{6,7},{7,6},{8,9},{9,8},{10,11... | collective-permute-start | bytes 737288 | tf_op jit(solution)/shard_map/ppermute | solution.py:285
  (4 other events, 6.3 us)

commit v7 on v5

--- a/solution.py
+++ b/solution.py
@@ -54,25 +54,32 @@
 DIGIT = 32
 
 
-def pack_body(width, tests_ref, omega_ref, perms_ref, out_ref, packed_ref, order_ref, sems):
+def pack_body(
+    width, tests_hbm, omega_hbm, perms_ref, out_hbm, packed_hbm, tests_ref, omega_ref, order_ref, sems
+):
     rows, cols = omega_ref.shape
-    chips = out_ref.shape[0]
-    copies = [pltpu.make_async_copy(omega_ref, packed_ref.at[:rows], sems.at[chips])]
+    chips = out_hbm.shape[0]
+    come = [pltpu.make_async_copy(omega_hbm, omega_ref, sems.at[0])]
+    go = [pltpu.make_async_copy(omega_ref, packed_hbm.at[:rows], sems.at[1])]
     for chip in range(chips):
-        copies.append(
-            pltpu.make_async_copy(
-                tests_ref.at[:, chip * width : (chip + 1) * width], out_ref.at[chip], sems.at[chip]
-            )
+        part = slice(chip * width, (chip + 1) * width)
+        come.append(
+            pltpu.make_async_copy(tests_hbm.at[:, part], tests_ref.at[chip], sems.at[2 + 2 * chip])
         )
-    for copy in copies:
+        go.append(pltpu.make_async_copy(tests_ref.at[chip], out_hbm.at[chip], sems.at[3 + 2 * chip]))
+    for copy in come:
         copy.start()
     order = perms_ref[0, 1:2, :cols]
     row = lax.broadcasted_iota(jnp.int32, order_ref.shape, 0)
     digits = jnp.where(row == 0, order // DIGIT, jnp.where(row == 1, order % DIGIT, 0))
     order_ref[...] = digits.astype(F32).astype(BF)
-    copies.append(pltpu.make_async_copy(order_ref, packed_ref.at[rows:], sems.at[chips + 1]))
-    copies[-1].start()
-    for copy in copies:
+    last = pltpu.make_async_copy(order_ref, packed_hbm.at[rows:], sems.at[2 + 2 * chips])
+    last.start()
+    for first, second in zip(come, go):
+        first.wait()
+        second.start()
+    last.wait()
+    for copy in go:
         copy.wait()
 
 
@@ -109,8 +116,18 @@
 
 
 def halo_body(
-    dense_ref, near_ref, tests_ref, omega_ref, inner_ref, outer_ref, beside_ref, mine_ref, other_ref
+    dense_ref,
+    near_ref,
+    tests_ref,
+    omega_ref,
+    inner_ref,
+    outer_ref,
+    after_ref,
+    beside_ref,
+    mine_ref,
+    other_ref,
 ):
+    del after_ref
     rows = dense_ref.shape[0]
     rank = near_ref.shape[0]
     half = omega_ref.shape[1] // 2
@@ -134,10 +151,12 @@
         out_ref[rank:] = mm(tests_ref[...], own).astype(BF)
 
 
-def maps_body(maps_ref, perms_ref, keep_ref, *out_refs):
+def maps_body(first, maps_ref, perms_ref, *out_refs):
     rank = maps_ref.shape[-1]
     unit = eye(rank)
-    for level, out_ref in enumerate(out_refs):
+    if first == 0:
+        keep_ref, *out_refs = out_refs
+    for level, out_ref in enumerate(out_refs, first):
         row_interp, col_interp, low_high, high_low = (maps_ref[0, level, i] for i in range(4))
         row_hot = one_hot(perms_ref[0, level, 0:1, :], 2 * rank)
         col_hot = one_hot(perms_ref[0, level, 1:2, :], 2 * rank)
@@ -171,50 +190,55 @@
     return kept + wide[:rank], wide[rank:]
 
 
+def node_body(maps_ref, mine_ref, other_ref, out_ref):
+    rank = mine_ref.shape[0] // 2
+    core = lax.axis_index("sub") & 1
+    kept, tests = merged(
+        maps_ref, 0, core, mine_ref[:rank], mine_ref[rank:], other_ref[:rank], other_ref[rank:], rank
+    )
+    out_ref[:rank] = kept.astype(BF)
+    out_ref[rank:] = tests.astype(BF)
+
+
+def halves(panel_ref):
+    rows = panel_ref.shape[1] // 2
+    core = lax.axis_index("sub") & 1
+    return [panel_ref[:, pl.ds(pl.multiple_of(at * rows, 128), rows)] for at in (core, 1 - core)]
+
+
+def edge_body(beside_ref, beside_other, panel_ref, near_out, far_out):
+    rank = near_out.shape[0]
+    panel, panel_other = halves(panel_ref)
+    mine = mm_t(beside_ref[rank:], panel)
+    other = mm_t(beside_other[rank:], panel_other)
+    near = near_rim()
+    near_out[...] = jnp.where(near, mine, other).astype(BF)
+    far_out[...] = jnp.where(near, other, mine).astype(BF)
+
+
 def adjoint_body(
-    maps_ref,
-    fwd_ref,
-    fwd_other,
-    keep_ref,
-    keep_other,
-    beside_ref,
-    beside_other,
-    panel_ref,
-    after_ref,
-    out_ref,
-    near_out,
-    far_out,
+    maps_ref, keep_ref, keep_other, beside_ref, beside_other, panel_ref, after_ref, out_ref
 ):
     del after_ref
-    rows = keep_ref.shape[1]
     rank = keep_ref.shape[0] // 2
     core = lax.axis_index("sub") & 1
-    kept, tests = merged(
-        maps_ref, 0, core, fwd_ref[:rank], fwd_ref[rank:], fwd_other[:rank], fwd_other[rank:], rank
-    )
-    out_ref[0, :rank] = kept.astype(BF)
-    out_ref[0, rank:] = tests.astype(BF)
-    panel = panel_ref[:, pl.ds(pl.multiple_of(core * rows, 128), rows)]
-    panel_other = panel_ref[:, pl.ds(pl.multiple_of((1 - core) * rows, 128), rows)]
+    panel, panel_other = halves(panel_ref)
     mine = mm_t(keep_ref[...], panel)
     other = mm_t(keep_other[...], panel_other)
-    from_mine = mm_t(beside_ref[...], panel)
-    from_other = mm_t(beside_other[...], panel_other)
+    to_other = mm_t(beside_ref[:rank], panel)
+    to_mine = mm_t(beside_other[:rank], panel_other)
     kept, tests = merged(
         maps_ref,
         1,
         core,
-        (mine[:rank] + from_other[:rank]).astype(BF),
+        (mine[:rank] + to_mine).astype(BF),
         mine[rank:].astype(BF),
-        (other[:rank] + from_mine[:rank]).astype(BF),
+        (other[:rank] + to_other).astype(BF),
         other[rank:].astype(BF),
         rank,
     )
-    out_ref[1, :rank] = kept.astype(BF)
-    out_ref[1, rank:] = tests.astype(BF)
-    near = near_rim()
-    near_out[...] = jnp.where(near, from_mine[rank:], from_other[rank:]).astype(BF)
-    far_out[...] = jnp.where(near, from_other[rank:], from_mine[rank:]).astype(BF)
+    out_ref[:rank] = kept.astype(BF)
+    out_ref[rank:] = tests.astype(BF)
 
 
 def rim_body(keep_ref, near_ref, far_ref, out_ref):
@@ -223,17 +247,21 @@
     out_ref[...] = added.astype(BF)
 
 
-def joined_body(bit, maps_ref, mine_ref, other_ref, added_ref, given_ref, out_ref, node_ref):
+def joined_body(
+    bit, maps_ref, fwd_ref, fwd_other, adj_ref, adj_other, added_ref, given_ref, out_ref, node_ref
+):
     rank = added_ref.shape[0]
     side = (lax.axis_index("sub") >> bit) & 1
-    mine = (mine_ref[1, :rank].astype(F32) + added_ref[...].astype(F32)).astype(BF)
-    other = (other_ref[1, :rank].astype(F32) + given_ref[...].astype(F32)).astype(BF)
-    node_ref[0] = mine_ref[0, :rank]
+    mine = (adj_ref[:rank].astype(F32) + added_ref[...].astype(F32)).astype(BF)
+    other = (adj_other[:rank].astype(F32) + given_ref[...].astype(F32)).astype(BF)
+    node_ref[0] = fwd_ref[:rank]
     node_ref[1] = mine
-    for kind, (first, second) in enumerate(((mine_ref[0, :rank], other_ref[0, :rank]), (mine, other))):
-        kept, tests = merged(
-            maps_ref, kind, side, first, mine_ref[kind, rank:], second, other_ref[kind, rank:], rank
-        )
+    chains = (
+        (fwd_ref[:rank], fwd_ref[rank:], fwd_other[:rank], fwd_other[rank:]),
+        (mine, adj_ref[rank:], other, adj_other[rank:]),
+    )
+    for kind, panels in enumerate(chains):
+        kept, tests = merged(maps_ref, kind, side, *panels, rank)
         out_ref[kind, :rank] = kept.astype(BF)
         out_ref[kind, rank:] = tests.astype(BF)
 
@@ -293,15 +321,21 @@
     count = lax.axis_size("sub")
     chips = count // 2
     sub_bits = count.bit_length() - 1
-    outward = [(i, j) for i in range(1, count - 1, 2) for j in (i + 1,)]
-    outward += [(j, i) for i, j in outward]
+    outward = [(i, i + 1) for i in range(1, count - 1, 2)]
+    outward += [(j, i) for i, j in outward] + [(0, 0), (count - 1, count - 1)]
 
     blocks, packed = call(
         functools.partial(pack_body, 2 * rows),
         [shape((chips, vectors, 2 * rows)), shape((rows + 16, samples))],
         (adj_tests, omega, leaf_perms),
-        scratch=[pltpu.VMEM((16, samples), BF), pltpu.SemaphoreType.DMA((chips + 2,))],
+        scratch=[
+            pltpu.VMEM((chips, vectors, 2 * rows), BF),
+            pltpu.VMEM(omega.shape, BF),
+            pltpu.VMEM((16, samples), BF),
+            pltpu.SemaphoreType.DMA((2 * chips + 3,)),
+        ],
         specs="hhv",
+        out="a",
         limit=56 << 20,
     )
     packed_outer = lax.ppermute(packed, "sub", outward)
@@ -311,9 +345,10 @@
         blocks, "sub", split_axis=0, concat_axis=0, tiled=True, axis_index_groups=groups
     ).reshape(half, 2 * rows)
 
-    picks, *maps = call(
-        maps_body,
-        [shape((2, rank, rank))] + [shape((2, 2, 3 * rank, rank))] * levels,
+    tables = shape((2, 2, 3 * rank, rank))
+    picks, first_maps = call(
+        functools.partial(maps_body, 0),
+        [shape((2, rank, rank)), tables],
         (node_maps, node_perms),
         flops=4 << 30,
     )
@@ -325,34 +360,52 @@
             shape((rank, rows)),
             shape((rows, 3 * rows)),
         ],
-        (tile_cols, near_tiles, leaf_perms, jnp.swapaxes(leaf_interp, 2, 3), maps[0]),
+        (tile_cols, near_tiles, leaf_perms, jnp.swapaxes(leaf_interp, 2, 3), first_maps),
         specs="svvva",
-        flops=4 << 30,
+        flops=1 << 30,
     )
     keep_other = swapped(keep, "sub", 0)
+    picks_other = swapped(picks, "sub", 1)
     beside, fwd_mine, fwd_send = call(
         halo_body,
         [shape((2 * rank, rows))] + [shape((2 * rank, half))] * 2,
-        (dense, near, tests, omega, packed_inner, packed_outer),
+        (dense, near, tests, omega, packed_inner, packed_outer, picks_other),
+        specs="vvvvvva",
     )
     beside_other = swapped(beside, "sub", 0)
-    fwd_other = swapped(fwd_send, "sub", 0)
-
-    picks_other = swapped(picks, "sub", 1)
-    x, near_rims, far_rims = call(
+    fwd = call(
+        node_body, shape((2 * rank, half)), (first_maps, fwd_mine, swapped(fwd_send, "sub", 0))
+    )
+    near_rims, far_rims = call(
+        edge_body, [shape((rank, half))] * 2, (beside, beside_other, panel)
+    )
+    ring = list(range(1, chips, 2)) + list(range(chips - 2, -1, -2))
+    route = [(2 * a + c, 2 * b + c) for a, b in zip(ring, ring[1:] + ring[:1]) for c in range(2)]
+    far_rims = lax.ppermute(far_rims, "sub", route)
+    adj = call(
         adjoint_body,
-        [shape((2, 2 * rank, half))] + [shape((rank, half))] * 2,
-        (maps[0], fwd_mine, fwd_other, keep, keep_other, beside, beside_other, panel, picks_other),
-        specs="vvvvvvvva",
-    )
-    route = [(i, i + 4 if i & 2 else i - 4) for i in range(count)]
-    far_rims = lax.ppermute(far_rims, "sub", [(i, j) for i, j in route if 0 <= j < count])
-    x_other = swapped(x, "sub", 1)
+        shape((2 * rank, half)),
+        (first_maps, keep, keep_other, beside, beside_other, panel, near_rims),
+        specs="vvvvvva",
+        flops=4 << 30,
+    )
     given = call(rim_body, shape((rank, half)), (picks_other, near_rims, far_rims))
+    more_maps = call(
+        functools.partial(maps_body, 1), [tables] * (levels - 1), (node_maps, node_perms)
+    )
+    maps = [first_maps, *more_maps]
     new, node = call(
         functools.partial(joined_body, 1),
         [shape((2, 2 * rank, half)), shape((2, rank, half))],
-        (maps[1], x, x_other, swapped(given, "sub", 1), given),
+        (
+            maps[1],
+            fwd,
+            swapped(fwd, "sub", 1),
+            adj,
+            swapped(adj, "sub", 1),
+            swapped(given, "sub", 1),
+            given,
+        ),
     )
     nodes, x = [node], new
     steps = [("sub", bit) for bit in range(2, sub_bits)]

time: 61.3 us -> 55.6 us (0.907)
  waiting for transfers between devices: 23.2 us -> 13 us
  starting transfers between devices: 21.9 us -> 26.8 us
  local copies, waits for them, and re-layouts: 3.16 us -> 1.76 us
    ppermute x11 -> x12, waiting for transfers between devices: 18.8 us -> 12.7 us  [swapped(): lax.ppermute(x, axis, [(i, i ^ 1 << bit) for i in range(lax.axis_size(axi...]
    ppermute x1, waiting for transfers between devices: 4.42 us -> 0.35 us  [local(): far_rims = lax.ppermute(far_rims, 'sub', route)]
    all_to_all x1, starting transfers between devices: 4.88 us -> 7.72 us  [local(): lax.all_to_all(blocks, 'sub', split_axis=0, concat_axis=0, tiled=True, ax...]
    ppermute x11 -> x12, starting transfers between devices: 15.1 us -> 17.4 us  [swapped(): lax.ppermute(x, axis, [(i, i ^ 1 << bit) for i in range(lax.axis_size(axi...]
    unnamed x18, local copies, waits for them, and re-layouts: 3.16 us -> 1.76 us
    ppermute x1, starting transfers between devices: 1.28 us -> 0.09 us  [local(): far_rims = lax.ppermute(far_rims, 'sub', route)]
    ppermute x1, starting transfers between devices: 0.69 us -> 1.65 us  [local(): packed_outer = lax.ppermute(packed, 'sub', outward)]
    pallas_call x11 -> x14, Pallas kernels: 12.4 us -> 12.9 us  [call(): pl.pallas_call(body, out_shape=out_shape, in_specs=[SPACES[c] for c in sp...]
  transfers between devices with their start and end apart: 14 -> 15, of which waited for: 7 -> 7; matrix products, arithmetic and copies ran while one was open for 0% -> 0% of each run, Pallas kernels for 12% -> 15%
where the time goes in v7:
time: 55.6 us; the launch traced here: 54.7 us
  starting transfers between devices  26.8 us (48%)
  waiting for transfers between devices  13 us (23%)
  Pallas kernels  12.9 us (23%)
  local copies, waits for them, and re-layouts  1.76 us (3%)
    ppermute x12, starting transfers between devices, swapped(): lax.ppermute(x, axis, [(i, i ^ 1 << bit) for i in range(lax.axis_size(axi...  17.4 us
    pallas_call x14, Pallas kernels, call(): pl.pallas_call(body, out_shape=out_shape, in_specs=[SPACES[c] for c in sp...  12.9 us
    ppermute x12, waiting for transfers between devices, swapped(): lax.ppermute(x, axis, [(i, i ^ 1 << bit) for i in range(lax.axis_size(axi...  12.7 us
    all_to_all x1, starting transfers between devices, local(): lax.all_to_all(blocks, 'sub', split_axis=0, concat_axis=0, tiled=True, ax...  7.72 us
    unnamed x18, local copies, waits for them, and re-layouts  1.76 us
    ppermute x1, starting transfers between devices, local(): packed_outer = lax.ppermute(packed, 'sub', outward)  1.65 us
  transfers between devices with their start and end apart: 15, of which 7 were waited for; matrix products, arithmetic and copies ran while one was open for 0% of the time, Pallas kernels for 15%

profile of v7, /device:TPU:0, one launch (start us, length us, event | category | flops | bytes accessed | tf_op | source)
XLA Modules:
  0.0 54.7 jit_solution(4322054842703740978)
XLA Ops:
  0.0 2.7 %shard_map.85 = (bf16[8,16,1536]{2,1,0:T(8,128)(2,1)}, bf16[784,256]{1,0:T(8,128)(2,1)}) custom-call(bf16[16,12288]{1,0:T(8,128)(2,1)} %tests_hbm.1, bf16[768,256]{1,0:T(8,128)(2,1)} %omega_ref.1, s32[1,2,768]{2,1,0:T(2,128)} %perms_ref.7), custom_call_target="tpu_custom_call" | custom-call | flops 1000 | bytes 1000 | tf_op jit(solution)/shard_map/pallas_call | solution.py:39
  3.2 1.6 %collective-permute-start.1 = (bf16[784,256]{1,0:T(8,128)(2,1)}, bf16[784,256]{1,0:T(8,128)(2,1)S(1)}, u32[]{:S(2)}, u32[]{:S(2)}) collective-permute-start(bf16[784,256]{1,0:T(8,128)(2,1)} %get-tuple-element.32), channel_id=1, source_target_pairs={{1,2},{3,4},{5,6},{7,8},{9,10},{11,12},{13,14},{2,1},{4,3},{6,5},{... | collective-permute-start | bytes 1204232 | tf_op jit(solution)/shard_map/ppermute | solution.py:341
  4.9 7.7 %all-to-all-start = ((bf16[8,16,1536]{2,1,0:T(8,128)(2,1)}), bf16[8,16,1536]{2,1,0:T(8,128)(2,1)S(1)}, u32[]{:S(2)}, u32[]{:S(2)}) async-start(bf16[8,16,1536]{2,1,0:T(8,128)(2,1)} %get-tuple-element.38), calls=%async_computation | async-start | bytes 786432 | tf_op jit(solution)/shard_map/all_to_all | solution.py:344
  12.6 1.0 %copy-done.1 = bf16[1,5,4,96,96]{4,3,2,1,0:T(8,128)(2,1)S(1)} copy-done((bf16[1,5,4,96,96]{4,3,2,1,0:T(8,128)(2,1)S(1)}, bf16[1,5,4,96,96]{4,3,2,1,0:T(8,128)(2,1)}, u32[]{:S(2)}) %copy-start.1) | copy-done | bytes 368664
  13.6 0.7 %copy-done.3 = s32[1,5,2,192]{3,2,1,0:T(2,128)S(1)} copy-done((s32[1,5,2,192]{3,2,1,0:T(2,128)S(1)}, s32[1,5,2,192]{3,2,1,0:T(2,128)}, u32[]{:S(2)}) %copy-start.3) | copy-done | bytes 7704
  14.3 0.6 %shard_map.83 = (bf16[2,96,96]{2,1,0:T(8,128)(2,1)S(1)}, bf16[2,2,288,96]{3,2,1,0:T(8,128)(2,1)S(1)}) custom-call(bf16[1,5,4,96,96]{4,3,2,1,0:T(8,128)(2,1)S(1)} %copy-done.1, s32[1,5,2,192]{3,2,1,0:T(2,128)S(1)} %copy-done.3), custom_call_target="tpu_custom_call" | custom-call | flops 4294967296 | bytes 1000 | tf_op jit(solution)/shard_map/pallas_call | solution.py:39
  14.9 2.1 %collective-permute-start.2 = (bf16[2,96,96]{2,1,0:T(8,128)(2,1)S(1)}, bf16[2,96,96]{2,1,0:T(8,128)(2,1)S(1)}, u32[]{:S(2)}, u32[]{:S(2)}) collective-permute-start(bf16[2,96,96]{2,1,0:T(8,128)(2,1)S(1)} %get-tuple-element.33), channel_id=1, source_target_pairs={{0,2},{1,3},{2,0},{3,1},{4,6},{5,7},{6,4},{7,5},{8,10},{9,11},{10,... | collective-permute-start | bytes 110600 | tf_op jit(solution)/shard_map/ppermute | solution.py:312
  17.0 3.2 %shard_map.84 = (bf16[192,768]{1,0:T(8,128)(2,1)S(1)}, bf16[96,2304]{1,0:T(8,128)(2,1)S(1)}, bf16[96,768]{1,0:T(8,128)(2,1)S(1)}, bf16[768,2304]{1,0:T(8,128)(2,1)S(1)}) custom-call(s32[6,12]{1,0:T(8,128)S(1)} %copy-done.8, bf16[6,12,128,128]{3,2,1,0:T(8,128)(2,1)S(1)} %copy-done.6, s32[1,2,768]{2,1,0:T(2,128)S(1)} %copy-done.5, ...), custom_call_target="tpu_custom_call" | custom-call | flops 1073741824 | bytes 1000 | tf_op jit(solution)/shard_map/pallas_call | solution.py:39
  20.3 1.3 %shard_map.86 = (bf16[192,768]{1,0:T(8,128)(2,1)S(1)}, bf16[192,128]{1,0:T(8,128)(2,1)S(1)}, bf16[192,128]{1,0:T(8,128)(2,1)S(1)}) custom-call(bf16[768,2304]{1,0:T(8,128)(2,1)S(1)} %get-tuple-element.29.dense_ref, bf16[96,2304]{1,0:T(8,128)(2,1)S(1)} %get-tuple-element.30.near_ref, bf16[96,768]{1,0:T(8,128)(2,1)S(1)} %get-tuple-element.31.tests_ref, ...), custom_call_target="tpu_custom_call" | custom-call | flops 1000 | bytes 1000 | tf_op jit(solution)/shard_map/pallas_call | solution.py:39
  21.6 1.8 %collective-permute-start.6 = (bf16[192,768]{1,0:T(8,128)(2,1)S(1)}, bf16[192,768]{1,0:T(8,128)(2,1)S(1)}, u32[]{:S(2)}, u32[]{:S(2)}) collective-permute-start(bf16[192,768]{1,0:T(8,128)(2,1)S(1)} %get-tuple-element.37.beside_ref), channel_id=1, source_target_pairs={{0,1},{1,0},{2,3},{3,2},{4,5},{5,4},{6,7},{7,6},{8,9},{9,8},{10,11... | collective-permute-start | bytes 884744 | tf_op jit(solution)/shard_map/ppermute | solution.py:312
  23.9 1.2 %collective-permute-done.3.other_ref = bf16[192,128]{1,0:T(8,128)(2,1)S(1)} collective-permute-done((bf16[192,128]{1,0:T(8,128)(2,1)S(1)}, bf16[192,128]{1,0:T(8,128)(2,1)S(1)}, u32[]{:S(2)}, u32[]{:S(2)}) %collective-permute-start.3) | collective-permute-done | bytes 49184 | tf_op jit(solution)/shard_map/ppermute | solution.py:312
  25.3 2.6 %collective-permute-start.4 = (bf16[192,128]{1,0:T(8,128)(2,1)S(1)}, bf16[192,128]{1,0:T(8,128)(2,1)S(1)}, u32[]{:S(2)}, u32[]{:S(2)}) collective-permute-start(bf16[192,128]{1,0:T(8,128)(2,1)S(1)} %shard_map.87.fwd_ref), channel_id=1, source_target_pairs={{0,2},{1,3},{2,0},{3,1},{4,6},{5,7},{6,4},{7,5},{8,10},{9,11},{10,... | collective-permute-start | bytes 147464 | tf_op jit(solution)/shard_map/ppermute | solution.py:312
  28.2 0.6 %shard_map.89.adj_ref = bf16[192,128]{1,0:T(8,128)(2,1)S(1)} custom-call(bf16[2,2,288,96]{3,2,1,0:T(8,128)(2,1)S(1)} %get-tuple-element.28.after_ref.maps_ref, bf16[192,768]{1,0:T(8,128)(2,1)S(1)} %get-tuple-element.36.keep_ref, bf16[192,768]{1,0:T(8,128)(2,1)S(1)} %collective-permute-done.5.keep_other, bf16[192,768]{1,0:T(8,128)(2,1)S(1)} %get-tuple-element.37.beside_ref, ...), custom_call_target="tpu_custom_call" | custom-call | flops 4294967296 | bytes 1000 | tf_op jit(solution)/shard_map/pallas_call | solution.py:39
  28.8 2.8 %collective-permute-start.7 = (bf16[192,128]{1,0:T(8,128)(2,1)S(1)}, bf16[192,128]{1,0:T(8,128)(2,1)S(1)}, u32[]{:S(2)}, u32[]{:S(2)}) collective-permute-start(bf16[192,128]{1,0:T(8,128)(2,1)S(1)} %shard_map.89.adj_ref), channel_id=1, source_target_pairs={{0,2},{1,3},{2,0},{3,1},{4,6},{5,7},{6,4},{7,5},{8,10},{9,11},{10,... | collective-permute-start | bytes 147464 | tf_op jit(solution)/shard_map/ppermute | solution.py:312
  32.7 1.9 %shard_map.82 = (bf16[2,2,288,96]{3,2,1,0:T(8,128)(2,1)S(1)}, bf16[2,2,288,96]{3,2,1,0:T(8,128)(2,1)S(1)}, bf16[2,2,288,96]{3,2,1,0:T(8,128)(2,1)S(1)}, bf16[2,2,288,96]{3,2,1,0:T(8,128)(2,1)S(1)}) custom-call(bf16[1,5,4,96,96]{4,3,2,1,0:T(8,128)(2,1)S(1)} %copy-done.2, s32[1,5,2,192]{3,2,1,0:T(2,128)S(1)} %copy-done.4), custom_call_target="tpu_custom_call" | custom-call | flops 1000 | bytes 1000 | tf_op jit(solution)/shard_map/pallas_call | solution.py:39
  34.7 1.4 %collective-permute-done.9.added_ref = bf16[96,128]{1,0:T(8,128)(2,1)S(1)} collective-permute-done((bf16[96,128]{1,0:T(8,128)(2,1)S(1)}, bf16[96,128]{1,0:T(8,128)(2,1)S(1)}, u32[]{:S(2)}, u32[]{:S(2)}) %collective-permute-start.9) | collective-permute-done | bytes 24608 | tf_op jit(solution)/shard_map/ppermute | solution.py:312
  36.3 1.8 %collective-permute-start.10 = (bf16[2,192,128]{2,1,0:T(8,128)(2,1)S(1)}, bf16[2,192,128]{2,1,0:T(8,128)(2,1)S(1)}, u32[]{:S(2)}, u32[]{:S(2)}) collective-permute-start(bf16[2,192,128]{2,1,0:T(8,128)(2,1)S(1)} %get-tuple-element.41.mine_ref.refs_1_), channel_id=1, source_target_pairs={{0,4},{1,5},{2,6},{3,7},{4,0},{5,1},{6,2},{7,3},{8,12},{9,13},{10,... | collective-permute-start | bytes 294920 | tf_op jit(solution)/shard_map/ppermute | solution.py:312
  38.1 2.9 %collective-permute-done.10.other_ref = bf16[2,192,128]{2,1,0:T(8,128)(2,1)S(1)} collective-permute-done((bf16[2,192,128]{2,1,0:T(8,128)(2,1)S(1)}, bf16[2,192,128]{2,1,0:T(8,128)(2,1)S(1)}, u32[]{:S(2)}, u32[]{:S(2)}) %collective-permute-start.10) | collective-permute-done | bytes 98336 | tf_op jit(solution)/shard_map/ppermute | solution.py:312
  41.2 3.1 %collective-permute-start.11 = (bf16[2,192,128]{2,1,0:T(8,128)(2,1)S(1)}, bf16[2,192,128]{2,1,0:T(8,128)(2,1)S(1)}, u32[]{:S(2)}, u32[]{:S(2)}) collective-permute-start(bf16[2,192,128]{2,1,0:T(8,128)(2,1)S(1)} %shard_map.92.mine_ref.refs_2_), channel_id=1, source_target_pairs={{0,8},{1,9},{2,10},{3,11},{4,12},{5,13},{6,14},{7,15},{8,0},{9,1},... | collective-permute-start | bytes 294920 | tf_op jit(solution)/shard_map/ppermute | solution.py:312
  44.3 2.6 %collective-permute-done.11.other_ref = bf16[2,192,128]{2,1,0:T(8,128)(2,1)S(1)} collective-permute-done((bf16[2,192,128]{2,1,0:T(8,128)(2,1)S(1)}, bf16[2,192,128]{2,1,0:T(8,128)(2,1)S(1)}, u32[]{:S(2)}, u32[]{:S(2)}) %collective-permute-start.11) | collective-permute-done | bytes 98336 | tf_op jit(solution)/shard_map/ppermute | solution.py:312
  47.1 1.6 %collective-permute-start.12 = (bf16[2,192,128]{2,1,0:T(8,128)(2,1)S(1)}, bf16[2,192,128]{2,1,0:T(8,128)(2,1)S(1)}, u32[]{:S(2)}, u32[]{:S(2)}) collective-permute-start(bf16[2,192,128]{2,1,0:T(8,128)(2,1)S(1)} %shard_map.93.mine_ref), channel_id=1, source_target_pairs={{0,16},{16,0},{1,17},{17,1},{2,18},{18,2},{3,19},{19,3},{4,20},{20... | collective-permute-start | bytes 294920 | tf_op jit(solution)/shard_map/ppermute | solution.py:312
  48.7 3.1 %collective-permute-done.12.other_ref = bf16[2,192,128]{2,1,0:T(8,128)(2,1)S(1)} collective-permute-done((bf16[2,192,128]{2,1,0:T(8,128)(2,1)S(1)}, bf16[2,192,128]{2,1,0:T(8,128)(2,1)S(1)}, u32[]{:S(2)}, u32[]{:S(2)}) %collective-permute-start.12) | collective-permute-done | bytes 98336 | tf_op jit(solution)/shard_map/ppermute | solution.py:312
  52.1 1.5 %collective-permute-done.13.other_ref = bf16[5,2,96,128]{3,2,1,0:T(8,128)(2,1)S(1)} collective-permute-done((bf16[5,2,96,128]{3,2,1,0:T(8,128)(2,1)S(1)}, bf16[5,2,96,128]{3,2,1,0:T(8,128)(2,1)S(1)}, u32[]{:S(2)}, u32[]{:S(2)}) %collective-permute-start.13) | collective-permute-done | bytes 245792 | tf_op jit(solution)/shard_map/ppermute | solution.py:312
  53.6 1.1 %shard_map.95 = bf16[1,5,2,96,256]{4,3,2,1,0:T(8,128)(2,1)} custom-call(bf16[5,2,96,128]{3,2,1,0:T(8,128)(2,1)S(1)} %shard_map.94.mine_ref, bf16[5,2,96,128]{3,2,1,0:T(8,128)(2,1)S(1)} %collective-permute-done.13.other_ref), custom_call_target="tpu_custom_call" | custom-call | flops 1000 | bytes 1000 | tf_op jit(solution)/shard_map/pallas_call | solution.py:39
  (38 shorter events, 3.6 us)
Async XLA Ops:
  2.7 17.6 %collective-permute-start = (bf16[784,256]{1,0:T(8,128)(2,1)}, bf16[784,256]{1,0:T(8,128)(2,1)S(1)}, u32[]{:S(2)}, u32[]{:S(2)}) collective-permute-start(bf16[784,256]{1,0:T(8,128)(2,1)} %get-tuple-element.32), channel_id=1, source_target_pairs={{0,1},{1,0},{2,3},{3,2},{4,5},{5,4},{6,7},{7,6},{8,9},{9,8},{10,11... | collective-permute-start | bytes 1204232 | tf_op jit(solution)/shard_map/ppermute | solution.py:312
  3.2 17.1 %collective-permute-start.1 = (bf16[784,256]{1,0:T(8,128)(2,1)}, bf16[784,256]{1,0:T(8,128)(2,1)S(1)}, u32[]{:S(2)}, u32[]{:S(2)}) collective-permute-start(bf16[784,256]{1,0:T(8,128)(2,1)} %get-tuple-element.32), channel_id=1, source_target_pairs={{1,2},{3,4},{5,6},{7,8},{9,10},{11,12},{13,14},{2,1},{4,3},{6,5},{... | collective-permute-start | bytes 1204232 | tf_op jit(solution)/shard_map/ppermute | solution.py:341
  4.9 23.0 %all-to-all-start = ((bf16[8,16,1536]{2,1,0:T(8,128)(2,1)}), bf16[8,16,1536]{2,1,0:T(8,128)(2,1)S(1)}, u32[]{:S(2)}, u32[]{:S(2)}) async-start(bf16[8,16,1536]{2,1,0:T(8,128)(2,1)} %get-tuple-element.38), calls=%async_computation | async-start | bytes 786432 | tf_op jit(solution)/shard_map/all_to_all | solution.py:344
  12.6 1.0 %copy-start.1 = (bf16[1,5,4,96,96]{4,3,2,1,0:T(8,128)(2,1)S(1)}, bf16[1,5,4,96,96]{4,3,2,1,0:T(8,128)(2,1)}, u32[]{:S(2)}) copy-start(bf16[1,5,4,96,96]{4,3,2,1,0:T(8,128)(2,1)} %maps_ref.3) | copy-start | bytes 1105924
  13.6 0.7 %copy-start.3 = (s32[1,5,2,192]{3,2,1,0:T(2,128)S(1)}, s32[1,5,2,192]{3,2,1,0:T(2,128)}, u32[]{:S(2)}) copy-start(s32[1,5,2,192]{3,2,1,0:T(2,128)} %perms_ref.5) | copy-start | bytes 23044
  14.3 2.7 %copy-start.5 = (s32[1,2,768]{2,1,0:T(2,128)S(1)}, s32[1,2,768]{2,1,0:T(2,128)}, u32[]{:S(2)}) copy-start(s32[1,2,768]{2,1,0:T(2,128)} %perms_ref.7) | copy-start | bytes 18436
  14.3 2.7 %copy-start.6 = (bf16[6,12,128,128]{3,2,1,0:T(8,128)(2,1)S(1)}, bf16[6,12,128,128]{3,2,1,0:T(8,128)(2,1)}, u32[]{:S(2)}) copy-start(bf16[6,12,128,128]{3,2,1,0:T(8,128)(2,1)} %tiles_ref.1) | copy-start | bytes 7077892
  14.3 2.7 %copy-start.7 = (bf16[1,2,672,96]{2,3,1,0:T(8,128)(2,1)S(1)}, bf16[1,2,672,96]{2,3,1,0:T(8,128)(2,1)}, u32[]{:S(2)}) copy-start(bf16[1,2,672,96]{2,3,1,0:T(8,128)(2,1)} %param.13) | copy-start | bytes 774148
  14.3 2.7 %copy-start.8 = (s32[6,12]{1,0:T(8,128)S(1)}, s32[6,12]{1,0:T(8,128)}, u32[]{:S(2)}) copy-start(s32[6,12]{1,0:T(8,128)} %cols_ref.1) | copy-start | bytes 868
  14.9 5.4 %copy-start = (bf16[768,256]{1,0:T(8,128)(2,1)S(1)}, bf16[768,256]{1,0:T(8,128)(2,1)}, u32[]{:S(2)}) copy-start(bf16[768,256]{1,0:T(8,128)(2,1)} %omega_ref.1) | copy-start | bytes 1179652
  14.9 5.3 %collective-permute-start.2 = (bf16[2,96,96]{2,1,0:T(8,128)(2,1)S(1)}, bf16[2,96,96]{2,1,0:T(8,128)(2,1)S(1)}, u32[]{:S(2)}, u32[]{:S(2)}) collective-permute-start(bf16[2,96,96]{2,1,0:T(8,128)(2,1)S(1)} %get-tuple-element.33), channel_id=1, source_target_pairs={{0,2},{1,3},{2,0},{3,1},{4,6},{5,7},{6,4},{7,5},{8,10},{9,11},{10,... | collective-permute-start | bytes 110600 | tf_op jit(solution)/shard_map/ppermute | solution.py:312
  21.6 6.3 %collective-permute-start.6 = (bf16[192,768]{1,0:T(8,128)(2,1)S(1)}, bf16[192,768]{1,0:T(8,128)(2,1)S(1)}, u32[]{:S(2)}, u32[]{:S(2)}) collective-permute-start(bf16[192,768]{1,0:T(8,128)(2,1)S(1)} %get-tuple-element.37.beside_ref), channel_id=1, source_target_pairs={{0,1},{1,0},{2,3},{3,2},{4,5},{5,4},{6,7},{7,6},{8,9},{9,8},{10,11... | collective-permute-start | bytes 884744 | tf_op jit(solution)/shard_map/ppermute | solution.py:312
  23.4 4.8 %collective-permute-start.5 = (bf16[192,768]{1,0:T(8,128)(2,1)S(1)}, bf16[192,768]{1,0:T(8,128)(2,1)S(1)}, u32[]{:S(2)}, u32[]{:S(2)}) collective-permute-start(bf16[192,768]{1,0:T(8,128)(2,1)S(1)} %get-tuple-element.36.keep_ref), channel_id=1, source_target_pairs={{0,1},{1,0},{2,3},{3,2},{4,5},{5,4},{6,7},{7,6},{8,9},{9,8},{10,11... | collective-permute-start | bytes 884744 | tf_op jit(solution)/shard_map/ppermute | solution.py:312
  23.5 1.6 %collective-permute-start.3 = (bf16[192,128]{1,0:T(8,128)(2,1)S(1)}, bf16[192,128]{1,0:T(8,128)(2,1)S(1)}, u32[]{:S(2)}, u32[]{:S(2)}) collective-permute-start(bf16[192,128]{1,0:T(8,128)(2,1)S(1)} %get-tuple-element.35), channel_id=1, source_target_pairs={{0,1},{1,0},{2,3},{3,2},{4,5},{5,4},{6,7},{7,6},{8,9},{9,8},{10,11... | collective-permute-start | bytes 147464 | tf_op jit(solution)/shard_map/ppermute | solution.py:312
  25.3 9.4 %collective-permute-start.4 = (bf16[192,128]{1,0:T(8,128)(2,1)S(1)}, bf16[192,128]{1,0:T(8,128)(2,1)S(1)}, u32[]{:S(2)}, u32[]{:S(2)}) collective-permute-start(bf16[192,128]{1,0:T(8,128)(2,1)S(1)} %shard_map.87.fwd_ref), channel_id=1, source_target_pairs={{0,2},{1,3},{2,0},{3,1},{4,6},{5,7},{6,4},{7,5},{8,10},{9,11},{10,... | collective-permute-start | bytes 147464 | tf_op jit(solution)/shard_map/ppermute | solution.py:312
  28.1 3.9 %collective-permute-start.8 = (bf16[96,128]{1,0:T(8,128)(2,1)S(1)}, bf16[96,128]{1,0:T(8,128)(2,1)S(1)}, u32[]{:S(2)}, u32[]{:S(2)}) collective-permute-start(bf16[96,128]{1,0:T(8,128)(2,1)S(1)} %get-tuple-element.40), channel_id=1, source_target_pairs={{2,6},{3,7},{6,10},{7,11},{10,14},{11,15},{14,12},{15,13},{12,8},{... | collective-permute-start | bytes 73736 | tf_op jit(solution)/shard_map/ppermute | solution.py:384
  28.2 4.5 %copy-start.2 = (bf16[1,5,4,96,96]{4,3,2,1,0:T(8,128)(2,1)S(1)}, bf16[1,5,4,96,96]{4,3,2,1,0:T(8,128)(2,1)}, u32[]{:S(2)}) copy-start(bf16[1,5,4,96,96]{4,3,2,1,0:T(8,128)(2,1)} %maps_ref.3) | copy-start | bytes 1105924
  28.2 4.5 %copy-start.4 = (s32[1,5,2,192]{3,2,1,0:T(2,128)S(1)}, s32[1,5,2,192]{3,2,1,0:T(2,128)}, u32[]{:S(2)}) copy-start(s32[1,5,2,192]{3,2,1,0:T(2,128)} %perms_ref.5) | copy-start | bytes 23044
  28.8 7.2 %collective-permute-start.7 = (bf16[192,128]{1,0:T(8,128)(2,1)S(1)}, bf16[192,128]{1,0:T(8,128)(2,1)S(1)}, u32[]{:S(2)}, u32[]{:S(2)}) collective-permute-start(bf16[192,128]{1,0:T(8,128)(2,1)S(1)} %shard_map.89.adj_ref), channel_id=1, source_target_pairs={{0,2},{1,3},{2,0},{3,1},{4,6},{5,7},{6,4},{7,5},{8,10},{9,11},{10,... | collective-permute-start | bytes 147464 | tf_op jit(solution)/shard_map/ppermute | solution.py:312
  32.2 3.9 %collective-permute-start.9 = (bf16[96,128]{1,0:T(8,128)(2,1)S(1)}, bf16[96,128]{1,0:T(8,128)(2,1)S(1)}, u32[]{:S(2)}, u32[]{:S(2)}) collective-permute-start(bf16[96,128]{1,0:T(8,128)(2,1)S(1)} %shard_map.90.given_ref), channel_id=1, source_target_pairs={{0,2},{1,3},{2,0},{3,1},{4,6},{5,7},{6,4},{7,5},{8,10},{9,11},{10,... | collective-permute-start | bytes 73736 | tf_op jit(solution)/shard_map/ppermute | solution.py:312
  36.3 4.7 %collective-permute-start.10 = (bf16[2,192,128]{2,1,0:T(8,128)(2,1)S(1)}, bf16[2,192,128]{2,1,0:T(8,128)(2,1)S(1)}, u32[]{:S(2)}, u32[]{:S(2)}) collective-permute-start(bf16[2,192,128]{2,1,0:T(8,128)(2,1)S(1)} %get-tuple-element.41.mine_ref.refs_1_), channel_id=1, source_target_pairs={{0,4},{1,5},{2,6},{3,7},{4,0},{5,1},{6,2},{7,3},{8,12},{9,13},{10,... | collective-permute-start | bytes 294920 | tf_op jit(solution)/shard_map/ppermute | solution.py:312
  41.2 5.6 %collective-permute-start.11 = (bf16[2,192,128]{2,1,0:T(8,128)(2,1)S(1)}, bf16[2,192,128]{2,1,0:T(8,128)(2,1)S(1)}, u32[]{:S(2)}, u32[]{:S(2)}) collective-permute-start(bf16[2,192,128]{2,1,0:T(8,128)(2,1)S(1)} %shard_map.92.mine_ref.refs_2_), channel_id=1, source_target_pairs={{0,8},{1,9},{2,10},{3,11},{4,12},{5,13},{6,14},{7,15},{8,0},{9,1},... | collective-permute-start | bytes 294920 | tf_op jit(solution)/shard_map/ppermute | solution.py:312
  47.1 4.7 %collective-permute-start.12 = (bf16[2,192,128]{2,1,0:T(8,128)(2,1)S(1)}, bf16[2,192,128]{2,1,0:T(8,128)(2,1)S(1)}, u32[]{:S(2)}, u32[]{:S(2)}) collective-permute-start(bf16[2,192,128]{2,1,0:T(8,128)(2,1)S(1)} %shard_map.93.mine_ref), channel_id=1, source_target_pairs={{0,16},{16,0},{1,17},{17,1},{2,18},{18,2},{3,19},{19,3},{4,20},{20... | collective-permute-start | bytes 294920 | tf_op jit(solution)/shard_map/ppermute | solution.py:312
  52.0 1.6 %collective-permute-start.13 = (bf16[5,2,96,128]{3,2,1,0:T(8,128)(2,1)S(1)}, bf16[5,2,96,128]{3,2,1,0:T(8,128)(2,1)S(1)}, u32[]{:S(2)}, u32[]{:S(2)}) collective-permute-start(bf16[5,2,96,128]{3,2,1,0:T(8,128)(2,1)S(1)} %shard_map.94.mine_ref), channel_id=1, source_target_pairs={{0,1},{1,0},{2,3},{3,2},{4,5},{5,4},{6,7},{7,6},{8,9},{9,8},{10,11... | collective-permute-start | bytes 737288 | tf_op jit(solution)/shard_map/ppermute | solution.py:312

commit v8 on v7

--- a/solution.py
+++ b/solution.py
@@ -55,9 +55,9 @@
 
 
 def pack_body(
-    width, tests_hbm, omega_hbm, perms_ref, out_hbm, packed_hbm, tests_ref, omega_ref, order_ref, sems
+    width, tests_hbm, omega_hbm, perms_ref, nodes_ref, out_hbm, packed_hbm, tests_ref, omega_ref, order_ref, sems
 ):
-    rows, cols = omega_ref.shape
+    rows = omega_ref.shape[0]
     chips = out_hbm.shape[0]
     come = [pltpu.make_async_copy(omega_hbm, omega_ref, sems.at[0])]
     go = [pltpu.make_async_copy(omega_ref, packed_hbm.at[:rows], sems.at[1])]
@@ -69,10 +69,13 @@
         go.append(pltpu.make_async_copy(tests_ref.at[chip], out_hbm.at[chip], sems.at[3 + 2 * chip]))
     for copy in come:
         copy.start()
-    order = perms_ref[0, 1:2, :cols]
-    row = lax.broadcasted_iota(jnp.int32, order_ref.shape, 0)
-    digits = jnp.where(row == 0, order // DIGIT, jnp.where(row == 1, order % DIGIT, 0))
-    order_ref[...] = digits.astype(F32).astype(BF)
+    kept = nodes_ref.shape[-1] // 2
+    for order, at in ((perms_ref[0, 1:2, :kept], 0), (nodes_ref[0, 0, 1:2, :kept], 2)):
+        row = lax.broadcasted_iota(jnp.int32, (order_ref.shape[0], kept), 0)
+        digits = jnp.where(row == at, order // DIGIT, jnp.where(row == at + 1, order % DIGIT, 0))
+        total = digits if at == 0 else total + digits
+    order_ref[...] = jnp.zeros_like(order_ref)
+    order_ref[:, :kept] = total.astype(F32).astype(BF)
     last = pltpu.make_async_copy(order_ref, packed_hbm.at[rows:], sems.at[2 + 2 * chips])
     last.start()
     for first, second in zip(come, go):
@@ -115,6 +118,11 @@
     near_ref[...] = mm(keeps[0], dense_ref[...]).astype(BF)
 
 
+def from_digits(digits, at):
+    digits = digits.astype(F32)
+    return (digits[at : at + 1] * DIGIT + digits[at + 1 : at + 2]).astype(jnp.int32)
+
+
 def halo_body(
     dense_ref,
     near_ref,
@@ -122,23 +130,22 @@
     omega_ref,
     inner_ref,
     outer_ref,
-    after_ref,
     beside_ref,
     mine_ref,
     other_ref,
 ):
-    del after_ref
     rows = dense_ref.shape[0]
     rank = near_ref.shape[0]
     half = omega_ref.shape[1] // 2
     core = lax.axis_index("sub") & 1
     unit = eye(rank)
     for b, ref in enumerate((inner_ref, outer_ref)):
-        digits = ref[rows:].astype(F32)
-        order = (digits[0:1, :rank] * DIGIT + digits[1:2, :rank]).astype(jnp.int32)
+        order = from_digits(ref[rows:, :rank], 0)
         keep = mm_t(unit, one_hot(order, rows)).astype(BF)
         block = dense_ref[:, (b + 1) * rows : (b + 2) * rows]
         beside_ref[b * rank : (b + 1) * rank] = mm_t(keep, block).astype(BF)
+    beside_ref[2 * rank :] = jnp.zeros_like(beside_ref[2 * rank :])
+    beside_ref[2 * rank :, : outer_ref.shape[1]] = outer_ref[rows:]
     for out_ref, place in ((mine_ref, core), (other_ref, 1 - core)):
         cols = pl.ds(pl.multiple_of(place * half, half), half)
         own = omega_ref[:, cols]
@@ -154,8 +161,6 @@
 def maps_body(first, maps_ref, perms_ref, *out_refs):
     rank = maps_ref.shape[-1]
     unit = eye(rank)
-    if first == 0:
-        keep_ref, *out_refs = out_refs
     for level, out_ref in enumerate(out_refs, first):
         row_interp, col_interp, low_high, high_low = (maps_ref[0, level, i] for i in range(4))
         row_hot = one_hot(perms_ref[0, level, 0:1, :], 2 * rank)
@@ -164,9 +169,6 @@
         col_all = mm(col_hot, jnp.concatenate([unit, col_interp], axis=0)).astype(BF)
         for kind, (hot, every) in enumerate(((row_hot, col_all), (col_hot, row_all))):
             keep = [mm_t(unit, hot[side * rank : (side + 1) * rank, :rank]).astype(BF) for side in range(2)]
-            if level == 0 and kind == 1:
-                for side in range(2):
-                    keep_ref[side] = keep[side]
             if kind == 0:
                 cross = [mm(keep[1], high_low), mm(keep[0], low_high)]
             else:
@@ -209,8 +211,8 @@
 def edge_body(beside_ref, beside_other, panel_ref, near_out, far_out):
     rank = near_out.shape[0]
     panel, panel_other = halves(panel_ref)
-    mine = mm_t(beside_ref[rank:], panel)
-    other = mm_t(beside_other[rank:], panel_other)
+    mine = mm_t(beside_ref[rank : 2 * rank], panel)
+    other = mm_t(beside_other[rank : 2 * rank], panel_other)
     near = near_rim()
     near_out[...] = jnp.where(near, mine, other).astype(BF)
     far_out[...] = jnp.where(near, other, mine).astype(BF)
@@ -241,10 +243,17 @@
     out_ref[rank:] = tests.astype(BF)
 
 
-def rim_body(keep_ref, near_ref, far_ref, out_ref):
+def rim_body(beside_ref, beside_other, near_ref, far_ref, out_ref):
+    rank = near_ref.shape[0]
     chip = (lax.axis_index("sub") >> 1) & 1
-    added = mm(keep_ref[chip], near_ref[...]) + mm(keep_ref[1 - chip], far_ref[...])
-    out_ref[...] = added.astype(BF)
+    digits = [ref[2 * rank :, :rank].astype(F32) for ref in (beside_ref, beside_other)]
+    order = from_digits(jnp.where(near_rim(), *digits), 2)
+    hot = one_hot(order, 2 * rank)
+    keeps = [mm_t(eye(rank), hot[side * rank : (side + 1) * rank]) for side in range(2)]
+    upper = chip == 1
+    near_keep = jnp.where(upper, keeps[1], keeps[0]).astype(BF)
+    far_keep = jnp.where(upper, keeps[0], keeps[1]).astype(BF)
+    out_ref[...] = (mm(near_keep, near_ref[...]) + mm(far_keep, far_ref[...])).astype(BF)
 
 
 def joined_body(
@@ -327,14 +336,14 @@
     blocks, packed = call(
         functools.partial(pack_body, 2 * rows),
         [shape((chips, vectors, 2 * rows)), shape((rows + 16, samples))],
-        (adj_tests, omega, leaf_perms),
+        (adj_tests, omega, leaf_perms, node_perms),
         scratch=[
             pltpu.VMEM((chips, vectors, 2 * rows), BF),
             pltpu.VMEM(omega.shape, BF),
             pltpu.VMEM((16, samples), BF),
             pltpu.SemaphoreType.DMA((2 * chips + 3,)),
         ],
-        specs="hhv",
+        specs="hhvv",
         out="a",
         limit=56 << 20,
     )
@@ -346,11 +355,11 @@
     ).reshape(half, 2 * rows)
 
     tables = shape((2, 2, 3 * rank, rank))
-    picks, first_maps = call(
+    [first_maps] = call(
         functools.partial(maps_body, 0),
-        [shape((2, rank, rank)), tables],
+        [tables],
         (node_maps, node_perms),
-        flops=4 << 30,
+        flops=1 << 30,
     )
     keep, near, tests, dense = call(
         dense_body,
@@ -365,12 +374,10 @@
         flops=1 << 30,
     )
     keep_other = swapped(keep, "sub", 0)
-    picks_other = swapped(picks, "sub", 1)
     beside, fwd_mine, fwd_send = call(
         halo_body,
-        [shape((2 * rank, rows))] + [shape((2 * rank, half))] * 2,
-        (dense, near, tests, omega, packed_inner, packed_outer, picks_other),
-        specs="vvvvvva",
+        [shape((2 * rank + 16, rows))] + [shape((2 * rank, half))] * 2,
+        (dense, near, tests, omega, packed_inner, packed_outer),
     )
     beside_other = swapped(beside, "sub", 0)
     fwd = call(
@@ -389,7 +396,7 @@
         specs="vvvvvva",
         flops=4 << 30,
     )
-    given = call(rim_body, shape((rank, half)), (picks_other, near_rims, far_rims))
+    given = call(rim_body, shape((rank, half)), (beside, beside_other, near_rims, far_rims))
     more_maps = call(
         functools.partial(maps_body, 1), [tables] * (levels - 1), (node_maps, node_perms)
     )

time: 55.6 us -> 55.8 us (level)
  starting transfers between devices: 26.8 us -> 23.8 us
  waiting for transfers between devices: 13 us -> 15.5 us
  local copies, waits for them, and re-layouts: 1.76 us -> 2.81 us
    ppermute x12 -> x11, starting transfers between devices: 17.4 us -> 14.4 us  [swapped(): lax.ppermute(x, axis, [(i, i ^ 1 << bit) for i in range(lax.axis_size(axi...]
    ppermute x12 -> x11, waiting for transfers between devices: 12.7 us -> 14.3 us  [swapped(): lax.ppermute(x, axis, [(i, i ^ 1 << bit) for i in range(lax.axis_size(axi...]
    unnamed x18, local copies, waits for them, and re-layouts: 1.76 us -> 2.81 us
    ppermute x1, waiting for transfers between devices: 0.35 us -> 1.15 us  [local(): far_rims = lax.ppermute(far_rims, 'sub', route)]
  transfers between devices with their start and end apart: 15 -> 14, of which waited for: 7 -> 7; matrix products, arithmetic and copies ran while one was open for 0% -> 0% of each run, Pallas kernels for 15% -> 15%
where the time goes in v8:
time: 55.8 us; the launch traced here: 55.4 us
  starting transfers between devices  23.8 us (43%)
  waiting for transfers between devices  15.5 us (28%)
  Pallas kernels  13.1 us (23%)
  local copies, waits for them, and re-layouts  2.81 us (5%)
    ppermute x11, starting transfers between devices, swapped(): lax.ppermute(x, axis, [(i, i ^ 1 << bit) for i in range(lax.axis_size(axi...  14.4 us
    ppermute x11, waiting for transfers between devices, swapped(): lax.ppermute(x, axis, [(i, i ^ 1 << bit) for i in range(lax.axis_size(axi...  14.3 us
    pallas_call x14, Pallas kernels, call(): pl.pallas_call(body, out_shape=out_shape, in_specs=[SPACES[c] for c in sp...  13.1 us
    all_to_all x1, starting transfers between devices, local(): lax.all_to_all(blocks, 'sub', split_axis=0, concat_axis=0, tiled=True, ax...  7.72 us
    unnamed x18, local copies, waits for them, and re-layouts  2.81 us
    ppermute x1, starting transfers between devices, local(): packed_outer = lax.ppermute(packed, 'sub', outward)  1.65 us
    ppermute x1, waiting for transfers between devices, local(): far_rims = lax.ppermute(far_rims, 'sub', route)  1.15 us
  transfers between devices with their start and end apart: 14, of which 7 were waited for; matrix products, arithmetic and copies ran while one was open for 0% of the time, Pallas kernels for 15%

profile of v8, /device:TPU:0, one launch (start us, length us, event | category | flops | bytes accessed | tf_op | source)
XLA Modules:
  0.0 55.4 jit_solution(5476890600862752733)
XLA Ops:
  0.0 2.8 %shard_map.85 = (bf16[8,16,1536]{2,1,0:T(8,128)(2,1)}, bf16[784,256]{1,0:T(8,128)(2,1)}) custom-call(bf16[16,12288]{1,0:T(8,128)(2,1)} %tests_hbm.1, bf16[768,256]{1,0:T(8,128)(2,1)} %omega_ref.1, s32[1,2,768]{2,1,0:T(2,128)} %perms_ref.7, s32[1,5,2,192]{3,2,1,0:T(2,128)} %nodes_ref.1), custom_call_target="tpu_custom_call" | custom-call | flops 1000 | bytes 1000 | tf_op jit(solution)/shard_map/pallas_call | solution.py:39
  3.3 1.6 %collective-permute-start.1 = (bf16[784,256]{1,0:T(8,128)(2,1)}, bf16[784,256]{1,0:T(8,128)(2,1)S(1)}, u32[]{:S(2)}, u32[]{:S(2)}) collective-permute-start(bf16[784,256]{1,0:T(8,128)(2,1)} %get-tuple-element.29), channel_id=1, source_target_pairs={{1,2},{3,4},{5,6},{7,8},{9,10},{11,12},{13,14},{2,1},{4,3},{6,5},{... | collective-permute-start | bytes 1204232 | tf_op jit(solution)/shard_map/ppermute | solution.py:350
  5.0 7.7 %all-to-all-start = ((bf16[8,16,1536]{2,1,0:T(8,128)(2,1)}), bf16[8,16,1536]{2,1,0:T(8,128)(2,1)S(1)}, u32[]{:S(2)}, u32[]{:S(2)}) async-start(bf16[8,16,1536]{2,1,0:T(8,128)(2,1)} %get-tuple-element.34), calls=%async_computation | async-start | bytes 786432 | tf_op jit(solution)/shard_map/all_to_all | solution.py:353
  12.7 1.0 %copy-done.1 = bf16[1,5,4,96,96]{4,3,2,1,0:T(8,128)(2,1)S(1)} copy-done((bf16[1,5,4,96,96]{4,3,2,1,0:T(8,128)(2,1)S(1)}, bf16[1,5,4,96,96]{4,3,2,1,0:T(8,128)(2,1)}, u32[]{:S(2)}) %copy-start.1) | copy-done | bytes 368664
  13.7 0.7 %copy-done.3 = s32[1,5,2,192]{3,2,1,0:T(2,128)S(1)} copy-done((s32[1,5,2,192]{3,2,1,0:T(2,128)S(1)}, s32[1,5,2,192]{3,2,1,0:T(2,128)}, u32[]{:S(2)}) %copy-start.3) | copy-done | bytes 7704
  15.0 1.1 %copy-done.6 = bf16[6,12,128,128]{3,2,1,0:T(8,128)(2,1)S(1)} copy-done((bf16[6,12,128,128]{3,2,1,0:T(8,128)(2,1)S(1)}, bf16[6,12,128,128]{3,2,1,0:T(8,128)(2,1)}, u32[]{:S(2)}) %copy-start.6) | copy-done | bytes 2359320
  16.1 3.2 %shard_map.84 = (bf16[192,768]{1,0:T(8,128)(2,1)S(1)}, bf16[96,2304]{1,0:T(8,128)(2,1)S(1)}, bf16[96,768]{1,0:T(8,128)(2,1)S(1)}, bf16[768,2304]{1,0:T(8,128)(2,1)S(1)}) custom-call(s32[6,12]{1,0:T(8,128)S(1)} %copy-done.8, bf16[6,12,128,128]{3,2,1,0:T(8,128)(2,1)S(1)} %copy-done.6, s32[1,2,768]{2,1,0:T(2,128)S(1)} %copy-done.5, ...), custom_call_target="tpu_custom_call" | custom-call | flops 1073741824 | bytes 1000 | tf_op jit(solution)/shard_map/pallas_call | solution.py:39
  19.4 1.3 %shard_map.86 = (bf16[208,768]{1,0:T(8,128)(2,1)S(1)}, bf16[192,128]{1,0:T(8,128)(2,1)S(1)}, bf16[192,128]{1,0:T(8,128)(2,1)S(1)}) custom-call(bf16[768,2304]{1,0:T(8,128)(2,1)S(1)} %get-tuple-element.26.dense_ref, bf16[96,2304]{1,0:T(8,128)(2,1)S(1)} %get-tuple-element.27.near_ref, bf16[96,768]{1,0:T(8,128)(2,1)S(1)} %get-tuple-element.28.tests_ref, ...), custom_call_target="tpu_custom_call" | custom-call | flops 1000 | bytes 1000 | tf_op jit(solution)/shard_map/pallas_call | solution.py:39
  20.7 1.3 %collective-permute-start.5 = (bf16[208,768]{1,0:T(8,128)(2,1)S(1)}, bf16[208,768]{1,0:T(8,128)(2,1)S(1)}, u32[]{:S(2)}, u32[]{:S(2)}) collective-permute-start(bf16[208,768]{1,0:T(8,128)(2,1)S(1)} %get-tuple-element.33.beside_ref), channel_id=1, source_target_pairs={{0,1},{1,0},{2,3},{3,2},{4,5},{5,4},{6,7},{7,6},{8,9},{9,8},{10,11... | collective-permute-start | bytes 958472 | tf_op jit(solution)/shard_map/ppermute | solution.py:321
  22.5 1.2 %collective-permute-done.2.other_ref = bf16[192,128]{1,0:T(8,128)(2,1)S(1)} collective-permute-done((bf16[192,128]{1,0:T(8,128)(2,1)S(1)}, bf16[192,128]{1,0:T(8,128)(2,1)S(1)}, u32[]{:S(2)}, u32[]{:S(2)}) %collective-permute-start.2) | collective-permute-done | bytes 49184 | tf_op jit(solution)/shard_map/ppermute | solution.py:321
  23.9 2.7 %collective-permute-start.3 = (bf16[192,128]{1,0:T(8,128)(2,1)S(1)}, bf16[192,128]{1,0:T(8,128)(2,1)S(1)}, u32[]{:S(2)}, u32[]{:S(2)}) collective-permute-start(bf16[192,128]{1,0:T(8,128)(2,1)S(1)} %shard_map.87.fwd_ref), channel_id=1, source_target_pairs={{0,2},{1,3},{2,0},{3,1},{4,6},{5,7},{6,4},{7,5},{8,10},{9,11},{10,... | collective-permute-start | bytes 147464 | tf_op jit(solution)/shard_map/ppermute | solution.py:321
  27.0 0.6 %shard_map.89.adj_ref = bf16[192,128]{1,0:T(8,128)(2,1)S(1)} custom-call(bf16[2,2,288,96]{3,2,1,0:T(8,128)(2,1)S(1)} %shard_map.83.after_ref.maps_ref, bf16[192,768]{1,0:T(8,128)(2,1)S(1)} %get-tuple-element.32.keep_ref, bf16[192,768]{1,0:T(8,128)(2,1)S(1)} %collective-permute-done.4.keep_other, bf16[208,768]{1,0:T(8,128)(2,1)S(1)} %get-tuple-element.33.beside_ref, ...), custom_call_target="tpu_custom_call" | custom-call | flops 4294967296 | bytes 1000 | tf_op jit(solution)/shard_map/pallas_call | solution.py:39
  27.6 2.0 %collective-permute-start.6 = (bf16[192,128]{1,0:T(8,128)(2,1)S(1)}, bf16[192,128]{1,0:T(8,128)(2,1)S(1)}, u32[]{:S(2)}, u32[]{:S(2)}) collective-permute-start(bf16[192,128]{1,0:T(8,128)(2,1)S(1)} %shard_map.89.adj_ref), channel_id=1, source_target_pairs={{0,2},{1,3},{2,0},{3,1},{4,6},{5,7},{6,4},{7,5},{8,10},{9,11},{10,... | collective-permute-start | bytes 147464 | tf_op jit(solution)/shard_map/ppermute | solution.py:321
  29.6 1.1 %collective-permute-done.7.far_ref = bf16[96,128]{1,0:T(8,128)(2,1)S(1)} collective-permute-done((bf16[96,128]{1,0:T(8,128)(2,1)S(1)}, bf16[96,128]{1,0:T(8,128)(2,1)S(1)}, u32[]{:S(2)}, u32[]{:S(2)}) %collective-permute-start.7) | collective-permute-done | bytes 24608 | tf_op jit(solution)/shard_map/ppermute | solution.py:391
  31.3 1.9 %shard_map.82 = (bf16[2,2,288,96]{3,2,1,0:T(8,128)(2,1)S(1)}, bf16[2,2,288,96]{3,2,1,0:T(8,128)(2,1)S(1)}, bf16[2,2,288,96]{3,2,1,0:T(8,128)(2,1)S(1)}, bf16[2,2,288,96]{3,2,1,0:T(8,128)(2,1)S(1)}) custom-call(bf16[1,5,4,96,96]{4,3,2,1,0:T(8,128)(2,1)S(1)} %copy-done.2, s32[1,5,2,192]{3,2,1,0:T(2,128)S(1)} %copy-done.4), custom_call_target="tpu_custom_call" | custom-call | flops 1000 | bytes 1000 | tf_op jit(solution)/shard_map/pallas_call | solution.py:39
  33.3 1.7 %collective-permute-done.8.added_ref = bf16[96,128]{1,0:T(8,128)(2,1)S(1)} collective-permute-done((bf16[96,128]{1,0:T(8,128)(2,1)S(1)}, bf16[96,128]{1,0:T(8,128)(2,1)S(1)}, u32[]{:S(2)}, u32[]{:S(2)}) %collective-permute-start.8) | collective-permute-done | bytes 24608 | tf_op jit(solution)/shard_map/ppermute | solution.py:321
  35.2 1.5 %collective-permute-start.9 = (bf16[2,192,128]{2,1,0:T(8,128)(2,1)S(1)}, bf16[2,192,128]{2,1,0:T(8,128)(2,1)S(1)}, u32[]{:S(2)}, u32[]{:S(2)}) collective-permute-start(bf16[2,192,128]{2,1,0:T(8,128)(2,1)S(1)} %get-tuple-element.37.mine_ref.refs_1_), channel_id=1, source_target_pairs={{0,4},{1,5},{2,6},{3,7},{4,0},{5,1},{6,2},{7,3},{8,12},{9,13},{10,... | collective-permute-start | bytes 294920 | tf_op jit(solution)/shard_map/ppermute | solution.py:321
  36.7 3.2 %collective-permute-done.9.other_ref = bf16[2,192,128]{2,1,0:T(8,128)(2,1)S(1)} collective-permute-done((bf16[2,192,128]{2,1,0:T(8,128)(2,1)S(1)}, bf16[2,192,128]{2,1,0:T(8,128)(2,1)S(1)}, u32[]{:S(2)}, u32[]{:S(2)}) %collective-permute-start.9) | collective-permute-done | bytes 98336 | tf_op jit(solution)/shard_map/ppermute | solution.py:321
  40.1 3.9 %collective-permute-start.10 = (bf16[2,192,128]{2,1,0:T(8,128)(2,1)S(1)}, bf16[2,192,128]{2,1,0:T(8,128)(2,1)S(1)}, u32[]{:S(2)}, u32[]{:S(2)}) collective-permute-start(bf16[2,192,128]{2,1,0:T(8,128)(2,1)S(1)} %shard_map.92.mine_ref.refs_2_), channel_id=1, source_target_pairs={{0,8},{1,9},{2,10},{3,11},{4,12},{5,13},{6,14},{7,15},{8,0},{9,1},... | collective-permute-start | bytes 294920 | tf_op jit(solution)/shard_map/ppermute | solution.py:321
  44.0 3.6 %collective-permute-done.10.other_ref = bf16[2,192,128]{2,1,0:T(8,128)(2,1)S(1)} collective-permute-done((bf16[2,192,128]{2,1,0:T(8,128)(2,1)S(1)}, bf16[2,192,128]{2,1,0:T(8,128)(2,1)S(1)}, u32[]{:S(2)}, u32[]{:S(2)}) %collective-permute-start.10) | collective-permute-done | bytes 98336 | tf_op jit(solution)/shard_map/ppermute | solution.py:321
  47.8 1.6 %collective-permute-start.11 = (bf16[2,192,128]{2,1,0:T(8,128)(2,1)S(1)}, bf16[2,192,128]{2,1,0:T(8,128)(2,1)S(1)}, u32[]{:S(2)}, u32[]{:S(2)}) collective-permute-start(bf16[2,192,128]{2,1,0:T(8,128)(2,1)S(1)} %shard_map.93.mine_ref), channel_id=1, source_target_pairs={{0,16},{16,0},{1,17},{17,1},{2,18},{18,2},{3,19},{19,3},{4,20},{20... | collective-permute-start | bytes 294920 | tf_op jit(solution)/shard_map/ppermute | solution.py:321
  49.4 3.1 %collective-permute-done.11.other_ref = bf16[2,192,128]{2,1,0:T(8,128)(2,1)S(1)} collective-permute-done((bf16[2,192,128]{2,1,0:T(8,128)(2,1)S(1)}, bf16[2,192,128]{2,1,0:T(8,128)(2,1)S(1)}, u32[]{:S(2)}, u32[]{:S(2)}) %collective-permute-start.11) | collective-permute-done | bytes 98336 | tf_op jit(solution)/shard_map/ppermute | solution.py:321
  52.8 1.5 %collective-permute-done.12.other_ref = bf16[5,2,96,128]{3,2,1,0:T(8,128)(2,1)S(1)} collective-permute-done((bf16[5,2,96,128]{3,2,1,0:T(8,128)(2,1)S(1)}, bf16[5,2,96,128]{3,2,1,0:T(8,128)(2,1)S(1)}, u32[]{:S(2)}, u32[]{:S(2)}) %collective-permute-start.12) | collective-permute-done | bytes 245792 | tf_op jit(solution)/shard_map/ppermute | solution.py:321
  54.3 1.1 %shard_map.95 = bf16[1,5,2,96,256]{4,3,2,1,0:T(8,128)(2,1)} custom-call(bf16[5,2,96,128]{3,2,1,0:T(8,128)(2,1)S(1)} %shard_map.94.mine_ref, bf16[5,2,96,128]{3,2,1,0:T(8,128)(2,1)S(1)} %collective-permute-done.12.other_ref), custom_call_target="tpu_custom_call" | custom-call | flops 1000 | bytes 1000 | tf_op jit(solution)/shard_map/pallas_call | solution.py:39
  (36 shorter events, 3.7 us)
Async XLA Ops:
  0.0 15.0 %copy-start.5 = (s32[1,2,768]{2,1,0:T(2,128)S(1)}, s32[1,2,768]{2,1,0:T(2,128)}, u32[]{:S(2)}) copy-start(s32[1,2,768]{2,1,0:T(2,128)} %perms_ref.7) | copy-start | bytes 18436
  0.0 15.0 %copy-start.7 = (bf16[1,2,672,96]{2,3,1,0:T(8,128)(2,1)S(1)}, bf16[1,2,672,96]{2,3,1,0:T(8,128)(2,1)}, u32[]{:S(2)}) copy-start(bf16[1,2,672,96]{2,3,1,0:T(8,128)(2,1)} %param.13) | copy-start | bytes 774148
  0.0 15.0 %copy-start.8 = (s32[6,12]{1,0:T(8,128)S(1)}, s32[6,12]{1,0:T(8,128)}, u32[]{:S(2)}) copy-start(s32[6,12]{1,0:T(8,128)} %cols_ref.1) | copy-start | bytes 868
  2.8 16.5 %collective-permute-start = (bf16[784,256]{1,0:T(8,128)(2,1)}, bf16[784,256]{1,0:T(8,128)(2,1)S(1)}, u32[]{:S(2)}, u32[]{:S(2)}) collective-permute-start(bf16[784,256]{1,0:T(8,128)(2,1)} %get-tuple-element.29), channel_id=1, source_target_pairs={{0,1},{1,0},{2,3},{3,2},{4,5},{5,4},{6,7},{7,6},{8,9},{9,8},{10,11... | collective-permute-start | bytes 1204232 | tf_op jit(solution)/shard_map/ppermute | solution.py:321
  3.3 16.0 %collective-permute-start.1 = (bf16[784,256]{1,0:T(8,128)(2,1)}, bf16[784,256]{1,0:T(8,128)(2,1)S(1)}, u32[]{:S(2)}, u32[]{:S(2)}) collective-permute-start(bf16[784,256]{1,0:T(8,128)(2,1)} %get-tuple-element.29), channel_id=1, source_target_pairs={{1,2},{3,4},{5,6},{7,8},{9,10},{11,12},{13,14},{2,1},{4,3},{6,5},{... | collective-permute-start | bytes 1204232 | tf_op jit(solution)/shard_map/ppermute | solution.py:350
  5.0 21.6 %all-to-all-start = ((bf16[8,16,1536]{2,1,0:T(8,128)(2,1)}), bf16[8,16,1536]{2,1,0:T(8,128)(2,1)S(1)}, u32[]{:S(2)}, u32[]{:S(2)}) async-start(bf16[8,16,1536]{2,1,0:T(8,128)(2,1)} %get-tuple-element.34), calls=%async_computation | async-start | bytes 786432 | tf_op jit(solution)/shard_map/all_to_all | solution.py:353
  12.7 1.0 %copy-start.1 = (bf16[1,5,4,96,96]{4,3,2,1,0:T(8,128)(2,1)S(1)}, bf16[1,5,4,96,96]{4,3,2,1,0:T(8,128)(2,1)}, u32[]{:S(2)}) copy-start(bf16[1,5,4,96,96]{4,3,2,1,0:T(8,128)(2,1)} %maps_ref.3) | copy-start | bytes 1105924
  13.7 0.7 %copy-start.3 = (s32[1,5,2,192]{3,2,1,0:T(2,128)S(1)}, s32[1,5,2,192]{3,2,1,0:T(2,128)}, u32[]{:S(2)}) copy-start(s32[1,5,2,192]{3,2,1,0:T(2,128)} %nodes_ref.1) | copy-start | bytes 23044
  14.4 1.7 %copy-start.6 = (bf16[6,12,128,128]{3,2,1,0:T(8,128)(2,1)S(1)}, bf16[6,12,128,128]{3,2,1,0:T(8,128)(2,1)}, u32[]{:S(2)}) copy-start(bf16[6,12,128,128]{3,2,1,0:T(8,128)(2,1)} %tiles_ref.1) | copy-start | bytes 7077892
  14.4 4.9 %copy-start = (bf16[768,256]{1,0:T(8,128)(2,1)S(1)}, bf16[768,256]{1,0:T(8,128)(2,1)}, u32[]{:S(2)}) copy-start(bf16[768,256]{1,0:T(8,128)(2,1)} %omega_ref.1) | copy-start | bytes 1179652
  20.7 6.0 %collective-permute-start.5 = (bf16[208,768]{1,0:T(8,128)(2,1)S(1)}, bf16[208,768]{1,0:T(8,128)(2,1)S(1)}, u32[]{:S(2)}, u32[]{:S(2)}) collective-permute-start(bf16[208,768]{1,0:T(8,128)(2,1)S(1)} %get-tuple-element.33.beside_ref), channel_id=1, source_target_pairs={{0,1},{1,0},{2,3},{3,2},{4,5},{5,4},{6,7},{7,6},{8,9},{9,8},{10,11... | collective-permute-start | bytes 958472 | tf_op jit(solution)/shard_map/ppermute | solution.py:321
  22.0 5.0 %collective-permute-start.4 = (bf16[192,768]{1,0:T(8,128)(2,1)S(1)}, bf16[192,768]{1,0:T(8,128)(2,1)S(1)}, u32[]{:S(2)}, u32[]{:S(2)}) collective-permute-start(bf16[192,768]{1,0:T(8,128)(2,1)S(1)} %get-tuple-element.32.keep_ref), channel_id=1, source_target_pairs={{0,1},{1,0},{2,3},{3,2},{4,5},{5,4},{6,7},{7,6},{8,9},{9,8},{10,11... | collective-permute-start | bytes 884744 | tf_op jit(solution)/shard_map/ppermute | solution.py:321
  22.1 1.7 %collective-permute-start.2 = (bf16[192,128]{1,0:T(8,128)(2,1)S(1)}, bf16[192,128]{1,0:T(8,128)(2,1)S(1)}, u32[]{:S(2)}, u32[]{:S(2)}) collective-permute-start(bf16[192,128]{1,0:T(8,128)(2,1)S(1)} %get-tuple-element.31), channel_id=1, source_target_pairs={{0,1},{1,0},{2,3},{3,2},{4,5},{5,4},{6,7},{7,6},{8,9},{9,8},{10,11... | collective-permute-start | bytes 147464 | tf_op jit(solution)/shard_map/ppermute | solution.py:321
  23.9 9.4 %collective-permute-start.3 = (bf16[192,128]{1,0:T(8,128)(2,1)S(1)}, bf16[192,128]{1,0:T(8,128)(2,1)S(1)}, u32[]{:S(2)}, u32[]{:S(2)}) collective-permute-start(bf16[192,128]{1,0:T(8,128)(2,1)S(1)} %shard_map.87.fwd_ref), channel_id=1, source_target_pairs={{0,2},{1,3},{2,0},{3,1},{4,6},{5,7},{6,4},{7,5},{8,10},{9,11},{10,... | collective-permute-start | bytes 147464 | tf_op jit(solution)/shard_map/ppermute | solution.py:321
  26.9 3.9 %collective-permute-start.7 = (bf16[96,128]{1,0:T(8,128)(2,1)S(1)}, bf16[96,128]{1,0:T(8,128)(2,1)S(1)}, u32[]{:S(2)}, u32[]{:S(2)}) collective-permute-start(bf16[96,128]{1,0:T(8,128)(2,1)S(1)} %get-tuple-element.36), channel_id=1, source_target_pairs={{2,6},{3,7},{6,10},{7,11},{10,14},{11,15},{14,12},{15,13},{12,8},{... | collective-permute-start | bytes 73736 | tf_op jit(solution)/shard_map/ppermute | solution.py:391
  27.0 4.3 %copy-start.2 = (bf16[1,5,4,96,96]{4,3,2,1,0:T(8,128)(2,1)S(1)}, bf16[1,5,4,96,96]{4,3,2,1,0:T(8,128)(2,1)}, u32[]{:S(2)}) copy-start(bf16[1,5,4,96,96]{4,3,2,1,0:T(8,128)(2,1)} %maps_ref.3) | copy-start | bytes 1105924
  27.0 4.3 %copy-start.4 = (s32[1,5,2,192]{3,2,1,0:T(2,128)S(1)}, s32[1,5,2,192]{3,2,1,0:T(2,128)}, u32[]{:S(2)}) copy-start(s32[1,5,2,192]{3,2,1,0:T(2,128)} %nodes_ref.1) | copy-start | bytes 23044
  27.6 7.4 %collective-permute-start.6 = (bf16[192,128]{1,0:T(8,128)(2,1)S(1)}, bf16[192,128]{1,0:T(8,128)(2,1)S(1)}, u32[]{:S(2)}, u32[]{:S(2)}) collective-permute-start(bf16[192,128]{1,0:T(8,128)(2,1)S(1)} %shard_map.89.adj_ref), channel_id=1, source_target_pairs={{0,2},{1,3},{2,0},{3,1},{4,6},{5,7},{6,4},{7,5},{8,10},{9,11},{10,... | collective-permute-start | bytes 147464 | tf_op jit(solution)/shard_map/ppermute | solution.py:321
  31.1 3.9 %collective-permute-start.8 = (bf16[96,128]{1,0:T(8,128)(2,1)S(1)}, bf16[96,128]{1,0:T(8,128)(2,1)S(1)}, u32[]{:S(2)}, u32[]{:S(2)}) collective-permute-start(bf16[96,128]{1,0:T(8,128)(2,1)S(1)} %shard_map.90.given_ref), channel_id=1, source_target_pairs={{0,2},{1,3},{2,0},{3,1},{4,6},{5,7},{6,4},{7,5},{8,10},{9,11},{10,... | collective-permute-start | bytes 73736 | tf_op jit(solution)/shard_map/ppermute | solution.py:321
  35.2 4.7 %collective-permute-start.9 = (bf16[2,192,128]{2,1,0:T(8,128)(2,1)S(1)}, bf16[2,192,128]{2,1,0:T(8,128)(2,1)S(1)}, u32[]{:S(2)}, u32[]{:S(2)}) collective-permute-start(bf16[2,192,128]{2,1,0:T(8,128)(2,1)S(1)} %get-tuple-element.37.mine_ref.refs_1_), channel_id=1, source_target_pairs={{0,4},{1,5},{2,6},{3,7},{4,0},{5,1},{6,2},{7,3},{8,12},{9,13},{10,... | collective-permute-start | bytes 294920 | tf_op jit(solution)/shard_map/ppermute | solution.py:321
  40.1 7.5 %collective-permute-start.10 = (bf16[2,192,128]{2,1,0:T(8,128)(2,1)S(1)}, bf16[2,192,128]{2,1,0:T(8,128)(2,1)S(1)}, u32[]{:S(2)}, u32[]{:S(2)}) collective-permute-start(bf16[2,192,128]{2,1,0:T(8,128)(2,1)S(1)} %shard_map.92.mine_ref.refs_2_), channel_id=1, source_target_pairs={{0,8},{1,9},{2,10},{3,11},{4,12},{5,13},{6,14},{7,15},{8,0},{9,1},... | collective-permute-start | bytes 294920 | tf_op jit(solution)/shard_map/ppermute | solution.py:321
  47.8 4.7 %collective-permute-start.11 = (bf16[2,192,128]{2,1,0:T(8,128)(2,1)S(1)}, bf16[2,192,128]{2,1,0:T(8,128)(2,1)S(1)}, u32[]{:S(2)}, u32[]{:S(2)}) collective-permute-start(bf16[2,192,128]{2,1,0:T(8,128)(2,1)S(1)} %shard_map.93.mine_ref), channel_id=1, source_target_pairs={{0,16},{16,0},{1,17},{17,1},{2,18},{18,2},{3,19},{19,3},{4,20},{20... | collective-permute-start | bytes 294920 | tf_op jit(solution)/shard_map/ppermute | solution.py:321
  52.8 1.6 %collective-permute-start.12 = (bf16[5,2,96,128]{3,2,1,0:T(8,128)(2,1)S(1)}, bf16[5,2,96,128]{3,2,1,0:T(8,128)(2,1)S(1)}, u32[]{:S(2)}, u32[]{:S(2)}) collective-permute-start(bf16[5,2,96,128]{3,2,1,0:T(8,128)(2,1)S(1)} %shard_map.94.mine_ref), channel_id=1, source_target_pairs={{0,1},{1,0},{2,3},{3,2},{4,5},{5,4},{6,7},{7,6},{8,9},{9,8},{10,11... | collective-permute-start | bytes 737288 | tf_op jit(solution)/shard_map/ppermute | solution.py:321

commit v9 on v8

--- a/solution.py
+++ b/solution.py
@@ -256,48 +256,47 @@
     out_ref[...] = (mm(near_keep, near_ref[...]) + mm(far_keep, far_ref[...])).astype(BF)
 
 
-def joined_body(
-    bit, maps_ref, fwd_ref, fwd_other, adj_ref, adj_other, added_ref, given_ref, out_ref, node_ref
-):
+def joined_body(bit, maps_ref, mine_ref, other_ref, added_ref, given_ref, out_ref, node_ref):
     rank = added_ref.shape[0]
     side = (lax.axis_index("sub") >> bit) & 1
-    mine = (adj_ref[:rank].astype(F32) + added_ref[...].astype(F32)).astype(BF)
-    other = (adj_other[:rank].astype(F32) + given_ref[...].astype(F32)).astype(BF)
-    node_ref[0] = fwd_ref[:rank]
-    node_ref[1] = mine
-    chains = (
-        (fwd_ref[:rank], fwd_ref[rank:], fwd_other[:rank], fwd_other[rank:]),
-        (mine, adj_ref[rank:], other, adj_other[rank:]),
-    )
-    for kind, panels in enumerate(chains):
-        kept, tests = merged(maps_ref, kind, side, *panels, rank)
-        out_ref[kind, :rank] = kept.astype(BF)
-        out_ref[kind, rank:] = tests.astype(BF)
-
-
-def level_body(axis, bit, last, maps_ref, mine_ref, other_ref, *refs):
-    rank = mine_ref.shape[1] // 2
+    mine = (mine_ref[:rank].astype(F32) + added_ref[...].astype(F32)).astype(BF)
+    other = (other_ref[:rank].astype(F32) + given_ref[...].astype(F32)).astype(BF)
+    node_ref[...] = mine
+    kept, tests = merged(maps_ref, 1, side, mine, mine_ref[rank:], other, other_ref[rank:], rank)
+    out_ref[:rank] = kept.astype(BF)
+    out_ref[rank:] = tests.astype(BF)
+
+
+def level_body(kind, axis, bit, maps_ref, mine_ref, other_ref, out_ref):
+    rank = mine_ref.shape[0] // 2
     side = (lax.axis_index(axis) >> bit) & 1
+    kept, tests = merged(
+        maps_ref, kind, side, mine_ref[:rank], mine_ref[rank:], other_ref[:rank], other_ref[rank:], rank
+    )
+    out_ref[:rank] = kept.astype(BF)
+    out_ref[rank:] = tests.astype(BF)
+
+
+def last_body(axis, bit, levels, maps_ref, *refs):
     out_ref = refs[-1]
-    if last:
-        for level, ref in enumerate((*refs[:-1], mine_ref)):
-            out_ref[level] = ref[:, :rank]
+    rank = out_ref.shape[2]
+    side = (lax.axis_index(axis) >> bit) & 1
     for kind in range(2):
-        kept, tests = merged(
+        nodes = refs[kind * levels : kind * levels + levels - 1]
+        mine_ref, other_ref = nodes[-1], refs[kind * levels + levels - 1]
+        for level, ref in enumerate(nodes):
+            out_ref[level, kind] = ref[:rank]
+        kept, _ = merged(
             maps_ref,
             kind,
             side,
-            mine_ref[kind, :rank],
-            mine_ref[kind, rank:],
-            other_ref[kind, :rank],
-            other_ref[kind, rank:],
+            mine_ref[:rank],
+            mine_ref[rank:],
+            other_ref[:rank],
+            other_ref[rank:],
             rank,
         )
-        if last:
-            out_ref[len(refs), kind] = kept.astype(BF)
-        else:
-            out_ref[kind, :rank] = kept.astype(BF)
-            out_ref[kind, rank:] = tests.astype(BF)
+        out_ref[levels - 1, kind] = kept.astype(BF)
 
 
 def output_body(vectors, mine_ref, other_ref, out_ref):
@@ -403,29 +402,29 @@
     maps = [first_maps, *more_maps]
     new, node = call(
         functools.partial(joined_body, 1),
-        [shape((2, 2 * rank, half)), shape((2, rank, half))],
-        (
-            maps[1],
-            fwd,
-            swapped(fwd, "sub", 1),
-            adj,
-            swapped(adj, "sub", 1),
-            swapped(given, "sub", 1),
-            given,
-        ),
-    )
-    nodes, x = [node], new
-    steps = [("sub", bit) for bit in range(2, sub_bits)]
+        [shape((2 * rank, half)), shape((rank, half))],
+        (maps[1], adj, swapped(adj, "sub", 1), swapped(given, "sub", 1), given),
+    )
+    chains = [[fwd], [node, new]]
+    steps = [("sub", bit) for bit in range(1, sub_bits)]
     steps += [("grp", bit) for bit in range(levels - sub_bits)]
-    for level, (axis, bit) in enumerate(steps, 2):
-        last = level == levels - 1
-        new = call(
-            functools.partial(level_body, axis, bit, last),
-            shape((levels, 2, rank, half) if last else (2, 2 * rank, half)),
-            (maps[level], x, swapped(x, axis, bit), *(nodes if last else ())),
-        )
-        nodes.append(x)
-        x = new
+    for level, (axis, bit) in enumerate(steps[:-1], 1):
+        for kind, chain in enumerate(chains):
+            if len(chain) == level:
+                chain.append(
+                    call(
+                        functools.partial(level_body, kind, axis, bit),
+                        shape((2 * rank, half)),
+                        (maps[level], chain[-1], swapped(chain[-1], axis, bit)),
+                    )
+                )
+    axis, bit = steps[-1]
+    ends = [swapped(chain[-1], axis, bit) for chain in chains]
+    x = call(
+        functools.partial(last_body, axis, bit, levels),
+        shape((levels, 2, rank, half)),
+        (maps[-1], *chains[0], ends[0], *chains[1], ends[1]),
+    )
     return call(
         functools.partial(output_body, vectors),
         shape((1, levels, 2, rank, samples)),

time: 55.8 us -> 54 us (0.968)
  waiting for transfers between devices: 15.5 us -> 8.84 us
  starting transfers between devices: 23.8 us -> 28.2 us
    ppermute x11 -> x14, waiting for transfers between devices: 14.3 us -> 7.69 us  [swapped(): lax.ppermute(x, axis, [(i, i ^ 1 << bit) for i in range(lax.axis_size(axi...]
    ppermute x11 -> x14, starting transfers between devices: 14.4 us -> 18.7 us  [swapped(): lax.ppermute(x, axis, [(i, i ^ 1 << bit) for i in range(lax.axis_size(axi...]
    pallas_call x14 -> x17, Pallas kernels: 13.1 us -> 13.5 us  [call(): pl.pallas_call(body, out_shape=out_shape, in_specs=[SPACES[c] for c in sp...]
  transfers between devices with their start and end apart: 14 -> 17, of which waited for: 7 -> 6; matrix products, arithmetic and copies ran while one was open for 0% -> 0% of each run, Pallas kernels for 15% -> 17%
where the time goes in v9:
time: 54 us; the launch traced here: 53.5 us
  starting transfers between devices  28.2 us (52%)
  Pallas kernels  13.5 us (25%)
  waiting for transfers between devices  8.84 us (16%)
  local copies, waits for them, and re-layouts  2.81 us (5%)
    ppermute x14, starting transfers between devices, swapped(): lax.ppermute(x, axis, [(i, i ^ 1 << bit) for i in range(lax.axis_size(axi...  18.7 us
    pallas_call x17, Pallas kernels, call(): pl.pallas_call(body, out_shape=out_shape, in_specs=[SPACES[c] for c in sp...  13.5 us
    all_to_all x1, starting transfers between devices, local(): lax.all_to_all(blocks, 'sub', split_axis=0, concat_axis=0, tiled=True, ax...  7.72 us
    ppermute x14, waiting for transfers between devices, swapped(): lax.ppermute(x, axis, [(i, i ^ 1 << bit) for i in range(lax.axis_size(axi...  7.69 us
    unnamed x18, local copies, waits for them, and re-layouts  2.81 us
    ppermute x1, starting transfers between devices, local(): packed_outer = lax.ppermute(packed, 'sub', outward)  1.65 us
    ppermute x1, waiting for transfers between devices, local(): far_rims = lax.ppermute(far_rims, 'sub', route)  1.15 us
  transfers between devices with their start and end apart: 17, of which 6 were waited for; matrix products, arithmetic and copies ran while one was open for 0% of the time, Pallas kernels for 17%

profile of v9, /device:TPU:0, one launch (start us, length us, event | category | flops | bytes accessed | tf_op | source)
XLA Modules:
  0.0 53.5 jit_solution(4435575530554474568)
XLA Ops:
  0.0 2.8 %shard_map.85 = (bf16[8,16,1536]{2,1,0:T(8,128)(2,1)}, bf16[784,256]{1,0:T(8,128)(2,1)}) custom-call(bf16[16,12288]{1,0:T(8,128)(2,1)} %tests_hbm.1, bf16[768,256]{1,0:T(8,128)(2,1)} %omega_ref.1, s32[1,2,768]{2,1,0:T(2,128)} %perms_ref.7, s32[1,5,2,192]{3,2,1,0:T(2,128)} %nodes_ref.1), custom_call_target="tpu_custom_call" | custom-call | flops 1000 | bytes 1000 | tf_op jit(solution)/shard_map/pallas_call | solution.py:39
  3.3 1.6 %collective-permute-start.1 = (bf16[784,256]{1,0:T(8,128)(2,1)}, bf16[784,256]{1,0:T(8,128)(2,1)S(1)}, u32[]{:S(2)}, u32[]{:S(2)}) collective-permute-start(bf16[784,256]{1,0:T(8,128)(2,1)} %get-tuple-element.26), channel_id=1, source_target_pairs={{1,2},{3,4},{5,6},{7,8},{9,10},{11,12},{13,14},{2,1},{4,3},{6,5},{... | collective-permute-start | bytes 1204232 | tf_op jit(solution)/shard_map/ppermute | solution.py:349
  5.0 7.7 %all-to-all-start = ((bf16[8,16,1536]{2,1,0:T(8,128)(2,1)}), bf16[8,16,1536]{2,1,0:T(8,128)(2,1)S(1)}, u32[]{:S(2)}, u32[]{:S(2)}) async-start(bf16[8,16,1536]{2,1,0:T(8,128)(2,1)} %get-tuple-element.34), calls=%async_computation | async-start | bytes 786432 | tf_op jit(solution)/shard_map/all_to_all | solution.py:352
  12.7 1.0 %copy-done.1 = bf16[1,5,4,96,96]{4,3,2,1,0:T(8,128)(2,1)S(1)} copy-done((bf16[1,5,4,96,96]{4,3,2,1,0:T(8,128)(2,1)S(1)}, bf16[1,5,4,96,96]{4,3,2,1,0:T(8,128)(2,1)}, u32[]{:S(2)}) %copy-start.1) | copy-done | bytes 368664
  15.0 1.1 %copy-done.6 = bf16[6,12,128,128]{3,2,1,0:T(8,128)(2,1)S(1)} copy-done((bf16[6,12,128,128]{3,2,1,0:T(8,128)(2,1)S(1)}, bf16[6,12,128,128]{3,2,1,0:T(8,128)(2,1)}, u32[]{:S(2)}) %copy-start.6) | copy-done | bytes 2359320
  16.1 3.2 %shard_map.84 = (bf16[192,768]{1,0:T(8,128)(2,1)S(1)}, bf16[96,2304]{1,0:T(8,128)(2,1)S(1)}, bf16[96,768]{1,0:T(8,128)(2,1)S(1)}, bf16[768,2304]{1,0:T(8,128)(2,1)S(1)}) custom-call(s32[6,12]{1,0:T(8,128)S(1)} %copy-done.8, bf16[6,12,128,128]{3,2,1,0:T(8,128)(2,1)S(1)} %copy-done.6, s32[1,2,768]{2,1,0:T(2,128)S(1)} %copy-done.5, ...), custom_call_target="tpu_custom_call" | custom-call | flops 1073741824 | bytes 1000 | tf_op jit(solution)/shard_map/pallas_call | solution.py:39
  19.4 1.3 %shard_map.86 = (bf16[208,768]{1,0:T(8,128)(2,1)S(1)}, bf16[192,128]{1,0:T(8,128)(2,1)S(1)}, bf16[192,128]{1,0:T(8,128)(2,1)S(1)}) custom-call(bf16[768,2304]{1,0:T(8,128)(2,1)S(1)} %get-tuple-element.23.dense_ref, bf16[96,2304]{1,0:T(8,128)(2,1)S(1)} %get-tuple-element.24.near_ref, bf16[96,768]{1,0:T(8,128)(2,1)S(1)} %get-tuple-element.25.tests_ref, ...), custom_call_target="tpu_custom_call" | custom-call | flops 1000 | bytes 1000 | tf_op jit(solution)/shard_map/pallas_call | solution.py:39
  20.7 1.3 %collective-permute-start.8 = (bf16[208,768]{1,0:T(8,128)(2,1)S(1)}, bf16[208,768]{1,0:T(8,128)(2,1)S(1)}, u32[]{:S(2)}, u32[]{:S(2)}) collective-permute-start(bf16[208,768]{1,0:T(8,128)(2,1)S(1)} %get-tuple-element.33.beside_ref), channel_id=1, source_target_pairs={{0,1},{1,0},{2,3},{3,2},{4,5},{5,4},{6,7},{7,6},{8,9},{9,8},{10,11... | collective-permute-start | bytes 958472 | tf_op jit(solution)/shard_map/ppermute | solution.py:320
  22.5 1.2 %collective-permute-done.2.other_ref = bf16[192,128]{1,0:T(8,128)(2,1)S(1)} collective-permute-done((bf16[192,128]{1,0:T(8,128)(2,1)S(1)}, bf16[192,128]{1,0:T(8,128)(2,1)S(1)}, u32[]{:S(2)}, u32[]{:S(2)}) %collective-permute-start.2) | collective-permute-done | bytes 49184 | tf_op jit(solution)/shard_map/ppermute | solution.py:320
  23.9 2.7 %collective-permute-start.3 = (bf16[192,128]{1,0:T(8,128)(2,1)S(1)}, bf16[192,128]{1,0:T(8,128)(2,1)S(1)}, u32[]{:S(2)}, u32[]{:S(2)}) collective-permute-start(bf16[192,128]{1,0:T(8,128)(2,1)S(1)} %shard_map.87.mine_ref.refs_0_), channel_id=1, source_target_pairs={{0,2},{1,3},{2,0},{3,1},{4,6},{5,7},{6,4},{7,5},{8,10},{9,11},{10,... | collective-permute-start | bytes 147464 | tf_op jit(solution)/shard_map/ppermute | solution.py:320
  27.6 2.0 %collective-permute-start.9 = (bf16[192,128]{1,0:T(8,128)(2,1)S(1)}, bf16[192,128]{1,0:T(8,128)(2,1)S(1)}, u32[]{:S(2)}, u32[]{:S(2)}) collective-permute-start(bf16[192,128]{1,0:T(8,128)(2,1)S(1)} %shard_map.92.mine_ref), channel_id=1, source_target_pairs={{0,2},{1,3},{2,0},{3,1},{4,6},{5,7},{6,4},{7,5},{8,10},{9,11},{10,... | collective-permute-start | bytes 147464 | tf_op jit(solution)/shard_map/ppermute | solution.py:320
  29.6 1.1 %collective-permute-done.10.far_ref = bf16[96,128]{1,0:T(8,128)(2,1)S(1)} collective-permute-done((bf16[96,128]{1,0:T(8,128)(2,1)S(1)}, bf16[96,128]{1,0:T(8,128)(2,1)S(1)}, u32[]{:S(2)}, u32[]{:S(2)}) %collective-permute-start.10) | collective-permute-done | bytes 24608 | tf_op jit(solution)/shard_map/ppermute | solution.py:390
  31.3 1.9 %shard_map.82 = (bf16[2,2,288,96]{3,2,1,0:T(8,128)(2,1)S(1)}, bf16[2,2,288,96]{3,2,1,0:T(8,128)(2,1)S(1)}, bf16[2,2,288,96]{3,2,1,0:T(8,128)(2,1)S(1)}, bf16[2,2,288,96]{3,2,1,0:T(8,128)(2,1)S(1)}) custom-call(bf16[1,5,4,96,96]{4,3,2,1,0:T(8,128)(2,1)S(1)} %copy-done.2, s32[1,5,2,192]{3,2,1,0:T(2,128)S(1)} %copy-done.4), custom_call_target="tpu_custom_call" | custom-call | flops 1000 | bytes 1000 | tf_op jit(solution)/shard_map/pallas_call | solution.py:39
  33.5 1.9 %collective-permute-start.4 = (bf16[192,128]{1,0:T(8,128)(2,1)S(1)}, bf16[192,128]{1,0:T(8,128)(2,1)S(1)}, u32[]{:S(2)}, u32[]{:S(2)}) collective-permute-start(bf16[192,128]{1,0:T(8,128)(2,1)S(1)} %shard_map.88.mine_ref.refs_1_), channel_id=1, source_target_pairs={{0,4},{1,5},{2,6},{3,7},{4,0},{5,1},{6,2},{7,3},{8,12},{9,13},{10,... | collective-permute-start | bytes 147464 | tf_op jit(solution)/shard_map/ppermute | solution.py:320
  35.5 1.1 %collective-permute-start.12 = (bf16[192,128]{1,0:T(8,128)(2,1)S(1)}, bf16[192,128]{1,0:T(8,128)(2,1)S(1)}, u32[]{:S(2)}, u32[]{:S(2)}) collective-permute-start(bf16[192,128]{1,0:T(8,128)(2,1)S(1)} %get-tuple-element.38.mine_ref.refs_6_), channel_id=1, source_target_pairs={{0,4},{1,5},{2,6},{3,7},{4,0},{5,1},{6,2},{7,3},{8,12},{9,13},{10,... | collective-permute-start | bytes 147464 | tf_op jit(solution)/shard_map/ppermute | solution.py:320
  36.6 1.0 %collective-permute-done.4.other_ref = bf16[192,128]{1,0:T(8,128)(2,1)S(1)} collective-permute-done((bf16[192,128]{1,0:T(8,128)(2,1)S(1)}, bf16[192,128]{1,0:T(8,128)(2,1)S(1)}, u32[]{:S(2)}, u32[]{:S(2)}) %collective-permute-start.4) | collective-permute-done | bytes 49184 | tf_op jit(solution)/shard_map/ppermute | solution.py:320
  37.8 3.2 %collective-permute-start.5 = (bf16[192,128]{1,0:T(8,128)(2,1)S(1)}, bf16[192,128]{1,0:T(8,128)(2,1)S(1)}, u32[]{:S(2)}, u32[]{:S(2)}) collective-permute-start(bf16[192,128]{1,0:T(8,128)(2,1)S(1)} %shard_map.89.mine_ref.refs_2_), channel_id=1, source_target_pairs={{0,8},{1,9},{2,10},{3,11},{4,12},{5,13},{6,14},{7,15},{8,0},{9,1},... | collective-permute-start | bytes 147464 | tf_op jit(solution)/shard_map/ppermute | solution.py:320
  41.2 1.9 %collective-permute-start.13 = (bf16[192,128]{1,0:T(8,128)(2,1)S(1)}, bf16[192,128]{1,0:T(8,128)(2,1)S(1)}, u32[]{:S(2)}, u32[]{:S(2)}) collective-permute-start(bf16[192,128]{1,0:T(8,128)(2,1)S(1)} %shard_map.95.mine_ref.refs_7_), channel_id=1, source_target_pairs={{0,8},{1,9},{2,10},{3,11},{4,12},{5,13},{6,14},{7,15},{8,0},{9,1},... | collective-permute-start | bytes 147464 | tf_op jit(solution)/shard_map/ppermute | solution.py:320
  43.3 1.6 %collective-permute-start.6 = (bf16[192,128]{1,0:T(8,128)(2,1)S(1)}, bf16[192,128]{1,0:T(8,128)(2,1)S(1)}, u32[]{:S(2)}, u32[]{:S(2)}) collective-permute-start(bf16[192,128]{1,0:T(8,128)(2,1)S(1)} %shard_map.90.refs_3_), channel_id=1, source_target_pairs={{0,16},{16,0},{1,17},{17,1},{2,18},{18,2},{3,19},{19,3},{4,20},{20... | collective-permute-start | bytes 147464 | tf_op jit(solution)/shard_map/ppermute | solution.py:320
  44.9 1.4 %collective-permute-done.13.other_ref = bf16[192,128]{1,0:T(8,128)(2,1)S(1)} collective-permute-done((bf16[192,128]{1,0:T(8,128)(2,1)S(1)}, bf16[192,128]{1,0:T(8,128)(2,1)S(1)}, u32[]{:S(2)}, u32[]{:S(2)}) %collective-permute-start.13) | collective-permute-done | bytes 49184 | tf_op jit(solution)/shard_map/ppermute | solution.py:320
  46.5 1.6 %collective-permute-start.14 = (bf16[192,128]{1,0:T(8,128)(2,1)S(1)}, bf16[192,128]{1,0:T(8,128)(2,1)S(1)}, u32[]{:S(2)}, u32[]{:S(2)}) collective-permute-start(bf16[192,128]{1,0:T(8,128)(2,1)S(1)} %shard_map.96.refs_8_), channel_id=1, source_target_pairs={{0,16},{16,0},{1,17},{17,1},{2,18},{18,2},{3,19},{19,3},{4,20},{20... | collective-permute-start | bytes 147464 | tf_op jit(solution)/shard_map/ppermute | solution.py:320
  48.1 2.6 %collective-permute-done.14.refs_9_ = bf16[192,128]{1,0:T(8,128)(2,1)S(1)} collective-permute-done((bf16[192,128]{1,0:T(8,128)(2,1)S(1)}, bf16[192,128]{1,0:T(8,128)(2,1)S(1)}, u32[]{:S(2)}, u32[]{:S(2)}) %collective-permute-start.14) | collective-permute-done | bytes 49184 | tf_op jit(solution)/shard_map/ppermute | solution.py:320
  51.0 1.5 %collective-permute-done.15.other_ref = bf16[5,2,96,128]{3,2,1,0:T(8,128)(2,1)S(1)} collective-permute-done((bf16[5,2,96,128]{3,2,1,0:T(8,128)(2,1)S(1)}, bf16[5,2,96,128]{3,2,1,0:T(8,128)(2,1)S(1)}, u32[]{:S(2)}, u32[]{:S(2)}) %collective-permute-start.15) | collective-permute-done | bytes 245792 | tf_op jit(solution)/shard_map/ppermute | solution.py:320
  52.5 1.1 %shard_map.98 = bf16[1,5,2,96,256]{4,3,2,1,0:T(8,128)(2,1)} custom-call(bf16[5,2,96,128]{3,2,1,0:T(8,128)(2,1)S(1)} %shard_map.97.mine_ref, bf16[5,2,96,128]{3,2,1,0:T(8,128)(2,1)S(1)} %collective-permute-done.15.other_ref), custom_call_target="tpu_custom_call" | custom-call | flops 1000 | bytes 1000 | tf_op jit(solution)/shard_map/pallas_call | solution.py:39
  (45 shorter events, 5.4 us)
Async XLA Ops:
  0.0 15.0 %copy-start.5 = (s32[1,2,768]{2,1,0:T(2,128)S(1)}, s32[1,2,768]{2,1,0:T(2,128)}, u32[]{:S(2)}) copy-start(s32[1,2,768]{2,1,0:T(2,128)} %perms_ref.7) | copy-start | bytes 18436
  0.0 15.0 %copy-start.7 = (bf16[1,2,672,96]{2,3,1,0:T(8,128)(2,1)S(1)}, bf16[1,2,672,96]{2,3,1,0:T(8,128)(2,1)}, u32[]{:S(2)}) copy-start(bf16[1,2,672,96]{2,3,1,0:T(8,128)(2,1)} %param.13) | copy-start | bytes 774148
  0.0 15.0 %copy-start.8 = (s32[6,12]{1,0:T(8,128)S(1)}, s32[6,12]{1,0:T(8,128)}, u32[]{:S(2)}) copy-start(s32[6,12]{1,0:T(8,128)} %cols_ref.1) | copy-start | bytes 868
  2.8 16.5 %collective-permute-start = (bf16[784,256]{1,0:T(8,128)(2,1)}, bf16[784,256]{1,0:T(8,128)(2,1)S(1)}, u32[]{:S(2)}, u32[]{:S(2)}) collective-permute-start(bf16[784,256]{1,0:T(8,128)(2,1)} %get-tuple-element.26), channel_id=1, source_target_pairs={{0,1},{1,0},{2,3},{3,2},{4,5},{5,4},{6,7},{7,6},{8,9},{9,8},{10,11... | collective-permute-start | bytes 1204232 | tf_op jit(solution)/shard_map/ppermute | solution.py:320
  3.3 16.0 %collective-permute-start.1 = (bf16[784,256]{1,0:T(8,128)(2,1)}, bf16[784,256]{1,0:T(8,128)(2,1)S(1)}, u32[]{:S(2)}, u32[]{:S(2)}) collective-permute-start(bf16[784,256]{1,0:T(8,128)(2,1)} %get-tuple-element.26), channel_id=1, source_target_pairs={{1,2},{3,4},{5,6},{7,8},{9,10},{11,12},{13,14},{2,1},{4,3},{6,5},{... | collective-permute-start | bytes 1204232 | tf_op jit(solution)/shard_map/ppermute | solution.py:349
  5.0 21.6 %all-to-all-start = ((bf16[8,16,1536]{2,1,0:T(8,128)(2,1)}), bf16[8,16,1536]{2,1,0:T(8,128)(2,1)S(1)}, u32[]{:S(2)}, u32[]{:S(2)}) async-start(bf16[8,16,1536]{2,1,0:T(8,128)(2,1)} %get-tuple-element.34), calls=%async_computation | async-start | bytes 786432 | tf_op jit(solution)/shard_map/all_to_all | solution.py:352
  14.4 1.7 %copy-start.6 = (bf16[6,12,128,128]{3,2,1,0:T(8,128)(2,1)S(1)}, bf16[6,12,128,128]{3,2,1,0:T(8,128)(2,1)}, u32[]{:S(2)}) copy-start(bf16[6,12,128,128]{3,2,1,0:T(8,128)(2,1)} %tiles_ref.1) | copy-start | bytes 7077892
  14.4 4.9 %copy-start = (bf16[768,256]{1,0:T(8,128)(2,1)S(1)}, bf16[768,256]{1,0:T(8,128)(2,1)}, u32[]{:S(2)}) copy-start(bf16[768,256]{1,0:T(8,128)(2,1)} %omega_ref.1) | copy-start | bytes 1179652
  20.7 6.0 %collective-permute-start.8 = (bf16[208,768]{1,0:T(8,128)(2,1)S(1)}, bf16[208,768]{1,0:T(8,128)(2,1)S(1)}, u32[]{:S(2)}, u32[]{:S(2)}) collective-permute-start(bf16[208,768]{1,0:T(8,128)(2,1)S(1)} %get-tuple-element.33.beside_ref), channel_id=1, source_target_pairs={{0,1},{1,0},{2,3},{3,2},{4,5},{5,4},{6,7},{7,6},{8,9},{9,8},{10,11... | collective-permute-start | bytes 958472 | tf_op jit(solution)/shard_map/ppermute | solution.py:320
  22.0 5.0 %collective-permute-start.7 = (bf16[192,768]{1,0:T(8,128)(2,1)S(1)}, bf16[192,768]{1,0:T(8,128)(2,1)S(1)}, u32[]{:S(2)}, u32[]{:S(2)}) collective-permute-start(bf16[192,768]{1,0:T(8,128)(2,1)S(1)} %get-tuple-element.32.keep_ref), channel_id=1, source_target_pairs={{0,1},{1,0},{2,3},{3,2},{4,5},{5,4},{6,7},{7,6},{8,9},{9,8},{10,11... | collective-permute-start | bytes 884744 | tf_op jit(solution)/shard_map/ppermute | solution.py:320
  22.1 1.7 %collective-permute-start.2 = (bf16[192,128]{1,0:T(8,128)(2,1)S(1)}, bf16[192,128]{1,0:T(8,128)(2,1)S(1)}, u32[]{:S(2)}, u32[]{:S(2)}) collective-permute-start(bf16[192,128]{1,0:T(8,128)(2,1)S(1)} %get-tuple-element.28), channel_id=1, source_target_pairs={{0,1},{1,0},{2,3},{3,2},{4,5},{5,4},{6,7},{7,6},{8,9},{9,8},{10,11... | collective-permute-start | bytes 147464 | tf_op jit(solution)/shard_map/ppermute | solution.py:320
  23.9 9.4 %collective-permute-start.3 = (bf16[192,128]{1,0:T(8,128)(2,1)S(1)}, bf16[192,128]{1,0:T(8,128)(2,1)S(1)}, u32[]{:S(2)}, u32[]{:S(2)}) collective-permute-start(bf16[192,128]{1,0:T(8,128)(2,1)S(1)} %shard_map.87.mine_ref.refs_0_), channel_id=1, source_target_pairs={{0,2},{1,3},{2,0},{3,1},{4,6},{5,7},{6,4},{7,5},{8,10},{9,11},{10,... | collective-permute-start | bytes 147464 | tf_op jit(solution)/shard_map/ppermute | solution.py:320
  26.9 3.9 %collective-permute-start.10 = (bf16[96,128]{1,0:T(8,128)(2,1)S(1)}, bf16[96,128]{1,0:T(8,128)(2,1)S(1)}, u32[]{:S(2)}, u32[]{:S(2)}) collective-permute-start(bf16[96,128]{1,0:T(8,128)(2,1)S(1)} %get-tuple-element.36), channel_id=1, source_target_pairs={{2,6},{3,7},{6,10},{7,11},{10,14},{11,15},{14,12},{15,13},{12,8},{... | collective-permute-start | bytes 73736 | tf_op jit(solution)/shard_map/ppermute | solution.py:390
  27.0 4.3 %copy-start.2 = (bf16[1,5,4,96,96]{4,3,2,1,0:T(8,128)(2,1)S(1)}, bf16[1,5,4,96,96]{4,3,2,1,0:T(8,128)(2,1)}, u32[]{:S(2)}) copy-start(bf16[1,5,4,96,96]{4,3,2,1,0:T(8,128)(2,1)} %maps_ref.3) | copy-start | bytes 1105924
  27.0 4.3 %copy-start.4 = (s32[1,5,2,192]{3,2,1,0:T(2,128)S(1)}, s32[1,5,2,192]{3,2,1,0:T(2,128)}, u32[]{:S(2)}) copy-start(s32[1,5,2,192]{3,2,1,0:T(2,128)} %nodes_ref.1) | copy-start | bytes 23044
  27.6 7.7 %collective-permute-start.9 = (bf16[192,128]{1,0:T(8,128)(2,1)S(1)}, bf16[192,128]{1,0:T(8,128)(2,1)S(1)}, u32[]{:S(2)}, u32[]{:S(2)}) collective-permute-start(bf16[192,128]{1,0:T(8,128)(2,1)S(1)} %shard_map.92.mine_ref), channel_id=1, source_target_pairs={{0,2},{1,3},{2,0},{3,1},{4,6},{5,7},{6,4},{7,5},{8,10},{9,11},{10,... | collective-permute-start | bytes 147464 | tf_op jit(solution)/shard_map/ppermute | solution.py:320
  31.1 4.3 %collective-permute-start.11 = (bf16[96,128]{1,0:T(8,128)(2,1)S(1)}, bf16[96,128]{1,0:T(8,128)(2,1)S(1)}, u32[]{:S(2)}, u32[]{:S(2)}) collective-permute-start(bf16[96,128]{1,0:T(8,128)(2,1)S(1)} %shard_map.93.given_ref), channel_id=1, source_target_pairs={{0,2},{1,3},{2,0},{3,1},{4,6},{5,7},{6,4},{7,5},{8,10},{9,11},{10,... | collective-permute-start | bytes 73736 | tf_op jit(solution)/shard_map/ppermute | solution.py:320
  33.5 4.2 %collective-permute-start.4 = (bf16[192,128]{1,0:T(8,128)(2,1)S(1)}, bf16[192,128]{1,0:T(8,128)(2,1)S(1)}, u32[]{:S(2)}, u32[]{:S(2)}) collective-permute-start(bf16[192,128]{1,0:T(8,128)(2,1)S(1)} %shard_map.88.mine_ref.refs_1_), channel_id=1, source_target_pairs={{0,4},{1,5},{2,6},{3,7},{4,0},{5,1},{6,2},{7,3},{8,12},{9,13},{10,... | collective-permute-start | bytes 147464 | tf_op jit(solution)/shard_map/ppermute | solution.py:320
  35.5 5.5 %collective-permute-start.12 = (bf16[192,128]{1,0:T(8,128)(2,1)S(1)}, bf16[192,128]{1,0:T(8,128)(2,1)S(1)}, u32[]{:S(2)}, u32[]{:S(2)}) collective-permute-start(bf16[192,128]{1,0:T(8,128)(2,1)S(1)} %get-tuple-element.38.mine_ref.refs_6_), channel_id=1, source_target_pairs={{0,4},{1,5},{2,6},{3,7},{4,0},{5,1},{6,2},{7,3},{8,12},{9,13},{10,... | collective-permute-start | bytes 147464 | tf_op jit(solution)/shard_map/ppermute | solution.py:320
  37.8 5.3 %collective-permute-start.5 = (bf16[192,128]{1,0:T(8,128)(2,1)S(1)}, bf16[192,128]{1,0:T(8,128)(2,1)S(1)}, u32[]{:S(2)}, u32[]{:S(2)}) collective-permute-start(bf16[192,128]{1,0:T(8,128)(2,1)S(1)} %shard_map.89.mine_ref.refs_2_), channel_id=1, source_target_pairs={{0,8},{1,9},{2,10},{3,11},{4,12},{5,13},{6,14},{7,15},{8,0},{9,1},... | collective-permute-start | bytes 147464 | tf_op jit(solution)/shard_map/ppermute | solution.py:320
  41.2 5.1 %collective-permute-start.13 = (bf16[192,128]{1,0:T(8,128)(2,1)S(1)}, bf16[192,128]{1,0:T(8,128)(2,1)S(1)}, u32[]{:S(2)}, u32[]{:S(2)}) collective-permute-start(bf16[192,128]{1,0:T(8,128)(2,1)S(1)} %shard_map.95.mine_ref.refs_7_), channel_id=1, source_target_pairs={{0,8},{1,9},{2,10},{3,11},{4,12},{5,13},{6,14},{7,15},{8,0},{9,1},... | collective-permute-start | bytes 147464 | tf_op jit(solution)/shard_map/ppermute | solution.py:320
  43.3 4.7 %collective-permute-start.6 = (bf16[192,128]{1,0:T(8,128)(2,1)S(1)}, bf16[192,128]{1,0:T(8,128)(2,1)S(1)}, u32[]{:S(2)}, u32[]{:S(2)}) collective-permute-start(bf16[192,128]{1,0:T(8,128)(2,1)S(1)} %shard_map.90.refs_3_), channel_id=1, source_target_pairs={{0,16},{16,0},{1,17},{17,1},{2,18},{18,2},{3,19},{19,3},{4,20},{20... | collective-permute-start | bytes 147464 | tf_op jit(solution)/shard_map/ppermute | solution.py:320
  46.5 4.2 %collective-permute-start.14 = (bf16[192,128]{1,0:T(8,128)(2,1)S(1)}, bf16[192,128]{1,0:T(8,128)(2,1)S(1)}, u32[]{:S(2)}, u32[]{:S(2)}) collective-permute-start(bf16[192,128]{1,0:T(8,128)(2,1)S(1)} %shard_map.96.refs_8_), channel_id=1, source_target_pairs={{0,16},{16,0},{1,17},{17,1},{2,18},{18,2},{3,19},{19,3},{4,20},{20... | collective-permute-start | bytes 147464 | tf_op jit(solution)/shard_map/ppermute | solution.py:320
  50.9 1.6 %collective-permute-start.15 = (bf16[5,2,96,128]{3,2,1,0:T(8,128)(2,1)S(1)}, bf16[5,2,96,128]{3,2,1,0:T(8,128)(2,1)S(1)}, u32[]{:S(2)}, u32[]{:S(2)}) collective-permute-start(bf16[5,2,96,128]{3,2,1,0:T(8,128)(2,1)S(1)} %shard_map.97.mine_ref), channel_id=1, source_target_pairs={{0,1},{1,0},{2,3},{3,2},{4,5},{5,4},{6,7},{7,6},{8,9},{9,8},{10,11... | collective-permute-start | bytes 737288 | tf_op jit(solution)/shard_map/ppermute | solution.py:320
  (2 other events, 1.7 us)

commit v10 on v9

--- a/solution.py
+++ b/solution.py
@@ -158,10 +158,10 @@
         out_ref[rank:] = mm(tests_ref[...], own).astype(BF)
 
 
-def maps_body(first, maps_ref, perms_ref, *out_refs):
+def maps_body(maps_ref, perms_ref, *out_refs):
     rank = maps_ref.shape[-1]
     unit = eye(rank)
-    for level, out_ref in enumerate(out_refs, first):
+    for level, out_ref in enumerate(out_refs):
         row_interp, col_interp, low_high, high_low = (maps_ref[0, level, i] for i in range(4))
         row_hot = one_hot(perms_ref[0, level, 0:1, :], 2 * rank)
         col_hot = one_hot(perms_ref[0, level, 1:2, :], 2 * rank)
@@ -192,7 +192,8 @@
     return kept + wide[:rank], wide[rank:]
 
 
-def node_body(maps_ref, mine_ref, other_ref, out_ref):
+def node_body(maps_ref, mine_ref, other_ref, after_ref, out_ref):
+    del after_ref
     rank = mine_ref.shape[0] // 2
     core = lax.axis_index("sub") & 1
     kept, tests = merged(
@@ -354,9 +355,9 @@
     ).reshape(half, 2 * rows)
 
     tables = shape((2, 2, 3 * rank, rank))
-    [first_maps] = call(
-        functools.partial(maps_body, 0),
-        [tables],
+    maps = call(
+        maps_body,
+        [tables] * levels,
         (node_maps, node_perms),
         flops=1 << 30,
     )
@@ -368,7 +369,7 @@
             shape((rank, rows)),
             shape((rows, 3 * rows)),
         ],
-        (tile_cols, near_tiles, leaf_perms, jnp.swapaxes(leaf_interp, 2, 3), first_maps),
+        (tile_cols, near_tiles, leaf_perms, jnp.swapaxes(leaf_interp, 2, 3), maps[0]),
         specs="svvva",
         flops=1 << 30,
     )
@@ -379,27 +380,27 @@
         (dense, near, tests, omega, packed_inner, packed_outer),
     )
     beside_other = swapped(beside, "sub", 0)
-    fwd = call(
-        node_body, shape((2 * rank, half)), (first_maps, fwd_mine, swapped(fwd_send, "sub", 0))
-    )
+    fwd_other = swapped(fwd_send, "sub", 0)
     near_rims, far_rims = call(
         edge_body, [shape((rank, half))] * 2, (beside, beside_other, panel)
     )
     ring = list(range(1, chips, 2)) + list(range(chips - 2, -1, -2))
     route = [(2 * a + c, 2 * b + c) for a, b in zip(ring, ring[1:] + ring[:1]) for c in range(2)]
     far_rims = lax.ppermute(far_rims, "sub", route)
+    fwd = call(
+        node_body,
+        shape((2 * rank, half)),
+        (maps[0], fwd_mine, fwd_other, near_rims),
+        specs="vvva",
+    )
     adj = call(
         adjoint_body,
         shape((2 * rank, half)),
-        (first_maps, keep, keep_other, beside, beside_other, panel, near_rims),
+        (maps[0], keep, keep_other, beside, beside_other, panel, near_rims),
         specs="vvvvvva",
         flops=4 << 30,
     )
     given = call(rim_body, shape((rank, half)), (beside, beside_other, near_rims, far_rims))
-    more_maps = call(
-        functools.partial(maps_body, 1), [tables] * (levels - 1), (node_maps, node_perms)
-    )
-    maps = [first_maps, *more_maps]
     new, node = call(
         functools.partial(joined_body, 1),
         [shape((2 * rank, half)), shape((rank, half))],

time: 54 us -> 52.8 us (0.978)
  starting transfers between devices: 28.2 us -> 25 us
  waiting for transfers between devices: 8.84 us -> 10.8 us
  local copies, waits for them, and re-layouts: 2.81 us -> 1.75 us
  Pallas kernels: 13.5 us -> 14.5 us
    all_to_all x1, starting transfers between devices: 7.72 us -> 4.88 us  [local(): lax.all_to_all(blocks, 'sub', split_axis=0, concat_axis=0, tiled=True, ax...]
    all_to_all x1, waiting for transfers between devices: 0.01 us -> 2.29 us  [local(): lax.all_to_all(blocks, 'sub', split_axis=0, concat_axis=0, tiled=True, ax...]
    ppermute x14, starting transfers between devices: 18.7 us -> 17 us  [swapped(): lax.ppermute(x, axis, [(i, i ^ 1 << bit) for i in range(lax.axis_size(axi...]
    ppermute x1, starting transfers between devices: 0.09 us -> 1.52 us  [local(): far_rims = lax.ppermute(far_rims, 'sub', route)]
    ppermute x1, waiting for transfers between devices: 1.15 us -> 0.01 us  [local(): far_rims = lax.ppermute(far_rims, 'sub', route)]
    pallas_call x17 -> x16, Pallas kernels: 13.5 us -> 14.5 us  [call(): pl.pallas_call(body, out_shape=out_shape, in_specs=[SPACES[c] for c in sp...]
    unnamed x18 -> x14, local copies, waits for them, and re-layouts: 2.81 us -> 1.75 us
    ppermute x14, waiting for transfers between devices: 7.69 us -> 8.54 us  [swapped(): lax.ppermute(x, axis, [(i, i ^ 1 << bit) for i in range(lax.axis_size(axi...]
  transfers between devices with their start and end apart: 17 -> 17, of which waited for: 6 -> 8; matrix products, arithmetic and copies ran while one was open for 0% -> 0% of each run, Pallas kernels for 17% -> 20%
where the time goes in v10:
time: 52.8 us; the launch traced here: 52.3 us
  starting transfers between devices  25 us (47%)
  Pallas kernels  14.5 us (27%)
  waiting for transfers between devices  10.8 us (20%)
  local copies, waits for them, and re-layouts  1.75 us (3%)
    ppermute x14, starting transfers between devices, swapped(): lax.ppermute(x, axis, [(i, i ^ 1 << bit) for i in range(lax.axis_size(axi...  17 us
    pallas_call x16, Pallas kernels, call(): pl.pallas_call(body, out_shape=out_shape, in_specs=[SPACES[c] for c in sp...  14.5 us
    ppermute x14, waiting for transfers between devices, swapped(): lax.ppermute(x, axis, [(i, i ^ 1 << bit) for i in range(lax.axis_size(axi...  8.54 us
    all_to_all x1, starting transfers between devices, local(): lax.all_to_all(blocks, 'sub', split_axis=0, concat_axis=0, tiled=True, ax...  4.88 us
    all_to_all x1, waiting for transfers between devices, local(): lax.all_to_all(blocks, 'sub', split_axis=0, concat_axis=0, tiled=True, ax...  2.29 us
    unnamed x14, local copies, waits for them, and re-layouts  1.75 us
    ppermute x1, starting transfers between devices, local(): packed_outer = lax.ppermute(packed, 'sub', outward)  1.66 us
    ppermute x1, starting transfers between devices, local(): far_rims = lax.ppermute(far_rims, 'sub', route)  1.52 us
  transfers between devices with their start and end apart: 17, of which 8 were waited for; matrix products, arithmetic and copies ran while one was open for 0% of the time, Pallas kernels for 20%

profile of v10, /device:TPU:0, one launch (start us, length us, event | category | flops | bytes accessed | tf_op | source)
XLA Modules:
  0.0 52.3 jit_solution(10035071062730914112)
XLA Ops:
  0.0 2.8 %shard_map.84 = (bf16[8,16,1536]{2,1,0:T(8,128)(2,1)}, bf16[784,256]{1,0:T(8,128)(2,1)}) custom-call(bf16[16,12288]{1,0:T(8,128)(2,1)} %tests_hbm.1, bf16[768,256]{1,0:T(8,128)(2,1)} %omega_ref.1, s32[1,2,768]{2,1,0:T(2,128)} %perms_ref.5, s32[1,5,2,192]{3,2,1,0:T(2,128)} %nodes_ref.1), custom_call_target="tpu_custom_call" | custom-call | flops 1000 | bytes 1000 | tf_op jit(solution)/shard_map/pallas_call | solution.py:39
  2.8 1.7 %collective-permute-start.1 = (bf16[784,256]{1,0:T(8,128)(2,1)}, bf16[784,256]{1,0:T(8,128)(2,1)S(1)}, u32[]{:S(2)}, u32[]{:S(2)}) collective-permute-start(bf16[784,256]{1,0:T(8,128)(2,1)} %get-tuple-element.28), channel_id=1, source_target_pairs={{1,2},{3,4},{5,6},{7,8},{9,10},{11,12},{13,14},{2,1},{4,3},{6,5},{... | collective-permute-start | bytes 1204232 | tf_op jit(solution)/shard_map/ppermute | solution.py:350
  4.5 3.4 %collective-permute-start = (bf16[784,256]{1,0:T(8,128)(2,1)}, bf16[784,256]{1,0:T(8,128)(2,1)S(1)}, u32[]{:S(2)}, u32[]{:S(2)}) collective-permute-start(bf16[784,256]{1,0:T(8,128)(2,1)} %get-tuple-element.28), channel_id=1, source_target_pairs={{0,1},{1,0},{2,3},{3,2},{4,5},{5,4},{6,7},{7,6},{8,9},{9,8},{10,11... | collective-permute-start | bytes 1204232 | tf_op jit(solution)/shard_map/ppermute | solution.py:321
  7.8 4.9 %all-to-all-start = ((bf16[8,16,1536]{2,1,0:T(8,128)(2,1)}), bf16[8,16,1536]{2,1,0:T(8,128)(2,1)S(1)}, u32[]{:S(2)}, u32[]{:S(2)}) async-start(bf16[8,16,1536]{2,1,0:T(8,128)(2,1)} %get-tuple-element.32), calls=%async_computation | async-start | bytes 786432 | tf_op jit(solution)/shard_map/all_to_all | solution.py:353
  13.4 1.0 %copy-done.4 = bf16[1,5,4,96,96]{4,3,2,1,0:T(8,128)(2,1)S(1)} copy-done((bf16[1,5,4,96,96]{4,3,2,1,0:T(8,128)(2,1)S(1)}, bf16[1,5,4,96,96]{4,3,2,1,0:T(8,128)(2,1)}, u32[]{:S(2)}) %copy-start.4) | copy-done | bytes 368664
  14.5 2.4 %shard_map.82 = (bf16[2,2,288,96]{3,2,1,0:T(8,128)(2,1)S(1)}, bf16[2,2,288,96]{3,2,1,0:T(8,128)(2,1)S(1)}, bf16[2,2,288,96]{3,2,1,0:T(8,128)(2,1)S(1)}, bf16[2,2...) custom-call(bf16[1,5,4,96,96]{4,3,2,1,0:T(8,128)(2,1)S(1)} %copy-done.4, s32[1,5,2,192]{3,2,1,0:T(2,128)S(1)} %copy-done.1), custom_call_target="tpu_custom_call" | custom-call | flops 1073741824 | bytes 1000 | tf_op jit(solution)/shard_map/pallas_call | solution.py:39
  16.9 3.5 %shard_map.83 = (bf16[192,768]{1,0:T(8,128)(2,1)}, bf16[96,2304]{1,0:T(8,128)(2,1)S(1)}, bf16[96,768]{1,0:T(8,128)(2,1)S(1)}, bf16[768,2304]{1,0:T(8,128)(2,1)S(1)}) custom-call(s32[6,12]{1,0:T(8,128)S(1)} %copy-done.6, bf16[6,12,128,128]{3,2,1,0:T(8,128)(2,1)S(1)} %copy-done.3, s32[1,2,768]{2,1,0:T(2,128)S(1)} %copy-done.2, ...), custom_call_target="tpu_custom_call" | custom-call | flops 1073741824 | bytes 1000 | tf_op jit(solution)/shard_map/pallas_call | solution.py:39
  20.3 1.3 %shard_map.85 = (bf16[208,768]{1,0:T(8,128)(2,1)S(1)}, bf16[192,128]{1,0:T(8,128)(2,1)S(1)}, bf16[192,128]{1,0:T(8,128)(2,1)S(1)}) custom-call(bf16[768,2304]{1,0:T(8,128)(2,1)S(1)} %get-tuple-element.25.dense_ref, bf16[96,2304]{1,0:T(8,128)(2,1)S(1)} %get-tuple-element.26.near_ref, bf16[96,768]{1,0:T(8,128)(2,1)S(1)} %get-tuple-element.27.tests_ref, ...), custom_call_target="tpu_custom_call" | custom-call | flops 1000 | bytes 1000 | tf_op jit(solution)/shard_map/pallas_call | solution.py:39
  22.3 2.3 %all-to-all-done = bf16[8,16,1536]{2,1,0:T(8,128)(2,1)S(1)} async-done(((bf16[8,16,1536]{2,1,0:T(8,128)(2,1)}), bf16[8,16,1536]{2,1,0:T(8,128)(2,1)S(1)}, u32[]{:S(2)}, u32[]{:S(2)}) %all-to-all-start) | async-done | bytes 393248 | tf_op jit(solution)/shard_map/all_to_all | solution.py:353
  24.9 1.5 %collective-permute-start.10 = (bf16[96,128]{1,0:T(8,128)(2,1)S(1)}, bf16[96,128]{1,0:T(8,128)(2,1)S(1)}, u32[]{:S(2)}, u32[]{:S(2)}) collective-permute-start(bf16[96,128]{1,0:T(8,128)(2,1)S(1)} %get-tuple-element.38), channel_id=1, source_target_pairs={{2,6},{3,7},{6,10},{7,11},{10,14},{11,15},{14,12},{15,13},{12,8},{... | collective-permute-start | bytes 73736 | tf_op jit(solution)/shard_map/ppermute | solution.py:389
  26.6 1.2 %collective-permute-start.4 = (bf16[192,128]{1,0:T(8,128)(2,1)S(1)}, bf16[192,128]{1,0:T(8,128)(2,1)S(1)}, u32[]{:S(2)}, u32[]{:S(2)}) collective-permute-start(bf16[192,128]{1,0:T(8,128)(2,1)S(1)} %shard_map.87.mine_ref.refs_0_), channel_id=1, source_target_pairs={{0,2},{1,3},{2,0},{3,1},{4,6},{5,7},{6,4},{7,5},{8,10},{9,11},{10,... | collective-permute-start | bytes 147464 | tf_op jit(solution)/shard_map/ppermute | solution.py:321
  27.7 1.5 %shard_map.91.mine_ref = bf16[192,128]{1,0:T(8,128)(2,1)S(1)} custom-call(bf16[2,2,288,96]{3,2,1,0:T(8,128)(2,1)S(1)} %get-tuple-element.24.after_ref.maps_ref, bf16[192,768]{1,0:T(8,128)(2,1)} %get-tuple-element.37.keep_ref, bf16[192,768]{1,0:T(8,128)(2,1)S(1)} %collective-permute-done.8.keep_other, bf16[208,768]{1,0:T(8,128)(2,1)S(1)} %get-tuple-element.31.beside_ref, ...), custom_call_target="tpu_custom_call" | custom-call | flops 4294967296 | bytes 1000 | tf_op jit(solution)/shard_map/pallas_call | solution.py:39
  30.6 1.2 %collective-permute-start.11 = (bf16[96,128]{1,0:T(8,128)(2,1)S(1)}, bf16[96,128]{1,0:T(8,128)(2,1)S(1)}, u32[]{:S(2)}, u32[]{:S(2)}) collective-permute-start(bf16[96,128]{1,0:T(8,128)(2,1)S(1)} %shard_map.92.given_ref), channel_id=1, source_target_pairs={{0,2},{1,3},{2,0},{3,1},{4,6},{5,7},{6,4},{7,5},{8,10},{9,11},{10,... | collective-permute-start | bytes 73736 | tf_op jit(solution)/shard_map/ppermute | solution.py:321
  31.9 2.2 %collective-permute-start.5 = (bf16[192,128]{1,0:T(8,128)(2,1)S(1)}, bf16[192,128]{1,0:T(8,128)(2,1)S(1)}, u32[]{:S(2)}, u32[]{:S(2)}) collective-permute-start(bf16[192,128]{1,0:T(8,128)(2,1)S(1)} %shard_map.88.mine_ref.refs_1_), channel_id=1, source_target_pairs={{0,4},{1,5},{2,6},{3,7},{4,0},{5,1},{6,2},{7,3},{8,12},{9,13},{10,... | collective-permute-start | bytes 147464 | tf_op jit(solution)/shard_map/ppermute | solution.py:321
  34.6 1.4 %collective-permute-start.12 = (bf16[192,128]{1,0:T(8,128)(2,1)S(1)}, bf16[192,128]{1,0:T(8,128)(2,1)S(1)}, u32[]{:S(2)}, u32[]{:S(2)}) collective-permute-start(bf16[192,128]{1,0:T(8,128)(2,1)S(1)} %get-tuple-element.40.mine_ref.refs_6_), channel_id=1, source_target_pairs={{0,4},{1,5},{2,6},{3,7},{4,0},{5,1},{6,2},{7,3},{8,12},{9,13},{10,... | collective-permute-start | bytes 147464 | tf_op jit(solution)/shard_map/ppermute | solution.py:321
  36.8 1.7 %collective-permute-start.6 = (bf16[192,128]{1,0:T(8,128)(2,1)S(1)}, bf16[192,128]{1,0:T(8,128)(2,1)S(1)}, u32[]{:S(2)}, u32[]{:S(2)}) collective-permute-start(bf16[192,128]{1,0:T(8,128)(2,1)S(1)} %shard_map.89.mine_ref.refs_2_), channel_id=1, source_target_pairs={{0,8},{1,9},{2,10},{3,11},{4,12},{5,13},{6,14},{7,15},{8,0},{9,1},... | collective-permute-start | bytes 147464 | tf_op jit(solution)/shard_map/ppermute | solution.py:321
  39.5 1.1 %collective-permute-start.13 = (bf16[192,128]{1,0:T(8,128)(2,1)S(1)}, bf16[192,128]{1,0:T(8,128)(2,1)S(1)}, u32[]{:S(2)}, u32[]{:S(2)}) collective-permute-start(bf16[192,128]{1,0:T(8,128)(2,1)S(1)} %shard_map.94.mine_ref.refs_7_), channel_id=1, source_target_pairs={{0,8},{1,9},{2,10},{3,11},{4,12},{5,13},{6,14},{7,15},{8,0},{9,1},... | collective-permute-start | bytes 147464 | tf_op jit(solution)/shard_map/ppermute | solution.py:321
  40.6 1.5 %collective-permute-done.6.other_ref = bf16[192,128]{1,0:T(8,128)(2,1)S(1)} collective-permute-done((bf16[192,128]{1,0:T(8,128)(2,1)S(1)}, bf16[192,128]{1,0:T(8,128)(2,1)S(1)}, u32[]{:S(2)}, u32[]{:S(2)}) %collective-permute-start.6) | collective-permute-done | bytes 49184 | tf_op jit(solution)/shard_map/ppermute | solution.py:321
  42.3 1.6 %collective-permute-start.7 = (bf16[192,128]{1,0:T(8,128)(2,1)S(1)}, bf16[192,128]{1,0:T(8,128)(2,1)S(1)}, u32[]{:S(2)}, u32[]{:S(2)}) collective-permute-start(bf16[192,128]{1,0:T(8,128)(2,1)S(1)} %shard_map.90.refs_3_), channel_id=1, source_target_pairs={{0,16},{16,0},{1,17},{17,1},{2,18},{18,2},{3,19},{19,3},{4,20},{20... | collective-permute-start | bytes 147464 | tf_op jit(solution)/shard_map/ppermute | solution.py:321
  43.8 1.2 %collective-permute-done.13.other_ref = bf16[192,128]{1,0:T(8,128)(2,1)S(1)} collective-permute-done((bf16[192,128]{1,0:T(8,128)(2,1)S(1)}, bf16[192,128]{1,0:T(8,128)(2,1)S(1)}, u32[]{:S(2)}, u32[]{:S(2)}) %collective-permute-start.13) | collective-permute-done | bytes 49184 | tf_op jit(solution)/shard_map/ppermute | solution.py:321
  45.3 1.6 %collective-permute-start.14 = (bf16[192,128]{1,0:T(8,128)(2,1)S(1)}, bf16[192,128]{1,0:T(8,128)(2,1)S(1)}, u32[]{:S(2)}, u32[]{:S(2)}) collective-permute-start(bf16[192,128]{1,0:T(8,128)(2,1)S(1)} %shard_map.95.refs_8_), channel_id=1, source_target_pairs={{0,16},{16,0},{1,17},{17,1},{2,18},{18,2},{3,19},{19,3},{4,20},{20... | collective-permute-start | bytes 147464 | tf_op jit(solution)/shard_map/ppermute | solution.py:321
  46.9 2.6 %collective-permute-done.14.refs_9_ = bf16[192,128]{1,0:T(8,128)(2,1)S(1)} collective-permute-done((bf16[192,128]{1,0:T(8,128)(2,1)S(1)}, bf16[192,128]{1,0:T(8,128)(2,1)S(1)}, u32[]{:S(2)}, u32[]{:S(2)}) %collective-permute-start.14) | collective-permute-done | bytes 49184 | tf_op jit(solution)/shard_map/ppermute | solution.py:321
  49.8 1.5 %collective-permute-done.15.other_ref = bf16[5,2,96,128]{3,2,1,0:T(8,128)(2,1)S(1)} collective-permute-done((bf16[5,2,96,128]{3,2,1,0:T(8,128)(2,1)S(1)}, bf16[5,2,96,128]{3,2,1,0:T(8,128)(2,1)S(1)}, u32[]{:S(2)}, u32[]{:S(2)}) %collective-permute-start.15) | collective-permute-done | bytes 245792 | tf_op jit(solution)/shard_map/ppermute | solution.py:321
  51.3 1.1 %shard_map.97 = bf16[1,5,2,96,256]{4,3,2,1,0:T(8,128)(2,1)} custom-call(bf16[5,2,96,128]{3,2,1,0:T(8,128)(2,1)S(1)} %shard_map.96.mine_ref, bf16[5,2,96,128]{3,2,1,0:T(8,128)(2,1)S(1)} %collective-permute-done.15.other_ref), custom_call_target="tpu_custom_call" | custom-call | flops 1000 | bytes 1000 | tf_op jit(solution)/shard_map/pallas_call | solution.py:39
  (40 shorter events, 6.2 us)
Async XLA Ops:
  0.0 16.8 %copy-start.2 = (s32[1,2,768]{2,1,0:T(2,128)S(1)}, s32[1,2,768]{2,1,0:T(2,128)}, u32[]{:S(2)}) copy-start(s32[1,2,768]{2,1,0:T(2,128)} %perms_ref.5) | copy-start | bytes 18436
  0.0 16.8 %copy-start.6 = (s32[6,12]{1,0:T(8,128)S(1)}, s32[6,12]{1,0:T(8,128)}, u32[]{:S(2)}) copy-start(s32[6,12]{1,0:T(8,128)} %cols_ref.1) | copy-start | bytes 868
  2.8 17.5 %collective-permute-start.1 = (bf16[784,256]{1,0:T(8,128)(2,1)}, bf16[784,256]{1,0:T(8,128)(2,1)S(1)}, u32[]{:S(2)}, u32[]{:S(2)}) collective-permute-start(bf16[784,256]{1,0:T(8,128)(2,1)} %get-tuple-element.28), channel_id=1, source_target_pairs={{1,2},{3,4},{5,6},{7,8},{9,10},{11,12},{13,14},{2,1},{4,3},{6,5},{... | collective-permute-start | bytes 1204232 | tf_op jit(solution)/shard_map/ppermute | solution.py:350
  4.5 15.9 %collective-permute-start = (bf16[784,256]{1,0:T(8,128)(2,1)}, bf16[784,256]{1,0:T(8,128)(2,1)S(1)}, u32[]{:S(2)}, u32[]{:S(2)}) collective-permute-start(bf16[784,256]{1,0:T(8,128)(2,1)} %get-tuple-element.28), channel_id=1, source_target_pairs={{0,1},{1,0},{2,3},{3,2},{4,5},{5,4},{6,7},{7,6},{8,9},{9,8},{10,11... | collective-permute-start | bytes 1204232 | tf_op jit(solution)/shard_map/ppermute | solution.py:321
  7.8 16.7 %all-to-all-start = ((bf16[8,16,1536]{2,1,0:T(8,128)(2,1)}), bf16[8,16,1536]{2,1,0:T(8,128)(2,1)S(1)}, u32[]{:S(2)}, u32[]{:S(2)}) async-start(bf16[8,16,1536]{2,1,0:T(8,128)(2,1)} %get-tuple-element.32), calls=%async_computation | async-start | bytes 786432 | tf_op jit(solution)/shard_map/all_to_all | solution.py:353
  12.7 0.7 %copy-start.1 = (s32[1,5,2,192]{3,2,1,0:T(2,128)S(1)}, s32[1,5,2,192]{3,2,1,0:T(2,128)}, u32[]{:S(2)}) copy-start(s32[1,5,2,192]{3,2,1,0:T(2,128)} %nodes_ref.1) | copy-start | bytes 23044
  13.4 1.0 %copy-start.4 = (bf16[1,5,4,96,96]{4,3,2,1,0:T(8,128)(2,1)S(1)}, bf16[1,5,4,96,96]{4,3,2,1,0:T(8,128)(2,1)}, u32[]{:S(2)}) copy-start(bf16[1,5,4,96,96]{4,3,2,1,0:T(8,128)(2,1)} %maps_ref.1) | copy-start | bytes 1105924
  14.4 2.4 %copy-start.3 = (bf16[6,12,128,128]{3,2,1,0:T(8,128)(2,1)S(1)}, bf16[6,12,128,128]{3,2,1,0:T(8,128)(2,1)}, u32[]{:S(2)}) copy-start(bf16[6,12,128,128]{3,2,1,0:T(8,128)(2,1)} %tiles_ref.1) | copy-start | bytes 7077892
  14.5 2.4 %copy-start.5 = (bf16[1,2,672,96]{2,3,1,0:T(8,128)(2,1)S(1)}, bf16[1,2,672,96]{2,3,1,0:T(8,128)(2,1)}, u32[]{:S(2)}) copy-start(bf16[1,2,672,96]{2,3,1,0:T(8,128)(2,1)} %param.13) | copy-start | bytes 774148
  14.5 5.9 %copy-start = (bf16[768,256]{1,0:T(8,128)(2,1)S(1)}, bf16[768,256]{1,0:T(8,128)(2,1)}, u32[]{:S(2)}) copy-start(bf16[768,256]{1,0:T(8,128)(2,1)} %omega_ref.1) | copy-start | bytes 1179652
  21.6 2.9 %collective-permute-start.3 = (bf16[208,768]{1,0:T(8,128)(2,1)S(1)}, bf16[208,768]{1,0:T(8,128)(2,1)S(1)}, u32[]{:S(2)}, u32[]{:S(2)}) collective-permute-start(bf16[208,768]{1,0:T(8,128)(2,1)S(1)} %get-tuple-element.31.beside_ref), channel_id=1, source_target_pairs={{0,1},{1,0},{2,3},{3,2},{4,5},{5,4},{6,7},{7,6},{8,9},{9,8},{10,11... | collective-permute-start | bytes 958472 | tf_op jit(solution)/shard_map/ppermute | solution.py:321
  21.7 6.0 %collective-permute-start.8 = (bf16[192,768]{1,0:T(8,128)(2,1)}, bf16[192,768]{1,0:T(8,128)(2,1)S(1)}, u32[]{:S(2)}, u32[]{:S(2)}) collective-permute-start(bf16[192,768]{1,0:T(8,128)(2,1)} %get-tuple-element.37.keep_ref), channel_id=1, source_target_pairs={{0,1},{1,0},{2,3},{3,2},{4,5},{5,4},{6,7},{7,6},{8,9},{9,8},{10,11... | collective-permute-start | bytes 884744 | tf_op jit(solution)/shard_map/ppermute | solution.py:321
  22.2 4.2 %collective-permute-start.2 = (bf16[192,128]{1,0:T(8,128)(2,1)S(1)}, bf16[192,128]{1,0:T(8,128)(2,1)S(1)}, u32[]{:S(2)}, u32[]{:S(2)}) collective-permute-start(bf16[192,128]{1,0:T(8,128)(2,1)S(1)} %get-tuple-element.30), channel_id=1, source_target_pairs={{0,1},{1,0},{2,3},{3,2},{4,5},{5,4},{6,7},{7,6},{8,9},{9,8},{10,11... | collective-permute-start | bytes 147464 | tf_op jit(solution)/shard_map/ppermute | solution.py:321
  24.9 5.4 %collective-permute-start.10 = (bf16[96,128]{1,0:T(8,128)(2,1)S(1)}, bf16[96,128]{1,0:T(8,128)(2,1)S(1)}, u32[]{:S(2)}, u32[]{:S(2)}) collective-permute-start(bf16[96,128]{1,0:T(8,128)(2,1)S(1)} %get-tuple-element.38), channel_id=1, source_target_pairs={{2,6},{3,7},{6,10},{7,11},{10,14},{11,15},{14,12},{15,13},{12,8},{... | collective-permute-start | bytes 73736 | tf_op jit(solution)/shard_map/ppermute | solution.py:389
  26.6 5.2 %collective-permute-start.4 = (bf16[192,128]{1,0:T(8,128)(2,1)S(1)}, bf16[192,128]{1,0:T(8,128)(2,1)S(1)}, u32[]{:S(2)}, u32[]{:S(2)}) collective-permute-start(bf16[192,128]{1,0:T(8,128)(2,1)S(1)} %shard_map.87.mine_ref.refs_0_), channel_id=1, source_target_pairs={{0,2},{1,3},{2,0},{3,1},{4,6},{5,7},{6,4},{7,5},{8,10},{9,11},{10,... | collective-permute-start | bytes 147464 | tf_op jit(solution)/shard_map/ppermute | solution.py:321
  29.3 5.2 %collective-permute-start.9 = (bf16[192,128]{1,0:T(8,128)(2,1)S(1)}, bf16[192,128]{1,0:T(8,128)(2,1)S(1)}, u32[]{:S(2)}, u32[]{:S(2)}) collective-permute-start(bf16[192,128]{1,0:T(8,128)(2,1)S(1)} %shard_map.91.mine_ref), channel_id=1, source_target_pairs={{0,2},{1,3},{2,0},{3,1},{4,6},{5,7},{6,4},{7,5},{8,10},{9,11},{10,... | collective-permute-start | bytes 147464 | tf_op jit(solution)/shard_map/ppermute | solution.py:321
  30.6 3.9 %collective-permute-start.11 = (bf16[96,128]{1,0:T(8,128)(2,1)S(1)}, bf16[96,128]{1,0:T(8,128)(2,1)S(1)}, u32[]{:S(2)}, u32[]{:S(2)}) collective-permute-start(bf16[96,128]{1,0:T(8,128)(2,1)S(1)} %shard_map.92.given_ref), channel_id=1, source_target_pairs={{0,2},{1,3},{2,0},{3,1},{4,6},{5,7},{6,4},{7,5},{8,10},{9,11},{10,... | collective-permute-start | bytes 73736 | tf_op jit(solution)/shard_map/ppermute | solution.py:321
  31.9 4.7 %collective-permute-start.5 = (bf16[192,128]{1,0:T(8,128)(2,1)S(1)}, bf16[192,128]{1,0:T(8,128)(2,1)S(1)}, u32[]{:S(2)}, u32[]{:S(2)}) collective-permute-start(bf16[192,128]{1,0:T(8,128)(2,1)S(1)} %shard_map.88.mine_ref.refs_1_), channel_id=1, source_target_pairs={{0,4},{1,5},{2,6},{3,7},{4,0},{5,1},{6,2},{7,3},{8,12},{9,13},{10,... | collective-permute-start | bytes 147464 | tf_op jit(solution)/shard_map/ppermute | solution.py:321
  34.6 4.7 %collective-permute-start.12 = (bf16[192,128]{1,0:T(8,128)(2,1)S(1)}, bf16[192,128]{1,0:T(8,128)(2,1)S(1)}, u32[]{:S(2)}, u32[]{:S(2)}) collective-permute-start(bf16[192,128]{1,0:T(8,128)(2,1)S(1)} %get-tuple-element.40.mine_ref.refs_6_), channel_id=1, source_target_pairs={{0,4},{1,5},{2,6},{3,7},{4,0},{5,1},{6,2},{7,3},{8,12},{9,13},{10,... | collective-permute-start | bytes 147464 | tf_op jit(solution)/shard_map/ppermute | solution.py:321
  36.8 5.3 %collective-permute-start.6 = (bf16[192,128]{1,0:T(8,128)(2,1)S(1)}, bf16[192,128]{1,0:T(8,128)(2,1)S(1)}, u32[]{:S(2)}, u32[]{:S(2)}) collective-permute-start(bf16[192,128]{1,0:T(8,128)(2,1)S(1)} %shard_map.89.mine_ref.refs_2_), channel_id=1, source_target_pairs={{0,8},{1,9},{2,10},{3,11},{4,12},{5,13},{6,14},{7,15},{8,0},{9,1},... | collective-permute-start | bytes 147464 | tf_op jit(solution)/shard_map/ppermute | solution.py:321
  39.5 5.6 %collective-permute-start.13 = (bf16[192,128]{1,0:T(8,128)(2,1)S(1)}, bf16[192,128]{1,0:T(8,128)(2,1)S(1)}, u32[]{:S(2)}, u32[]{:S(2)}) collective-permute-start(bf16[192,128]{1,0:T(8,128)(2,1)S(1)} %shard_map.94.mine_ref.refs_7_), channel_id=1, source_target_pairs={{0,8},{1,9},{2,10},{3,11},{4,12},{5,13},{6,14},{7,15},{8,0},{9,1},... | collective-permute-start | bytes 147464 | tf_op jit(solution)/shard_map/ppermute | solution.py:321
  42.3 4.6 %collective-permute-start.7 = (bf16[192,128]{1,0:T(8,128)(2,1)S(1)}, bf16[192,128]{1,0:T(8,128)(2,1)S(1)}, u32[]{:S(2)}, u32[]{:S(2)}) collective-permute-start(bf16[192,128]{1,0:T(8,128)(2,1)S(1)} %shard_map.90.refs_3_), channel_id=1, source_target_pairs={{0,16},{16,0},{1,17},{17,1},{2,18},{18,2},{3,19},{19,3},{4,20},{20... | collective-permute-start | bytes 147464 | tf_op jit(solution)/shard_map/ppermute | solution.py:321
  45.3 4.2 %collective-permute-start.14 = (bf16[192,128]{1,0:T(8,128)(2,1)S(1)}, bf16[192,128]{1,0:T(8,128)(2,1)S(1)}, u32[]{:S(2)}, u32[]{:S(2)}) collective-permute-start(bf16[192,128]{1,0:T(8,128)(2,1)S(1)} %shard_map.95.refs_8_), channel_id=1, source_target_pairs={{0,16},{16,0},{1,17},{17,1},{2,18},{18,2},{3,19},{19,3},{4,20},{20... | collective-permute-start | bytes 147464 | tf_op jit(solution)/shard_map/ppermute | solution.py:321
  49.7 1.6 %collective-permute-start.15 = (bf16[5,2,96,128]{3,2,1,0:T(8,128)(2,1)S(1)}, bf16[5,2,96,128]{3,2,1,0:T(8,128)(2,1)S(1)}, u32[]{:S(2)}, u32[]{:S(2)}) collective-permute-start(bf16[5,2,96,128]{3,2,1,0:T(8,128)(2,1)S(1)} %shard_map.96.mine_ref), channel_id=1, source_target_pairs={{0,1},{1,0},{2,3},{3,2},{4,5},{5,4},{6,7},{7,6},{8,9},{9,8},{10,11... | collective-permute-start | bytes 737288 | tf_op jit(solution)/shard_map/ppermute | solution.py:321

commit v11 on v10

--- a/solution.py
+++ b/solution.py
@@ -124,13 +124,14 @@
 
 
 def halo_body(
+    keep_ref,
     dense_ref,
     near_ref,
     tests_ref,
     omega_ref,
     inner_ref,
     outer_ref,
-    beside_ref,
+    sel_ref,
     mine_ref,
     other_ref,
 ):
@@ -139,13 +140,13 @@
     half = omega_ref.shape[1] // 2
     core = lax.axis_index("sub") & 1
     unit = eye(rank)
-    for b, ref in enumerate((inner_ref, outer_ref)):
-        order = from_digits(ref[rows:, :rank], 0)
-        keep = mm_t(unit, one_hot(order, rows)).astype(BF)
-        block = dense_ref[:, (b + 1) * rows : (b + 2) * rows]
-        beside_ref[b * rank : (b + 1) * rank] = mm_t(keep, block).astype(BF)
-    beside_ref[2 * rank :] = jnp.zeros_like(beside_ref[2 * rank :])
-    beside_ref[2 * rank :, : outer_ref.shape[1]] = outer_ref[rows:]
+    sel_ref[: 2 * rank] = keep_ref[...]
+    for b, ref in enumerate((inner_ref, outer_ref), 1):
+        keep = mm_t(unit, one_hot(from_digits(ref[rows:, :rank], 0), rows)).astype(BF)
+        block = dense_ref[:, b * rows : (b + 1) * rows]
+        sel_ref[(b + 1) * rank : (b + 2) * rank] = mm_t(keep, block).astype(BF)
+    sel_ref[4 * rank :] = jnp.zeros_like(sel_ref[4 * rank :])
+    sel_ref[4 * rank :, : outer_ref.shape[1]] = outer_ref[rows:]
     for out_ref, place in ((mine_ref, core), (other_ref, 1 - core)):
         cols = pl.ds(pl.multiple_of(place * half, half), half)
         own = omega_ref[:, cols]
@@ -209,61 +210,59 @@
     return [panel_ref[:, pl.ds(pl.multiple_of(at * rows, 128), rows)] for at in (core, 1 - core)]
 
 
-def edge_body(beside_ref, beside_other, panel_ref, near_out, far_out):
+def edge_body(sel_ref, sel_other, panel_ref, near_out, far_out):
     rank = near_out.shape[0]
     panel, panel_other = halves(panel_ref)
-    mine = mm_t(beside_ref[rank : 2 * rank], panel)
-    other = mm_t(beside_other[rank : 2 * rank], panel_other)
+    mine = mm_t(sel_ref[3 * rank : 4 * rank], panel)
+    other = mm_t(sel_other[3 * rank : 4 * rank], panel_other)
     near = near_rim()
     near_out[...] = jnp.where(near, mine, other).astype(BF)
     far_out[...] = jnp.where(near, other, mine).astype(BF)
 
 
-def adjoint_body(
-    maps_ref, keep_ref, keep_other, beside_ref, beside_other, panel_ref, after_ref, out_ref
-):
+def adjoint_body(maps_ref, sel_ref, sel_other, panel_ref, after_ref, out_ref):
     del after_ref
-    rank = keep_ref.shape[0] // 2
+    rank = out_ref.shape[0] // 2
     core = lax.axis_index("sub") & 1
     panel, panel_other = halves(panel_ref)
-    mine = mm_t(keep_ref[...], panel)
-    other = mm_t(keep_other[...], panel_other)
-    to_other = mm_t(beside_ref[:rank], panel)
-    to_mine = mm_t(beside_other[:rank], panel_other)
+    mine = mm_t(sel_ref[: 3 * rank], panel)
+    other = mm_t(sel_other[: 3 * rank], panel_other)
     kept, tests = merged(
         maps_ref,
         1,
         core,
-        (mine[:rank] + to_mine).astype(BF),
-        mine[rank:].astype(BF),
-        (other[:rank] + to_other).astype(BF),
-        other[rank:].astype(BF),
+        (mine[:rank] + other[2 * rank :]).astype(BF),
+        mine[rank : 2 * rank].astype(BF),
+        (other[:rank] + mine[2 * rank :]).astype(BF),
+        other[rank : 2 * rank].astype(BF),
         rank,
     )
     out_ref[:rank] = kept.astype(BF)
     out_ref[rank:] = tests.astype(BF)
 
 
-def rim_body(beside_ref, beside_other, near_ref, far_ref, out_ref):
+def rim_body(sel_ref, sel_other, near_ref, far_ref, adj_ref, out_ref):
     rank = near_ref.shape[0]
     chip = (lax.axis_index("sub") >> 1) & 1
-    digits = [ref[2 * rank :, :rank].astype(F32) for ref in (beside_ref, beside_other)]
+    digits = [ref[4 * rank :, :rank].astype(F32) for ref in (sel_ref, sel_other)]
     order = from_digits(jnp.where(near_rim(), *digits), 2)
     hot = one_hot(order, 2 * rank)
     keeps = [mm_t(eye(rank), hot[side * rank : (side + 1) * rank]) for side in range(2)]
     upper = chip == 1
     near_keep = jnp.where(upper, keeps[1], keeps[0]).astype(BF)
     far_keep = jnp.where(upper, keeps[0], keeps[1]).astype(BF)
-    out_ref[...] = (mm(near_keep, near_ref[...]) + mm(far_keep, far_ref[...])).astype(BF)
-
-
-def joined_body(bit, maps_ref, mine_ref, other_ref, added_ref, given_ref, out_ref, node_ref):
-    rank = added_ref.shape[0]
+    out_ref[: 2 * rank] = adj_ref[...]
+    out_ref[2 * rank :] = (mm(near_keep, near_ref[...]) + mm(far_keep, far_ref[...])).astype(BF)
+
+
+def joined_body(bit, maps_ref, mine_ref, other_ref, out_ref, node_ref):
+    rank = node_ref.shape[0]
     side = (lax.axis_index("sub") >> bit) & 1
-    mine = (mine_ref[:rank].astype(F32) + added_ref[...].astype(F32)).astype(BF)
-    other = (other_ref[:rank].astype(F32) + given_ref[...].astype(F32)).astype(BF)
+    a, p, r = (slice(i * rank, (i + 1) * rank) for i in range(3))
+    mine = (mine_ref[a].astype(F32) + other_ref[r].astype(F32)).astype(BF)
+    other = (other_ref[a].astype(F32) + mine_ref[r].astype(F32)).astype(BF)
     node_ref[...] = mine
-    kept, tests = merged(maps_ref, 1, side, mine, mine_ref[rank:], other, other_ref[rank:], rank)
+    kept, tests = merged(maps_ref, 1, side, mine, mine_ref[p], other, other_ref[p], rank)
     out_ref[:rank] = kept.astype(BF)
     out_ref[rank:] = tests.astype(BF)
 
@@ -373,17 +372,14 @@
         specs="svvva",
         flops=1 << 30,
     )
-    keep_other = swapped(keep, "sub", 0)
-    beside, fwd_mine, fwd_send = call(
+    sel, fwd_mine, fwd_send = call(
         halo_body,
-        [shape((2 * rank + 16, rows))] + [shape((2 * rank, half))] * 2,
-        (dense, near, tests, omega, packed_inner, packed_outer),
-    )
-    beside_other = swapped(beside, "sub", 0)
+        [shape((4 * rank + 16, rows))] + [shape((2 * rank, half))] * 2,
+        (keep, dense, near, tests, omega, packed_inner, packed_outer),
+    )
+    sel_other = swapped(sel, "sub", 0)
     fwd_other = swapped(fwd_send, "sub", 0)
-    near_rims, far_rims = call(
-        edge_body, [shape((rank, half))] * 2, (beside, beside_other, panel)
-    )
+    near_rims, far_rims = call(edge_body, [shape((rank, half))] * 2, (sel, sel_other, panel))
     ring = list(range(1, chips, 2)) + list(range(chips - 2, -1, -2))
     route = [(2 * a + c, 2 * b + c) for a, b in zip(ring, ring[1:] + ring[:1]) for c in range(2)]
     far_rims = lax.ppermute(far_rims, "sub", route)
@@ -396,15 +392,15 @@
     adj = call(
         adjoint_body,
         shape((2 * rank, half)),
-        (maps[0], keep, keep_other, beside, beside_other, panel, near_rims),
-        specs="vvvvvva",
+        (maps[0], sel, sel_other, panel, fwd),
+        specs="vvvva",
         flops=4 << 30,
     )
-    given = call(rim_body, shape((rank, half)), (beside, beside_other, near_rims, far_rims))
+    adj = call(rim_body, shape((3 * rank, half)), (sel, sel_other, near_rims, far_rims, adj))
     new, node = call(
         functools.partial(joined_body, 1),
         [shape((2 * rank, half)), shape((rank, half))],
-        (maps[1], adj, swapped(adj, "sub", 1), swapped(given, "sub", 1), given),
+        (maps[1], adj, swapped(adj, "sub", 1)),
     )
     chains = [[fwd], [node, new]]
     steps = [("sub", bit) for bit in range(1, sub_bits)]

time: 52.8 us -> 56.4 us (1.068)
  waiting for transfers between devices: 10.8 us -> 16.1 us
  starting transfers between devices: 25 us -> 24 us
    ppermute x14 -> x12, waiting for transfers between devices: 8.54 us -> 13.1 us  [swapped(): lax.ppermute(x, axis, [(i, i ^ 1 << bit) for i in range(lax.axis_size(axi...]
    ppermute x14 -> x12, starting transfers between devices: 17 us -> 15.4 us  [swapped(): lax.ppermute(x, axis, [(i, i ^ 1 << bit) for i in range(lax.axis_size(axi...]
    ppermute x1, waiting for transfers between devices: 0.01 us -> 0.97 us  [local(): far_rims = lax.ppermute(far_rims, 'sub', route)]
    ppermute x1, starting transfers between devices: 1.52 us -> 2.1 us  [local(): far_rims = lax.ppermute(far_rims, 'sub', route)]
  transfers between devices with their start and end apart: 17 -> 15, of which waited for: 8 -> 8; matrix products, arithmetic and copies ran while one was open for 0% -> 0% of each run, Pallas kernels for 20% -> 17%
where the time goes in v11:
time: 56.4 us; the launch traced here: 56.1 us
  starting transfers between devices  24 us (43%)
  waiting for transfers between devices  16.1 us (29%)
  Pallas kernels  14 us (25%)
  local copies, waits for them, and re-layouts  1.75 us (3%)
    ppermute x12, starting transfers between devices, swapped(): lax.ppermute(x, axis, [(i, i ^ 1 << bit) for i in range(lax.axis_size(axi...  15.4 us
    pallas_call x16, Pallas kernels, call(): pl.pallas_call(body, out_shape=out_shape, in_specs=[SPACES[c] for c in sp...  14 us
    ppermute x12, waiting for transfers between devices, swapped(): lax.ppermute(x, axis, [(i, i ^ 1 << bit) for i in range(lax.axis_size(axi...  13.1 us
    all_to_all x1, starting transfers between devices, local(): lax.all_to_all(blocks, 'sub', split_axis=0, concat_axis=0, tiled=True, ax...  4.88 us
    ppermute x1, starting transfers between devices, local(): far_rims = lax.ppermute(far_rims, 'sub', route)  2.1 us
    all_to_all x1, waiting for transfers between devices, local(): lax.all_to_all(blocks, 'sub', split_axis=0, concat_axis=0, tiled=True, ax...  1.99 us
    unnamed x14, local copies, waits for them, and re-layouts  1.75 us
    ppermute x1, starting transfers between devices, local(): packed_outer = lax.ppermute(packed, 'sub', outward)  1.66 us
  transfers between devices with their start and end apart: 15, of which 8 were waited for; matrix products, arithmetic and copies ran while one was open for 0% of the time, Pallas kernels for 17%

profile of v11, /device:TPU:0, one launch (start us, length us, event | category | flops | bytes accessed | tf_op | source)
XLA Modules:
  0.0 56.1 jit_solution(14056339606785795857)
XLA Ops:
  0.0 2.8 %shard_map.84 = (bf16[8,16,1536]{2,1,0:T(8,128)(2,1)}, bf16[784,256]{1,0:T(8,128)(2,1)}) custom-call(bf16[16,12288]{1,0:T(8,128)(2,1)} %tests_hbm.1, bf16[768,256]{1,0:T(8,128)(2,1)} %omega_ref.1, s32[1,2,768]{2,1,0:T(2,128)} %perms_ref.5, s32[1,5,2,192]{3,2,1,0:T(2,128)} %nodes_ref.1), custom_call_target="tpu_custom_call" | custom-call | flops 1000 | bytes 1000 | tf_op jit(solution)/shard_map/pallas_call | solution.py:39
  2.8 1.7 %collective-permute-start.1 = (bf16[784,256]{1,0:T(8,128)(2,1)}, bf16[784,256]{1,0:T(8,128)(2,1)S(1)}, u32[]{:S(2)}, u32[]{:S(2)}) collective-permute-start(bf16[784,256]{1,0:T(8,128)(2,1)} %get-tuple-element.29), channel_id=1, source_target_pairs={{1,2},{3,4},{5,6},{7,8},{9,10},{11,12},{13,14},{2,1},{4,3},{6,5},{... | collective-permute-start | bytes 1204232 | tf_op jit(solution)/shard_map/ppermute | solution.py:349
  4.5 3.4 %collective-permute-start = (bf16[784,256]{1,0:T(8,128)(2,1)}, bf16[784,256]{1,0:T(8,128)(2,1)S(1)}, u32[]{:S(2)}, u32[]{:S(2)}) collective-permute-start(bf16[784,256]{1,0:T(8,128)(2,1)} %get-tuple-element.29), channel_id=1, source_target_pairs={{0,1},{1,0},{2,3},{3,2},{4,5},{5,4},{6,7},{7,6},{8,9},{9,8},{10,11... | collective-permute-start | bytes 1204232 | tf_op jit(solution)/shard_map/ppermute | solution.py:320
  7.8 4.9 %all-to-all-start = ((bf16[8,16,1536]{2,1,0:T(8,128)(2,1)}), bf16[8,16,1536]{2,1,0:T(8,128)(2,1)S(1)}, u32[]{:S(2)}, u32[]{:S(2)}) async-start(bf16[8,16,1536]{2,1,0:T(8,128)(2,1)} %get-tuple-element.33), calls=%async_computation | async-start | bytes 786432 | tf_op jit(solution)/shard_map/all_to_all | solution.py:352
  12.7 0.7 %copy-done.1 = s32[1,5,2,192]{3,2,1,0:T(2,128)S(1)} copy-done((s32[1,5,2,192]{3,2,1,0:T(2,128)S(1)}, s32[1,5,2,192]{3,2,1,0:T(2,128)}, u32[]{:S(2)}) %copy-start.1) | copy-done | bytes 7704
  13.4 1.0 %copy-done.4 = bf16[1,5,4,96,96]{4,3,2,1,0:T(8,128)(2,1)S(1)} copy-done((bf16[1,5,4,96,96]{4,3,2,1,0:T(8,128)(2,1)S(1)}, bf16[1,5,4,96,96]{4,3,2,1,0:T(8,128)(2,1)}, u32[]{:S(2)}) %copy-start.4) | copy-done | bytes 368664
  14.5 2.4 %shard_map.82 = (bf16[2,2,288,96]{3,2,1,0:T(8,128)(2,1)S(1)}, bf16[2,2,288,96]{3,2,1,0:T(8,128)(2,1)S(1)}, bf16[2,2,288,96]{3,2,1,0:T(8,128)(2,1)S(1)}, bf16[2,2...) custom-call(bf16[1,5,4,96,96]{4,3,2,1,0:T(8,128)(2,1)S(1)} %copy-done.4, s32[1,5,2,192]{3,2,1,0:T(2,128)S(1)} %copy-done.1), custom_call_target="tpu_custom_call" | custom-call | flops 1073741824 | bytes 1000 | tf_op jit(solution)/shard_map/pallas_call | solution.py:39
  16.9 3.2 %shard_map.83 = (bf16[192,768]{1,0:T(8,128)(2,1)S(1)}, bf16[96,2304]{1,0:T(8,128)(2,1)S(1)}, bf16[96,768]{1,0:T(8,128)(2,1)S(1)}, bf16[768,2304]{1,0:T(8,128)(2,1)S(1)}) custom-call(s32[6,12]{1,0:T(8,128)S(1)} %copy-done.6, bf16[6,12,128,128]{3,2,1,0:T(8,128)(2,1)S(1)} %copy-done.3, s32[1,2,768]{2,1,0:T(2,128)S(1)} %copy-done.2, ...), custom_call_target="tpu_custom_call" | custom-call | flops 1073741824 | bytes 1000 | tf_op jit(solution)/shard_map/pallas_call | solution.py:39
  20.2 1.9 %shard_map.85 = (bf16[400,768]{1,0:T(8,128)(2,1)S(1)}, bf16[192,128]{1,0:T(8,128)(2,1)S(1)}, bf16[192,128]{1,0:T(8,128)(2,1)}) custom-call(bf16[192,768]{1,0:T(8,128)(2,1)S(1)} %get-tuple-element.25.keep_ref, bf16[768,2304]{1,0:T(8,128)(2,1)S(1)} %get-tuple-element.26.dense_ref, bf16[96,2304]{1,0:T(8,128)(2,1)S(1)} %get-tuple-element.27.near_ref, ...), custom_call_target="tpu_custom_call" | custom-call | flops 1000 | bytes 1000 | tf_op jit(solution)/shard_map/pallas_call | solution.py:39
  22.6 2.0 %all-to-all-done = bf16[8,16,1536]{2,1,0:T(8,128)(2,1)S(1)} async-done(((bf16[8,16,1536]{2,1,0:T(8,128)(2,1)}), bf16[8,16,1536]{2,1,0:T(8,128)(2,1)S(1)}, u32[]{:S(2)}, u32[]{:S(2)}) %all-to-all-start) | async-done | bytes 393248 | tf_op jit(solution)/shard_map/all_to_all | solution.py:352
  24.9 2.1 %collective-permute-start.8 = (bf16[96,128]{1,0:T(8,128)(2,1)S(1)}, bf16[96,128]{1,0:T(8,128)(2,1)S(1)}, u32[]{:S(2)}, u32[]{:S(2)}) collective-permute-start(bf16[96,128]{1,0:T(8,128)(2,1)S(1)} %get-tuple-element.38), channel_id=1, source_target_pairs={{2,6},{3,7},{6,10},{7,11},{10,14},{11,15},{14,12},{15,13},{12,8},{... | collective-permute-start | bytes 73736 | tf_op jit(solution)/shard_map/ppermute | solution.py:385
  27.8 1.0 %collective-permute-done.8.far_ref = bf16[96,128]{1,0:T(8,128)(2,1)S(1)} collective-permute-done((bf16[96,128]{1,0:T(8,128)(2,1)S(1)}, bf16[96,128]{1,0:T(8,128)(2,1)S(1)}, u32[]{:S(2)}, u32[]{:S(2)}) %collective-permute-start.8) | collective-permute-done | bytes 24608 | tf_op jit(solution)/shard_map/ppermute | solution.py:385
  29.0 2.1 %collective-permute-start.9 = (bf16[288,128]{1,0:T(8,128)(2,1)S(1)}, bf16[288,128]{1,0:T(8,128)(2,1)S(1)}, u32[]{:S(2)}, u32[]{:S(2)}) collective-permute-start(bf16[288,128]{1,0:T(8,128)(2,1)S(1)} %shard_map.92.mine_ref), channel_id=1, source_target_pairs={{0,2},{1,3},{2,0},{3,1},{4,6},{5,7},{6,4},{7,5},{8,10},{9,11},{10,... | collective-permute-start | bytes 221192 | tf_op jit(solution)/shard_map/ppermute | solution.py:320
  31.2 4.0 %collective-permute-done.4.other_ref = bf16[192,128]{1,0:T(8,128)(2,1)S(1)} collective-permute-done((bf16[192,128]{1,0:T(8,128)(2,1)S(1)}, bf16[192,128]{1,0:T(8,128)(2,1)S(1)}, u32[]{:S(2)}, u32[]{:S(2)}) %collective-permute-start.4) | collective-permute-done | bytes 49184 | tf_op jit(solution)/shard_map/ppermute | solution.py:320
  35.4 1.6 %collective-permute-start.5 = (bf16[192,128]{1,0:T(8,128)(2,1)S(1)}, bf16[192,128]{1,0:T(8,128)(2,1)S(1)}, u32[]{:S(2)}, u32[]{:S(2)}) collective-permute-start(bf16[192,128]{1,0:T(8,128)(2,1)S(1)} %shard_map.88.mine_ref.refs_1_), channel_id=1, source_target_pairs={{0,4},{1,5},{2,6},{3,7},{4,0},{5,1},{6,2},{7,3},{8,12},{9,13},{10,... | collective-permute-start | bytes 147464 | tf_op jit(solution)/shard_map/ppermute | solution.py:320
  37.8 1.8 %collective-permute-done.5.other_ref = bf16[192,128]{1,0:T(8,128)(2,1)S(1)} collective-permute-done((bf16[192,128]{1,0:T(8,128)(2,1)S(1)}, bf16[192,128]{1,0:T(8,128)(2,1)S(1)}, u32[]{:S(2)}, u32[]{:S(2)}) %collective-permute-start.5) | collective-permute-done | bytes 49184 | tf_op jit(solution)/shard_map/ppermute | solution.py:320
  39.8 3.3 %collective-permute-start.6 = (bf16[192,128]{1,0:T(8,128)(2,1)S(1)}, bf16[192,128]{1,0:T(8,128)(2,1)S(1)}, u32[]{:S(2)}, u32[]{:S(2)}) collective-permute-start(bf16[192,128]{1,0:T(8,128)(2,1)S(1)} %shard_map.89.mine_ref.refs_2_), channel_id=1, source_target_pairs={{0,8},{1,9},{2,10},{3,11},{4,12},{5,13},{6,14},{7,15},{8,0},{9,1},... | collective-permute-start | bytes 147464 | tf_op jit(solution)/shard_map/ppermute | solution.py:320
  43.9 1.3 %collective-permute-done.6.other_ref = bf16[192,128]{1,0:T(8,128)(2,1)S(1)} collective-permute-done((bf16[192,128]{1,0:T(8,128)(2,1)S(1)}, bf16[192,128]{1,0:T(8,128)(2,1)S(1)}, u32[]{:S(2)}, u32[]{:S(2)}) %collective-permute-start.6) | collective-permute-done | bytes 49184 | tf_op jit(solution)/shard_map/ppermute | solution.py:320
  45.4 1.6 %collective-permute-start.7 = (bf16[192,128]{1,0:T(8,128)(2,1)S(1)}, bf16[192,128]{1,0:T(8,128)(2,1)S(1)}, u32[]{:S(2)}, u32[]{:S(2)}) collective-permute-start(bf16[192,128]{1,0:T(8,128)(2,1)S(1)} %shard_map.90.refs_3_), channel_id=1, source_target_pairs={{0,16},{16,0},{1,17},{17,1},{2,18},{18,2},{3,19},{19,3},{4,20},{20... | collective-permute-start | bytes 147464 | tf_op jit(solution)/shard_map/ppermute | solution.py:320
  46.9 1.9 %collective-permute-done.11.other_ref = bf16[192,128]{1,0:T(8,128)(2,1)S(1)} collective-permute-done((bf16[192,128]{1,0:T(8,128)(2,1)S(1)}, bf16[192,128]{1,0:T(8,128)(2,1)S(1)}, u32[]{:S(2)}, u32[]{:S(2)}) %collective-permute-start.11) | collective-permute-done | bytes 49184 | tf_op jit(solution)/shard_map/ppermute | solution.py:320
  49.0 1.6 %collective-permute-start.12 = (bf16[192,128]{1,0:T(8,128)(2,1)S(1)}, bf16[192,128]{1,0:T(8,128)(2,1)S(1)}, u32[]{:S(2)}, u32[]{:S(2)}) collective-permute-start(bf16[192,128]{1,0:T(8,128)(2,1)S(1)} %shard_map.95.refs_8_), channel_id=1, source_target_pairs={{0,16},{16,0},{1,17},{17,1},{2,18},{18,2},{3,19},{19,3},{4,20},{20... | collective-permute-start | bytes 147464 | tf_op jit(solution)/shard_map/ppermute | solution.py:320
  50.6 2.6 %collective-permute-done.12.refs_9_ = bf16[192,128]{1,0:T(8,128)(2,1)S(1)} collective-permute-done((bf16[192,128]{1,0:T(8,128)(2,1)S(1)}, bf16[192,128]{1,0:T(8,128)(2,1)S(1)}, u32[]{:S(2)}, u32[]{:S(2)}) %collective-permute-start.12) | collective-permute-done | bytes 49184 | tf_op jit(solution)/shard_map/ppermute | solution.py:320
  53.5 1.5 %collective-permute-done.13.other_ref = bf16[5,2,96,128]{3,2,1,0:T(8,128)(2,1)S(1)} collective-permute-done((bf16[5,2,96,128]{3,2,1,0:T(8,128)(2,1)S(1)}, bf16[5,2,96,128]{3,2,1,0:T(8,128)(2,1)S(1)}, u32[]{:S(2)}, u32[]{:S(2)}) %collective-permute-start.13) | collective-permute-done | bytes 245792 | tf_op jit(solution)/shard_map/ppermute | solution.py:320
  55.0 1.1 %shard_map.97 = bf16[1,5,2,96,256]{4,3,2,1,0:T(8,128)(2,1)} custom-call(bf16[5,2,96,128]{3,2,1,0:T(8,128)(2,1)S(1)} %shard_map.96.mine_ref, bf16[5,2,96,128]{3,2,1,0:T(8,128)(2,1)S(1)} %collective-permute-done.13.other_ref), custom_call_target="tpu_custom_call" | custom-call | flops 1000 | bytes 1000 | tf_op jit(solution)/shard_map/pallas_call | solution.py:39
  (36 shorter events, 4.4 us)
Async XLA Ops:
  0.0 16.8 %copy-start.2 = (s32[1,2,768]{2,1,0:T(2,128)S(1)}, s32[1,2,768]{2,1,0:T(2,128)}, u32[]{:S(2)}) copy-start(s32[1,2,768]{2,1,0:T(2,128)} %perms_ref.5) | copy-start | bytes 18436
  0.0 16.9 %copy-start.5 = (bf16[1,2,672,96]{2,3,1,0:T(8,128)(2,1)S(1)}, bf16[1,2,672,96]{2,3,1,0:T(8,128)(2,1)}, u32[]{:S(2)}) copy-start(bf16[1,2,672,96]{2,3,1,0:T(8,128)(2,1)} %param.13) | copy-start | bytes 774148
  0.0 16.9 %copy-start.6 = (s32[6,12]{1,0:T(8,128)S(1)}, s32[6,12]{1,0:T(8,128)}, u32[]{:S(2)}) copy-start(s32[6,12]{1,0:T(8,128)} %cols_ref.1) | copy-start | bytes 868
  2.8 17.3 %collective-permute-start.1 = (bf16[784,256]{1,0:T(8,128)(2,1)}, bf16[784,256]{1,0:T(8,128)(2,1)S(1)}, u32[]{:S(2)}, u32[]{:S(2)}) collective-permute-start(bf16[784,256]{1,0:T(8,128)(2,1)} %get-tuple-element.29), channel_id=1, source_target_pairs={{1,2},{3,4},{5,6},{7,8},{9,10},{11,12},{13,14},{2,1},{4,3},{6,5},{... | collective-permute-start | bytes 1204232 | tf_op jit(solution)/shard_map/ppermute | solution.py:349
  4.5 15.7 %collective-permute-start = (bf16[784,256]{1,0:T(8,128)(2,1)}, bf16[784,256]{1,0:T(8,128)(2,1)S(1)}, u32[]{:S(2)}, u32[]{:S(2)}) collective-permute-start(bf16[784,256]{1,0:T(8,128)(2,1)} %get-tuple-element.29), channel_id=1, source_target_pairs={{0,1},{1,0},{2,3},{3,2},{4,5},{5,4},{6,7},{7,6},{8,9},{9,8},{10,11... | collective-permute-start | bytes 1204232 | tf_op jit(solution)/shard_map/ppermute | solution.py:320
  7.8 16.7 %all-to-all-start = ((bf16[8,16,1536]{2,1,0:T(8,128)(2,1)}), bf16[8,16,1536]{2,1,0:T(8,128)(2,1)S(1)}, u32[]{:S(2)}, u32[]{:S(2)}) async-start(bf16[8,16,1536]{2,1,0:T(8,128)(2,1)} %get-tuple-element.33), calls=%async_computation | async-start | bytes 786432 | tf_op jit(solution)/shard_map/all_to_all | solution.py:352
  12.7 0.7 %copy-start.1 = (s32[1,5,2,192]{3,2,1,0:T(2,128)S(1)}, s32[1,5,2,192]{3,2,1,0:T(2,128)}, u32[]{:S(2)}) copy-start(s32[1,5,2,192]{3,2,1,0:T(2,128)} %nodes_ref.1) | copy-start | bytes 23044
  13.4 1.0 %copy-start.4 = (bf16[1,5,4,96,96]{4,3,2,1,0:T(8,128)(2,1)S(1)}, bf16[1,5,4,96,96]{4,3,2,1,0:T(8,128)(2,1)}, u32[]{:S(2)}) copy-start(bf16[1,5,4,96,96]{4,3,2,1,0:T(8,128)(2,1)} %maps_ref.1) | copy-start | bytes 1105924
  14.5 2.4 %copy-start.3 = (bf16[6,12,128,128]{3,2,1,0:T(8,128)(2,1)S(1)}, bf16[6,12,128,128]{3,2,1,0:T(8,128)(2,1)}, u32[]{:S(2)}) copy-start(bf16[6,12,128,128]{3,2,1,0:T(8,128)(2,1)} %tiles_ref.1) | copy-start | bytes 7077892
  14.5 5.7 %copy-start = (bf16[768,256]{1,0:T(8,128)(2,1)S(1)}, bf16[768,256]{1,0:T(8,128)(2,1)}, u32[]{:S(2)}) copy-start(bf16[768,256]{1,0:T(8,128)(2,1)} %omega_ref.1) | copy-start | bytes 1179652
  22.1 2.5 %collective-permute-start.3 = (bf16[400,768]{1,0:T(8,128)(2,1)S(1)}, bf16[400,768]{1,0:T(8,128)(2,1)S(1)}, u32[]{:S(2)}, u32[]{:S(2)}) collective-permute-start(bf16[400,768]{1,0:T(8,128)(2,1)S(1)} %get-tuple-element.32.sel_ref), channel_id=1, source_target_pairs={{0,1},{1,0},{2,3},{3,2},{4,5},{5,4},{6,7},{7,6},{8,9},{9,8},{10,11... | collective-permute-start | bytes 1843208 | tf_op jit(solution)/shard_map/ppermute | solution.py:320
  22.3 4.7 %collective-permute-start.2 = (bf16[192,128]{1,0:T(8,128)(2,1)}, bf16[192,128]{1,0:T(8,128)(2,1)S(1)}, u32[]{:S(2)}, u32[]{:S(2)}) collective-permute-start(bf16[192,128]{1,0:T(8,128)(2,1)} %get-tuple-element.31), channel_id=1, source_target_pairs={{0,1},{1,0},{2,3},{3,2},{4,5},{5,4},{6,7},{7,6},{8,9},{9,8},{10,11... | collective-permute-start | bytes 147464 | tf_op jit(solution)/shard_map/ppermute | solution.py:320
  24.9 3.9 %collective-permute-start.8 = (bf16[96,128]{1,0:T(8,128)(2,1)S(1)}, bf16[96,128]{1,0:T(8,128)(2,1)S(1)}, u32[]{:S(2)}, u32[]{:S(2)}) collective-permute-start(bf16[96,128]{1,0:T(8,128)(2,1)S(1)} %get-tuple-element.38), channel_id=1, source_target_pairs={{2,6},{3,7},{6,10},{7,11},{10,14},{11,15},{14,12},{15,13},{12,8},{... | collective-permute-start | bytes 73736 | tf_op jit(solution)/shard_map/ppermute | solution.py:385
  29.0 8.0 %collective-permute-start.9 = (bf16[288,128]{1,0:T(8,128)(2,1)S(1)}, bf16[288,128]{1,0:T(8,128)(2,1)S(1)}, u32[]{:S(2)}, u32[]{:S(2)}) collective-permute-start(bf16[288,128]{1,0:T(8,128)(2,1)S(1)} %shard_map.92.mine_ref), channel_id=1, source_target_pairs={{0,2},{1,3},{2,0},{3,1},{4,6},{5,7},{6,4},{7,5},{8,10},{9,11},{10,... | collective-permute-start | bytes 221192 | tf_op jit(solution)/shard_map/ppermute | solution.py:320
  31.1 4.1 %collective-permute-start.4 = (bf16[192,128]{1,0:T(8,128)(2,1)S(1)}, bf16[192,128]{1,0:T(8,128)(2,1)S(1)}, u32[]{:S(2)}, u32[]{:S(2)}) collective-permute-start(bf16[192,128]{1,0:T(8,128)(2,1)S(1)} %shard_map.87.mine_ref.after_ref.refs_0_), channel_id=1, source_target_pairs={{0,2},{1,3},{2,0},{3,1},{4,6},{5,7},{6,4},{7,5},{8,10},{9,11},{10,... | collective-permute-start | bytes 147464 | tf_op jit(solution)/shard_map/ppermute | solution.py:320
  35.4 4.2 %collective-permute-start.5 = (bf16[192,128]{1,0:T(8,128)(2,1)S(1)}, bf16[192,128]{1,0:T(8,128)(2,1)S(1)}, u32[]{:S(2)}, u32[]{:S(2)}) collective-permute-start(bf16[192,128]{1,0:T(8,128)(2,1)S(1)} %shard_map.88.mine_ref.refs_1_), channel_id=1, source_target_pairs={{0,4},{1,5},{2,6},{3,7},{4,0},{5,1},{6,2},{7,3},{8,12},{9,13},{10,... | collective-permute-start | bytes 147464 | tf_op jit(solution)/shard_map/ppermute | solution.py:320
  37.2 5.9 %collective-permute-start.10 = (bf16[192,128]{1,0:T(8,128)(2,1)S(1)}, bf16[192,128]{1,0:T(8,128)(2,1)S(1)}, u32[]{:S(2)}, u32[]{:S(2)}) collective-permute-start(bf16[192,128]{1,0:T(8,128)(2,1)S(1)} %get-tuple-element.40.mine_ref.refs_6_), channel_id=1, source_target_pairs={{0,4},{1,5},{2,6},{3,7},{4,0},{5,1},{6,2},{7,3},{8,12},{9,13},{10,... | collective-permute-start | bytes 147464 | tf_op jit(solution)/shard_map/ppermute | solution.py:320
  39.8 5.4 %collective-permute-start.6 = (bf16[192,128]{1,0:T(8,128)(2,1)S(1)}, bf16[192,128]{1,0:T(8,128)(2,1)S(1)}, u32[]{:S(2)}, u32[]{:S(2)}) collective-permute-start(bf16[192,128]{1,0:T(8,128)(2,1)S(1)} %shard_map.89.mine_ref.refs_2_), channel_id=1, source_target_pairs={{0,8},{1,9},{2,10},{3,11},{4,12},{5,13},{6,14},{7,15},{8,0},{9,1},... | collective-permute-start | bytes 147464 | tf_op jit(solution)/shard_map/ppermute | solution.py:320
  43.3 5.5 %collective-permute-start.11 = (bf16[192,128]{1,0:T(8,128)(2,1)S(1)}, bf16[192,128]{1,0:T(8,128)(2,1)S(1)}, u32[]{:S(2)}, u32[]{:S(2)}) collective-permute-start(bf16[192,128]{1,0:T(8,128)(2,1)S(1)} %shard_map.94.mine_ref.refs_7_), channel_id=1, source_target_pairs={{0,8},{1,9},{2,10},{3,11},{4,12},{5,13},{6,14},{7,15},{8,0},{9,1},... | collective-permute-start | bytes 147464 | tf_op jit(solution)/shard_map/ppermute | solution.py:320
  45.4 5.2 %collective-permute-start.7 = (bf16[192,128]{1,0:T(8,128)(2,1)S(1)}, bf16[192,128]{1,0:T(8,128)(2,1)S(1)}, u32[]{:S(2)}, u32[]{:S(2)}) collective-permute-start(bf16[192,128]{1,0:T(8,128)(2,1)S(1)} %shard_map.90.refs_3_), channel_id=1, source_target_pairs={{0,16},{16,0},{1,17},{17,1},{2,18},{18,2},{3,19},{19,3},{4,20},{20... | collective-permute-start | bytes 147464 | tf_op jit(solution)/shard_map/ppermute | solution.py:320
  49.0 4.2 %collective-permute-start.12 = (bf16[192,128]{1,0:T(8,128)(2,1)S(1)}, bf16[192,128]{1,0:T(8,128)(2,1)S(1)}, u32[]{:S(2)}, u32[]{:S(2)}) collective-permute-start(bf16[192,128]{1,0:T(8,128)(2,1)S(1)} %shard_map.95.refs_8_), channel_id=1, source_target_pairs={{0,16},{16,0},{1,17},{17,1},{2,18},{18,2},{3,19},{19,3},{4,20},{20... | collective-permute-start | bytes 147464 | tf_op jit(solution)/shard_map/ppermute | solution.py:320
  53.4 1.6 %collective-permute-start.13 = (bf16[5,2,96,128]{3,2,1,0:T(8,128)(2,1)S(1)}, bf16[5,2,96,128]{3,2,1,0:T(8,128)(2,1)S(1)}, u32[]{:S(2)}, u32[]{:S(2)}) collective-permute-start(bf16[5,2,96,128]{3,2,1,0:T(8,128)(2,1)S(1)} %shard_map.96.mine_ref), channel_id=1, source_target_pairs={{0,1},{1,0},{2,3},{3,2},{4,5},{5,4},{6,7},{7,6},{8,9},{9,8},{10,11... | collective-permute-start | bytes 737288 | tf_op jit(solution)/shard_map/ppermute | solution.py:320

commit v12 on v11

--- a/solution.py
+++ b/solution.py
@@ -392,11 +392,16 @@
     adj = call(
         adjoint_body,
         shape((2 * rank, half)),
-        (maps[0], sel, sel_other, panel, fwd),
+        (maps[0], sel, sel_other, panel, near_rims),
         specs="vvvva",
         flops=4 << 30,
     )
-    adj = call(rim_body, shape((3 * rank, half)), (sel, sel_other, near_rims, far_rims, adj))
+    adj = call(
+        rim_body,
+        shape((3 * rank, half)),
+        (sel, sel_other, near_rims, far_rims, adj),
+        flops=1000,
+    )
     new, node = call(
         functools.partial(joined_body, 1),
         [shape((2 * rank, half)), shape((rank, half))],
@@ -413,6 +418,7 @@
                         functools.partial(level_body, kind, axis, bit),
                         shape((2 * rank, half)),
                         (maps[level], chain[-1], swapped(chain[-1], axis, bit)),
+                        flops=4 << 30 if (level, kind) == (1, 0) else 1000,
                     )
                 )
     axis, bit = steps[-1]

time: 56.4 us -> 52.1 us (0.924)
  waiting for transfers between devices: 16.1 us -> 8.49 us
  starting transfers between devices: 24 us -> 27.2 us
    ppermute x12, waiting for transfers between devices: 13.1 us -> 6.49 us  [swapped(): lax.ppermute(x, axis, [(i, i ^ 1 << bit) for i in range(lax.axis_size(axi...]
    ppermute x12, starting transfers between devices: 15.4 us -> 18.6 us  [swapped(): lax.ppermute(x, axis, [(i, i ^ 1 << bit) for i in range(lax.axis_size(axi...]
    ppermute x1, waiting for transfers between devices: 0.97 us -> 0.01 us  [local(): far_rims = lax.ppermute(far_rims, 'sub', route)]
  transfers between devices with their start and end apart: 15 -> 15, of which waited for: 8 -> 8; matrix products, arithmetic and copies ran while one was open for 0% -> 0% of each run, Pallas kernels for 17% -> 19%
where the time goes in v12:
time: 52.1 us; the launch traced here: 51.7 us
  starting transfers between devices  27.2 us (52%)
  Pallas kernels  14 us (27%)
  waiting for transfers between devices  8.49 us (16%)
  local copies, waits for them, and re-layouts  1.75 us (3%)
    ppermute x12, starting transfers between devices, swapped(): lax.ppermute(x, axis, [(i, i ^ 1 << bit) for i in range(lax.axis_size(axi...  18.6 us
    pallas_call x16, Pallas kernels, call(): pl.pallas_call(body, out_shape=out_shape, in_specs=[SPACES[c] for c in sp...  14 us
    ppermute x12, waiting for transfers between devices, swapped(): lax.ppermute(x, axis, [(i, i ^ 1 << bit) for i in range(lax.axis_size(axi...  6.49 us
    all_to_all x1, starting transfers between devices, local(): lax.all_to_all(blocks, 'sub', split_axis=0, concat_axis=0, tiled=True, ax...  4.88 us
    ppermute x1, starting transfers between devices, local(): far_rims = lax.ppermute(far_rims, 'sub', route)  2.1 us
    all_to_all x1, waiting for transfers between devices, local(): lax.all_to_all(blocks, 'sub', split_axis=0, concat_axis=0, tiled=True, ax...  1.99 us
    unnamed x14, local copies, waits for them, and re-layouts  1.75 us
    ppermute x1, starting transfers between devices, local(): packed_outer = lax.ppermute(packed, 'sub', outward)  1.66 us
  transfers between devices with their start and end apart: 15, of which 8 were waited for; matrix products, arithmetic and copies ran while one was open for 0% of the time, Pallas kernels for 19%

profile of v12, /device:TPU:0, one launch (start us, length us, event | category | flops | bytes accessed | tf_op | source)
XLA Modules:
  0.0 51.7 jit_solution(16108863442920465436)
XLA Ops:
  0.0 2.8 %shard_map.84 = (bf16[8,16,1536]{2,1,0:T(8,128)(2,1)}, bf16[784,256]{1,0:T(8,128)(2,1)}) custom-call(bf16[16,12288]{1,0:T(8,128)(2,1)} %tests_hbm.1, bf16[768,256]{1,0:T(8,128)(2,1)} %omega_ref.1, s32[1,2,768]{2,1,0:T(2,128)} %perms_ref.5, s32[1,5,2,192]{3,2,1,0:T(2,128)} %nodes_ref.1), custom_call_target="tpu_custom_call" | custom-call | flops 1000 | bytes 1000 | tf_op jit(solution)/shard_map/pallas_call | solution.py:39
  2.8 1.7 %collective-permute-start.1 = (bf16[784,256]{1,0:T(8,128)(2,1)}, bf16[784,256]{1,0:T(8,128)(2,1)S(1)}, u32[]{:S(2)}, u32[]{:S(2)}) collective-permute-start(bf16[784,256]{1,0:T(8,128)(2,1)} %get-tuple-element.29), channel_id=1, source_target_pairs={{1,2},{3,4},{5,6},{7,8},{9,10},{11,12},{13,14},{2,1},{4,3},{6,5},{... | collective-permute-start | bytes 1204232 | tf_op jit(solution)/shard_map/ppermute | solution.py:349
  4.5 3.4 %collective-permute-start = (bf16[784,256]{1,0:T(8,128)(2,1)}, bf16[784,256]{1,0:T(8,128)(2,1)S(1)}, u32[]{:S(2)}, u32[]{:S(2)}) collective-permute-start(bf16[784,256]{1,0:T(8,128)(2,1)} %get-tuple-element.29), channel_id=1, source_target_pairs={{0,1},{1,0},{2,3},{3,2},{4,5},{5,4},{6,7},{7,6},{8,9},{9,8},{10,11... | collective-permute-start | bytes 1204232 | tf_op jit(solution)/shard_map/ppermute | solution.py:320
  7.8 4.9 %all-to-all-start = ((bf16[8,16,1536]{2,1,0:T(8,128)(2,1)}), bf16[8,16,1536]{2,1,0:T(8,128)(2,1)S(1)}, u32[]{:S(2)}, u32[]{:S(2)}) async-start(bf16[8,16,1536]{2,1,0:T(8,128)(2,1)} %get-tuple-element.33), calls=%async_computation | async-start | bytes 786432 | tf_op jit(solution)/shard_map/all_to_all | solution.py:352
  13.4 1.0 %copy-done.4 = bf16[1,5,4,96,96]{4,3,2,1,0:T(8,128)(2,1)S(1)} copy-done((bf16[1,5,4,96,96]{4,3,2,1,0:T(8,128)(2,1)S(1)}, bf16[1,5,4,96,96]{4,3,2,1,0:T(8,128)(2,1)}, u32[]{:S(2)}) %copy-start.4) | copy-done | bytes 368664
  14.5 2.4 %shard_map.82 = (bf16[2,2,288,96]{3,2,1,0:T(8,128)(2,1)S(1)}, bf16[2,2,288,96]{3,2,1,0:T(8,128)(2,1)S(1)}, bf16[2,2,288,96]{3,2,1,0:T(8,128)(2,1)S(1)}, bf16[2,2...) custom-call(bf16[1,5,4,96,96]{4,3,2,1,0:T(8,128)(2,1)S(1)} %copy-done.4, s32[1,5,2,192]{3,2,1,0:T(2,128)S(1)} %copy-done.1), custom_call_target="tpu_custom_call" | custom-call | flops 1073741824 | bytes 1000 | tf_op jit(solution)/shard_map/pallas_call | solution.py:39
  16.9 3.2 %shard_map.83 = (bf16[192,768]{1,0:T(8,128)(2,1)S(1)}, bf16[96,2304]{1,0:T(8,128)(2,1)S(1)}, bf16[96,768]{1,0:T(8,128)(2,1)S(1)}, bf16[768,2304]{1,0:T(8,128)(2,1)S(1)}) custom-call(s32[6,12]{1,0:T(8,128)S(1)} %copy-done.6, bf16[6,12,128,128]{3,2,1,0:T(8,128)(2,1)S(1)} %copy-done.3, s32[1,2,768]{2,1,0:T(2,128)S(1)} %copy-done.2, ...), custom_call_target="tpu_custom_call" | custom-call | flops 1073741824 | bytes 1000 | tf_op jit(solution)/shard_map/pallas_call | solution.py:39
  20.2 1.9 %shard_map.85 = (bf16[400,768]{1,0:T(8,128)(2,1)S(1)}, bf16[192,128]{1,0:T(8,128)(2,1)S(1)}, bf16[192,128]{1,0:T(8,128)(2,1)}) custom-call(bf16[192,768]{1,0:T(8,128)(2,1)S(1)} %get-tuple-element.25.keep_ref, bf16[768,2304]{1,0:T(8,128)(2,1)S(1)} %get-tuple-element.26.dense_ref, bf16[96,2304]{1,0:T(8,128)(2,1)S(1)} %get-tuple-element.27.near_ref, ...), custom_call_target="tpu_custom_call" | custom-call | flops 1000 | bytes 1000 | tf_op jit(solution)/shard_map/pallas_call | solution.py:39
  22.6 2.0 %all-to-all-done = bf16[8,16,1536]{2,1,0:T(8,128)(2,1)S(1)} async-done(((bf16[8,16,1536]{2,1,0:T(8,128)(2,1)}), bf16[8,16,1536]{2,1,0:T(8,128)(2,1)S(1)}, u32[]{:S(2)}, u32[]{:S(2)}) %all-to-all-start) | async-done | bytes 393248 | tf_op jit(solution)/shard_map/all_to_all | solution.py:352
  24.9 2.1 %collective-permute-start.8 = (bf16[96,128]{1,0:T(8,128)(2,1)S(1)}, bf16[96,128]{1,0:T(8,128)(2,1)S(1)}, u32[]{:S(2)}, u32[]{:S(2)}) collective-permute-start(bf16[96,128]{1,0:T(8,128)(2,1)S(1)} %get-tuple-element.38), channel_id=1, source_target_pairs={{2,6},{3,7},{6,10},{7,11},{10,14},{11,15},{14,12},{15,13},{12,8},{... | collective-permute-start | bytes 73736 | tf_op jit(solution)/shard_map/ppermute | solution.py:385
  27.1 1.6 %collective-permute-start.4 = (bf16[192,128]{1,0:T(8,128)(2,1)S(1)}, bf16[192,128]{1,0:T(8,128)(2,1)S(1)}, u32[]{:S(2)}, u32[]{:S(2)}) collective-permute-start(bf16[192,128]{1,0:T(8,128)(2,1)S(1)} %shard_map.87.mine_ref.refs_0_), channel_id=1, source_target_pairs={{0,2},{1,3},{2,0},{3,1},{4,6},{5,7},{6,4},{7,5},{8,10},{9,11},{10,... | collective-permute-start | bytes 147464 | tf_op jit(solution)/shard_map/ppermute | solution.py:320
  29.7 1.4 %collective-permute-start.9 = (bf16[288,128]{1,0:T(8,128)(2,1)S(1)}, bf16[288,128]{1,0:T(8,128)(2,1)S(1)}, u32[]{:S(2)}, u32[]{:S(2)}) collective-permute-start(bf16[288,128]{1,0:T(8,128)(2,1)S(1)} %shard_map.92.mine_ref), channel_id=1, source_target_pairs={{0,2},{1,3},{2,0},{3,1},{4,6},{5,7},{6,4},{7,5},{8,10},{9,11},{10,... | collective-permute-start | bytes 221192 | tf_op jit(solution)/shard_map/ppermute | solution.py:320
  31.5 1.8 %collective-permute-start.5 = (bf16[192,128]{1,0:T(8,128)(2,1)S(1)}, bf16[192,128]{1,0:T(8,128)(2,1)S(1)}, u32[]{:S(2)}, u32[]{:S(2)}) collective-permute-start(bf16[192,128]{1,0:T(8,128)(2,1)S(1)} %shard_map.88.mine_ref.refs_1_), channel_id=1, source_target_pairs={{0,4},{1,5},{2,6},{3,7},{4,0},{5,1},{6,2},{7,3},{8,12},{9,13},{10,... | collective-permute-start | bytes 147464 | tf_op jit(solution)/shard_map/ppermute | solution.py:320
  33.3 0.8 %collective-permute-done.9.other_ref = bf16[288,128]{1,0:T(8,128)(2,1)S(1)} collective-permute-done((bf16[288,128]{1,0:T(8,128)(2,1)S(1)}, bf16[288,128]{1,0:T(8,128)(2,1)S(1)}, u32[]{:S(2)}, u32[]{:S(2)}) %collective-permute-start.9) | collective-permute-done | bytes 73760 | tf_op jit(solution)/shard_map/ppermute | solution.py:320
  34.3 2.2 %collective-permute-start.10 = (bf16[192,128]{1,0:T(8,128)(2,1)S(1)}, bf16[192,128]{1,0:T(8,128)(2,1)S(1)}, u32[]{:S(2)}, u32[]{:S(2)}) collective-permute-start(bf16[192,128]{1,0:T(8,128)(2,1)S(1)} %get-tuple-element.40.mine_ref.refs_6_), channel_id=1, source_target_pairs={{0,4},{1,5},{2,6},{3,7},{4,0},{5,1},{6,2},{7,3},{8,12},{9,13},{10,... | collective-permute-start | bytes 147464 | tf_op jit(solution)/shard_map/ppermute | solution.py:320
  36.7 2.5 %collective-permute-start.6 = (bf16[192,128]{1,0:T(8,128)(2,1)S(1)}, bf16[192,128]{1,0:T(8,128)(2,1)S(1)}, u32[]{:S(2)}, u32[]{:S(2)}) collective-permute-start(bf16[192,128]{1,0:T(8,128)(2,1)S(1)} %shard_map.89.mine_ref.refs_2_), channel_id=1, source_target_pairs={{0,8},{1,9},{2,10},{3,11},{4,12},{5,13},{6,14},{7,15},{8,0},{9,1},... | collective-permute-start | bytes 147464 | tf_op jit(solution)/shard_map/ppermute | solution.py:320
  39.4 1.9 %collective-permute-start.11 = (bf16[192,128]{1,0:T(8,128)(2,1)S(1)}, bf16[192,128]{1,0:T(8,128)(2,1)S(1)}, u32[]{:S(2)}, u32[]{:S(2)}) collective-permute-start(bf16[192,128]{1,0:T(8,128)(2,1)S(1)} %shard_map.94.mine_ref.refs_7_), channel_id=1, source_target_pairs={{0,8},{1,9},{2,10},{3,11},{4,12},{5,13},{6,14},{7,15},{8,0},{9,1},... | collective-permute-start | bytes 147464 | tf_op jit(solution)/shard_map/ppermute | solution.py:320
  41.3 1.3 %collective-permute-done.6.other_ref = bf16[192,128]{1,0:T(8,128)(2,1)S(1)} collective-permute-done((bf16[192,128]{1,0:T(8,128)(2,1)S(1)}, bf16[192,128]{1,0:T(8,128)(2,1)S(1)}, u32[]{:S(2)}, u32[]{:S(2)}) %collective-permute-start.6) | collective-permute-done | bytes 49184 | tf_op jit(solution)/shard_map/ppermute | solution.py:320
  42.8 1.6 %collective-permute-start.7 = (bf16[192,128]{1,0:T(8,128)(2,1)S(1)}, bf16[192,128]{1,0:T(8,128)(2,1)S(1)}, u32[]{:S(2)}, u32[]{:S(2)}) collective-permute-start(bf16[192,128]{1,0:T(8,128)(2,1)S(1)} %shard_map.90.refs_3_), channel_id=1, source_target_pairs={{0,16},{16,0},{1,17},{17,1},{2,18},{18,2},{3,19},{19,3},{4,20},{20... | collective-permute-start | bytes 147464 | tf_op jit(solution)/shard_map/ppermute | solution.py:320
  44.6 1.6 %collective-permute-start.12 = (bf16[192,128]{1,0:T(8,128)(2,1)S(1)}, bf16[192,128]{1,0:T(8,128)(2,1)S(1)}, u32[]{:S(2)}, u32[]{:S(2)}) collective-permute-start(bf16[192,128]{1,0:T(8,128)(2,1)S(1)} %shard_map.95.refs_8_), channel_id=1, source_target_pairs={{0,16},{16,0},{1,17},{17,1},{2,18},{18,2},{3,19},{19,3},{4,20},{20... | collective-permute-start | bytes 147464 | tf_op jit(solution)/shard_map/ppermute | solution.py:320
  46.2 0.7 %collective-permute-done.7.refs_4_ = bf16[192,128]{1,0:T(8,128)(2,1)S(1)} collective-permute-done((bf16[192,128]{1,0:T(8,128)(2,1)S(1)}, bf16[192,128]{1,0:T(8,128)(2,1)S(1)}, u32[]{:S(2)}, u32[]{:S(2)}) %collective-permute-start.7) | collective-permute-done | bytes 49184 | tf_op jit(solution)/shard_map/ppermute | solution.py:320
  46.9 1.8 %collective-permute-done.12.refs_9_ = bf16[192,128]{1,0:T(8,128)(2,1)S(1)} collective-permute-done((bf16[192,128]{1,0:T(8,128)(2,1)S(1)}, bf16[192,128]{1,0:T(8,128)(2,1)S(1)}, u32[]{:S(2)}, u32[]{:S(2)}) %collective-permute-start.12) | collective-permute-done | bytes 49184 | tf_op jit(solution)/shard_map/ppermute | solution.py:320
  49.1 1.5 %collective-permute-done.13.other_ref = bf16[5,2,96,128]{3,2,1,0:T(8,128)(2,1)S(1)} collective-permute-done((bf16[5,2,96,128]{3,2,1,0:T(8,128)(2,1)S(1)}, bf16[5,2,96,128]{3,2,1,0:T(8,128)(2,1)S(1)}, u32[]{:S(2)}, u32[]{:S(2)}) %collective-permute-start.13) | collective-permute-done | bytes 245792 | tf_op jit(solution)/shard_map/ppermute | solution.py:320
  50.6 1.1 %shard_map.97 = bf16[1,5,2,96,256]{4,3,2,1,0:T(8,128)(2,1)} custom-call(bf16[5,2,96,128]{3,2,1,0:T(8,128)(2,1)S(1)} %shard_map.96.mine_ref, bf16[5,2,96,128]{3,2,1,0:T(8,128)(2,1)S(1)} %collective-permute-done.13.other_ref), custom_call_target="tpu_custom_call" | custom-call | flops 1000 | bytes 1000 | tf_op jit(solution)/shard_map/pallas_call | solution.py:39
  (36 shorter events, 4.2 us)
Async XLA Ops:
  0.0 16.8 %copy-start.2 = (s32[1,2,768]{2,1,0:T(2,128)S(1)}, s32[1,2,768]{2,1,0:T(2,128)}, u32[]{:S(2)}) copy-start(s32[1,2,768]{2,1,0:T(2,128)} %perms_ref.5) | copy-start | bytes 18436
  0.0 16.9 %copy-start.5 = (bf16[1,2,672,96]{2,3,1,0:T(8,128)(2,1)S(1)}, bf16[1,2,672,96]{2,3,1,0:T(8,128)(2,1)}, u32[]{:S(2)}) copy-start(bf16[1,2,672,96]{2,3,1,0:T(8,128)(2,1)} %param.13) | copy-start | bytes 774148
  0.0 16.9 %copy-start.6 = (s32[6,12]{1,0:T(8,128)S(1)}, s32[6,12]{1,0:T(8,128)}, u32[]{:S(2)}) copy-start(s32[6,12]{1,0:T(8,128)} %cols_ref.1) | copy-start | bytes 868
  2.8 17.3 %collective-permute-start.1 = (bf16[784,256]{1,0:T(8,128)(2,1)}, bf16[784,256]{1,0:T(8,128)(2,1)S(1)}, u32[]{:S(2)}, u32[]{:S(2)}) collective-permute-start(bf16[784,256]{1,0:T(8,128)(2,1)} %get-tuple-element.29), channel_id=1, source_target_pairs={{1,2},{3,4},{5,6},{7,8},{9,10},{11,12},{13,14},{2,1},{4,3},{6,5},{... | collective-permute-start | bytes 1204232 | tf_op jit(solution)/shard_map/ppermute | solution.py:349
  4.5 15.7 %collective-permute-start = (bf16[784,256]{1,0:T(8,128)(2,1)}, bf16[784,256]{1,0:T(8,128)(2,1)S(1)}, u32[]{:S(2)}, u32[]{:S(2)}) collective-permute-start(bf16[784,256]{1,0:T(8,128)(2,1)} %get-tuple-element.29), channel_id=1, source_target_pairs={{0,1},{1,0},{2,3},{3,2},{4,5},{5,4},{6,7},{7,6},{8,9},{9,8},{10,11... | collective-permute-start | bytes 1204232 | tf_op jit(solution)/shard_map/ppermute | solution.py:320
  7.8 16.7 %all-to-all-start = ((bf16[8,16,1536]{2,1,0:T(8,128)(2,1)}), bf16[8,16,1536]{2,1,0:T(8,128)(2,1)S(1)}, u32[]{:S(2)}, u32[]{:S(2)}) async-start(bf16[8,16,1536]{2,1,0:T(8,128)(2,1)} %get-tuple-element.33), calls=%async_computation | async-start | bytes 786432 | tf_op jit(solution)/shard_map/all_to_all | solution.py:352
  12.7 0.7 %copy-start.1 = (s32[1,5,2,192]{3,2,1,0:T(2,128)S(1)}, s32[1,5,2,192]{3,2,1,0:T(2,128)}, u32[]{:S(2)}) copy-start(s32[1,5,2,192]{3,2,1,0:T(2,128)} %nodes_ref.1) | copy-start | bytes 23044
  13.4 1.0 %copy-start.4 = (bf16[1,5,4,96,96]{4,3,2,1,0:T(8,128)(2,1)S(1)}, bf16[1,5,4,96,96]{4,3,2,1,0:T(8,128)(2,1)}, u32[]{:S(2)}) copy-start(bf16[1,5,4,96,96]{4,3,2,1,0:T(8,128)(2,1)} %maps_ref.1) | copy-start | bytes 1105924
  14.5 2.4 %copy-start.3 = (bf16[6,12,128,128]{3,2,1,0:T(8,128)(2,1)S(1)}, bf16[6,12,128,128]{3,2,1,0:T(8,128)(2,1)}, u32[]{:S(2)}) copy-start(bf16[6,12,128,128]{3,2,1,0:T(8,128)(2,1)} %tiles_ref.1) | copy-start | bytes 7077892
  14.5 5.7 %copy-start = (bf16[768,256]{1,0:T(8,128)(2,1)S(1)}, bf16[768,256]{1,0:T(8,128)(2,1)}, u32[]{:S(2)}) copy-start(bf16[768,256]{1,0:T(8,128)(2,1)} %omega_ref.1) | copy-start | bytes 1179652
  22.1 2.5 %collective-permute-start.3 = (bf16[400,768]{1,0:T(8,128)(2,1)S(1)}, bf16[400,768]{1,0:T(8,128)(2,1)S(1)}, u32[]{:S(2)}, u32[]{:S(2)}) collective-permute-start(bf16[400,768]{1,0:T(8,128)(2,1)S(1)} %get-tuple-element.32.sel_ref), channel_id=1, source_target_pairs={{0,1},{1,0},{2,3},{3,2},{4,5},{5,4},{6,7},{7,6},{8,9},{9,8},{10,11... | collective-permute-start | bytes 1843208 | tf_op jit(solution)/shard_map/ppermute | solution.py:320
  22.3 4.7 %collective-permute-start.2 = (bf16[192,128]{1,0:T(8,128)(2,1)}, bf16[192,128]{1,0:T(8,128)(2,1)S(1)}, u32[]{:S(2)}, u32[]{:S(2)}) collective-permute-start(bf16[192,128]{1,0:T(8,128)(2,1)} %get-tuple-element.31), channel_id=1, source_target_pairs={{0,1},{1,0},{2,3},{3,2},{4,5},{5,4},{6,7},{7,6},{8,9},{9,8},{10,11... | collective-permute-start | bytes 147464 | tf_op jit(solution)/shard_map/ppermute | solution.py:320
  24.9 4.5 %collective-permute-start.8 = (bf16[96,128]{1,0:T(8,128)(2,1)S(1)}, bf16[96,128]{1,0:T(8,128)(2,1)S(1)}, u32[]{:S(2)}, u32[]{:S(2)}) collective-permute-start(bf16[96,128]{1,0:T(8,128)(2,1)S(1)} %get-tuple-element.38), channel_id=1, source_target_pairs={{2,6},{3,7},{6,10},{7,11},{10,14},{11,15},{14,12},{15,13},{12,8},{... | collective-permute-start | bytes 73736 | tf_op jit(solution)/shard_map/ppermute | solution.py:385
  27.1 4.2 %collective-permute-start.4 = (bf16[192,128]{1,0:T(8,128)(2,1)S(1)}, bf16[192,128]{1,0:T(8,128)(2,1)S(1)}, u32[]{:S(2)}, u32[]{:S(2)}) collective-permute-start(bf16[192,128]{1,0:T(8,128)(2,1)S(1)} %shard_map.87.mine_ref.refs_0_), channel_id=1, source_target_pairs={{0,2},{1,3},{2,0},{3,1},{4,6},{5,7},{6,4},{7,5},{8,10},{9,11},{10,... | collective-permute-start | bytes 147464 | tf_op jit(solution)/shard_map/ppermute | solution.py:320
  29.7 4.4 %collective-permute-start.9 = (bf16[288,128]{1,0:T(8,128)(2,1)S(1)}, bf16[288,128]{1,0:T(8,128)(2,1)S(1)}, u32[]{:S(2)}, u32[]{:S(2)}) collective-permute-start(bf16[288,128]{1,0:T(8,128)(2,1)S(1)} %shard_map.92.mine_ref), channel_id=1, source_target_pairs={{0,2},{1,3},{2,0},{3,1},{4,6},{5,7},{6,4},{7,5},{8,10},{9,11},{10,... | collective-permute-start | bytes 221192 | tf_op jit(solution)/shard_map/ppermute | solution.py:320
  31.5 5.0 %collective-permute-start.5 = (bf16[192,128]{1,0:T(8,128)(2,1)S(1)}, bf16[192,128]{1,0:T(8,128)(2,1)S(1)}, u32[]{:S(2)}, u32[]{:S(2)}) collective-permute-start(bf16[192,128]{1,0:T(8,128)(2,1)S(1)} %shard_map.88.mine_ref.refs_1_), channel_id=1, source_target_pairs={{0,4},{1,5},{2,6},{3,7},{4,0},{5,1},{6,2},{7,3},{8,12},{9,13},{10,... | collective-permute-start | bytes 147464 | tf_op jit(solution)/shard_map/ppermute | solution.py:320
  34.3 4.9 %collective-permute-start.10 = (bf16[192,128]{1,0:T(8,128)(2,1)S(1)}, bf16[192,128]{1,0:T(8,128)(2,1)S(1)}, u32[]{:S(2)}, u32[]{:S(2)}) collective-permute-start(bf16[192,128]{1,0:T(8,128)(2,1)S(1)} %get-tuple-element.40.mine_ref.refs_6_), channel_id=1, source_target_pairs={{0,4},{1,5},{2,6},{3,7},{4,0},{5,1},{6,2},{7,3},{8,12},{9,13},{10,... | collective-permute-start | bytes 147464 | tf_op jit(solution)/shard_map/ppermute | solution.py:320
  36.7 5.9 %collective-permute-start.6 = (bf16[192,128]{1,0:T(8,128)(2,1)S(1)}, bf16[192,128]{1,0:T(8,128)(2,1)S(1)}, u32[]{:S(2)}, u32[]{:S(2)}) collective-permute-start(bf16[192,128]{1,0:T(8,128)(2,1)S(1)} %shard_map.89.mine_ref.refs_2_), channel_id=1, source_target_pairs={{0,8},{1,9},{2,10},{3,11},{4,12},{5,13},{6,14},{7,15},{8,0},{9,1},... | collective-permute-start | bytes 147464 | tf_op jit(solution)/shard_map/ppermute | solution.py:320
  39.4 5.1 %collective-permute-start.11 = (bf16[192,128]{1,0:T(8,128)(2,1)S(1)}, bf16[192,128]{1,0:T(8,128)(2,1)S(1)}, u32[]{:S(2)}, u32[]{:S(2)}) collective-permute-start(bf16[192,128]{1,0:T(8,128)(2,1)S(1)} %shard_map.94.mine_ref.refs_7_), channel_id=1, source_target_pairs={{0,8},{1,9},{2,10},{3,11},{4,12},{5,13},{6,14},{7,15},{8,0},{9,1},... | collective-permute-start | bytes 147464 | tf_op jit(solution)/shard_map/ppermute | solution.py:320
  42.8 4.2 %collective-permute-start.7 = (bf16[192,128]{1,0:T(8,128)(2,1)S(1)}, bf16[192,128]{1,0:T(8,128)(2,1)S(1)}, u32[]{:S(2)}, u32[]{:S(2)}) collective-permute-start(bf16[192,128]{1,0:T(8,128)(2,1)S(1)} %shard_map.90.refs_3_), channel_id=1, source_target_pairs={{0,16},{16,0},{1,17},{17,1},{2,18},{18,2},{3,19},{19,3},{4,20},{20... | collective-permute-start | bytes 147464 | tf_op jit(solution)/shard_map/ppermute | solution.py:320
  44.6 4.2 %collective-permute-start.12 = (bf16[192,128]{1,0:T(8,128)(2,1)S(1)}, bf16[192,128]{1,0:T(8,128)(2,1)S(1)}, u32[]{:S(2)}, u32[]{:S(2)}) collective-permute-start(bf16[192,128]{1,0:T(8,128)(2,1)S(1)} %shard_map.95.refs_8_), channel_id=1, source_target_pairs={{0,16},{16,0},{1,17},{17,1},{2,18},{18,2},{3,19},{19,3},{4,20},{20... | collective-permute-start | bytes 147464 | tf_op jit(solution)/shard_map/ppermute | solution.py:320
  49.0 1.6 %collective-permute-start.13 = (bf16[5,2,96,128]{3,2,1,0:T(8,128)(2,1)S(1)}, bf16[5,2,96,128]{3,2,1,0:T(8,128)(2,1)S(1)}, u32[]{:S(2)}, u32[]{:S(2)}) collective-permute-start(bf16[5,2,96,128]{3,2,1,0:T(8,128)(2,1)S(1)} %shard_map.96.mine_ref), channel_id=1, source_target_pairs={{0,1},{1,0},{2,3},{3,2},{4,5},{5,4},{6,7},{7,6},{8,9},{9,8},{10,11... | collective-permute-start | bytes 737288 | tf_op jit(solution)/shard_map/ppermute | solution.py:320

commit v13 on v12

--- a/solution.py
+++ b/solution.py
@@ -55,7 +55,19 @@
 
 
 def pack_body(
-    width, tests_hbm, omega_hbm, perms_ref, nodes_ref, out_hbm, packed_hbm, tests_ref, omega_ref, order_ref, sems
+    width,
+    tests_hbm,
+    omega_hbm,
+    perms_hbm,
+    nodes_hbm,
+    out_hbm,
+    packed_hbm,
+    tests_ref,
+    omega_ref,
+    perms_ref,
+    nodes_ref,
+    order_ref,
+    sems,
 ):
     rows = omega_ref.shape[0]
     chips = out_hbm.shape[0]
@@ -67,8 +79,14 @@
             pltpu.make_async_copy(tests_hbm.at[:, part], tests_ref.at[chip], sems.at[2 + 2 * chip])
         )
         go.append(pltpu.make_async_copy(tests_ref.at[chip], out_hbm.at[chip], sems.at[3 + 2 * chip]))
-    for copy in come:
+    small = [
+        pltpu.make_async_copy(perms_hbm, perms_ref, sems.at[3 + 2 * chips]),
+        pltpu.make_async_copy(nodes_hbm, nodes_ref, sems.at[4 + 2 * chips]),
+    ]
+    for copy in small + come:
         copy.start()
+    for copy in small:
+        copy.wait()
     kept = nodes_ref.shape[-1] // 2
     for order, at in ((perms_ref[0, 1:2, :kept], 0), (nodes_ref[0, 0, 1:2, :kept], 2)):
         row = lax.broadcasted_iota(jnp.int32, (order_ref.shape[0], kept), 0)
@@ -133,7 +151,6 @@
     outer_ref,
     sel_ref,
     mine_ref,
-    other_ref,
 ):
     rows = dense_ref.shape[0]
     rank = near_ref.shape[0]
@@ -145,9 +162,11 @@
         keep = mm_t(unit, one_hot(from_digits(ref[rows:, :rank], 0), rows)).astype(BF)
         block = dense_ref[:, b * rows : (b + 1) * rows]
         sel_ref[(b + 1) * rank : (b + 2) * rank] = mm_t(keep, block).astype(BF)
-    sel_ref[4 * rank :] = jnp.zeros_like(sel_ref[4 * rank :])
-    sel_ref[4 * rank :, : outer_ref.shape[1]] = outer_ref[rows:]
-    for out_ref, place in ((mine_ref, core), (other_ref, 1 - core)):
+    spare = sel_ref.shape[0] - 4 * rank
+    sel_ref[4 * rank :] = jnp.zeros((spare, rows), BF)
+    sel_ref[4 * rank : 4 * rank + 16, : outer_ref.shape[1]] = outer_ref[rows:]
+    panels = []
+    for place in (core, 1 - core):
         cols = pl.ds(pl.multiple_of(place * half, half), half)
         own = omega_ref[:, cols]
         fwd = (
@@ -155,13 +174,18 @@
             + mm(near_ref[:, rows : 2 * rows], inner_ref[:rows, cols])
             + mm(near_ref[:, 2 * rows :], outer_ref[:rows, cols])
         )
-        out_ref[:rank] = fwd.astype(BF)
-        out_ref[rank:] = mm(tests_ref[...], own).astype(BF)
-
-
-def maps_body(maps_ref, perms_ref, *out_refs):
+        panels.append(jnp.concatenate([fwd, mm(tests_ref[...], own)], axis=0).astype(BF))
+    mine_ref[...] = panels[0]
+    height = sel_ref.shape[0] - 4 * rank - 16
+    for at in range(2 * rank // height):
+        part = panels[1][at * height : (at + 1) * height]
+        sel_ref[4 * rank + 16 :, at * half : (at + 1) * half] = part
+
+
+def maps_body(maps_ref, perms_ref, order_ref, *out_refs):
     rank = maps_ref.shape[-1]
     unit = eye(rank)
+    order_ref[...] = jnp.zeros_like(order_ref)
     for level, out_ref in enumerate(out_refs):
         row_interp, col_interp, low_high, high_low = (maps_ref[0, level, i] for i in range(4))
         row_hot = one_hot(perms_ref[0, level, 0:1, :], 2 * rank)
@@ -193,12 +217,18 @@
     return kept + wide[:rank], wide[rank:]
 
 
-def node_body(maps_ref, mine_ref, other_ref, after_ref, out_ref):
+def node_body(maps_ref, mine_ref, sel_other, after_ref, out_ref):
     del after_ref
     rank = mine_ref.shape[0] // 2
-    core = lax.axis_index("sub") & 1
+    half = mine_ref.shape[1]
+    core = lax.axis_index("sub") & 1
+    height = sel_other.shape[0] - 4 * rank - 16
+    parts = [
+        sel_other[4 * rank + 16 :, at * half : (at + 1) * half] for at in range(2 * rank // height)
+    ]
+    other = jnp.concatenate(parts, axis=0)
     kept, tests = merged(
-        maps_ref, 0, core, mine_ref[:rank], mine_ref[rank:], other_ref[:rank], other_ref[rank:], rank
+        maps_ref, 0, core, mine_ref[:rank], mine_ref[rank:], other[:rank], other[rank:], rank
     )
     out_ref[:rank] = kept.astype(BF)
     out_ref[rank:] = tests.astype(BF)
@@ -244,7 +274,7 @@
 def rim_body(sel_ref, sel_other, near_ref, far_ref, adj_ref, out_ref):
     rank = near_ref.shape[0]
     chip = (lax.axis_index("sub") >> 1) & 1
-    digits = [ref[4 * rank :, :rank].astype(F32) for ref in (sel_ref, sel_other)]
+    digits = [ref[4 * rank : 4 * rank + 16, :rank].astype(F32) for ref in (sel_ref, sel_other)]
     order = from_digits(jnp.where(near_rim(), *digits), 2)
     hot = one_hot(order, 2 * rank)
     keeps = [mm_t(eye(rank), hot[side * rank : (side + 1) * rank]) for side in range(2)]
@@ -299,7 +329,7 @@
         out_ref[levels - 1, kind] = kept.astype(BF)
 
 
-def output_body(vectors, mine_ref, other_ref, out_ref):
+def output_body(vectors, mine_ref, other_ref, out_hbm, out_ref, sems):
     half = mine_ref.shape[-1]
     core = lax.axis_index("sub") & 1
     k = lax.broadcasted_iota(jnp.int32, (half, 2 * half), 0)
@@ -309,11 +339,16 @@
     to_other = jnp.where(s == base + (1 - core) * vectors, 1.0, 0.0).astype(BF)
     mine_cols = pl.ds(pl.multiple_of(core * half, half), half)
     other_cols = pl.ds(pl.multiple_of((1 - core) * half, half), half)
+    copies = []
     for level in range(mine_ref.shape[0]):
         mine, other = mine_ref[level], other_ref[level]
-        out_ref[0, level, 0, :, mine_cols] = mine[0]
-        out_ref[0, level, 0, :, other_cols] = other[0]
-        out_ref[0, level, 1] = (mm(mine[1], to_mine) + mm(other[1], to_other)).astype(BF)
+        out_ref[level, 0, :, mine_cols] = mine[0]
+        out_ref[level, 0, :, other_cols] = other[0]
+        out_ref[level, 1] = (mm(mine[1], to_mine) + mm(other[1], to_other)).astype(BF)
+        copies.append(pltpu.make_async_copy(out_ref.at[level], out_hbm.at[0, level], sems.at[level]))
+        copies[-1].start()
+    for copy in copies:
+        copy.wait()
 
 
 def swapped(x, axis, bit):
@@ -339,10 +374,12 @@
         scratch=[
             pltpu.VMEM((chips, vectors, 2 * rows), BF),
             pltpu.VMEM(omega.shape, BF),
+            pltpu.VMEM(leaf_perms.shape, jnp.int32),
+            pltpu.VMEM(node_perms.shape, jnp.int32),
             pltpu.VMEM((16, samples), BF),
-            pltpu.SemaphoreType.DMA((2 * chips + 3,)),
+            pltpu.SemaphoreType.DMA((2 * chips + 5,)),
         ],
-        specs="hhvv",
+        specs="hhhh",
         out="a",
         limit=56 << 20,
     )
@@ -354,9 +391,9 @@
     ).reshape(half, 2 * rows)
 
     tables = shape((2, 2, 3 * rank, rank))
-    maps = call(
+    order, *maps = call(
         maps_body,
-        [tables] * levels,
+        [shape((16, 128))] + [tables] * levels,
         (node_maps, node_perms),
         flops=1 << 30,
     )
@@ -368,17 +405,19 @@
             shape((rank, rows)),
             shape((rows, 3 * rows)),
         ],
-        (tile_cols, near_tiles, leaf_perms, jnp.swapaxes(leaf_interp, 2, 3), maps[0]),
+        (tile_cols, near_tiles, leaf_perms, jnp.swapaxes(leaf_interp, 2, 3), order),
         specs="svvva",
         flops=1 << 30,
     )
-    sel, fwd_mine, fwd_send = call(
+    height = -(-2 * rank * half // rows // 16) * 16
+    while 2 * rank % height:
+        height += 16
+    sel, fwd_mine = call(
         halo_body,
-        [shape((4 * rank + 16, rows))] + [shape((2 * rank, half))] * 2,
+        [shape((4 * rank + 16 + height, rows)), shape((2 * rank, half))],
         (keep, dense, near, tests, omega, packed_inner, packed_outer),
     )
     sel_other = swapped(sel, "sub", 0)
-    fwd_other = swapped(fwd_send, "sub", 0)
     near_rims, far_rims = call(edge_body, [shape((rank, half))] * 2, (sel, sel_other, panel))
     ring = list(range(1, chips, 2)) + list(range(chips - 2, -1, -2))
     route = [(2 * a + c, 2 * b + c) for a, b in zip(ring, ring[1:] + ring[:1]) for c in range(2)]
@@ -386,7 +425,7 @@
     fwd = call(
         node_body,
         shape((2 * rank, half)),
-        (maps[0], fwd_mine, fwd_other, near_rims),
+        (maps[0], fwd_mine, sel_other, near_rims),
         specs="vvva",
     )
     adj = call(
@@ -432,6 +471,8 @@
         functools.partial(output_body, vectors),
         shape((1, levels, 2, rank, samples)),
         (x, swapped(x, "sub", 0)),
+        scratch=[pltpu.VMEM((levels, 2, rank, samples), BF), pltpu.SemaphoreType.DMA((levels,))],
+        out="a",
     )
 
 

time: 52.1 us -> 51.7 us (level)
  waiting for transfers between devices: 8.49 us -> 11.8 us
  starting transfers between devices: 27.2 us -> 23.9 us
  Pallas kernels: 14 us -> 12.7 us
  local copies, waits for them, and re-layouts: 1.75 us -> 2.71 us
    ppermute x12 -> x11, starting transfers between devices: 18.6 us -> 15.8 us  [swapped(): lax.ppermute(x, axis, [(i, i ^ 1 << bit) for i in range(lax.axis_size(axi...]
    ppermute x12 -> x11, waiting for transfers between devices: 6.49 us -> 9 us  [swapped(): lax.ppermute(x, axis, [(i, i ^ 1 << bit) for i in range(lax.axis_size(axi...]
    pallas_call x16, Pallas kernels: 14 us -> 12.7 us  [call(): pl.pallas_call(body, out_shape=out_shape, in_specs=[SPACES[c] for c in sp...]
    unnamed x14 -> x18, local copies, waits for them, and re-layouts: 1.75 us -> 2.71 us
    all_to_all x1, waiting for transfers between devices: 1.99 us -> 2.84 us  [local(): lax.all_to_all(blocks, 'sub', split_axis=0, concat_axis=0, tiled=True, ax...]
    ppermute x1, starting transfers between devices: 2.1 us -> 1.55 us  [local(): far_rims = lax.ppermute(far_rims, 'sub', route)]
  transfers between devices with their start and end apart: 15 -> 14, of which waited for: 8 -> 8; matrix products, arithmetic and copies ran while one was open for 0% -> 0% of each run, Pallas kernels for 19% -> 18%
where the time goes in v13:
time: 51.7 us; the launch traced here: 51.3 us
  starting transfers between devices  23.9 us (46%)
  Pallas kernels  12.7 us (25%)
  waiting for transfers between devices  11.8 us (23%)
  local copies, waits for them, and re-layouts  2.71 us (5%)
    ppermute x11, starting transfers between devices, swapped(): lax.ppermute(x, axis, [(i, i ^ 1 << bit) for i in range(lax.axis_size(axi...  15.8 us
    pallas_call x16, Pallas kernels, call(): pl.pallas_call(body, out_shape=out_shape, in_specs=[SPACES[c] for c in sp...  12.7 us
    ppermute x11, waiting for transfers between devices, swapped(): lax.ppermute(x, axis, [(i, i ^ 1 << bit) for i in range(lax.axis_size(axi...  9 us
    all_to_all x1, starting transfers between devices, local(): lax.all_to_all(blocks, 'sub', split_axis=0, concat_axis=0, tiled=True, ax...  4.88 us
    all_to_all x1, waiting for transfers between devices, local(): lax.all_to_all(blocks, 'sub', split_axis=0, concat_axis=0, tiled=True, ax...  2.84 us
    unnamed x18, local copies, waits for them, and re-layouts  2.71 us
    ppermute x1, starting transfers between devices, local(): packed_outer = lax.ppermute(packed, 'sub', outward)  1.66 us
    ppermute x1, starting transfers between devices, local(): far_rims = lax.ppermute(far_rims, 'sub', route)  1.55 us
  transfers between devices with their start and end apart: 14, of which 8 were waited for; matrix products, arithmetic and copies ran while one was open for 0% of the time, Pallas kernels for 18%

profile of v13, /device:TPU:0, one launch (start us, length us, event | category | flops | bytes accessed | tf_op | source)
XLA Modules:
  0.0 51.3 jit_solution(17529729111076619198)
XLA Ops:
  0.0 2.1 %shard_map.84 = (bf16[8,16,1536]{2,1,0:T(8,128)(2,1)}, bf16[784,256]{1,0:T(8,128)(2,1)}) custom-call(bf16[16,12288]{1,0:T(8,128)(2,1)} %tests_hbm.1, bf16[768,256]{1,0:T(8,128)(2,1)} %omega_ref.1, s32[1,2,768]{2,1,0:T(2,128)} %perms_hbm.1, s32[1,5,2,192]{3,2,1,0:T(2,128)} %nodes_hbm.1), custom_call_target="tpu_custom_call" | custom-call | flops 1000 | bytes 1000 | tf_op jit(solution)/shard_map/pallas_call | solution.py:39
  2.1 1.7 %collective-permute-start.1 = (bf16[784,256]{1,0:T(8,128)(2,1)}, bf16[784,256]{1,0:T(8,128)(2,1)S(1)}, u32[]{:S(2)}, u32[]{:S(2)}) collective-permute-start(bf16[784,256]{1,0:T(8,128)(2,1)} %get-tuple-element.30), channel_id=1, source_target_pairs={{1,2},{3,4},{5,6},{7,8},{9,10},{11,12},{13,14},{2,1},{4,3},{6,5},{... | collective-permute-start | bytes 1204232 | tf_op jit(solution)/shard_map/ppermute | solution.py:386
  3.8 3.4 %collective-permute-start = (bf16[784,256]{1,0:T(8,128)(2,1)}, bf16[784,256]{1,0:T(8,128)(2,1)S(1)}, u32[]{:S(2)}, u32[]{:S(2)}) collective-permute-start(bf16[784,256]{1,0:T(8,128)(2,1)} %get-tuple-element.30), channel_id=1, source_target_pairs={{0,1},{1,0},{2,3},{3,2},{4,5},{5,4},{6,7},{7,6},{8,9},{9,8},{10,11... | collective-permute-start | bytes 1204232 | tf_op jit(solution)/shard_map/ppermute | solution.py:355
  7.2 4.9 %all-to-all-start = ((bf16[8,16,1536]{2,1,0:T(8,128)(2,1)}), bf16[8,16,1536]{2,1,0:T(8,128)(2,1)S(1)}, u32[]{:S(2)}, u32[]{:S(2)}) async-start(bf16[8,16,1536]{2,1,0:T(8,128)(2,1)} %get-tuple-element.33), calls=%async_computation | async-start | bytes 786432 | tf_op jit(solution)/shard_map/all_to_all | solution.py:389
  12.8 1.0 %copy-done.6 = bf16[1,5,4,96,96]{4,3,2,1,0:T(8,128)(2,1)S(1)} copy-done((bf16[1,5,4,96,96]{4,3,2,1,0:T(8,128)(2,1)S(1)}, bf16[1,5,4,96,96]{4,3,2,1,0:T(8,128)(2,1)}, u32[]{:S(2)}) %copy-start.6) | copy-done | bytes 368664
  13.8 2.4 %shard_map.82 = (bf16[16,128]{1,0:T(8,128)(2,1)S(1)}, bf16[2,2,288,96]{3,2,1,0:T(8,128)(2,1)S(1)}, bf16[2,2,288,96]{3,2,1,0:T(8,128)(2,1)S(1)}, bf16[2,2,288,96]...) custom-call(bf16[1,5,4,96,96]{4,3,2,1,0:T(8,128)(2,1)S(1)} %copy-done.6, ...), custom_call_target="tpu_custom_call" | custom-call | flops 1073741824 | bytes 1000 | tf_op jit(solution)/shard_map/pallas_call | solution.py:39
  16.2 3.2 %shard_map.83 = (bf16[192,768]{1,0:T(8,128)(2,1)S(1)}, bf16[96,2304]{1,0:T(8,128)(2,1)S(1)}, bf16[96,768]{1,0:T(8,128)(2,1)S(1)}, bf16[768,2304]{1,0:T(8,128)(2,1)S(1)}) custom-call(s32[6,12]{1,0:T(8,128)S(1)} %copy-done.8, bf16[6,12,128,128]{3,2,1,0:T(8,128)(2,1)S(1)} %copy-done.5, s32[1,2,768]{2,1,0:T(2,128)S(1)} %copy-done.4, ...), custom_call_target="tpu_custom_call" | custom-call | flops 1073741824 | bytes 1000 | tf_op jit(solution)/shard_map/pallas_call | solution.py:39
  19.5 1.3 %shard_map.85 = (bf16[432,768]{1,0:T(8,128)(2,1)S(1)}, bf16[192,128]{1,0:T(8,128)(2,1)S(1)}) custom-call(bf16[192,768]{1,0:T(8,128)(2,1)S(1)} %get-tuple-element.26.keep_ref, bf16[768,2304]{1,0:T(8,128)(2,1)S(1)} %get-tuple-element.27.dense_ref, bf16[96,2304]{1,0:T(8,128)(2,1)S(1)} %get-tuple-element.28.near_ref, ...), custom_call_target="tpu_custom_call" | custom-call | flops 1000 | bytes 1000 | tf_op jit(solution)/shard_map/pallas_call | solution.py:39
  21.1 2.8 %all-to-all-done = bf16[8,16,1536]{2,1,0:T(8,128)(2,1)S(1)} async-done(((bf16[8,16,1536]{2,1,0:T(8,128)(2,1)}), bf16[8,16,1536]{2,1,0:T(8,128)(2,1)S(1)}, u32[]{:S(2)}, u32[]{:S(2)}) %all-to-all-start) | async-done | bytes 393248 | tf_op jit(solution)/shard_map/all_to_all | solution.py:389
  24.2 1.5 %collective-permute-start.7 = (bf16[96,128]{1,0:T(8,128)(2,1)S(1)}, bf16[96,128]{1,0:T(8,128)(2,1)S(1)}, u32[]{:S(2)}, u32[]{:S(2)}) collective-permute-start(bf16[96,128]{1,0:T(8,128)(2,1)S(1)} %get-tuple-element.38), channel_id=1, source_target_pairs={{2,6},{3,7},{6,10},{7,11},{10,14},{11,15},{14,12},{15,13},{12,8},{... | collective-permute-start | bytes 73736 | tf_op jit(solution)/shard_map/ppermute | solution.py:424
  25.7 1.0 %copy-done.2 = bf16[2,2,288,96]{3,2,1,0:T(8,128)(2,1)S(1)} copy-done((bf16[2,2,288,96]{3,2,1,0:T(8,128)(2,1)S(1)}, bf16[2,2,288,96]{3,2,1,0:T(8,128)(2,1)}, u32[]{:S(2)}) %copy-start.2) | copy-done | bytes 221208
  26.9 1.6 %collective-permute-start.3 = (bf16[192,128]{1,0:T(8,128)(2,1)S(1)}, bf16[192,128]{1,0:T(8,128)(2,1)S(1)}, u32[]{:S(2)}, u32[]{:S(2)}) collective-permute-start(bf16[192,128]{1,0:T(8,128)(2,1)S(1)} %shard_map.87.mine_ref.refs_0_), channel_id=1, source_target_pairs={{0,2},{1,3},{2,0},{3,1},{4,6},{5,7},{6,4},{7,5},{8,10},{9,11},{10,... | collective-permute-start | bytes 147464 | tf_op jit(solution)/shard_map/ppermute | solution.py:355
  29.9 1.1 %collective-permute-done.3.other_ref = bf16[192,128]{1,0:T(8,128)(2,1)S(1)} collective-permute-done((bf16[192,128]{1,0:T(8,128)(2,1)S(1)}, bf16[192,128]{1,0:T(8,128)(2,1)S(1)}, u32[]{:S(2)}, u32[]{:S(2)}) %collective-permute-start.3) | collective-permute-done | bytes 49184 | tf_op jit(solution)/shard_map/ppermute | solution.py:355
  31.2 1.8 %collective-permute-start.4 = (bf16[192,128]{1,0:T(8,128)(2,1)S(1)}, bf16[192,128]{1,0:T(8,128)(2,1)S(1)}, u32[]{:S(2)}, u32[]{:S(2)}) collective-permute-start(bf16[192,128]{1,0:T(8,128)(2,1)S(1)} %shard_map.88.mine_ref.refs_1_), channel_id=1, source_target_pairs={{0,4},{1,5},{2,6},{3,7},{4,0},{5,1},{6,2},{7,3},{8,12},{9,13},{10,... | collective-permute-start | bytes 147464 | tf_op jit(solution)/shard_map/ppermute | solution.py:355
  34.0 2.2 %collective-permute-start.9 = (bf16[192,128]{1,0:T(8,128)(2,1)S(1)}, bf16[192,128]{1,0:T(8,128)(2,1)S(1)}, u32[]{:S(2)}, u32[]{:S(2)}) collective-permute-start(bf16[192,128]{1,0:T(8,128)(2,1)S(1)} %get-tuple-element.40.mine_ref.refs_6_), channel_id=1, source_target_pairs={{0,4},{1,5},{2,6},{3,7},{4,0},{5,1},{6,2},{7,3},{8,12},{9,13},{10,... | collective-permute-start | bytes 147464 | tf_op jit(solution)/shard_map/ppermute | solution.py:355
  36.4 1.5 %collective-permute-start.5 = (bf16[192,128]{1,0:T(8,128)(2,1)S(1)}, bf16[192,128]{1,0:T(8,128)(2,1)S(1)}, u32[]{:S(2)}, u32[]{:S(2)}) collective-permute-start(bf16[192,128]{1,0:T(8,128)(2,1)S(1)} %shard_map.89.mine_ref.refs_2_), channel_id=1, source_target_pairs={{0,8},{1,9},{2,10},{3,11},{4,12},{5,13},{6,14},{7,15},{8,0},{9,1},... | collective-permute-start | bytes 147464 | tf_op jit(solution)/shard_map/ppermute | solution.py:355
  38.5 1.8 %collective-permute-start.10 = (bf16[192,128]{1,0:T(8,128)(2,1)S(1)}, bf16[192,128]{1,0:T(8,128)(2,1)S(1)}, u32[]{:S(2)}, u32[]{:S(2)}) collective-permute-start(bf16[192,128]{1,0:T(8,128)(2,1)S(1)} %shard_map.94.mine_ref.refs_7_), channel_id=1, source_target_pairs={{0,8},{1,9},{2,10},{3,11},{4,12},{5,13},{6,14},{7,15},{8,0},{9,1},... | collective-permute-start | bytes 147464 | tf_op jit(solution)/shard_map/ppermute | solution.py:355
  40.3 2.1 %collective-permute-done.5.other_ref = bf16[192,128]{1,0:T(8,128)(2,1)S(1)} collective-permute-done((bf16[192,128]{1,0:T(8,128)(2,1)S(1)}, bf16[192,128]{1,0:T(8,128)(2,1)S(1)}, u32[]{:S(2)}, u32[]{:S(2)}) %collective-permute-start.5) | collective-permute-done | bytes 49184 | tf_op jit(solution)/shard_map/ppermute | solution.py:355
  42.5 1.6 %collective-permute-start.6 = (bf16[192,128]{1,0:T(8,128)(2,1)S(1)}, bf16[192,128]{1,0:T(8,128)(2,1)S(1)}, u32[]{:S(2)}, u32[]{:S(2)}) collective-permute-start(bf16[192,128]{1,0:T(8,128)(2,1)S(1)} %shard_map.90.refs_3_), channel_id=1, source_target_pairs={{0,16},{16,0},{1,17},{17,1},{2,18},{18,2},{3,19},{19,3},{4,20},{20... | collective-permute-start | bytes 147464 | tf_op jit(solution)/shard_map/ppermute | solution.py:355
  44.3 1.0 %collective-permute-start.11 = (bf16[192,128]{1,0:T(8,128)(2,1)S(1)}, bf16[192,128]{1,0:T(8,128)(2,1)S(1)}, u32[]{:S(2)}, u32[]{:S(2)}) collective-permute-start(bf16[192,128]{1,0:T(8,128)(2,1)S(1)} %shard_map.95.refs_8_), channel_id=1, source_target_pairs={{0,16},{16,0},{1,17},{17,1},{2,18},{18,2},{3,19},{19,3},{4,20},{20... | collective-permute-start | bytes 147464 | tf_op jit(solution)/shard_map/ppermute | solution.py:355
  45.3 1.4 %collective-permute-done.6.refs_4_ = bf16[192,128]{1,0:T(8,128)(2,1)S(1)} collective-permute-done((bf16[192,128]{1,0:T(8,128)(2,1)S(1)}, bf16[192,128]{1,0:T(8,128)(2,1)S(1)}, u32[]{:S(2)}, u32[]{:S(2)}) %collective-permute-start.6) | collective-permute-done | bytes 49184 | tf_op jit(solution)/shard_map/ppermute | solution.py:355
  46.7 1.8 %collective-permute-done.11.refs_9_ = bf16[192,128]{1,0:T(8,128)(2,1)S(1)} collective-permute-done((bf16[192,128]{1,0:T(8,128)(2,1)S(1)}, bf16[192,128]{1,0:T(8,128)(2,1)S(1)}, u32[]{:S(2)}, u32[]{:S(2)}) %collective-permute-start.11) | collective-permute-done | bytes 49184 | tf_op jit(solution)/shard_map/ppermute | solution.py:355
  48.8 1.5 %collective-permute-done.12.other_ref = bf16[5,2,96,128]{3,2,1,0:T(8,128)(2,1)S(1)} collective-permute-done((bf16[5,2,96,128]{3,2,1,0:T(8,128)(2,1)S(1)}, bf16[5,2,96,128]{3,2,1,0:T(8,128)(2,1)S(1)}, u32[]{:S(2)}, u32[]{:S(2)}) %collective-permute-start.12) | collective-permute-done | bytes 245792 | tf_op jit(solution)/shard_map/ppermute | solution.py:355
  50.3 1.0 %shard_map.97 = bf16[1,5,2,96,256]{4,3,2,1,0:T(8,128)(2,1)} custom-call(bf16[5,2,96,128]{3,2,1,0:T(8,128)(2,1)S(1)} %shard_map.96.mine_ref, bf16[5,2,96,128]{3,2,1,0:T(8,128)(2,1)S(1)} %collective-permute-done.12.other_ref), custom_call_target="tpu_custom_call" | custom-call | flops 1000 | bytes 1000 | tf_op jit(solution)/shard_map/pallas_call | solution.py:39
  (38 shorter events, 5.4 us)
Async XLA Ops:
  0.0 16.2 %copy-start.4 = (s32[1,2,768]{2,1,0:T(2,128)S(1)}, s32[1,2,768]{2,1,0:T(2,128)}, u32[]{:S(2)}) copy-start(s32[1,2,768]{2,1,0:T(2,128)} %perms_hbm.1) | copy-start | bytes 18436
  0.0 16.2 %copy-start.7 = (bf16[1,2,672,96]{2,3,1,0:T(8,128)(2,1)S(1)}, bf16[1,2,672,96]{2,3,1,0:T(8,128)(2,1)}, u32[]{:S(2)}) copy-start(bf16[1,2,672,96]{2,3,1,0:T(8,128)(2,1)} %param.13) | copy-start | bytes 774148
  0.0 16.2 %copy-start.8 = (s32[6,12]{1,0:T(8,128)S(1)}, s32[6,12]{1,0:T(8,128)}, u32[]{:S(2)}) copy-start(s32[6,12]{1,0:T(8,128)} %cols_ref.1) | copy-start | bytes 868
  2.1 17.3 %collective-permute-start.1 = (bf16[784,256]{1,0:T(8,128)(2,1)}, bf16[784,256]{1,0:T(8,128)(2,1)S(1)}, u32[]{:S(2)}, u32[]{:S(2)}) collective-permute-start(bf16[784,256]{1,0:T(8,128)(2,1)} %get-tuple-element.30), channel_id=1, source_target_pairs={{1,2},{3,4},{5,6},{7,8},{9,10},{11,12},{13,14},{2,1},{4,3},{6,5},{... | collective-permute-start | bytes 1204232 | tf_op jit(solution)/shard_map/ppermute | solution.py:386
  3.8 15.7 %collective-permute-start = (bf16[784,256]{1,0:T(8,128)(2,1)}, bf16[784,256]{1,0:T(8,128)(2,1)S(1)}, u32[]{:S(2)}, u32[]{:S(2)}) collective-permute-start(bf16[784,256]{1,0:T(8,128)(2,1)} %get-tuple-element.30), channel_id=1, source_target_pairs={{0,1},{1,0},{2,3},{3,2},{4,5},{5,4},{6,7},{7,6},{8,9},{9,8},{10,11... | collective-permute-start | bytes 1204232 | tf_op jit(solution)/shard_map/ppermute | solution.py:355
  7.2 16.7 %all-to-all-start = ((bf16[8,16,1536]{2,1,0:T(8,128)(2,1)}), bf16[8,16,1536]{2,1,0:T(8,128)(2,1)S(1)}, u32[]{:S(2)}, u32[]{:S(2)}) async-start(bf16[8,16,1536]{2,1,0:T(8,128)(2,1)} %get-tuple-element.33), calls=%async_computation | async-start | bytes 786432 | tf_op jit(solution)/shard_map/all_to_all | solution.py:389
  12.0 0.7 %copy-start.3 = (s32[1,5,2,192]{3,2,1,0:T(2,128)S(1)}, s32[1,5,2,192]{3,2,1,0:T(2,128)}, u32[]{:S(2)}) copy-start(s32[1,5,2,192]{3,2,1,0:T(2,128)} %nodes_hbm.1) | copy-start | bytes 23044
  12.7 1.0 %copy-start.6 = (bf16[1,5,4,96,96]{4,3,2,1,0:T(8,128)(2,1)S(1)}, bf16[1,5,4,96,96]{4,3,2,1,0:T(8,128)(2,1)}, u32[]{:S(2)}) copy-start(bf16[1,5,4,96,96]{4,3,2,1,0:T(8,128)(2,1)} %maps_ref.1) | copy-start | bytes 1105924
  13.8 2.4 %copy-start.5 = (bf16[6,12,128,128]{3,2,1,0:T(8,128)(2,1)S(1)}, bf16[6,12,128,128]{3,2,1,0:T(8,128)(2,1)}, u32[]{:S(2)}) copy-start(bf16[6,12,128,128]{3,2,1,0:T(8,128)(2,1)} %tiles_ref.1) | copy-start | bytes 7077892
  13.8 5.7 %copy-start = (bf16[768,256]{1,0:T(8,128)(2,1)S(1)}, bf16[768,256]{1,0:T(8,128)(2,1)}, u32[]{:S(2)}) copy-start(bf16[768,256]{1,0:T(8,128)(2,1)} %omega_ref.1) | copy-start | bytes 1179652
  16.2 3.3 %copy-start.1 = (bf16[2,2,288,96]{3,2,1,0:T(8,128)(2,1)}, bf16[2,2,288,96]{3,2,1,0:T(8,128)(2,1)S(1)}, u32[]{:S(2)}) copy-start(bf16[2,2,288,96]{3,2,1,0:T(8,128)(2,1)S(1)} %get-tuple-element.24.maps_ref) | copy-start | bytes 663556
  20.8 3.1 %collective-permute-start.2 = (bf16[432,768]{1,0:T(8,128)(2,1)S(1)}, bf16[432,768]{1,0:T(8,128)(2,1)S(1)}, u32[]{:S(2)}, u32[]{:S(2)}) collective-permute-start(bf16[432,768]{1,0:T(8,128)(2,1)S(1)} %get-tuple-element.32.sel_ref), channel_id=1, source_target_pairs={{0,1},{1,0},{2,3},{3,2},{4,5},{5,4},{6,7},{7,6},{8,9},{9,8},{10,11... | collective-permute-start | bytes 1990664 | tf_op jit(solution)/shard_map/ppermute | solution.py:355
  24.2 4.9 %collective-permute-start.7 = (bf16[96,128]{1,0:T(8,128)(2,1)S(1)}, bf16[96,128]{1,0:T(8,128)(2,1)S(1)}, u32[]{:S(2)}, u32[]{:S(2)}) collective-permute-start(bf16[96,128]{1,0:T(8,128)(2,1)S(1)} %get-tuple-element.38), channel_id=1, source_target_pairs={{2,6},{3,7},{6,10},{7,11},{10,14},{11,15},{14,12},{15,13},{12,8},{... | collective-permute-start | bytes 73736 | tf_op jit(solution)/shard_map/ppermute | solution.py:424
  25.7 1.0 %copy-start.2 = (bf16[2,2,288,96]{3,2,1,0:T(8,128)(2,1)S(1)}, bf16[2,2,288,96]{3,2,1,0:T(8,128)(2,1)}, u32[]{:S(2)}) copy-start(bf16[2,2,288,96]{3,2,1,0:T(8,128)(2,1)} %copy-done.1) | copy-start | bytes 663556
  26.9 4.2 %collective-permute-start.3 = (bf16[192,128]{1,0:T(8,128)(2,1)S(1)}, bf16[192,128]{1,0:T(8,128)(2,1)S(1)}, u32[]{:S(2)}, u32[]{:S(2)}) collective-permute-start(bf16[192,128]{1,0:T(8,128)(2,1)S(1)} %shard_map.87.mine_ref.refs_0_), channel_id=1, source_target_pairs={{0,2},{1,3},{2,0},{3,1},{4,6},{5,7},{6,4},{7,5},{8,10},{9,11},{10,... | collective-permute-start | bytes 147464 | tf_op jit(solution)/shard_map/ppermute | solution.py:355
  29.4 4.4 %collective-permute-start.8 = (bf16[288,128]{1,0:T(8,128)(2,1)S(1)}, bf16[288,128]{1,0:T(8,128)(2,1)S(1)}, u32[]{:S(2)}, u32[]{:S(2)}) collective-permute-start(bf16[288,128]{1,0:T(8,128)(2,1)S(1)} %shard_map.92.mine_ref), channel_id=1, source_target_pairs={{0,2},{1,3},{2,0},{3,1},{4,6},{5,7},{6,4},{7,5},{8,10},{9,11},{10,... | collective-permute-start | bytes 221192 | tf_op jit(solution)/shard_map/ppermute | solution.py:355
  31.2 5.0 %collective-permute-start.4 = (bf16[192,128]{1,0:T(8,128)(2,1)S(1)}, bf16[192,128]{1,0:T(8,128)(2,1)S(1)}, u32[]{:S(2)}, u32[]{:S(2)}) collective-permute-start(bf16[192,128]{1,0:T(8,128)(2,1)S(1)} %shard_map.88.mine_ref.refs_1_), channel_id=1, source_target_pairs={{0,4},{1,5},{2,6},{3,7},{4,0},{5,1},{6,2},{7,3},{8,12},{9,13},{10,... | collective-permute-start | bytes 147464 | tf_op jit(solution)/shard_map/ppermute | solution.py:355
  34.0 4.3 %collective-permute-start.9 = (bf16[192,128]{1,0:T(8,128)(2,1)S(1)}, bf16[192,128]{1,0:T(8,128)(2,1)S(1)}, u32[]{:S(2)}, u32[]{:S(2)}) collective-permute-start(bf16[192,128]{1,0:T(8,128)(2,1)S(1)} %get-tuple-element.40.mine_ref.refs_6_), channel_id=1, source_target_pairs={{0,4},{1,5},{2,6},{3,7},{4,0},{5,1},{6,2},{7,3},{8,12},{9,13},{10,... | collective-permute-start | bytes 147464 | tf_op jit(solution)/shard_map/ppermute | solution.py:355
  36.4 5.9 %collective-permute-start.5 = (bf16[192,128]{1,0:T(8,128)(2,1)S(1)}, bf16[192,128]{1,0:T(8,128)(2,1)S(1)}, u32[]{:S(2)}, u32[]{:S(2)}) collective-permute-start(bf16[192,128]{1,0:T(8,128)(2,1)S(1)} %shard_map.89.mine_ref.refs_2_), channel_id=1, source_target_pairs={{0,8},{1,9},{2,10},{3,11},{4,12},{5,13},{6,14},{7,15},{8,0},{9,1},... | collective-permute-start | bytes 147464 | tf_op jit(solution)/shard_map/ppermute | solution.py:355
  38.5 5.6 %collective-permute-start.10 = (bf16[192,128]{1,0:T(8,128)(2,1)S(1)}, bf16[192,128]{1,0:T(8,128)(2,1)S(1)}, u32[]{:S(2)}, u32[]{:S(2)}) collective-permute-start(bf16[192,128]{1,0:T(8,128)(2,1)S(1)} %shard_map.94.mine_ref.refs_7_), channel_id=1, source_target_pairs={{0,8},{1,9},{2,10},{3,11},{4,12},{5,13},{6,14},{7,15},{8,0},{9,1},... | collective-permute-start | bytes 147464 | tf_op jit(solution)/shard_map/ppermute | solution.py:355
  42.5 4.2 %collective-permute-start.6 = (bf16[192,128]{1,0:T(8,128)(2,1)S(1)}, bf16[192,128]{1,0:T(8,128)(2,1)S(1)}, u32[]{:S(2)}, u32[]{:S(2)}) collective-permute-start(bf16[192,128]{1,0:T(8,128)(2,1)S(1)} %shard_map.90.refs_3_), channel_id=1, source_target_pairs={{0,16},{16,0},{1,17},{17,1},{2,18},{18,2},{3,19},{19,3},{4,20},{20... | collective-permute-start | bytes 147464 | tf_op jit(solution)/shard_map/ppermute | solution.py:355
  44.3 4.2 %collective-permute-start.11 = (bf16[192,128]{1,0:T(8,128)(2,1)S(1)}, bf16[192,128]{1,0:T(8,128)(2,1)S(1)}, u32[]{:S(2)}, u32[]{:S(2)}) collective-permute-start(bf16[192,128]{1,0:T(8,128)(2,1)S(1)} %shard_map.95.refs_8_), channel_id=1, source_target_pairs={{0,16},{16,0},{1,17},{17,1},{2,18},{18,2},{3,19},{19,3},{4,20},{20... | collective-permute-start | bytes 147464 | tf_op jit(solution)/shard_map/ppermute | solution.py:355
  48.7 1.6 %collective-permute-start.12 = (bf16[5,2,96,128]{3,2,1,0:T(8,128)(2,1)S(1)}, bf16[5,2,96,128]{3,2,1,0:T(8,128)(2,1)S(1)}, u32[]{:S(2)}, u32[]{:S(2)}) collective-permute-start(bf16[5,2,96,128]{3,2,1,0:T(8,128)(2,1)S(1)} %shard_map.96.mine_ref), channel_id=1, source_target_pairs={{0,1},{1,0},{2,3},{3,2},{4,5},{5,4},{6,7},{7,6},{8,9},{9,8},{10,11... | collective-permute-start | bytes 737288 | tf_op jit(solution)/shard_map/ppermute | solution.py:355

commit v14 on v13

--- a/solution.py
+++ b/solution.py
@@ -182,11 +182,12 @@
         sel_ref[4 * rank + 16 :, at * half : (at + 1) * half] = part
 
 
-def maps_body(maps_ref, perms_ref, order_ref, *out_refs):
+def maps_body(first, maps_ref, perms_ref, after_ref, order_ref, *out_refs):
     rank = maps_ref.shape[-1]
     unit = eye(rank)
+    del after_ref
     order_ref[...] = jnp.zeros_like(order_ref)
-    for level, out_ref in enumerate(out_refs):
+    for level, out_ref in enumerate(out_refs, first):
         row_interp, col_interp, low_high, high_low = (maps_ref[0, level, i] for i in range(4))
         row_hot = one_hot(perms_ref[0, level, 0:1, :], 2 * rank)
         col_hot = one_hot(perms_ref[0, level, 1:2, :], 2 * rank)
@@ -240,7 +241,8 @@
     return [panel_ref[:, pl.ds(pl.multiple_of(at * rows, 128), rows)] for at in (core, 1 - core)]
 
 
-def edge_body(sel_ref, sel_other, panel_ref, near_out, far_out):
+def edge_body(sel_ref, sel_other, panel_ref, after_ref, near_out, far_out):
+    del after_ref
     rank = near_out.shape[0]
     panel, panel_other = halves(panel_ref)
     mine = mm_t(sel_ref[3 * rank : 4 * rank], panel)
@@ -392,9 +394,10 @@
 
     tables = shape((2, 2, 3 * rank, rank))
     order, *maps = call(
-        maps_body,
-        [shape((16, 128))] + [tables] * levels,
-        (node_maps, node_perms),
+        functools.partial(maps_body, 1),
+        [shape((16, 128))] + [tables] * (levels - 1),
+        (node_maps, node_perms, node_perms),
+        specs="vva",
         flops=1 << 30,
     )
     keep, near, tests, dense = call(
@@ -418,7 +421,16 @@
         (keep, dense, near, tests, omega, packed_inner, packed_outer),
     )
     sel_other = swapped(sel, "sub", 0)
-    near_rims, far_rims = call(edge_body, [shape((rank, half))] * 2, (sel, sel_other, panel))
+    order, first_maps = call(
+        functools.partial(maps_body, 0),
+        [shape((16, 128)), tables],
+        (node_maps, node_perms, fwd_mine),
+        specs="vva",
+    )
+    maps = [first_maps, *maps]
+    near_rims, far_rims = call(
+        edge_body, [shape((rank, half))] * 2, (sel, sel_other, panel, order), specs="vvva"
+    )
     ring = list(range(1, chips, 2)) + list(range(chips - 2, -1, -2))
     route = [(2 * a + c, 2 * b + c) for a, b in zip(ring, ring[1:] + ring[:1]) for c in range(2)]
     far_rims = lax.ppermute(far_rims, "sub", route)

time: 51.7 us -> 50.8 us (0.983)
  waiting for transfers between devices: 11.8 us -> 8.75 us
  starting transfers between devices: 23.9 us -> 26.9 us
  local copies, waits for them, and re-layouts: 2.71 us -> 1.76 us
    ppermute x11, starting transfers between devices: 15.8 us -> 18.8 us  [swapped(): lax.ppermute(x, axis, [(i, i ^ 1 << bit) for i in range(lax.axis_size(axi...]
    ppermute x11, waiting for transfers between devices: 9 us -> 6.49 us  [swapped(): lax.ppermute(x, axis, [(i, i ^ 1 << bit) for i in range(lax.axis_size(axi...]
    unnamed x18, local copies, waits for them, and re-layouts: 2.71 us -> 1.76 us
    all_to_all x1, waiting for transfers between devices: 2.84 us -> 2.26 us  [local(): lax.all_to_all(blocks, 'sub', split_axis=0, concat_axis=0, tiled=True, ax...]
    pallas_call x16 -> x17, Pallas kernels: 12.7 us -> 12.8 us  [call(): pl.pallas_call(body, out_shape=out_shape, in_specs=[SPACES[c] for c in sp...]
where the time goes in v14:
time: 50.8 us; the launch traced here: 50.4 us
  starting transfers between devices  26.9 us (53%)
  Pallas kernels  12.8 us (25%)
  waiting for transfers between devices  8.75 us (17%)
  local copies, waits for them, and re-layouts  1.76 us (3%)
    ppermute x11, starting transfers between devices, swapped(): lax.ppermute(x, axis, [(i, i ^ 1 << bit) for i in range(lax.axis_size(axi...  18.8 us
    pallas_call x17, Pallas kernels, call(): pl.pallas_call(body, out_shape=out_shape, in_specs=[SPACES[c] for c in sp...  12.8 us
    ppermute x11, waiting for transfers between devices, swapped(): lax.ppermute(x, axis, [(i, i ^ 1 << bit) for i in range(lax.axis_size(axi...  6.49 us
    all_to_all x1, starting transfers between devices, local(): lax.all_to_all(blocks, 'sub', split_axis=0, concat_axis=0, tiled=True, ax...  4.88 us
    all_to_all x1, waiting for transfers between devices, local(): lax.all_to_all(blocks, 'sub', split_axis=0, concat_axis=0, tiled=True, ax...  2.26 us
    unnamed x18, local copies, waits for them, and re-layouts  1.76 us
    ppermute x1, starting transfers between devices, local(): packed_outer = lax.ppermute(packed, 'sub', outward)  1.66 us
    ppermute x1, starting transfers between devices, local(): far_rims = lax.ppermute(far_rims, 'sub', route)  1.54 us
  transfers between devices with their start and end apart: 14, of which 8 were waited for; matrix products, arithmetic and copies ran while one was open for 0% of the time, Pallas kernels for 18%

profile of v14, /device:TPU:0, one launch (start us, length us, event | category | flops | bytes accessed | tf_op | source)
XLA Modules:
  0.0 50.4 jit_solution(8547852885104054823)
XLA Ops:
  0.0 2.1 %shard_map.84 = (bf16[8,16,1536]{2,1,0:T(8,128)(2,1)}, bf16[784,256]{1,0:T(8,128)(2,1)}) custom-call(bf16[16,12288]{1,0:T(8,128)(2,1)} %tests_hbm.1, bf16[768,256]{1,0:T(8,128)(2,1)} %omega_ref.1, s32[1,2,768]{2,1,0:T(2,128)} %perms_hbm.1, s32[1,5,2,192]{3,2,1,0:T(2,128)} %perms_ref.5), custom_call_target="tpu_custom_call" | custom-call | flops 1000 | bytes 1000 | tf_op jit(solution)/shard_map/pallas_call | solution.py:39
  2.1 1.7 %collective-permute-start.1 = (bf16[784,256]{1,0:T(8,128)(2,1)}, bf16[784,256]{1,0:T(8,128)(2,1)S(1)}, u32[]{:S(2)}, u32[]{:S(2)}) collective-permute-start(bf16[784,256]{1,0:T(8,128)(2,1)} %get-tuple-element.30), channel_id=1, source_target_pairs={{1,2},{3,4},{5,6},{7,8},{9,10},{11,12},{13,14},{2,1},{4,3},{6,5},{... | collective-permute-start | bytes 1204232 | tf_op jit(solution)/shard_map/ppermute | solution.py:388
  3.8 3.4 %collective-permute-start = (bf16[784,256]{1,0:T(8,128)(2,1)}, bf16[784,256]{1,0:T(8,128)(2,1)S(1)}, u32[]{:S(2)}, u32[]{:S(2)}) collective-permute-start(bf16[784,256]{1,0:T(8,128)(2,1)} %get-tuple-element.30), channel_id=1, source_target_pairs={{0,1},{1,0},{2,3},{3,2},{4,5},{5,4},{6,7},{7,6},{8,9},{9,8},{10,11... | collective-permute-start | bytes 1204232 | tf_op jit(solution)/shard_map/ppermute | solution.py:357
  7.2 4.9 %all-to-all-start = ((bf16[8,16,1536]{2,1,0:T(8,128)(2,1)}), bf16[8,16,1536]{2,1,0:T(8,128)(2,1)S(1)}, u32[]{:S(2)}, u32[]{:S(2)}) async-start(bf16[8,16,1536]{2,1,0:T(8,128)(2,1)} %get-tuple-element.34), calls=%async_computation | async-start | bytes 786432 | tf_op jit(solution)/shard_map/all_to_all | solution.py:391
  12.1 1.0 %copy-done.1 = bf16[1,5,4,96,96]{4,3,2,1,0:T(8,128)(2,1)S(1)} copy-done((bf16[1,5,4,96,96]{4,3,2,1,0:T(8,128)(2,1)S(1)}, bf16[1,5,4,96,96]{4,3,2,1,0:T(8,128)(2,1)}, u32[]{:S(2)}) %copy-start.1) | copy-done | bytes 368664
  13.8 1.9 %shard_map.82 = (bf16[16,128]{1,0:T(8,128)(2,1)S(1)}, bf16[2,2,288,96]{3,2,1,0:T(8,128)(2,1)S(1)}, bf16[2,2,288,96]{3,2,1,0:T(8,128)(2,1)S(1)}, bf16[2,2,288,96]...) custom-call(bf16[1,5,4,96,96]{4,3,2,1,0:T(8,128)(2,1)S(1)} %copy-done.1, s32[1,5,2,192]{3,2,1,0:T(2,128)S(1)} %copy-done.3, ...), custom_call_target="tpu_custom_call" | custom-call | flops 1073741824 | bytes 1000 | tf_op jit(solution)/shard_map/pallas_call | solution.py:39
  15.8 3.2 %shard_map.83 = (bf16[192,768]{1,0:T(8,128)(2,1)S(1)}, bf16[96,2304]{1,0:T(8,128)(2,1)S(1)}, bf16[96,768]{1,0:T(8,128)(2,1)S(1)}, bf16[768,2304]{1,0:T(8,128)(2,1)S(1)}) custom-call(s32[6,12]{1,0:T(8,128)S(1)} %copy-done.8, bf16[6,12,128,128]{3,2,1,0:T(8,128)(2,1)S(1)} %copy-done.6, s32[1,2,768]{2,1,0:T(2,128)S(1)} %copy-done.5, ...), custom_call_target="tpu_custom_call" | custom-call | flops 1073741824 | bytes 1000 | tf_op jit(solution)/shard_map/pallas_call | solution.py:39
  19.1 1.3 %shard_map.85 = (bf16[432,768]{1,0:T(8,128)(2,1)S(1)}, bf16[192,128]{1,0:T(8,128)(2,1)S(1)}) custom-call(bf16[192,768]{1,0:T(8,128)(2,1)S(1)} %get-tuple-element.26.keep_ref, bf16[768,2304]{1,0:T(8,128)(2,1)S(1)} %get-tuple-element.27.dense_ref, bf16[96,2304]{1,0:T(8,128)(2,1)S(1)} %get-tuple-element.28.near_ref, ...), custom_call_target="tpu_custom_call" | custom-call | flops 1000 | bytes 1000 | tf_op jit(solution)/shard_map/pallas_call | solution.py:39
  21.7 2.3 %all-to-all-done = bf16[8,16,1536]{2,1,0:T(8,128)(2,1)S(1)} async-done(((bf16[8,16,1536]{2,1,0:T(8,128)(2,1)}), bf16[8,16,1536]{2,1,0:T(8,128)(2,1)S(1)}, u32[]{:S(2)}, u32[]{:S(2)}) %all-to-all-start) | async-done | bytes 393248 | tf_op jit(solution)/shard_map/all_to_all | solution.py:391
  24.2 1.5 %collective-permute-start.7 = (bf16[96,128]{1,0:T(8,128)(2,1)S(1)}, bf16[96,128]{1,0:T(8,128)(2,1)S(1)}, u32[]{:S(2)}, u32[]{:S(2)}) collective-permute-start(bf16[96,128]{1,0:T(8,128)(2,1)S(1)} %get-tuple-element.40), channel_id=1, source_target_pairs={{2,6},{3,7},{6,10},{7,11},{10,14},{11,15},{14,12},{15,13},{12,8},{... | collective-permute-start | bytes 73736 | tf_op jit(solution)/shard_map/ppermute | solution.py:436
  25.9 1.6 %collective-permute-start.3 = (bf16[192,128]{1,0:T(8,128)(2,1)S(1)}, bf16[192,128]{1,0:T(8,128)(2,1)S(1)}, u32[]{:S(2)}, u32[]{:S(2)}) collective-permute-start(bf16[192,128]{1,0:T(8,128)(2,1)S(1)} %shard_map.88.mine_ref.refs_0_), channel_id=1, source_target_pairs={{0,2},{1,3},{2,0},{3,1},{4,6},{5,7},{6,4},{7,5},{8,10},{9,11},{10,... | collective-permute-start | bytes 147464 | tf_op jit(solution)/shard_map/ppermute | solution.py:357
  28.5 1.4 %collective-permute-start.8 = (bf16[288,128]{1,0:T(8,128)(2,1)S(1)}, bf16[288,128]{1,0:T(8,128)(2,1)S(1)}, u32[]{:S(2)}, u32[]{:S(2)}) collective-permute-start(bf16[288,128]{1,0:T(8,128)(2,1)S(1)} %shard_map.93.mine_ref), channel_id=1, source_target_pairs={{0,2},{1,3},{2,0},{3,1},{4,6},{5,7},{6,4},{7,5},{8,10},{9,11},{10,... | collective-permute-start | bytes 221192 | tf_op jit(solution)/shard_map/ppermute | solution.py:357
  30.3 1.8 %collective-permute-start.4 = (bf16[192,128]{1,0:T(8,128)(2,1)S(1)}, bf16[192,128]{1,0:T(8,128)(2,1)S(1)}, u32[]{:S(2)}, u32[]{:S(2)}) collective-permute-start(bf16[192,128]{1,0:T(8,128)(2,1)S(1)} %shard_map.89.mine_ref.refs_1_), channel_id=1, source_target_pairs={{0,4},{1,5},{2,6},{3,7},{4,0},{5,1},{6,2},{7,3},{8,12},{9,13},{10,... | collective-permute-start | bytes 147464 | tf_op jit(solution)/shard_map/ppermute | solution.py:357
  32.0 0.9 %collective-permute-done.8.other_ref = bf16[288,128]{1,0:T(8,128)(2,1)S(1)} collective-permute-done((bf16[288,128]{1,0:T(8,128)(2,1)S(1)}, bf16[288,128]{1,0:T(8,128)(2,1)S(1)}, u32[]{:S(2)}, u32[]{:S(2)}) %collective-permute-start.8) | collective-permute-done | bytes 73760 | tf_op jit(solution)/shard_map/ppermute | solution.py:357
  33.1 2.2 %collective-permute-start.9 = (bf16[192,128]{1,0:T(8,128)(2,1)S(1)}, bf16[192,128]{1,0:T(8,128)(2,1)S(1)}, u32[]{:S(2)}, u32[]{:S(2)}) collective-permute-start(bf16[192,128]{1,0:T(8,128)(2,1)S(1)} %get-tuple-element.42.mine_ref.refs_6_), channel_id=1, source_target_pairs={{0,4},{1,5},{2,6},{3,7},{4,0},{5,1},{6,2},{7,3},{8,12},{9,13},{10,... | collective-permute-start | bytes 147464 | tf_op jit(solution)/shard_map/ppermute | solution.py:357
  35.4 2.5 %collective-permute-start.5 = (bf16[192,128]{1,0:T(8,128)(2,1)S(1)}, bf16[192,128]{1,0:T(8,128)(2,1)S(1)}, u32[]{:S(2)}, u32[]{:S(2)}) collective-permute-start(bf16[192,128]{1,0:T(8,128)(2,1)S(1)} %shard_map.90.mine_ref.refs_2_), channel_id=1, source_target_pairs={{0,8},{1,9},{2,10},{3,11},{4,12},{5,13},{6,14},{7,15},{8,0},{9,1},... | collective-permute-start | bytes 147464 | tf_op jit(solution)/shard_map/ppermute | solution.py:357
  38.1 1.9 %collective-permute-start.10 = (bf16[192,128]{1,0:T(8,128)(2,1)S(1)}, bf16[192,128]{1,0:T(8,128)(2,1)S(1)}, u32[]{:S(2)}, u32[]{:S(2)}) collective-permute-start(bf16[192,128]{1,0:T(8,128)(2,1)S(1)} %shard_map.95.mine_ref.refs_7_), channel_id=1, source_target_pairs={{0,8},{1,9},{2,10},{3,11},{4,12},{5,13},{6,14},{7,15},{8,0},{9,1},... | collective-permute-start | bytes 147464 | tf_op jit(solution)/shard_map/ppermute | solution.py:357
  40.0 1.3 %collective-permute-done.5.other_ref = bf16[192,128]{1,0:T(8,128)(2,1)S(1)} collective-permute-done((bf16[192,128]{1,0:T(8,128)(2,1)S(1)}, bf16[192,128]{1,0:T(8,128)(2,1)S(1)}, u32[]{:S(2)}, u32[]{:S(2)}) %collective-permute-start.5) | collective-permute-done | bytes 49184 | tf_op jit(solution)/shard_map/ppermute | solution.py:357
  41.5 1.6 %collective-permute-start.6 = (bf16[192,128]{1,0:T(8,128)(2,1)S(1)}, bf16[192,128]{1,0:T(8,128)(2,1)S(1)}, u32[]{:S(2)}, u32[]{:S(2)}) collective-permute-start(bf16[192,128]{1,0:T(8,128)(2,1)S(1)} %shard_map.91.refs_3_), channel_id=1, source_target_pairs={{0,16},{16,0},{1,17},{17,1},{2,18},{18,2},{3,19},{19,3},{4,20},{20... | collective-permute-start | bytes 147464 | tf_op jit(solution)/shard_map/ppermute | solution.py:357
  43.4 1.6 %collective-permute-start.11 = (bf16[192,128]{1,0:T(8,128)(2,1)S(1)}, bf16[192,128]{1,0:T(8,128)(2,1)S(1)}, u32[]{:S(2)}, u32[]{:S(2)}) collective-permute-start(bf16[192,128]{1,0:T(8,128)(2,1)S(1)} %shard_map.96.refs_8_), channel_id=1, source_target_pairs={{0,16},{16,0},{1,17},{17,1},{2,18},{18,2},{3,19},{19,3},{4,20},{20... | collective-permute-start | bytes 147464 | tf_op jit(solution)/shard_map/ppermute | solution.py:357
  45.0 0.7 %collective-permute-done.6.refs_4_ = bf16[192,128]{1,0:T(8,128)(2,1)S(1)} collective-permute-done((bf16[192,128]{1,0:T(8,128)(2,1)S(1)}, bf16[192,128]{1,0:T(8,128)(2,1)S(1)}, u32[]{:S(2)}, u32[]{:S(2)}) %collective-permute-start.6) | collective-permute-done | bytes 49184 | tf_op jit(solution)/shard_map/ppermute | solution.py:357
  45.7 1.8 %collective-permute-done.11.refs_9_ = bf16[192,128]{1,0:T(8,128)(2,1)S(1)} collective-permute-done((bf16[192,128]{1,0:T(8,128)(2,1)S(1)}, bf16[192,128]{1,0:T(8,128)(2,1)S(1)}, u32[]{:S(2)}, u32[]{:S(2)}) %collective-permute-start.11) | collective-permute-done | bytes 49184 | tf_op jit(solution)/shard_map/ppermute | solution.py:357
  47.9 1.5 %collective-permute-done.12.other_ref = bf16[5,2,96,128]{3,2,1,0:T(8,128)(2,1)S(1)} collective-permute-done((bf16[5,2,96,128]{3,2,1,0:T(8,128)(2,1)S(1)}, bf16[5,2,96,128]{3,2,1,0:T(8,128)(2,1)S(1)}, u32[]{:S(2)}, u32[]{:S(2)}) %collective-permute-start.12) | collective-permute-done | bytes 245792 | tf_op jit(solution)/shard_map/ppermute | solution.py:357
  49.4 1.0 %shard_map.98 = bf16[1,5,2,96,256]{4,3,2,1,0:T(8,128)(2,1)} custom-call(bf16[5,2,96,128]{3,2,1,0:T(8,128)(2,1)S(1)} %shard_map.97.mine_ref, bf16[5,2,96,128]{3,2,1,0:T(8,128)(2,1)S(1)} %collective-permute-done.12.other_ref), custom_call_target="tpu_custom_call" | custom-call | flops 1000 | bytes 1000 | tf_op jit(solution)/shard_map/pallas_call | solution.py:39
  (39 shorter events, 4.9 us)
Async XLA Ops:
  0.0 15.7 %copy-start.5 = (s32[1,2,768]{2,1,0:T(2,128)S(1)}, s32[1,2,768]{2,1,0:T(2,128)}, u32[]{:S(2)}) copy-start(s32[1,2,768]{2,1,0:T(2,128)} %perms_hbm.1) | copy-start | bytes 18436
  0.0 15.7 %copy-start.7 = (bf16[1,2,672,96]{2,3,1,0:T(8,128)(2,1)S(1)}, bf16[1,2,672,96]{2,3,1,0:T(8,128)(2,1)}, u32[]{:S(2)}) copy-start(bf16[1,2,672,96]{2,3,1,0:T(8,128)(2,1)} %param.13) | copy-start | bytes 774148
  0.0 15.7 %copy-start.8 = (s32[6,12]{1,0:T(8,128)S(1)}, s32[6,12]{1,0:T(8,128)}, u32[]{:S(2)}) copy-start(s32[6,12]{1,0:T(8,128)} %cols_ref.1) | copy-start | bytes 868
  2.1 16.9 %collective-permute-start.1 = (bf16[784,256]{1,0:T(8,128)(2,1)}, bf16[784,256]{1,0:T(8,128)(2,1)S(1)}, u32[]{:S(2)}, u32[]{:S(2)}) collective-permute-start(bf16[784,256]{1,0:T(8,128)(2,1)} %get-tuple-element.30), channel_id=1, source_target_pairs={{1,2},{3,4},{5,6},{7,8},{9,10},{11,12},{13,14},{2,1},{4,3},{6,5},{... | collective-permute-start | bytes 1204232 | tf_op jit(solution)/shard_map/ppermute | solution.py:388
  3.8 15.3 %collective-permute-start = (bf16[784,256]{1,0:T(8,128)(2,1)}, bf16[784,256]{1,0:T(8,128)(2,1)S(1)}, u32[]{:S(2)}, u32[]{:S(2)}) collective-permute-start(bf16[784,256]{1,0:T(8,128)(2,1)} %get-tuple-element.30), channel_id=1, source_target_pairs={{0,1},{1,0},{2,3},{3,2},{4,5},{5,4},{6,7},{7,6},{8,9},{9,8},{10,11... | collective-permute-start | bytes 1204232 | tf_op jit(solution)/shard_map/ppermute | solution.py:357
  7.2 16.7 %all-to-all-start = ((bf16[8,16,1536]{2,1,0:T(8,128)(2,1)}), bf16[8,16,1536]{2,1,0:T(8,128)(2,1)S(1)}, u32[]{:S(2)}, u32[]{:S(2)}) async-start(bf16[8,16,1536]{2,1,0:T(8,128)(2,1)} %get-tuple-element.34), calls=%async_computation | async-start | bytes 786432 | tf_op jit(solution)/shard_map/all_to_all | solution.py:391
  12.1 1.0 %copy-start.1 = (bf16[1,5,4,96,96]{4,3,2,1,0:T(8,128)(2,1)S(1)}, bf16[1,5,4,96,96]{4,3,2,1,0:T(8,128)(2,1)}, u32[]{:S(2)}) copy-start(bf16[1,5,4,96,96]{4,3,2,1,0:T(8,128)(2,1)} %maps_ref.3) | copy-start | bytes 1105924
  13.1 0.7 %copy-start.3 = (s32[1,5,2,192]{3,2,1,0:T(2,128)S(1)}, s32[1,5,2,192]{3,2,1,0:T(2,128)}, u32[]{:S(2)}) copy-start(s32[1,5,2,192]{3,2,1,0:T(2,128)} %perms_ref.5) | copy-start | bytes 23044
  13.8 2.0 %copy-start.6 = (bf16[6,12,128,128]{3,2,1,0:T(8,128)(2,1)S(1)}, bf16[6,12,128,128]{3,2,1,0:T(8,128)(2,1)}, u32[]{:S(2)}) copy-start(bf16[6,12,128,128]{3,2,1,0:T(8,128)(2,1)} %tiles_ref.1) | copy-start | bytes 7077892
  13.8 5.3 %copy-start = (bf16[768,256]{1,0:T(8,128)(2,1)S(1)}, bf16[768,256]{1,0:T(8,128)(2,1)}, u32[]{:S(2)}) copy-start(bf16[768,256]{1,0:T(8,128)(2,1)} %omega_ref.1) | copy-start | bytes 1179652
  19.0 2.1 %copy-start.2 = (bf16[1,5,4,96,96]{4,3,2,1,0:T(8,128)(2,1)S(1)}, bf16[1,5,4,96,96]{4,3,2,1,0:T(8,128)(2,1)}, u32[]{:S(2)}) copy-start(bf16[1,5,4,96,96]{4,3,2,1,0:T(8,128)(2,1)} %maps_ref.3) | copy-start | bytes 1105924
  19.0 2.1 %copy-start.4 = (s32[1,5,2,192]{3,2,1,0:T(2,128)S(1)}, s32[1,5,2,192]{3,2,1,0:T(2,128)}, u32[]{:S(2)}) copy-start(s32[1,5,2,192]{3,2,1,0:T(2,128)} %perms_ref.5) | copy-start | bytes 23044
  20.4 3.6 %collective-permute-start.2 = (bf16[432,768]{1,0:T(8,128)(2,1)S(1)}, bf16[432,768]{1,0:T(8,128)(2,1)S(1)}, u32[]{:S(2)}, u32[]{:S(2)}) collective-permute-start(bf16[432,768]{1,0:T(8,128)(2,1)S(1)} %get-tuple-element.33.sel_ref), channel_id=1, source_target_pairs={{0,1},{1,0},{2,3},{3,2},{4,5},{5,4},{6,7},{7,6},{8,9},{9,8},{10,11... | collective-permute-start | bytes 1990664 | tf_op jit(solution)/shard_map/ppermute | solution.py:357
  24.2 4.0 %collective-permute-start.7 = (bf16[96,128]{1,0:T(8,128)(2,1)S(1)}, bf16[96,128]{1,0:T(8,128)(2,1)S(1)}, u32[]{:S(2)}, u32[]{:S(2)}) collective-permute-start(bf16[96,128]{1,0:T(8,128)(2,1)S(1)} %get-tuple-element.40), channel_id=1, source_target_pairs={{2,6},{3,7},{6,10},{7,11},{10,14},{11,15},{14,12},{15,13},{12,8},{... | collective-permute-start | bytes 73736 | tf_op jit(solution)/shard_map/ppermute | solution.py:436
  25.9 4.2 %collective-permute-start.3 = (bf16[192,128]{1,0:T(8,128)(2,1)S(1)}, bf16[192,128]{1,0:T(8,128)(2,1)S(1)}, u32[]{:S(2)}, u32[]{:S(2)}) collective-permute-start(bf16[192,128]{1,0:T(8,128)(2,1)S(1)} %shard_map.88.mine_ref.refs_0_), channel_id=1, source_target_pairs={{0,2},{1,3},{2,0},{3,1},{4,6},{5,7},{6,4},{7,5},{8,10},{9,11},{10,... | collective-permute-start | bytes 147464 | tf_op jit(solution)/shard_map/ppermute | solution.py:357
  28.5 4.4 %collective-permute-start.8 = (bf16[288,128]{1,0:T(8,128)(2,1)S(1)}, bf16[288,128]{1,0:T(8,128)(2,1)S(1)}, u32[]{:S(2)}, u32[]{:S(2)}) collective-permute-start(bf16[288,128]{1,0:T(8,128)(2,1)S(1)} %shard_map.93.mine_ref), channel_id=1, source_target_pairs={{0,2},{1,3},{2,0},{3,1},{4,6},{5,7},{6,4},{7,5},{8,10},{9,11},{10,... | collective-permute-start | bytes 221192 | tf_op jit(solution)/shard_map/ppermute | solution.py:357
  30.3 5.0 %collective-permute-start.4 = (bf16[192,128]{1,0:T(8,128)(2,1)S(1)}, bf16[192,128]{1,0:T(8,128)(2,1)S(1)}, u32[]{:S(2)}, u32[]{:S(2)}) collective-permute-start(bf16[192,128]{1,0:T(8,128)(2,1)S(1)} %shard_map.89.mine_ref.refs_1_), channel_id=1, source_target_pairs={{0,4},{1,5},{2,6},{3,7},{4,0},{5,1},{6,2},{7,3},{8,12},{9,13},{10,... | collective-permute-start | bytes 147464 | tf_op jit(solution)/shard_map/ppermute | solution.py:357
  33.1 4.9 %collective-permute-start.9 = (bf16[192,128]{1,0:T(8,128)(2,1)S(1)}, bf16[192,128]{1,0:T(8,128)(2,1)S(1)}, u32[]{:S(2)}, u32[]{:S(2)}) collective-permute-start(bf16[192,128]{1,0:T(8,128)(2,1)S(1)} %get-tuple-element.42.mine_ref.refs_6_), channel_id=1, source_target_pairs={{0,4},{1,5},{2,6},{3,7},{4,0},{5,1},{6,2},{7,3},{8,12},{9,13},{10,... | collective-permute-start | bytes 147464 | tf_op jit(solution)/shard_map/ppermute | solution.py:357
  35.4 5.9 %collective-permute-start.5 = (bf16[192,128]{1,0:T(8,128)(2,1)S(1)}, bf16[192,128]{1,0:T(8,128)(2,1)S(1)}, u32[]{:S(2)}, u32[]{:S(2)}) collective-permute-start(bf16[192,128]{1,0:T(8,128)(2,1)S(1)} %shard_map.90.mine_ref.refs_2_), channel_id=1, source_target_pairs={{0,8},{1,9},{2,10},{3,11},{4,12},{5,13},{6,14},{7,15},{8,0},{9,1},... | collective-permute-start | bytes 147464 | tf_op jit(solution)/shard_map/ppermute | solution.py:357
  38.1 5.1 %collective-permute-start.10 = (bf16[192,128]{1,0:T(8,128)(2,1)S(1)}, bf16[192,128]{1,0:T(8,128)(2,1)S(1)}, u32[]{:S(2)}, u32[]{:S(2)}) collective-permute-start(bf16[192,128]{1,0:T(8,128)(2,1)S(1)} %shard_map.95.mine_ref.refs_7_), channel_id=1, source_target_pairs={{0,8},{1,9},{2,10},{3,11},{4,12},{5,13},{6,14},{7,15},{8,0},{9,1},... | collective-permute-start | bytes 147464 | tf_op jit(solution)/shard_map/ppermute | solution.py:357
  41.5 4.2 %collective-permute-start.6 = (bf16[192,128]{1,0:T(8,128)(2,1)S(1)}, bf16[192,128]{1,0:T(8,128)(2,1)S(1)}, u32[]{:S(2)}, u32[]{:S(2)}) collective-permute-start(bf16[192,128]{1,0:T(8,128)(2,1)S(1)} %shard_map.91.refs_3_), channel_id=1, source_target_pairs={{0,16},{16,0},{1,17},{17,1},{2,18},{18,2},{3,19},{19,3},{4,20},{20... | collective-permute-start | bytes 147464 | tf_op jit(solution)/shard_map/ppermute | solution.py:357
  43.4 4.2 %collective-permute-start.11 = (bf16[192,128]{1,0:T(8,128)(2,1)S(1)}, bf16[192,128]{1,0:T(8,128)(2,1)S(1)}, u32[]{:S(2)}, u32[]{:S(2)}) collective-permute-start(bf16[192,128]{1,0:T(8,128)(2,1)S(1)} %shard_map.96.refs_8_), channel_id=1, source_target_pairs={{0,16},{16,0},{1,17},{17,1},{2,18},{18,2},{3,19},{19,3},{4,20},{20... | collective-permute-start | bytes 147464 | tf_op jit(solution)/shard_map/ppermute | solution.py:357
  47.8 1.6 %collective-permute-start.12 = (bf16[5,2,96,128]{3,2,1,0:T(8,128)(2,1)S(1)}, bf16[5,2,96,128]{3,2,1,0:T(8,128)(2,1)S(1)}, u32[]{:S(2)}, u32[]{:S(2)}) collective-permute-start(bf16[5,2,96,128]{3,2,1,0:T(8,128)(2,1)S(1)} %shard_map.97.mine_ref), channel_id=1, source_target_pairs={{0,1},{1,0},{2,3},{3,2},{4,5},{5,4},{6,7},{7,6},{8,9},{9,8},{10,11... | collective-permute-start | bytes 737288 | tf_op jit(solution)/shard_map/ppermute | solution.py:357

commit v15 on v14

--- a/solution.py
+++ b/solution.py
@@ -309,15 +309,19 @@
     out_ref[rank:] = tests.astype(BF)
 
 
-def last_body(axis, bit, levels, maps_ref, *refs):
+def collect_body(*refs):
     out_ref = refs[-1]
-    rank = out_ref.shape[2]
+    levels, _, rank, _ = out_ref.shape
+    for i, ref in enumerate(refs[:-2]):
+        out_ref[i % levels, i // levels] = ref[:rank]
+
+
+def last_body(axis, bit, maps_ref, *refs):
+    out_ref = refs[-1]
+    rank = out_ref.shape[1]
     side = (lax.axis_index(axis) >> bit) & 1
     for kind in range(2):
-        nodes = refs[kind * levels : kind * levels + levels - 1]
-        mine_ref, other_ref = nodes[-1], refs[kind * levels + levels - 1]
-        for level, ref in enumerate(nodes):
-            out_ref[level, kind] = ref[:rank]
+        mine_ref, other_ref = refs[2 * kind : 2 * kind + 2]
         kept, _ = merged(
             maps_ref,
             kind,
@@ -328,11 +332,12 @@
             other_ref[rank:],
             rank,
         )
-        out_ref[levels - 1, kind] = kept.astype(BF)
-
-
-def output_body(vectors, mine_ref, other_ref, out_hbm, out_ref, sems):
+        out_ref[kind] = kept.astype(BF)
+
+
+def output_body(vectors, early_ref, early_other, mine_ref, other_ref, out_hbm, out_ref, sems):
     half = mine_ref.shape[-1]
+    early = early_ref.shape[0]
     core = lax.axis_index("sub") & 1
     k = lax.broadcasted_iota(jnp.int32, (half, 2 * half), 0)
     s = lax.broadcasted_iota(jnp.int32, (half, 2 * half), 1)
@@ -342,8 +347,9 @@
     mine_cols = pl.ds(pl.multiple_of(core * half, half), half)
     other_cols = pl.ds(pl.multiple_of((1 - core) * half, half), half)
     copies = []
-    for level in range(mine_ref.shape[0]):
-        mine, other = mine_ref[level], other_ref[level]
+    for level in range(early + 1):
+        mine = early_ref[level] if level < early else mine_ref[...]
+        other = early_other[level] if level < early else other_ref[...]
         out_ref[level, 0, :, mine_cols] = mine[0]
         out_ref[level, 0, :, other_cols] = other[0]
         out_ref[level, 1] = (mm(mine[1], to_mine) + mm(other[1], to_other)).astype(BF)
@@ -474,15 +480,24 @@
                 )
     axis, bit = steps[-1]
     ends = [swapped(chain[-1], axis, bit) for chain in chains]
+    early = call(
+        collect_body,
+        shape((levels - 1, 2, rank, half)),
+        (*chains[0], *chains[1], ends[0]),
+        specs="v" * (2 * levels - 2) + "a",
+        flops=4 << 30,
+    )
+    early_other = swapped(early, "sub", 0)
     x = call(
-        functools.partial(last_body, axis, bit, levels),
-        shape((levels, 2, rank, half)),
-        (maps[-1], *chains[0], ends[0], *chains[1], ends[1]),
+        functools.partial(last_body, axis, bit),
+        shape((2, rank, half)),
+        (maps[-1], chains[0][-1], ends[0], chains[1][-1], ends[1]),
+        flops=4 << 30,
     )
     return call(
         functools.partial(output_body, vectors),
         shape((1, levels, 2, rank, samples)),
-        (x, swapped(x, "sub", 0)),
+        (early, early_other, x, swapped(x, "sub", 0)),
         scratch=[pltpu.VMEM((levels, 2, rank, samples), BF), pltpu.SemaphoreType.DMA((levels,))],
         out="a",
     )

time: 50.8 us -> 50.5 us (level)
    ppermute x11 -> x12, waiting for transfers between devices: 6.49 us -> 6.11 us  [swapped(): lax.ppermute(x, axis, [(i, i ^ 1 << bit) for i in range(lax.axis_size(axi...]
    ppermute x11 -> x12, starting transfers between devices: 18.8 us -> 18.9 us  [swapped(): lax.ppermute(x, axis, [(i, i ^ 1 << bit) for i in range(lax.axis_size(axi...]
    pallas_call x17 -> x18, Pallas kernels: 12.8 us -> 12.8 us  [call(): pl.pallas_call(body, out_shape=out_shape, in_specs=[SPACES[c] for c in sp...]
  transfers between devices with their start and end apart: 14 -> 15, of which waited for: 8 -> 8; matrix products, arithmetic and copies ran while one was open for 0% -> 0% of each run, Pallas kernels for 18% -> 19%
where the time goes in v15:
time: 50.5 us; the launch traced here: 50.1 us
  starting transfers between devices  26.9 us (53%)
  Pallas kernels  12.8 us (25%)
  waiting for transfers between devices  8.38 us (17%)
  local copies, waits for them, and re-layouts  1.76 us (3%)
    ppermute x12, starting transfers between devices, swapped(): lax.ppermute(x, axis, [(i, i ^ 1 << bit) for i in range(lax.axis_size(axi...  18.9 us
    pallas_call x18, Pallas kernels, call(): pl.pallas_call(body, out_shape=out_shape, in_specs=[SPACES[c] for c in sp...  12.8 us
    ppermute x12, waiting for transfers between devices, swapped(): lax.ppermute(x, axis, [(i, i ^ 1 << bit) for i in range(lax.axis_size(axi...  6.11 us
    all_to_all x1, starting transfers between devices, local(): lax.all_to_all(blocks, 'sub', split_axis=0, concat_axis=0, tiled=True, ax...  4.88 us
    all_to_all x1, waiting for transfers between devices, local(): lax.all_to_all(blocks, 'sub', split_axis=0, concat_axis=0, tiled=True, ax...  2.26 us
    unnamed x18, local copies, waits for them, and re-layouts  1.76 us
    ppermute x1, starting transfers between devices, local(): packed_outer = lax.ppermute(packed, 'sub', outward)  1.66 us
    ppermute x1, starting transfers between devices, local(): far_rims = lax.ppermute(far_rims, 'sub', route)  1.54 us
  transfers between devices with their start and end apart: 15, of which 8 were waited for; matrix products, arithmetic and copies ran while one was open for 0% of the time, Pallas kernels for 19%

profile of v15, /device:TPU:0, one launch (start us, length us, event | category | flops | bytes accessed | tf_op | source)
XLA Modules:
  0.0 50.1 jit_solution(10920423629174639284)
XLA Ops:
  0.0 2.1 %shard_map.84 = (bf16[8,16,1536]{2,1,0:T(8,128)(2,1)}, bf16[784,256]{1,0:T(8,128)(2,1)}) custom-call(bf16[16,12288]{1,0:T(8,128)(2,1)} %tests_hbm.1, bf16[768,256]{1,0:T(8,128)(2,1)} %omega_ref.1, s32[1,2,768]{2,1,0:T(2,128)} %perms_hbm.1, s32[1,5,2,192]{3,2,1,0:T(2,128)} %perms_ref.5), custom_call_target="tpu_custom_call" | custom-call | flops 1000 | bytes 1000 | tf_op jit(solution)/shard_map/pallas_call | solution.py:39
  2.1 1.7 %collective-permute-start.1 = (bf16[784,256]{1,0:T(8,128)(2,1)}, bf16[784,256]{1,0:T(8,128)(2,1)S(1)}, u32[]{:S(2)}, u32[]{:S(2)}) collective-permute-start(bf16[784,256]{1,0:T(8,128)(2,1)} %get-tuple-element.29), channel_id=1, source_target_pairs={{1,2},{3,4},{5,6},{7,8},{9,10},{11,12},{13,14},{2,1},{4,3},{6,5},{... | collective-permute-start | bytes 1204232 | tf_op jit(solution)/shard_map/ppermute | solution.py:394
  3.8 3.4 %collective-permute-start = (bf16[784,256]{1,0:T(8,128)(2,1)}, bf16[784,256]{1,0:T(8,128)(2,1)S(1)}, u32[]{:S(2)}, u32[]{:S(2)}) collective-permute-start(bf16[784,256]{1,0:T(8,128)(2,1)} %get-tuple-element.29), channel_id=1, source_target_pairs={{0,1},{1,0},{2,3},{3,2},{4,5},{5,4},{6,7},{7,6},{8,9},{9,8},{10,11... | collective-permute-start | bytes 1204232 | tf_op jit(solution)/shard_map/ppermute | solution.py:363
  7.2 4.9 %all-to-all-start = ((bf16[8,16,1536]{2,1,0:T(8,128)(2,1)}), bf16[8,16,1536]{2,1,0:T(8,128)(2,1)S(1)}, u32[]{:S(2)}, u32[]{:S(2)}) async-start(bf16[8,16,1536]{2,1,0:T(8,128)(2,1)} %get-tuple-element.33), calls=%async_computation | async-start | bytes 786432 | tf_op jit(solution)/shard_map/all_to_all | solution.py:397
  12.1 1.0 %copy-done.1 = bf16[1,5,4,96,96]{4,3,2,1,0:T(8,128)(2,1)S(1)} copy-done((bf16[1,5,4,96,96]{4,3,2,1,0:T(8,128)(2,1)S(1)}, bf16[1,5,4,96,96]{4,3,2,1,0:T(8,128)(2,1)}, u32[]{:S(2)}) %copy-start.1) | copy-done | bytes 368664
  13.8 1.9 %shard_map.82 = (bf16[16,128]{1,0:T(8,128)(2,1)S(1)}, bf16[2,2,288,96]{3,2,1,0:T(8,128)(2,1)S(1)}, bf16[2,2,288,96]{3,2,1,0:T(8,128)(2,1)S(1)}, bf16[2,2,288,96]...) custom-call(bf16[1,5,4,96,96]{4,3,2,1,0:T(8,128)(2,1)S(1)} %copy-done.1, s32[1,5,2,192]{3,2,1,0:T(2,128)S(1)} %copy-done.3, ...), custom_call_target="tpu_custom_call" | custom-call | flops 1073741824 | bytes 1000 | tf_op jit(solution)/shard_map/pallas_call | solution.py:39
  15.8 3.2 %shard_map.83 = (bf16[192,768]{1,0:T(8,128)(2,1)S(1)}, bf16[96,2304]{1,0:T(8,128)(2,1)S(1)}, bf16[96,768]{1,0:T(8,128)(2,1)S(1)}, bf16[768,2304]{1,0:T(8,128)(2,1)S(1)}) custom-call(s32[6,12]{1,0:T(8,128)S(1)} %copy-done.8, bf16[6,12,128,128]{3,2,1,0:T(8,128)(2,1)S(1)} %copy-done.6, s32[1,2,768]{2,1,0:T(2,128)S(1)} %copy-done.5, ...), custom_call_target="tpu_custom_call" | custom-call | flops 1073741824 | bytes 1000 | tf_op jit(solution)/shard_map/pallas_call | solution.py:39
  19.1 1.3 %shard_map.85 = (bf16[432,768]{1,0:T(8,128)(2,1)S(1)}, bf16[192,128]{1,0:T(8,128)(2,1)S(1)}) custom-call(bf16[192,768]{1,0:T(8,128)(2,1)S(1)} %get-tuple-element.25.keep_ref, bf16[768,2304]{1,0:T(8,128)(2,1)S(1)} %get-tuple-element.26.dense_ref, bf16[96,2304]{1,0:T(8,128)(2,1)S(1)} %get-tuple-element.27.near_ref, ...), custom_call_target="tpu_custom_call" | custom-call | flops 1000 | bytes 1000 | tf_op jit(solution)/shard_map/pallas_call | solution.py:39
  21.7 2.3 %all-to-all-done = bf16[8,16,1536]{2,1,0:T(8,128)(2,1)S(1)} async-done(((bf16[8,16,1536]{2,1,0:T(8,128)(2,1)}), bf16[8,16,1536]{2,1,0:T(8,128)(2,1)S(1)}, u32[]{:S(2)}, u32[]{:S(2)}) %all-to-all-start) | async-done | bytes 393248 | tf_op jit(solution)/shard_map/all_to_all | solution.py:397
  24.2 1.5 %collective-permute-start.6 = (bf16[96,128]{1,0:T(8,128)(2,1)S(1)}, bf16[96,128]{1,0:T(8,128)(2,1)S(1)}, u32[]{:S(2)}, u32[]{:S(2)}) collective-permute-start(bf16[96,128]{1,0:T(8,128)(2,1)S(1)} %get-tuple-element.39), channel_id=1, source_target_pairs={{2,6},{3,7},{6,10},{7,11},{10,14},{11,15},{14,12},{15,13},{12,8},{... | collective-permute-start | bytes 73736 | tf_op jit(solution)/shard_map/ppermute | solution.py:442
  25.9 1.6 %collective-permute-start.3 = (bf16[192,128]{1,0:T(8,128)(2,1)S(1)}, bf16[192,128]{1,0:T(8,128)(2,1)S(1)}, u32[]{:S(2)}, u32[]{:S(2)}) collective-permute-start(bf16[192,128]{1,0:T(8,128)(2,1)S(1)} %shard_map.88.mine_ref.refs_0_), channel_id=1, source_target_pairs={{0,2},{1,3},{2,0},{3,1},{4,6},{5,7},{6,4},{7,5},{8,10},{9,11},{10,... | collective-permute-start | bytes 147464 | tf_op jit(solution)/shard_map/ppermute | solution.py:363
  28.5 1.4 %collective-permute-start.7 = (bf16[288,128]{1,0:T(8,128)(2,1)S(1)}, bf16[288,128]{1,0:T(8,128)(2,1)S(1)}, u32[]{:S(2)}, u32[]{:S(2)}) collective-permute-start(bf16[288,128]{1,0:T(8,128)(2,1)S(1)} %shard_map.93.mine_ref), channel_id=1, source_target_pairs={{0,2},{1,3},{2,0},{3,1},{4,6},{5,7},{6,4},{7,5},{8,10},{9,11},{10,... | collective-permute-start | bytes 221192 | tf_op jit(solution)/shard_map/ppermute | solution.py:363
  30.2 1.8 %collective-permute-start.4 = (bf16[192,128]{1,0:T(8,128)(2,1)S(1)}, bf16[192,128]{1,0:T(8,128)(2,1)S(1)}, u32[]{:S(2)}, u32[]{:S(2)}) collective-permute-start(bf16[192,128]{1,0:T(8,128)(2,1)S(1)} %shard_map.89.mine_ref.refs_1_), channel_id=1, source_target_pairs={{0,4},{1,5},{2,6},{3,7},{4,0},{5,1},{6,2},{7,3},{8,12},{9,13},{10,... | collective-permute-start | bytes 147464 | tf_op jit(solution)/shard_map/ppermute | solution.py:363
  32.0 0.8 %collective-permute-done.7.other_ref = bf16[288,128]{1,0:T(8,128)(2,1)S(1)} collective-permute-done((bf16[288,128]{1,0:T(8,128)(2,1)S(1)}, bf16[288,128]{1,0:T(8,128)(2,1)S(1)}, u32[]{:S(2)}, u32[]{:S(2)}) %collective-permute-start.7) | collective-permute-done | bytes 73760 | tf_op jit(solution)/shard_map/ppermute | solution.py:363
  33.1 2.2 %collective-permute-start.8 = (bf16[192,128]{1,0:T(8,128)(2,1)S(1)}, bf16[192,128]{1,0:T(8,128)(2,1)S(1)}, u32[]{:S(2)}, u32[]{:S(2)}) collective-permute-start(bf16[192,128]{1,0:T(8,128)(2,1)S(1)} %get-tuple-element.41.mine_ref.refs_5_), channel_id=1, source_target_pairs={{0,4},{1,5},{2,6},{3,7},{4,0},{5,1},{6,2},{7,3},{8,12},{9,13},{10,... | collective-permute-start | bytes 147464 | tf_op jit(solution)/shard_map/ppermute | solution.py:363
  35.4 2.5 %collective-permute-start.5 = (bf16[192,128]{1,0:T(8,128)(2,1)S(1)}, bf16[192,128]{1,0:T(8,128)(2,1)S(1)}, u32[]{:S(2)}, u32[]{:S(2)}) collective-permute-start(bf16[192,128]{1,0:T(8,128)(2,1)S(1)} %shard_map.90.mine_ref.refs_2_), channel_id=1, source_target_pairs={{0,8},{1,9},{2,10},{3,11},{4,12},{5,13},{6,14},{7,15},{8,0},{9,1},... | collective-permute-start | bytes 147464 | tf_op jit(solution)/shard_map/ppermute | solution.py:363
  38.1 1.9 %collective-permute-start.9 = (bf16[192,128]{1,0:T(8,128)(2,1)S(1)}, bf16[192,128]{1,0:T(8,128)(2,1)S(1)}, u32[]{:S(2)}, u32[]{:S(2)}) collective-permute-start(bf16[192,128]{1,0:T(8,128)(2,1)S(1)} %shard_map.95.mine_ref.refs_6_), channel_id=1, source_target_pairs={{0,8},{1,9},{2,10},{3,11},{4,12},{5,13},{6,14},{7,15},{8,0},{9,1},... | collective-permute-start | bytes 147464 | tf_op jit(solution)/shard_map/ppermute | solution.py:363
  40.0 1.3 %collective-permute-done.5.other_ref = bf16[192,128]{1,0:T(8,128)(2,1)S(1)} collective-permute-done((bf16[192,128]{1,0:T(8,128)(2,1)S(1)}, bf16[192,128]{1,0:T(8,128)(2,1)S(1)}, u32[]{:S(2)}, u32[]{:S(2)}) %collective-permute-start.5) | collective-permute-done | bytes 49184 | tf_op jit(solution)/shard_map/ppermute | solution.py:363
  41.5 1.6 %collective-permute-start.10 = (bf16[192,128]{1,0:T(8,128)(2,1)S(1)}, bf16[192,128]{1,0:T(8,128)(2,1)S(1)}, u32[]{:S(2)}, u32[]{:S(2)}) collective-permute-start(bf16[192,128]{1,0:T(8,128)(2,1)S(1)} %shard_map.91.refs_3_.refs_0_), channel_id=1, source_target_pairs={{0,16},{16,0},{1,17},{17,1},{2,18},{18,2},{3,19},{19,3},{4,20},{20... | collective-permute-start | bytes 147464 | tf_op jit(solution)/shard_map/ppermute | solution.py:363
  43.4 1.6 %collective-permute-start.12 = (bf16[192,128]{1,0:T(8,128)(2,1)S(1)}, bf16[192,128]{1,0:T(8,128)(2,1)S(1)}, u32[]{:S(2)}, u32[]{:S(2)}) collective-permute-start(bf16[192,128]{1,0:T(8,128)(2,1)S(1)} %shard_map.96.refs_7_.refs_2_), channel_id=1, source_target_pairs={{0,16},{16,0},{1,17},{17,1},{2,18},{18,2},{3,19},{19,3},{4,20},{20... | collective-permute-start | bytes 147464 | tf_op jit(solution)/shard_map/ppermute | solution.py:363
  45.0 0.7 %collective-permute-done.10.refs_8_.refs_1_ = bf16[192,128]{1,0:T(8,128)(2,1)S(1)} collective-permute-done((bf16[192,128]{1,0:T(8,128)(2,1)S(1)}, bf16[192,128]{1,0:T(8,128)(2,1)S(1)}, u32[]{:S(2)}, u32[]{:S(2)}) %collective-permute-start.10) | collective-permute-done | bytes 49184 | tf_op jit(solution)/shard_map/ppermute | solution.py:363
  45.8 1.7 %collective-permute-done.12.refs_3_ = bf16[192,128]{1,0:T(8,128)(2,1)S(1)} collective-permute-done((bf16[192,128]{1,0:T(8,128)(2,1)S(1)}, bf16[192,128]{1,0:T(8,128)(2,1)S(1)}, u32[]{:S(2)}, u32[]{:S(2)}) %collective-permute-start.12) | collective-permute-done | bytes 49184 | tf_op jit(solution)/shard_map/ppermute | solution.py:363
  47.8 1.2 %collective-permute-done.13.other_ref = bf16[2,96,128]{2,1,0:T(8,128)(2,1)S(1)} collective-permute-done((bf16[2,96,128]{2,1,0:T(8,128)(2,1)S(1)}, bf16[2,96,128]{2,1,0:T(8,128)(2,1)S(1)}, u32[]{:S(2)}, u32[]{:S(2)}) %collective-permute-start.13) | collective-permute-done | bytes 49184 | tf_op jit(solution)/shard_map/ppermute | solution.py:363
  49.1 1.0 %shard_map.99 = bf16[1,5,2,96,256]{4,3,2,1,0:T(8,128)(2,1)} custom-call(bf16[4,2,96,128]{3,2,1,0:T(8,128)(2,1)S(1)} %shard_map.97.early_ref, bf16[4,2,96,128]{3,2,1,0:T(8,128)(2,1)S(1)} %collective-permute-done.11.early_other, bf16[2,96,128]{2,1,0:T(8,128)(2,1)S(1)} %shard_map.98.mine_ref, bf16[2,96,128]{2,1,0:T(8,128)(2,1)S(1)} %collective-permute-done.13.other_ref), custom_call_target="tpu_custom_call" | custom-call | flops 1000 | bytes 1000 | tf_op jit(solution)/shard_map/pallas_call | solution.py:39
  (42 shorter events, 5.0 us)
Async XLA Ops:
  0.0 15.7 %copy-start.5 = (s32[1,2,768]{2,1,0:T(2,128)S(1)}, s32[1,2,768]{2,1,0:T(2,128)}, u32[]{:S(2)}) copy-start(s32[1,2,768]{2,1,0:T(2,128)} %perms_hbm.1) | copy-start | bytes 18436
  0.0 15.7 %copy-start.7 = (bf16[1,2,672,96]{2,3,1,0:T(8,128)(2,1)S(1)}, bf16[1,2,672,96]{2,3,1,0:T(8,128)(2,1)}, u32[]{:S(2)}) copy-start(bf16[1,2,672,96]{2,3,1,0:T(8,128)(2,1)} %param.13) | copy-start | bytes 774148
  0.0 15.7 %copy-start.8 = (s32[6,12]{1,0:T(8,128)S(1)}, s32[6,12]{1,0:T(8,128)}, u32[]{:S(2)}) copy-start(s32[6,12]{1,0:T(8,128)} %cols_ref.1) | copy-start | bytes 868
  2.1 16.9 %collective-permute-start.1 = (bf16[784,256]{1,0:T(8,128)(2,1)}, bf16[784,256]{1,0:T(8,128)(2,1)S(1)}, u32[]{:S(2)}, u32[]{:S(2)}) collective-permute-start(bf16[784,256]{1,0:T(8,128)(2,1)} %get-tuple-element.29), channel_id=1, source_target_pairs={{1,2},{3,4},{5,6},{7,8},{9,10},{11,12},{13,14},{2,1},{4,3},{6,5},{... | collective-permute-start | bytes 1204232 | tf_op jit(solution)/shard_map/ppermute | solution.py:394
  3.8 15.3 %collective-permute-start = (bf16[784,256]{1,0:T(8,128)(2,1)}, bf16[784,256]{1,0:T(8,128)(2,1)S(1)}, u32[]{:S(2)}, u32[]{:S(2)}) collective-permute-start(bf16[784,256]{1,0:T(8,128)(2,1)} %get-tuple-element.29), channel_id=1, source_target_pairs={{0,1},{1,0},{2,3},{3,2},{4,5},{5,4},{6,7},{7,6},{8,9},{9,8},{10,11... | collective-permute-start | bytes 1204232 | tf_op jit(solution)/shard_map/ppermute | solution.py:363
  7.2 16.7 %all-to-all-start = ((bf16[8,16,1536]{2,1,0:T(8,128)(2,1)}), bf16[8,16,1536]{2,1,0:T(8,128)(2,1)S(1)}, u32[]{:S(2)}, u32[]{:S(2)}) async-start(bf16[8,16,1536]{2,1,0:T(8,128)(2,1)} %get-tuple-element.33), calls=%async_computation | async-start | bytes 786432 | tf_op jit(solution)/shard_map/all_to_all | solution.py:397
  12.0 1.0 %copy-start.1 = (bf16[1,5,4,96,96]{4,3,2,1,0:T(8,128)(2,1)S(1)}, bf16[1,5,4,96,96]{4,3,2,1,0:T(8,128)(2,1)}, u32[]{:S(2)}) copy-start(bf16[1,5,4,96,96]{4,3,2,1,0:T(8,128)(2,1)} %maps_ref.3) | copy-start | bytes 1105924
  13.1 0.7 %copy-start.3 = (s32[1,5,2,192]{3,2,1,0:T(2,128)S(1)}, s32[1,5,2,192]{3,2,1,0:T(2,128)}, u32[]{:S(2)}) copy-start(s32[1,5,2,192]{3,2,1,0:T(2,128)} %perms_ref.5) | copy-start | bytes 23044
  13.8 2.0 %copy-start.6 = (bf16[6,12,128,128]{3,2,1,0:T(8,128)(2,1)S(1)}, bf16[6,12,128,128]{3,2,1,0:T(8,128)(2,1)}, u32[]{:S(2)}) copy-start(bf16[6,12,128,128]{3,2,1,0:T(8,128)(2,1)} %tiles_ref.1) | copy-start | bytes 7077892
  13.8 5.3 %copy-start = (bf16[768,256]{1,0:T(8,128)(2,1)S(1)}, bf16[768,256]{1,0:T(8,128)(2,1)}, u32[]{:S(2)}) copy-start(bf16[768,256]{1,0:T(8,128)(2,1)} %omega_ref.1) | copy-start | bytes 1179652
  19.0 2.1 %copy-start.2 = (bf16[1,5,4,96,96]{4,3,2,1,0:T(8,128)(2,1)S(1)}, bf16[1,5,4,96,96]{4,3,2,1,0:T(8,128)(2,1)}, u32[]{:S(2)}) copy-start(bf16[1,5,4,96,96]{4,3,2,1,0:T(8,128)(2,1)} %maps_ref.3) | copy-start | bytes 1105924
  19.0 2.1 %copy-start.4 = (s32[1,5,2,192]{3,2,1,0:T(2,128)S(1)}, s32[1,5,2,192]{3,2,1,0:T(2,128)}, u32[]{:S(2)}) copy-start(s32[1,5,2,192]{3,2,1,0:T(2,128)} %perms_ref.5) | copy-start | bytes 23044
  20.4 3.6 %collective-permute-start.2 = (bf16[432,768]{1,0:T(8,128)(2,1)S(1)}, bf16[432,768]{1,0:T(8,128)(2,1)S(1)}, u32[]{:S(2)}, u32[]{:S(2)}) collective-permute-start(bf16[432,768]{1,0:T(8,128)(2,1)S(1)} %get-tuple-element.32.sel_ref), channel_id=1, source_target_pairs={{0,1},{1,0},{2,3},{3,2},{4,5},{5,4},{6,7},{7,6},{8,9},{9,8},{10,11... | collective-permute-start | bytes 1990664 | tf_op jit(solution)/shard_map/ppermute | solution.py:363
  24.2 4.0 %collective-permute-start.6 = (bf16[96,128]{1,0:T(8,128)(2,1)S(1)}, bf16[96,128]{1,0:T(8,128)(2,1)S(1)}, u32[]{:S(2)}, u32[]{:S(2)}) collective-permute-start(bf16[96,128]{1,0:T(8,128)(2,1)S(1)} %get-tuple-element.39), channel_id=1, source_target_pairs={{2,6},{3,7},{6,10},{7,11},{10,14},{11,15},{14,12},{15,13},{12,8},{... | collective-permute-start | bytes 73736 | tf_op jit(solution)/shard_map/ppermute | solution.py:442
  25.9 4.2 %collective-permute-start.3 = (bf16[192,128]{1,0:T(8,128)(2,1)S(1)}, bf16[192,128]{1,0:T(8,128)(2,1)S(1)}, u32[]{:S(2)}, u32[]{:S(2)}) collective-permute-start(bf16[192,128]{1,0:T(8,128)(2,1)S(1)} %shard_map.88.mine_ref.refs_0_), channel_id=1, source_target_pairs={{0,2},{1,3},{2,0},{3,1},{4,6},{5,7},{6,4},{7,5},{8,10},{9,11},{10,... | collective-permute-start | bytes 147464 | tf_op jit(solution)/shard_map/ppermute | solution.py:363
  28.5 4.4 %collective-permute-start.7 = (bf16[288,128]{1,0:T(8,128)(2,1)S(1)}, bf16[288,128]{1,0:T(8,128)(2,1)S(1)}, u32[]{:S(2)}, u32[]{:S(2)}) collective-permute-start(bf16[288,128]{1,0:T(8,128)(2,1)S(1)} %shard_map.93.mine_ref), channel_id=1, source_target_pairs={{0,2},{1,3},{2,0},{3,1},{4,6},{5,7},{6,4},{7,5},{8,10},{9,11},{10,... | collective-permute-start | bytes 221192 | tf_op jit(solution)/shard_map/ppermute | solution.py:363
  30.2 5.0 %collective-permute-start.4 = (bf16[192,128]{1,0:T(8,128)(2,1)S(1)}, bf16[192,128]{1,0:T(8,128)(2,1)S(1)}, u32[]{:S(2)}, u32[]{:S(2)}) collective-permute-start(bf16[192,128]{1,0:T(8,128)(2,1)S(1)} %shard_map.89.mine_ref.refs_1_), channel_id=1, source_target_pairs={{0,4},{1,5},{2,6},{3,7},{4,0},{5,1},{6,2},{7,3},{8,12},{9,13},{10,... | collective-permute-start | bytes 147464 | tf_op jit(solution)/shard_map/ppermute | solution.py:363
  33.1 4.9 %collective-permute-start.8 = (bf16[192,128]{1,0:T(8,128)(2,1)S(1)}, bf16[192,128]{1,0:T(8,128)(2,1)S(1)}, u32[]{:S(2)}, u32[]{:S(2)}) collective-permute-start(bf16[192,128]{1,0:T(8,128)(2,1)S(1)} %get-tuple-element.41.mine_ref.refs_5_), channel_id=1, source_target_pairs={{0,4},{1,5},{2,6},{3,7},{4,0},{5,1},{6,2},{7,3},{8,12},{9,13},{10,... | collective-permute-start | bytes 147464 | tf_op jit(solution)/shard_map/ppermute | solution.py:363
  35.4 5.9 %collective-permute-start.5 = (bf16[192,128]{1,0:T(8,128)(2,1)S(1)}, bf16[192,128]{1,0:T(8,128)(2,1)S(1)}, u32[]{:S(2)}, u32[]{:S(2)}) collective-permute-start(bf16[192,128]{1,0:T(8,128)(2,1)S(1)} %shard_map.90.mine_ref.refs_2_), channel_id=1, source_target_pairs={{0,8},{1,9},{2,10},{3,11},{4,12},{5,13},{6,14},{7,15},{8,0},{9,1},... | collective-permute-start | bytes 147464 | tf_op jit(solution)/shard_map/ppermute | solution.py:363
  38.1 5.1 %collective-permute-start.9 = (bf16[192,128]{1,0:T(8,128)(2,1)S(1)}, bf16[192,128]{1,0:T(8,128)(2,1)S(1)}, u32[]{:S(2)}, u32[]{:S(2)}) collective-permute-start(bf16[192,128]{1,0:T(8,128)(2,1)S(1)} %shard_map.95.mine_ref.refs_6_), channel_id=1, source_target_pairs={{0,8},{1,9},{2,10},{3,11},{4,12},{5,13},{6,14},{7,15},{8,0},{9,1},... | collective-permute-start | bytes 147464 | tf_op jit(solution)/shard_map/ppermute | solution.py:363
  41.5 4.2 %collective-permute-start.10 = (bf16[192,128]{1,0:T(8,128)(2,1)S(1)}, bf16[192,128]{1,0:T(8,128)(2,1)S(1)}, u32[]{:S(2)}, u32[]{:S(2)}) collective-permute-start(bf16[192,128]{1,0:T(8,128)(2,1)S(1)} %shard_map.91.refs_3_.refs_0_), channel_id=1, source_target_pairs={{0,16},{16,0},{1,17},{17,1},{2,18},{18,2},{3,19},{19,3},{4,20},{20... | collective-permute-start | bytes 147464 | tf_op jit(solution)/shard_map/ppermute | solution.py:363
  43.4 4.2 %collective-permute-start.12 = (bf16[192,128]{1,0:T(8,128)(2,1)S(1)}, bf16[192,128]{1,0:T(8,128)(2,1)S(1)}, u32[]{:S(2)}, u32[]{:S(2)}) collective-permute-start(bf16[192,128]{1,0:T(8,128)(2,1)S(1)} %shard_map.96.refs_7_.refs_2_), channel_id=1, source_target_pairs={{0,16},{16,0},{1,17},{17,1},{2,18},{18,2},{3,19},{19,3},{4,20},{20... | collective-permute-start | bytes 147464 | tf_op jit(solution)/shard_map/ppermute | solution.py:363
  45.7 3.3 %collective-permute-start.11 = (bf16[4,2,96,128]{3,2,1,0:T(8,128)(2,1)S(1)}, bf16[4,2,96,128]{3,2,1,0:T(8,128)(2,1)S(1)}, u32[]{:S(2)}, u32[]{:S(2)}) collective-permute-start(bf16[4,2,96,128]{3,2,1,0:T(8,128)(2,1)S(1)} %shard_map.97.early_ref), channel_id=1, source_target_pairs={{0,1},{1,0},{2,3},{3,2},{4,5},{5,4},{6,7},{7,6},{8,9},{9,8},{10,11... | collective-permute-start | bytes 589832 | tf_op jit(solution)/shard_map/ppermute | solution.py:363
  47.8 1.3 %collective-permute-start.13 = (bf16[2,96,128]{2,1,0:T(8,128)(2,1)S(1)}, bf16[2,96,128]{2,1,0:T(8,128)(2,1)S(1)}, u32[]{:S(2)}, u32[]{:S(2)}) collective-permute-start(bf16[2,96,128]{2,1,0:T(8,128)(2,1)S(1)} %shard_map.98.mine_ref), channel_id=1, source_target_pairs={{0,1},{1,0},{2,3},{3,2},{4,5},{5,4},{6,7},{7,6},{8,9},{9,8},{10,11... | collective-permute-start | bytes 147464 | tf_op jit(solution)/shard_map/ppermute | solution.py:363
